TPU v7x, 32 devices: a whole 2x2x4 slice. The times are simulated.
32 devices in a mesh: grp: 8 (over z, core), clu: 4 (over y, x).
Axes of the slice: x: 2, y: 2, z: 4, core: 2. Of those that a mesh axis runs over, the one named last changes fastest.
Arguments:
- strengths: bfloat16 [4096, 128], P(('grp', 'clu')), may hold values from -6 to 6
- adjoint_weights: bfloat16 [4096, 128], P(('grp', 'clu')), may hold values from -6 to 6
- kernels: bfloat16 [6144, 2, 128, 128], P(('grp', 'clu')), may hold values from -0.02734375 to 0.02734375
- target_ids: int32 [6144], P(('grp', 'clu')), may hold values from 0 to 31, as said below
- source_ids: int32 [6144], P(('grp', 'clu')), may hold values from 0 to 31, as said below
- live_slots: int32 [32], P(('grp', 'clu')), may hold values from 48 to 192, as said below
Outputs:
- potential: float32 [4096, 128], P(('grp', 'clu'))
- adjoint_field: float32 [4096, 128], P(('grp', 'clu'))
Inputs may be any that keep to these rules, and one draw needn't show every extreme that they name: `target_ids`: a slot's target block is one of the 4 blocks owned by the devices with the slot's grp index. `source_ids`: a slot's source block is owned by a device whose grp index equals that of the slot's device or differs from it by one. `live_slots`: some device uses all 192 slots.
All inputs are finite; a program needn't handle non-finite values.
Results may differ from a plain program's by a relative error of at most 0.0003.
Values may be sent and summed in bfloat16 or wider, within the bound.
No kernel may reach another device: no remote copies, remote signals or barrier semaphores. Data moves between devices by JAX's collectives and lax.ppermute only.
A program may use at most 128 MiB of HBM per device.

v0:
```python
import jax
import jax.numpy as jnp
from jax import lax
from jax.sharding import PartitionSpec as P


def with_halo(cells, sides, width):
    for axis, dim in sides:
        count = lax.axis_size(axis)
        ends = count - 1
        head = lax.slice_in_dim(cells, 0, width, axis=dim)
        tail = lax.slice_in_dim(cells, cells.shape[dim] - width, cells.shape[dim], axis=dim)
        cells = jnp.concatenate(
            [
                lax.ppermute(tail, axis, [(i, (i + 1) % count) for i in range(ends)]),
                cells,
                lax.ppermute(head, axis, [((i + 1) % count, i) for i in range(ends)]),
            ],
            axis=dim,
        )
    return cells


def shifted(value, axis, steps):
    count = lax.axis_size(axis)
    first, last = (max(0, -steps), min(count, count - steps))
    return lax.ppermute(value, axis, [(source, source + steps) for source in range(first, last)])


def complex_join(prod, half):
    real_part = prod[:, 0, :, :half] - prod[:, 1, :, half:]
    imag_part = prod[:, 0, :, half:] + prod[:, 1, :, :half]
    return jnp.concatenate([real_part, imag_part], axis=-1)


def local(strengths, adjoint_weights, kernels, target_ids, source_ids, live_slots):
    panels = kernels.shape[2]
    width = strengths.shape[1]
    half = width // 2
    blocks = strengths.shape[0] // panels
    slots = kernels.shape[0]
    group_index = lax.axis_index("grp")
    group_blocks = lax.axis_size("clu") * blocks
    live = (jnp.arange(slots, dtype=jnp.int32) < live_slots[0]).astype(jnp.float32)
    local_target = target_ids - group_index * group_blocks
    offset = source_ids // group_blocks - group_index + 1
    within = source_ids % group_blocks
    rims = with_halo(strengths, (("grp", 0),), blocks * panels)
    widened, group_mu = (
        lax.all_gather(rims, "clu", axis=0, tiled=True),
        lax.all_gather(adjoint_weights, "clu", axis=0, tiled=True),
    )
    source_index = within // blocks * (3 * blocks) + offset * blocks + within % blocks
    picked = jnp.take(widened.reshape(-1, panels, width), source_index, axis=0)
    forward = jnp.einsum("nkpq,nqc->nkpc", kernels, picked, preferred_element_type=jnp.float32)
    forward = complex_join(forward, half).reshape(slots, panels * width)
    weights_out = jnp.take(group_mu.reshape(group_blocks, panels, width), local_target, axis=0)
    backward = jnp.einsum(
        "nkpq,npc->nkqc", kernels, weights_out, preferred_element_type=jnp.float32
    )
    backward = complex_join(backward, half).reshape(slots, panels * width)
    target_table = (
        local_target[None, :] == jnp.arange(group_blocks, dtype=jnp.int32)[:, None]
    ).astype(jnp.float32) * live[None, :]
    potential = lax.psum_scatter(
        jnp.dot(
            target_table,
            forward,
            precision=lax.Precision.HIGHEST,
            preferred_element_type=jnp.float32,
        ),
        "clu",
        scatter_dimension=0,
        tiled=True,
    )
    row_match = (within[None, :] == jnp.arange(group_blocks, dtype=jnp.int32)[:, None]).astype(
        jnp.float32
    )
    side_match = (offset[None, :] == jnp.arange(3, dtype=jnp.int32)[:, None]).astype(
        jnp.float32
    ) * live[None, :]
    source_table = side_match[:, None, :] * row_match[None, :, :]
    partial_rows = jnp.einsum(
        "orn,nx->orx",
        source_table,
        backward,
        precision=lax.Precision.HIGHEST,
        preferred_element_type=jnp.float32,
    )
    from_upper = shifted(partial_rows[0], "grp", -1)
    from_lower = shifted(partial_rows[2], "grp", 1)
    adjoint = lax.psum_scatter(
        partial_rows[1] + from_upper + from_lower, "clu", scatter_dimension=0, tiled=True
    )
    return (potential.reshape(blocks * panels, width), adjoint.reshape(blocks * panels, width))


def solution(mesh):
    return jax.shard_map(
        local,
        mesh=mesh,
        in_specs=(
            P(("grp", "clu"), None),
            P(("grp", "clu"), None),
            P(("grp", "clu"), None, None, None),
            P(("grp", "clu")),
            P(("grp", "clu")),
            P(("grp", "clu")),
        ),
        out_specs=(P(("grp", "clu"), None), P(("grp", "clu"), None)),
        check_vma=False,
    )
```

profile of v0, /device:TPU:0, one launch (start us, length us, event | category | flops | bytes accessed | tf_op | source)
XLA Modules:
  0.0 268.1 jit_solution(13542739939517838041)
XLA Ops:
  7.2 2.4 collective-permute-start
  9.6 1.3 collective-permute-start.1
  11.6 9.5 %all_gather.7 = bf16[512,128]{1,0:T(8,128)(2,1)S(1)} all-gather(bf16[128,128]{1,0:T(8,128)(2,1)} %param.7), channel_id=1, replica_groups=mesh['grp'=8,'clu'=4] {'clu'}, dimensions={0}, use_global_device_ids=true | all-gather | bytes 163840 | tf_op jit(solution)/shard_map/all_gather | solution.py:51
  21.1 8.0 %gather_fusion.1 = bf16[192,128,128]{2,1,0:T(8,128)(2,1)} fusion(bf16[4,128,128]{2,1,0:T(8,128)(2,1)S(1)} %bitcast.66, s32[1024]{0:T(1024)S(1)} %pad_clamp_fusion), kind=kCustom, calls=%fused_computation.1 | custom fusion | bytes 12583680 | tf_op jit(solution)/shard_map/jit(_take)/gather | solution.py:57
  29.1 14.2 %convolution_bitcast_fusion = f32[192,2,128,128]{2,3,1,0:T(8,128)} fusion(bf16[192,2,128,128]{3,2,1,0:T(8,128)(2,1)} %param.8, bf16[192,128,128]{2,1,0:T(8,128)(2,1)} %gather_fusion.1, pred[192]{0:T(512)(128)(4,1)S(1)} %get-tuple-element.4), kind=kOutput, calls=%fused_computation.7 | convolution fusion | flops 1613758464 | bytes 44040384 | tf_op jit(solution)/shard_map/nkpq,npc->nkqc/dot_general | solution.py:58
  43.3 9.5 %fusion.3 = f32[192,128,64]{1,2,0:T(8,128)} fusion(f32[192,2,128,128]{2,3,1,0:T(8,128)} %convolution_bitcast_fusion), kind=kLoop, calls=%fused_computation.10 | loop fusion | flops 1572864 | bytes 18874368 | tf_op jit(solution)/shard_map/add | solution.py:32
  52.8 9.5 %fusion.5 = f32[192,128,64]{1,2,0:T(8,128)} fusion(f32[192,2,128,128]{2,3,1,0:T(8,128)} %convolution_bitcast_fusion), kind=kLoop, calls=%fused_computation.13 | loop fusion | flops 1572864 | bytes 18874368 | tf_op jit(solution)/shard_map/sub | solution.py:31
  62.3 11.3 %pad_maximum_fusion.1 = f32[192,128,128]{1,2,0:T(8,128)} fusion(f32[192,128,64]{1,2,0:T(8,128)} %fusion.3, f32[192,128,64]{1,2,0:T(8,128)} %fusion.5), kind=kLoop, calls=%fused_computation.6 | loop fusion | flops 3145728 | bytes 25165824 | tf_op jit(solution)/shard_map/concatenate | solution.py:33
  73.6 12.6 %copy.27 = f32[192,128,128]{2,1,0:T(8,128)} copy(f32[192,128,128]{1,2,0:T(8,128)} %pad_maximum_fusion.1) | data formatting | bytes 25165824 | tf_op jit(solution)/shard_map/concatenate | solution.py:33
  86.2 13.8 %reshape.119 = f32[192,16384,1]{1,0,2:T(8,128)} reshape(f32[192,128,128]{2,1,0:T(8,128)} %copy.27) | data formatting | bytes 25165824 | tf_op jit(solution)/shard_map/reshape | solution.py:61
  100.8 9.2 %fusion.19 = f32[3,4,16384]{2,1,0:T(4,128)S(1)} fusion(f32[192,16384,1]{1,0,2:T(8,128)} %reshape.119, f32[4,192]{1,0:T(4,128)S(1)} %fusion.25, f32[3,192]{1,0:T(4,128)S(1)} %fusion.24), kind=kOutput, calls=%fused_computation.35 | convolution fusion | flops 452987136 | bytes 13374720 | tf_op jit(solution)/shard_map/orn,nx->orx/dot_general | solution.py:83
  110.0 1.3 collective-permute-start.2
  111.3 3.3 %collective-permute-start.3 = (f32[4,16384]{1,0:T(4,128)S(1)}, f32[4,16384]{1,0:T(4,128)S(1)}, u32[]{:S(2)}, u32[]{:S(2)}) collective-permute-start(f32[4,16384]{1,0:T(4,128)S(1)} %get-tuple-element.11), channel_id=1, source_target_pairs={{0,4},{4,8},{8,12},{12,16},{16,20},{20,24},{24,28},{1,5},{5,9},{9,... | collective-permute-start | bytes 786440 | tf_op jit(solution)/shard_map/ppermute | solution.py:27
  114.7 9.1 %all_gather.6 = bf16[1536,128]{1,0:T(8,128)(2,1)S(1)} all-gather(bf16[384,128]{1,0:T(8,128)(2,1)S(1)} %pad_maximum_fusion.2), channel_id=1, replica_groups=mesh['grp'=8,'clu'=4] {'clu'}, dimensions={0}, use_global_device_ids=true | all-gather | bytes 491520 | tf_op jit(solution)/shard_map/all_gather | solution.py:50
  123.7 8.0 %gather_fusion = bf16[192,128,128]{2,1,0:T(8,128)(2,1)} fusion(bf16[12,128,128]{2,1,0:T(8,128)(2,1)S(1)} %bitcast.67, s32[1024]{0:T(1024)S(1)} %pad_clamp_fusion.1), kind=kCustom, calls=%fused_computation | custom fusion | bytes 12583680 | tf_op jit(solution)/shard_map/jit(_take)/gather | solution.py:54
  131.8 16.4 %convolution_bitcast_fusion.1 = f32[192,2,128,128]{2,3,1,0:T(8,128)} fusion(bf16[192,2,128,128]{3,2,1,0:T(8,128)(2,1)} %param.8, bf16[192,128,128]{2,1,0:T(8,128)(2,1)} %gather_fusion, pred[192]{0:T(512)(128)(4,1)S(1)} %get-tuple-element.6), kind=kOutput, calls=%fused_computation.8 | convolution fusion | flops 1613758464 | bytes 44040384 | tf_op jit(solution)/shard_map/nkpq,nqc->nkpc/dot_general | solution.py:55
  148.2 9.5 %fusion.6 = f32[192,128,64]{1,2,0:T(8,128)} fusion(f32[192,2,128,128]{2,3,1,0:T(8,128)} %convolution_bitcast_fusion.1), kind=kLoop, calls=%fused_computation.16 | loop fusion | flops 1572864 | bytes 18874368 | tf_op jit(solution)/shard_map/add | solution.py:32
  157.7 9.5 %fusion.8 = f32[192,128,64]{1,2,0:T(8,128)} fusion(f32[192,2,128,128]{2,3,1,0:T(8,128)} %convolution_bitcast_fusion.1), kind=kLoop, calls=%fused_computation.19 | loop fusion | flops 1572864 | bytes 18874368 | tf_op jit(solution)/shard_map/sub | solution.py:31
  167.2 11.3 %pad_maximum_fusion = f32[192,128,128]{1,2,0:T(8,128)} fusion(f32[192,128,64]{1,2,0:T(8,128)} %fusion.6, f32[192,128,64]{1,2,0:T(8,128)} %fusion.8), kind=kLoop, calls=%fused_computation.5 | loop fusion | flops 3145728 | bytes 25165824 | tf_op jit(solution)/shard_map/concatenate | solution.py:33
  178.5 12.6 %copy.23 = f32[192,128,128]{2,1,0:T(8,128)} copy(f32[192,128,128]{1,2,0:T(8,128)} %pad_maximum_fusion) | data formatting | bytes 25165824 | tf_op jit(solution)/shard_map/concatenate | solution.py:33
  191.1 18.4 %fusion = f32[4,16384]{1,0:T(4,128)} fusion(f32[24,8,128,128]{3,2,1,0:T(8,128)} %bitcast.68, f32[192]{0:T(256)S(1)} %compare_convert_fusion, s32[192]{0:T(256)S(1)} %get-tuple-element.5), kind=kOutput, calls=%fused_computation.2 | convolution fusion | flops 150996480 | bytes 12846592 | tf_op jit(solution)/shard_map/dot_general | solution.py:66
  209.6 0.8 fusion.18
  211.0 47.9 %all-reduce.5.cloned.1.call-done = (f32[4,16384]{1,0:T(4,128)}, f32[4,16384]{1,0:T(4,128)}) async-done(((f32[4,16384]{1,0:T(4,128)}, f32[4,16384]{1,0:T(4,128)}), (f32[4,16384]{1,0:T(4,128)}, f32[4,16384]{1,0:T(4,128)})) %all-reduce.5.cloned.1.call-update) | async-done | bytes 524304
  258.9 2.4 constant_dynamic-slice_fusion
  (23 shorter events, 1.4 us)
Async XLA Ops:
  7.2 251.7 %all-reduce.5.cloned.1.call-start = ((), (), s32[]{:S(2)}) async-start(), calls=%async_computation | async-start | bytes 1048576
  7.2 107.4 %collective-permute-start = (bf16[128,128]{1,0:T(8,128)(2,1)}, bf16[128,128]{1,0:T(8,128)(2,1)S(1)}, u32[]{:S(2)}, u32[]{:S(2)}) collective-permute-start(bf16[128,128]{1,0:T(8,128)(2,1)} %param.6), channel_id=1, source_target_pairs={{0,4},{4,8},{8,12},{12,16},{16,20},{20,24},{24,28},{1,5},{5,9},{9,... | collective-permute-start | bytes 98312 | tf_op jit(solution)/shard_map/ppermute | solution.py:15
  9.6 105.1 %collective-permute-start.1 = (bf16[128,128]{1,0:T(8,128)(2,1)}, bf16[128,128]{1,0:T(8,128)(2,1)S(1)}, u32[]{:S(2)}, u32[]{:S(2)}) collective-permute-start(bf16[128,128]{1,0:T(8,128)(2,1)} %param.6), channel_id=1, source_target_pairs={{4,0},{8,4},{12,8},{16,12},{20,16},{24,20},{28,24},{5,1},{9,5},{13... | collective-permute-start | bytes 98312 | tf_op jit(solution)/shard_map/ppermute | solution.py:17
  86.2 13.8 %copy-start.1 = (s32[192]{0:T(256)S(1)}, s32[192]{0:T(256)}, u32[]{:S(2)}) copy-start(s32[192]{0:T(256)} %param.10) | copy-start | bytes 2308
  100.8 13.9 %copy-start = (bf16[128,128]{1,0:T(8,128)(2,1)S(1)}, bf16[128,128]{1,0:T(8,128)(2,1)}, u32[]{:S(2)}) copy-start(bf16[128,128]{1,0:T(8,128)(2,1)} %param.6) | copy-start | bytes 98308
  110.0 99.5 %collective-permute-start.2 = (f32[4,16384]{1,0:T(4,128)S(1)}, f32[4,16384]{1,0:T(4,128)S(1)}, u32[]{:S(2)}, u32[]{:S(2)}) collective-permute-start(f32[4,16384]{1,0:T(4,128)S(1)} %get-tuple-element.10), channel_id=1, source_target_pairs={{4,0},{8,4},{12,8},{16,12},{20,16},{24,20},{28,24},{5,1},{9,5},{13... | collective-permute-start | bytes 786440 | tf_op jit(solution)/shard_map/ppermute | solution.py:27
  111.3 98.2 %collective-permute-start.3 = (f32[4,16384]{1,0:T(4,128)S(1)}, f32[4,16384]{1,0:T(4,128)S(1)}, u32[]{:S(2)}, u32[]{:S(2)}) collective-permute-start(f32[4,16384]{1,0:T(4,128)S(1)} %get-tuple-element.11), channel_id=1, source_target_pairs={{0,4},{4,8},{8,12},{12,16},{16,20},{20,24},{24,28},{1,5},{5,9},{9,... | collective-permute-start | bytes 786440 | tf_op jit(solution)/shard_map/ppermute | solution.py:27
  191.1 19.3 %copy-start.2 = (u32[32]{0:T(128)S(1)}, u32[32]{0:T(128)}, u32[]{:S(2)}) copy-start(u32[32]{0:T(128)} %constant.86) | copy-start | bytes 388
Sparse Core Ops, SparseCore 0:
  210.5 48.3 all-reduce.4
where the time goes:
time: 269 us; the launch traced here: 268 us
  other arithmetic  62.3 us (23%)
  matrix products  58.2 us (22%)
  local copies, waits for them, and re-layouts  58.1 us (22%)
  waiting for transfers between devices  47.9 us (18%)
  blocking collectives  18.5 us (7%)
  between operations  14.8 us (6%)
  starting transfers between devices  8.26 us (3%)
    unnamed x2, waiting for transfers between devices  47.9 us
    concatenate x2, local copies, waits for them, and re-layouts, complex_join(): return jnp.concatenate([real_part, imag_part], axis=-1)  25.2 us
    concatenate x2, other arithmetic, complex_join(): return jnp.concatenate([real_part, imag_part], axis=-1)  22.6 us
    sub x2, other arithmetic, complex_join(): real_part = prod[:, 0, :, :half] - prod[:, 1, :, half:]  19.1 us
    add x2, other arithmetic, complex_join(): imag_part = prod[:, 0, :, half:] + prod[:, 1, :, :half]  19 us
    dot_general x1, matrix products, local(): jnp.dot(target_table, forward, precision=lax.Precision.HIGHEST, preferred...  18.4 us
    dot_general x1, matrix products, local(): jnp.einsum('nkpq,nqc->nkpc', kernels, picked, preferred_element_type=jnp....  16.4 us
    dot_general x1, matrix products, local(): jnp.einsum('nkpq,npc->nkqc', kernels, weights_out, preferred_element_type...  14.2 us
  transfers between devices with their start and end apart: 5, of which 1 were waited for; matrix products, arithmetic and copies ran while one was open for 65% of the time, Pallas kernels for 0%

commit v1 on v0

v1 whole, which is shorter than its diff:
```python
import functools

import jax
import jax.numpy as jnp
from jax import lax
from jax.experimental import pallas as pl
from jax.experimental.pallas import tpu as pltpu
from jax.sharding import PartitionSpec as P

VMEM_BYTES = 50 * 1024 * 1024


def shifted(value, axis, steps):
    count = lax.axis_size(axis)
    first, last = (max(0, -steps), min(count, count - steps))
    return lax.ppermute(value, axis, [(source, source + steps) for source in range(first, last)])


def to_partner(value, axis, step):
    count = lax.axis_size(axis)
    return lax.ppermute(value, axis, [(i, i ^ step) for i in range(count)])


def turned(block):
    half = block.shape[1] // 2
    wide = pltpu.roll(block.astype(jnp.float32), half, axis=1)
    lane = lax.broadcasted_iota(jnp.int32, wide.shape, 1)
    return jnp.where(lane < half, -wide, wide).astype(block.dtype)


def turned_rows(block):
    half = block.shape[0] // 2
    return jnp.concatenate([-block[half:], block[:half]], axis=0)


def slot_place(target_ref, source_ref, slot, blocks, clusters):
    group, me = lax.axis_index("grp"), lax.axis_index("clu")
    group_blocks = blocks * clusters

    def relative(within):
        return ((within // blocks) ^ me) * blocks + within % blocks

    target = relative(target_ref[slot] - group * group_blocks)
    source = source_ref[slot] - (group - 1) * group_blocks
    return target, source // group_blocks * group_blocks + relative(source % group_blocks)


def start_fetch(live, chunk, kernels_ref, held, sems):
    for c in range(held.shape[0] // chunk):
        rows = pl.ds(c * chunk, chunk)

        @pl.when(c * chunk < live)
        def _():
            pltpu.make_async_copy(kernels_ref.at[rows], held.at[rows], sems.at[c]).start()


def each_slot(live, chunk, kernels_ref, held, sems, work):
    @pl.loop(0, pl.cdiv(live, chunk))
    def _(c):
        rows = pl.ds(c * chunk, chunk)
        pltpu.make_async_copy(kernels_ref.at[rows], held.at[rows], sems.at[c]).wait()

        @pl.loop(c * chunk, jnp.minimum((c + 1) * chunk, live))
        def _(slot):
            work(slot)


def combine_kernel(blocks, clusters, chunk, live_ref, target_ref, source_ref, kernels_ref, out_ref, held, total, sems):
    live = live_ref[0]
    sources = 3 * blocks * clusters
    start_fetch(live, chunk, kernels_ref, held, sems)

    @pl.loop(0, total.shape[0])
    def _(pair):
        total[pair] = jnp.zeros(total.shape[1:], total.dtype)

    def add(slot):
        target, source = slot_place(target_ref, source_ref, slot, blocks, clusters)
        pair = target * sources + source
        total[pair] += held[slot].reshape(total.shape[1:]).astype(jnp.float32)

    each_slot(live, chunk, kernels_ref, held, sems, add)

    @pl.loop(0, total.shape[0])
    def _(pair):
        value = total[pair]
        high = value.astype(jnp.bfloat16)
        out_ref[0, pair] = high
        out_ref[1, pair] = (value - high.astype(jnp.float32)).astype(jnp.bfloat16)


def weights_across(gathered, blocks, panels, part):
    across = []
    for ref in gathered:
        for b in range(blocks):
            block = ref[pl.ds((part * blocks + b) * panels, panels), :].astype(jnp.float32).T
            across += [block, turned_rows(block)]
    return jnp.concatenate(across, axis=1).astype(jnp.bfloat16)


def adjoint_of(pairs_ref, weights, sources, first, count, out_ref):
    targets = pairs_ref.shape[1] // sources
    width = pairs_ref.shape[3]
    both = jnp.concatenate([weights, weights], axis=1)
    step = 2 if count % 2 == 0 else 1
    for i in range(0, count, step):
        columns = []
        for j in range(step):
            tiles = [pairs_ref[h, t * sources + first + i + j] for h in range(2) for t in range(targets)]
            columns.append(jnp.concatenate(tiles, axis=0))
        rhs = jnp.concatenate(columns, axis=1)
        product = jnp.dot(both, rhs, preferred_element_type=jnp.float32)
        for j in range(step):
            out_ref[i + j] = product[:, j * width : (j + 1) * width]


def outer_kernel(blocks, clusters, panels, pairs_ref, *refs):
    gathered, (lower_ref, upper_ref) = refs[:clusters], refs[clusters:]
    group_blocks = blocks * clusters
    weights = weights_across(gathered, blocks, panels, 3)
    adjoint_of(pairs_ref, weights, 3 * group_blocks, 0, group_blocks, lower_ref)
    adjoint_of(pairs_ref, weights, 3 * group_blocks, 2 * group_blocks, group_blocks, upper_ref)


def inner_kernel(blocks, clusters, panels, pairs_ref, *refs):
    gathered, (potential_ref, middle_ref) = refs[:clusters], refs[clusters:]
    group_blocks = blocks * clusters
    sources = 3 * group_blocks
    weights = weights_across(gathered, blocks, panels, 3)
    adjoint_of(pairs_ref, weights, sources, group_blocks, group_blocks, middle_ref)
    stack = []
    for offset in range(3):
        for ref in gathered:
            for b in range(blocks):
                block = ref[pl.ds((offset * blocks + b) * panels, panels), :]
                stack += [block, turned(block)]
    stack = jnp.concatenate(stack, axis=0)
    for t in range(group_blocks):
        halves = []
        for h in range(2):
            tiles = []
            for s in range(sources):
                tiles += [pairs_ref[h, t * sources + s, :panels], pairs_ref[h, t * sources + s, panels:]]
            halves.append(jnp.concatenate(tiles, axis=1))
        product = jnp.dot(jnp.concatenate(halves, axis=0), stack, preferred_element_type=jnp.float32)
        potential_ref[t] = product[:panels] + product[panels:]


def slots_kernel(blocks, clusters, panels, chunk, live_ref, target_ref, source_ref, kernels_ref, *refs):
    gathered, rest = refs[:clusters], refs[clusters:]
    potential_ref, adjoint_ref, held, stack, across, sems = rest
    live = live_ref[0]
    group_blocks = blocks * clusters
    start_fetch(live, chunk, kernels_ref, held, sems)
    potential_ref[...] = jnp.zeros(potential_ref.shape, potential_ref.dtype)
    adjoint_ref[...] = jnp.zeros(adjoint_ref.shape, adjoint_ref.dtype)
    for k, ref in enumerate(gathered):
        for b in range(blocks):
            for offset in range(3):
                block = ref[pl.ds((offset * blocks + b) * panels, panels), :]
                place = offset * group_blocks + k * blocks + b
                stack[place] = jnp.concatenate([block, turned(block)], axis=0)
            block = ref[pl.ds((3 * blocks + b) * panels, panels), :].astype(jnp.float32).T
            wide = jnp.concatenate([block, turned_rows(block)], axis=1)
            across[k * blocks + b] = wide.astype(jnp.bfloat16)

    def work(slot):
        target, source = slot_place(target_ref, source_ref, slot, blocks, clusters)
        real, imag = held[slot, 0], held[slot, 1]
        potential_ref[target] += jnp.dot(
            jnp.concatenate([real, imag], axis=1), stack[source], preferred_element_type=jnp.float32
        )
        adjoint_ref[source] += jnp.dot(
            across[target], jnp.concatenate([real, imag], axis=0), preferred_element_type=jnp.float32
        )

    each_slot(live, chunk, kernels_ref, held, sems, work)


def finish_kernel(blocks, *refs):
    *parts, potential_ref, adjoint_ref = refs
    total = parts[0][...]
    for part in parts[1:]:
        total = total + part[...]
    panels = total.shape[1]
    for b in range(blocks):
        potential_ref[b * panels : (b + 1) * panels] = total[b]
        adjoint_ref[b * panels : (b + 1) * panels] = total[blocks + b].T


def local(strengths, adjoint_weights, kernels, target_ids, source_ids, live_slots):
    slots, _, panels, _ = kernels.shape
    width = strengths.shape[1]
    blocks = strengths.shape[0] // panels
    clusters = lax.axis_size("clu")
    group_blocks = clusters * blocks
    sources = 3 * group_blocks
    pairs = group_blocks * sources
    chunk = 8 if slots % 8 == 0 else 1
    in_vmem, in_smem = (pl.BlockSpec(memory_space=m) for m in (pltpu.VMEM, pltpu.SMEM))
    params = pltpu.CompilerParams(vmem_limit_bytes=VMEM_BYTES)
    f32, bf16 = jnp.float32, jnp.bfloat16
    slot_args = (live_slots, target_ids, source_ids, kernels)
    slot_specs = [in_smem] * 3 + [pl.BlockSpec(memory_space=pl.ANY)]
    fetch = [pltpu.VMEM(kernels.shape, bf16), pltpu.SemaphoreType.DMA((slots // chunk,))]

    from_lower, from_upper = shifted(strengths, "grp", 1), shifted(strengths, "grp", -1)
    mine = jnp.concatenate([from_lower, strengths, from_upper, adjoint_weights], axis=0)
    gathered = [mine] + [to_partner(mine, "clu", k) for k in range(1, clusters)]

    block_sums = jax.ShapeDtypeStruct((group_blocks, panels, width), f32)
    if pairs <= slots:
        pair_blocks = pl.pallas_call(
            functools.partial(combine_kernel, blocks, clusters, chunk),
            out_shape=jax.ShapeDtypeStruct((2, pairs, 2 * panels, panels), bf16),
            in_specs=slot_specs,
            out_specs=in_vmem,
            scratch_shapes=[fetch[0], pltpu.VMEM((pairs, 2 * panels, panels), f32), fetch[1]],
            compiler_params=params,
            cost_estimate=pl.CostEstimate(
                flops=slots * 2 * panels * panels, bytes_accessed=2 * kernels.size, transcendentals=0
            ),
        )(*slot_args)
        lower, upper = pl.pallas_call(
            functools.partial(outer_kernel, blocks, clusters, panels),
            out_shape=(block_sums, block_sums),
            in_specs=[in_vmem] * (1 + clusters),
            out_specs=(in_vmem, in_vmem),
            compiler_params=params,
        )(pair_blocks, *gathered)
        potential, middle = pl.pallas_call(
            functools.partial(inner_kernel, blocks, clusters, panels),
            out_shape=(block_sums, block_sums),
            in_specs=[in_vmem] * (1 + clusters),
            out_specs=(in_vmem, in_vmem),
            compiler_params=params,
        )(pair_blocks, *gathered)
    else:
        potential, adjoint = pl.pallas_call(
            functools.partial(slots_kernel, blocks, clusters, panels, chunk),
            out_shape=(block_sums, jax.ShapeDtypeStruct((sources, width, panels), f32)),
            in_specs=slot_specs + [in_vmem] * clusters,
            out_specs=(in_vmem, in_vmem),
            scratch_shapes=[
                fetch[0],
                pltpu.VMEM((sources, 2 * panels, width), bf16),
                pltpu.VMEM((group_blocks, width, 2 * panels), bf16),
                fetch[1],
            ],
            compiler_params=params,
        )(*slot_args, *gathered)
        lower, middle, upper = (adjoint[i * group_blocks : (i + 1) * group_blocks] for i in range(3))

    adjoint = middle + shifted(lower, "grp", -1) + shifted(upper, "grp", 1)
    parts = []
    for k in range(clusters):
        rows = slice(k * blocks, (k + 1) * blocks)
        part = jnp.concatenate([potential[rows], adjoint[rows]], axis=0)
        parts.append(to_partner(part, "clu", k) if k else part)
    out = jax.ShapeDtypeStruct((blocks * panels, width), f32)
    return tuple(
        pl.pallas_call(
            functools.partial(finish_kernel, blocks),
            out_shape=(out, out),
            in_specs=[in_vmem] * clusters,
            out_specs=(in_vmem, in_vmem),
            compiler_params=params,
        )(*parts)
    )


def solution(mesh):
    return jax.shard_map(
        local,
        mesh=mesh,
        in_specs=(
            P(("grp", "clu"), None),
            P(("grp", "clu"), None),
            P(("grp", "clu"), None, None, None),
            P(("grp", "clu")),
            P(("grp", "clu")),
            P(("grp", "clu")),
        ),
        out_specs=(P(("grp", "clu"), None), P(("grp", "clu"), None)),
        check_vma=False,
    )
```

time: 269 us -> 50.7 us (0.19)
  other arithmetic: 62.3 us -> 0.11 us
  matrix products: 58.2 us -> 0 us
  local copies, waits for them, and re-layouts: 58.1 us -> 2.94 us
  waiting for transfers between devices: 47.9 us -> 10.3 us
  blocking collectives: 18.5 us -> 0 us
  Pallas kernels: 0 us -> 17.8 us
  between operations: 14.8 us -> 1.44 us
  starting transfers between devices: 8.26 us -> 17.8 us
    dot_general x4 -> x0, matrix products: 58.2 us -> none  [the longest x1 18.4 us: local(): jnp.dot(target_table, forward, precision=lax.Precision.HIGHEST, preferred...]
    unnamed x2 -> x0, waiting for transfers between devices: 47.9 us -> none
    concatenate x2 -> x1, local copies, waits for them, and re-layouts: 25.2 us -> 0.77 us  [local(): jnp.concatenate([from_lower, strengths, from_upper, adjoint_weights], axi...]
    concatenate x3 -> x4, other arithmetic: 22.6 us -> 0.07 us  [local(): part = jnp.concatenate([potential[rows], adjoint[rows]], axis=0)]
    add x3 -> x1, other arithmetic: 19.8 us -> 0.04 us  [local(): adjoint = middle + shifted(lower, 'grp', -1) + shifted(upper, 'grp', 1)]
    sub x2 -> x0, other arithmetic: 19.1 us -> none  [complex_join(): real_part = prod[:, 0, :, :half] - prod[:, 1, :, half:]]
    all_gather x2 -> x0, blocking collectives: 18.5 us -> none  [the longest x1 9.5 us: local(): lax.all_gather(adjoint_weights, 'clu', axis=0, tiled=True)]
    pallas_call x0 -> x4, Pallas kernels: none -> 17.8 us  [the longest x1 8.54 us: local(): pl.pallas_call(functools.partial(combine_kernel, blocks, clusters, chunk)...]
  transfers between devices with their start and end apart: 5 -> 10, of which waited for: 1 -> 4; matrix products, arithmetic and copies ran while one was open for 65% -> 2% of each run, Pallas kernels for 0% -> 27%
where the time goes in v1:
time: 50.7 us; the launch traced here: 50.3 us
  starting transfers between devices  17.8 us (35%)
  Pallas kernels  17.8 us (35%)
  waiting for transfers between devices  10.3 us (20%)
  local copies, waits for them, and re-layouts  2.94 us (6%)
  between operations  1.44 us (3%)
    ppermute x4, starting transfers between devices, shifted(): lax.ppermute(value, axis, [(source, source + steps) for source in range(f...  10 us
    pallas_call x1, Pallas kernels, local(): pl.pallas_call(functools.partial(combine_kernel, blocks, clusters, chunk)...  8.54 us
    ppermute x6, starting transfers between devices, to_partner(): return lax.ppermute(value, axis, [(i, i ^ step) for i in range(count)])  7.73 us
    ppermute x6, waiting for transfers between devices, to_partner(): return lax.ppermute(value, axis, [(i, i ^ step) for i in range(count)])  6.91 us
    pallas_call x1, Pallas kernels, local(): pl.pallas_call(functools.partial(inner_kernel, blocks, clusters, panels),...  4.93 us
    pallas_call x1, Pallas kernels, local(): pl.pallas_call(functools.partial(outer_kernel, blocks, clusters, panels),...  3.55 us
    ppermute x4, waiting for transfers between devices, shifted(): lax.ppermute(value, axis, [(source, source + steps) for source in range(f...  3.42 us
    unnamed x7, local copies, waits for them, and re-layouts  2.13 us
  transfers between devices with their start and end apart: 10, of which 4 were waited for; matrix products, arithmetic and copies ran while one was open for 2% of the time, Pallas kernels for 27%

profile of v1, /device:TPU:0, one launch (start us, length us, event | category | flops | bytes accessed | tf_op | source)
XLA Modules:
  0.0 50.3 jit_solution(6030900254907014330)
XLA Ops:
  0.6 2.4 %collective-permute-start = (bf16[128,128]{1,0:T(8,128)(2,1)}, bf16[128,128]{1,0:T(8,128)(2,1)S(1)}, u32[]{:S(2)}, u32[]{:S(2)}) collective-permute-start(bf16[128,128]{1,0:T(8,128)(2,1)} %param.6), channel_id=1, source_target_pairs={{0,4},{4,8},{8,12},{12,16},{16,20},{20,24},{24,28},{1,5},{5,9},{9,... | collective-permute-start | bytes 98312 | tf_op jit(solution)/shard_map/ppermute | solution.py:16
  3.0 1.3 %collective-permute-start.1 = (bf16[128,128]{1,0:T(8,128)(2,1)}, bf16[128,128]{1,0:T(8,128)(2,1)S(1)}, u32[]{:S(2)}, u32[]{:S(2)}) collective-permute-start(bf16[128,128]{1,0:T(8,128)(2,1)} %param.6), channel_id=1, source_target_pairs={{4,0},{8,4},{12,8},{16,12},{20,16},{24,20},{28,24},{5,1},{9,5},{13... | collective-permute-start | bytes 98312 | tf_op jit(solution)/shard_map/ppermute | solution.py:16
  4.3 0.0 collective-permute-done
  4.3 0.8 %constant_dynamic-update-slice_fusion.2 = bf16[512,128]{1,0:T(8,128)(2,1)S(1)} fusion(bf16[512,128]{1,0:T(8,128)(2,1)S(1)} %constant_dynamic-update-slice_fusion.3, bf16[128,128]{1,0:T(8,128)(2,1)} %param.6), kind=kLoop, calls=%fused_computation.7 | loop fusion | bytes 65536
  5.1 3.4 %collective-permute-done.1 = bf16[128,128]{1,0:T(8,128)(2,1)S(1)} collective-permute-done((bf16[128,128]{1,0:T(8,128)(2,1)}, bf16[128,128]{1,0:T(8,128)(2,1)S(1)}, u32[]{:S(2)}, u32[]{:S(2)}) %collective-permute-start.1) | collective-permute-done | bytes 32800 | tf_op jit(solution)/shard_map/ppermute | solution.py:16
  8.5 0.8 %constant_dynamic-update-slice_fusion.refs_0_ = bf16[512,128]{1,0:T(8,128)(2,1)S(1)} fusion(bf16[512,128]{1,0:T(8,128)(2,1)S(1)} %constant_dynamic-update-slice_fusion.1, bf16[128,128]{1,0:T(8,128)(2,1)} %param.7), kind=kLoop, calls=%fused_computation.5 | loop fusion | bytes 65536 | tf_op jit(solution)/shard_map/concatenate | solution.py:208
  9.3 2.4 %collective-permute-start.4 = (bf16[512,128]{1,0:T(8,128)(2,1)S(1)}, bf16[512,128]{1,0:T(8,128)(2,1)S(1)}, u32[]{:S(2)}, u32[]{:S(2)}) collective-permute-start(bf16[512,128]{1,0:T(8,128)(2,1)S(1)} %constant_dynamic-update-slice_fusion.refs_0_), channel_id=1, source_target_pairs={{0,3},{1,2},{2,1},{3,0},{4,7},{5,6},{6,5},{7,4},{8,11},{9,10},{10,... | collective-permute-start | bytes 393224 | tf_op jit(solution)/shard_map/ppermute | solution.py:21
  11.7 0.5 %collective-permute-start.3 = (bf16[512,128]{1,0:T(8,128)(2,1)S(1)}, bf16[512,128]{1,0:T(8,128)(2,1)S(1)}, u32[]{:S(2)}, u32[]{:S(2)}) collective-permute-start(bf16[512,128]{1,0:T(8,128)(2,1)S(1)} %constant_dynamic-update-slice_fusion.refs_0_), channel_id=1, source_target_pairs={{0,2},{1,3},{2,0},{3,1},{4,6},{5,7},{6,4},{7,5},{8,10},{9,11},{10,... | collective-permute-start | bytes 393224 | tf_op jit(solution)/shard_map/ppermute | solution.py:21
  12.2 0.5 %collective-permute-start.2 = (bf16[512,128]{1,0:T(8,128)(2,1)S(1)}, bf16[512,128]{1,0:T(8,128)(2,1)S(1)}, u32[]{:S(2)}, u32[]{:S(2)}) collective-permute-start(bf16[512,128]{1,0:T(8,128)(2,1)S(1)} %constant_dynamic-update-slice_fusion.refs_0_), channel_id=1, source_target_pairs={{0,1},{1,0},{2,3},{3,2},{4,5},{5,4},{6,7},{7,6},{8,9},{9,8},{10,11... | collective-permute-start | bytes 393224 | tf_op jit(solution)/shard_map/ppermute | solution.py:21
  13.4 0.0 copy-start
  13.4 0.7 %copy-done = s32[192]{0:T(256)S(1)} copy-done((s32[192]{0:T(256)S(1)}, s32[192]{0:T(256)}, u32[]{:S(2)}) %copy-start) | copy-done | bytes 792
  14.1 0.7 %copy-done.1 = s32[192]{0:T(256)S(1)} copy-done((s32[192]{0:T(256)S(1)}, s32[192]{0:T(256)}, u32[]{:S(2)}) %copy-start.1) | copy-done | bytes 792
  14.8 8.5 %shard_map.77.pairs_ref = bf16[2,48,256,128]{3,2,1,0:T(8,128)(2,1)} custom-call(s32[1]{0:T(128)S(6)} %copy.11.live_ref, s32[192]{0:T(256)S(1)} %copy-done, s32[192]{0:T(256)S(1)} %copy-done.1, bf16[192,2,128,128]{3,2,1,0:T(8,128)(2,1)} %kernels_ref.1), custom_call_target="tpu_custom_call" | custom-call | flops 6291456 | bytes 12582912 | tf_op jit(solution)/shard_map/pallas_call | solution.py:213
  23.4 3.6 %shard_map.79 = (f32[4,128,128]{2,1,0:T(8,128)S(1)}, f32[4,128,128]{2,1,0:T(8,128)S(1)}) custom-call(bf16[2,48,256,128]{3,2,1,0:T(8,128)(2,1)} %shard_map.77.pairs_ref, bf16[512,128]{1,0:T(8,128)(2,1)S(1)} %constant_dynamic-update-slice_fusion.refs_0_, bf16[512,128]{1,0:T(8,128)(2,1)S(1)} %collective-permute-done.2.refs_1_, ...), custom_call_target="tpu_custom_call" | custom-call | tf_op jit(solution)/shard_map/pallas_call | solution.py:224
  26.9 1.3 %collective-permute-start.5 = (f32[4,128,128]{2,1,0:T(8,128)S(1)}, f32[4,128,128]{2,1,0:T(8,128)S(1)}, u32[]{:S(2)}, u32[]{:S(2)}) collective-permute-start(f32[4,128,128]{2,1,0:T(8,128)S(1)} %get-tuple-element.8), channel_id=1, source_target_pairs={{4,0},{8,4},{12,8},{16,12},{20,16},{24,20},{28,24},{5,1},{9,5},{13... | collective-permute-start | bytes 786440 | tf_op jit(solution)/shard_map/ppermute | solution.py:16
  28.2 5.1 %collective-permute-start.6 = (f32[4,128,128]{2,1,0:T(8,128)S(1)}, f32[4,128,128]{2,1,0:T(8,128)S(1)}, u32[]{:S(2)}, u32[]{:S(2)}) collective-permute-start(f32[4,128,128]{2,1,0:T(8,128)S(1)} %get-tuple-element.9), channel_id=1, source_target_pairs={{0,4},{4,8},{8,12},{12,16},{16,20},{20,24},{24,28},{1,5},{5,9},{9,... | collective-permute-start | bytes 786440 | tf_op jit(solution)/shard_map/ppermute | solution.py:16
  33.3 4.9 %shard_map.78 = (f32[4,128,128]{2,1,0:T(8,128)S(1)}, f32[4,128,128]{2,1,0:T(8,128)S(1)}) custom-call(bf16[2,48,256,128]{3,2,1,0:T(8,128)(2,1)} %shard_map.77.pairs_ref, bf16[512,128]{1,0:T(8,128)(2,1)S(1)} %constant_dynamic-update-slice_fusion.refs_0_, bf16[512,128]{1,0:T(8,128)(2,1)S(1)} %collective-permute-done.2.refs_1_, ...), custom_call_target="tpu_custom_call" | custom-call | tf_op jit(solution)/shard_map/pallas_call | solution.py:231
  38.4 1.2 %collective-permute-start.7 = (f32[2,128,128]{2,1,0:T(8,128)S(1)}, f32[2,128,128]{2,1,0:T(8,128)S(1)}, u32[]{:S(2)}, u32[]{:S(2)}) collective-permute-start(f32[2,128,128]{2,1,0:T(8,128)S(1)} %pad_maximum_fusion.1), channel_id=1, source_target_pairs={{0,1},{1,0},{2,3},{3,2},{4,5},{5,4},{6,7},{7,6},{8,9},{9,8},{10,11... | collective-permute-start | bytes 393224 | tf_op jit(solution)/shard_map/ppermute | solution.py:21
  39.6 3.0 %collective-permute-start.8 = (f32[2,128,128]{2,1,0:T(8,128)S(1)}, f32[2,128,128]{2,1,0:T(8,128)S(1)}, u32[]{:S(2)}, u32[]{:S(2)}) collective-permute-start(f32[2,128,128]{2,1,0:T(8,128)S(1)} %pad_maximum_fusion.2), channel_id=1, source_target_pairs={{0,2},{1,3},{2,0},{3,1},{4,6},{5,7},{6,4},{7,5},{8,10},{9,11},{10,... | collective-permute-start | bytes 393224 | tf_op jit(solution)/shard_map/ppermute | solution.py:21
  42.6 0.1 collective-permute-start.9
  42.7 1.4 %collective-permute-done.7.refs_1_ = f32[2,128,128]{2,1,0:T(8,128)S(1)} collective-permute-done((f32[2,128,128]{2,1,0:T(8,128)S(1)}, f32[2,128,128]{2,1,0:T(8,128)S(1)}, u32[]{:S(2)}, u32[]{:S(2)}) %collective-permute-start.7) | collective-permute-done | bytes 131104 | tf_op jit(solution)/shard_map/ppermute | solution.py:21
  44.1 4.5 %collective-permute-done.8.refs_2_ = f32[2,128,128]{2,1,0:T(8,128)S(1)} collective-permute-done((f32[2,128,128]{2,1,0:T(8,128)S(1)}, f32[2,128,128]{2,1,0:T(8,128)S(1)}, u32[]{:S(2)}, u32[]{:S(2)}) %collective-permute-start.8) | collective-permute-done | bytes 131104 | tf_op jit(solution)/shard_map/ppermute | solution.py:21
  48.6 1.0 %collective-permute-done.9.refs_3_ = f32[2,128,128]{2,1,0:T(8,128)S(1)} collective-permute-done((f32[2,128,128]{2,1,0:T(8,128)S(1)}, f32[2,128,128]{2,1,0:T(8,128)S(1)}, u32[]{:S(2)}, u32[]{:S(2)}) %collective-permute-start.9) | collective-permute-done | bytes 131104 | tf_op jit(solution)/shard_map/ppermute | solution.py:21
  49.6 0.7 %shard_map.80 = (f32[128,128]{1,0:T(8,128)}, f32[128,128]{1,0:T(8,128)}) custom-call(f32[2,128,128]{2,1,0:T(8,128)S(1)} %pad_maximum_fusion.refs_0_, f32[2,128,128]{2,1,0:T(8,128)S(1)} %collective-permute-done.7.refs_1_, f32[2,128,128]{2,1,0:T(8,128)S(1)} %collective-permute-done.8.refs_2_, f32[2,128,128]{2,1,0:T(8,128)S(1)} %collective-permute-done.9.refs_3_), custom_call_target="tpu_custom_call" | custom-call | tf_op jit(solution)/shard_map/pallas_call | solution.py:262
  (15 shorter events, 0.2 us)
Async XLA Ops:
  0.6 3.7 %collective-permute-start = (bf16[128,128]{1,0:T(8,128)(2,1)}, bf16[128,128]{1,0:T(8,128)(2,1)S(1)}, u32[]{:S(2)}, u32[]{:S(2)}) collective-permute-start(bf16[128,128]{1,0:T(8,128)(2,1)} %param.6), channel_id=1, source_target_pairs={{0,4},{4,8},{8,12},{12,16},{16,20},{20,24},{24,28},{1,5},{5,9},{9,... | collective-permute-start | bytes 98312 | tf_op jit(solution)/shard_map/ppermute | solution.py:16
  3.0 5.5 %collective-permute-start.1 = (bf16[128,128]{1,0:T(8,128)(2,1)}, bf16[128,128]{1,0:T(8,128)(2,1)S(1)}, u32[]{:S(2)}, u32[]{:S(2)}) collective-permute-start(bf16[128,128]{1,0:T(8,128)(2,1)} %param.6), channel_id=1, source_target_pairs={{4,0},{8,4},{12,8},{16,12},{20,16},{24,20},{28,24},{5,1},{9,5},{13... | collective-permute-start | bytes 98312 | tf_op jit(solution)/shard_map/ppermute | solution.py:16
  9.3 14.1 %collective-permute-start.4 = (bf16[512,128]{1,0:T(8,128)(2,1)S(1)}, bf16[512,128]{1,0:T(8,128)(2,1)S(1)}, u32[]{:S(2)}, u32[]{:S(2)}) collective-permute-start(bf16[512,128]{1,0:T(8,128)(2,1)S(1)} %constant_dynamic-update-slice_fusion.refs_0_), channel_id=1, source_target_pairs={{0,3},{1,2},{2,1},{3,0},{4,7},{5,6},{6,5},{7,4},{8,11},{9,10},{10,... | collective-permute-start | bytes 393224 | tf_op jit(solution)/shard_map/ppermute | solution.py:21
  11.7 11.6 %collective-permute-start.3 = (bf16[512,128]{1,0:T(8,128)(2,1)S(1)}, bf16[512,128]{1,0:T(8,128)(2,1)S(1)}, u32[]{:S(2)}, u32[]{:S(2)}) collective-permute-start(bf16[512,128]{1,0:T(8,128)(2,1)S(1)} %constant_dynamic-update-slice_fusion.refs_0_), channel_id=1, source_target_pairs={{0,2},{1,3},{2,0},{3,1},{4,6},{5,7},{6,4},{7,5},{8,10},{9,11},{10,... | collective-permute-start | bytes 393224 | tf_op jit(solution)/shard_map/ppermute | solution.py:21
  12.2 11.1 %collective-permute-start.2 = (bf16[512,128]{1,0:T(8,128)(2,1)S(1)}, bf16[512,128]{1,0:T(8,128)(2,1)S(1)}, u32[]{:S(2)}, u32[]{:S(2)}) collective-permute-start(bf16[512,128]{1,0:T(8,128)(2,1)S(1)} %constant_dynamic-update-slice_fusion.refs_0_), channel_id=1, source_target_pairs={{0,1},{1,0},{2,3},{3,2},{4,5},{5,4},{6,7},{7,6},{8,9},{9,8},{10,11... | collective-permute-start | bytes 393224 | tf_op jit(solution)/shard_map/ppermute | solution.py:21
  13.4 0.7 %copy-start = (s32[192]{0:T(256)S(1)}, s32[192]{0:T(256)}, u32[]{:S(2)}) copy-start(s32[192]{0:T(256)} %target_ref.1) | copy-start | bytes 2308
  14.1 0.7 %copy-start.1 = (s32[192]{0:T(256)S(1)}, s32[192]{0:T(256)}, u32[]{:S(2)}) copy-start(s32[192]{0:T(256)} %source_ref.1) | copy-start | bytes 2308
  26.9 11.4 %collective-permute-start.5 = (f32[4,128,128]{2,1,0:T(8,128)S(1)}, f32[4,128,128]{2,1,0:T(8,128)S(1)}, u32[]{:S(2)}, u32[]{:S(2)}) collective-permute-start(f32[4,128,128]{2,1,0:T(8,128)S(1)} %get-tuple-element.8), channel_id=1, source_target_pairs={{4,0},{8,4},{12,8},{16,12},{20,16},{24,20},{28,24},{5,1},{9,5},{13... | collective-permute-start | bytes 786440 | tf_op jit(solution)/shard_map/ppermute | solution.py:16
  28.2 10.1 %collective-permute-start.6 = (f32[4,128,128]{2,1,0:T(8,128)S(1)}, f32[4,128,128]{2,1,0:T(8,128)S(1)}, u32[]{:S(2)}, u32[]{:S(2)}) collective-permute-start(f32[4,128,128]{2,1,0:T(8,128)S(1)} %get-tuple-element.9), channel_id=1, source_target_pairs={{0,4},{4,8},{8,12},{12,16},{16,20},{20,24},{24,28},{1,5},{5,9},{9,... | collective-permute-start | bytes 786440 | tf_op jit(solution)/shard_map/ppermute | solution.py:16
  38.4 5.7 %collective-permute-start.7 = (f32[2,128,128]{2,1,0:T(8,128)S(1)}, f32[2,128,128]{2,1,0:T(8,128)S(1)}, u32[]{:S(2)}, u32[]{:S(2)}) collective-permute-start(f32[2,128,128]{2,1,0:T(8,128)S(1)} %pad_maximum_fusion.1), channel_id=1, source_target_pairs={{0,1},{1,0},{2,3},{3,2},{4,5},{5,4},{6,7},{7,6},{8,9},{9,8},{10,11... | collective-permute-start | bytes 393224 | tf_op jit(solution)/shard_map/ppermute | solution.py:21
  39.6 9.0 %collective-permute-start.8 = (f32[2,128,128]{2,1,0:T(8,128)S(1)}, f32[2,128,128]{2,1,0:T(8,128)S(1)}, u32[]{:S(2)}, u32[]{:S(2)}) collective-permute-start(f32[2,128,128]{2,1,0:T(8,128)S(1)} %pad_maximum_fusion.2), channel_id=1, source_target_pairs={{0,2},{1,3},{2,0},{3,1},{4,6},{5,7},{6,4},{7,5},{8,10},{9,11},{10,... | collective-permute-start | bytes 393224 | tf_op jit(solution)/shard_map/ppermute | solution.py:21
  42.6 7.0 %collective-permute-start.9 = (f32[2,128,128]{2,1,0:T(8,128)S(1)}, f32[2,128,128]{2,1,0:T(8,128)S(1)}, u32[]{:S(2)}, u32[]{:S(2)}) collective-permute-start(f32[2,128,128]{2,1,0:T(8,128)S(1)} %pad_maximum_fusion.3), channel_id=1, source_target_pairs={{0,3},{1,2},{2,1},{3,0},{4,7},{5,6},{6,5},{7,4},{8,11},{9,10},{10,... | collective-permute-start | bytes 393224 | tf_op jit(solution)/shard_map/ppermute | solution.py:21

commit v2 on v0

v2 whole, which is shorter than its diff:
```python
import functools

import jax
import jax.numpy as jnp
from jax import lax
from jax.experimental import pallas as pl
from jax.experimental.pallas import tpu as pltpu
from jax.sharding import PartitionSpec as P


def shifted(value, axis, steps):
    count = lax.axis_size(axis)
    first, last = (max(0, -steps), min(count, count - steps))
    return lax.ppermute(value, axis, [(source, source + steps) for source in range(first, last)])


def turned(block):
    half = block.shape[1] // 2
    wide = pltpu.roll(block.astype(jnp.float32), half, axis=1)
    lane = lax.broadcasted_iota(jnp.int32, wide.shape, 1)
    return jnp.where(lane < half, -wide, wide).astype(block.dtype)


def turned_rows(block):
    half = block.shape[0] // 2
    return jnp.concatenate([-block[half:], block[:half]], axis=0)


def place(target_ref, source_ref, slot, group_blocks):
    group = lax.axis_index("grp")
    return target_ref[slot] - group * group_blocks, source_ref[slot] - (group - 1) * group_blocks


def each_slot(chunk, refs, held, ids, id_sems, sems, prepare, work):
    live_ref, *id_refs, kernels_ref = refs
    chunks = held.shape[0] // chunk
    copies = [pltpu.make_async_copy(ref, kept, id_sems.at[i]) for i, (ref, kept) in enumerate(zip(id_refs, ids))]

    def fetch(c):
        rows = pl.ds(c * chunk, chunk)
        return pltpu.make_async_copy(kernels_ref.at[rows], held.at[rows], sems.at[c])

    for copy in copies:
        copy.start()
    for c in range(chunks):
        fetch(c).start()
    prepare()
    for copy in copies:
        copy.wait()
    live = live_ref[0]

    @pl.loop(0, chunks)
    def _(c):
        fetch(c).wait()
        first = c * chunk

        @pl.when(first + chunk <= live)
        def _():
            for i in range(chunk):
                work(first + i)

        @pl.when(first + chunk > live)
        def _():
            @pl.loop(first, jnp.maximum(live, first))
            def _(slot):
                work(slot)


def combine_kernel(group_blocks, chunk, *refs):
    slot_refs, (out_ref, held, total, *ids, id_sems, sems) = refs[:4], refs[4:]
    sources = 3 * group_blocks

    def clear():
        @pl.loop(0, total.shape[0])
        def _(pair):
            total[pair] = jnp.zeros(total.shape[1:], total.dtype)

    def add(slot):
        target, source = place(*ids, slot, group_blocks)
        pair = target * sources + source
        total[pair] += held[slot].reshape(total.shape[1:]).astype(jnp.float32)

    each_slot(chunk, slot_refs, held, ids, id_sems, sems, clear, add)

    @pl.loop(0, total.shape[0])
    def _(pair):
        value = total[pair]
        high = value.astype(jnp.bfloat16)
        out_ref[0, pair] = high
        out_ref[1, pair] = (value - high.astype(jnp.float32)).astype(jnp.bfloat16)


def gather_kernel(lower_ref, middle_ref, upper_ref, weights_ref, _, out_ref):
    rows = middle_ref.shape[0]
    for c in range(out_ref.shape[0]):
        for i, ref in enumerate((lower_ref, middle_ref, upper_ref, weights_ref)):
            out_ref[c, i * rows : (i + 1) * rows] = ref[...]


def part_of(gathered_ref, blocks, panels, part):
    for c in range(gathered_ref.shape[0]):
        for b in range(blocks):
            yield gathered_ref[c, pl.ds((part * blocks + b) * panels, panels), :]


def weights_across(gathered_ref, blocks, panels):
    across = []
    for block in part_of(gathered_ref, blocks, panels, 3):
        block = block.astype(jnp.float32).T
        across += [block, turned_rows(block)]
    return jnp.concatenate(across, axis=1).astype(jnp.bfloat16)


def strengths_stacked(gathered_ref, blocks, panels):
    stack = []
    for offset in range(3):
        for block in part_of(gathered_ref, blocks, panels, offset):
            stack += [block, turned(block)]
    return jnp.concatenate(stack, axis=0)


def adjoint_of(pairs_ref, weights, first, count):
    width = pairs_ref.shape[3]
    targets = weights.shape[1] // pairs_ref.shape[2]
    sources = pairs_ref.shape[1] // targets
    both = jnp.concatenate([weights, weights], axis=1)
    step = 2 if count % 2 == 0 else 1
    for i in range(0, count, step):
        columns = []
        for j in range(step):
            tiles = [pairs_ref[h, t * sources + first + i + j] for h in range(2) for t in range(targets)]
            columns.append(jnp.concatenate(tiles, axis=0))
        product = jnp.dot(both, jnp.concatenate(columns, axis=1), preferred_element_type=jnp.float32)
        for j in range(step):
            yield i + j, product[:, j * width : (j + 1) * width]


def outer_kernel(blocks, panels, pairs_ref, gathered_ref, lower_ref, upper_ref):
    count = lower_ref.shape[0]
    weights = weights_across(gathered_ref, blocks, panels)
    for i, value in adjoint_of(pairs_ref, weights, 0, count):
        lower_ref[i] = value
    for i, value in adjoint_of(pairs_ref, weights, 2 * count, count):
        upper_ref[i] = value


def forward_kernel(blocks, panels, pairs_ref, gathered_ref, potential_ref):
    targets = potential_ref.shape[0]
    sources = pairs_ref.shape[1] // targets
    stack = strengths_stacked(gathered_ref, blocks, panels)
    for t in range(targets):
        halves = []
        for h in range(2):
            tiles = []
            for s in range(sources):
                tiles += [pairs_ref[h, t * sources + s, :panels], pairs_ref[h, t * sources + s, panels:]]
            halves.append(jnp.concatenate(tiles, axis=1))
        product = jnp.dot(jnp.concatenate(halves, axis=0), stack, preferred_element_type=jnp.float32)
        potential_ref[t] = product[:panels] + product[panels:]


def middle_kernel(blocks, panels, pairs_ref, gathered_ref, potential_ref, above_ref, below_ref, out_ref):
    count = potential_ref.shape[0]
    weights = weights_across(gathered_ref, blocks, panels)
    for i, value in adjoint_of(pairs_ref, weights, count, count):
        owner, b = i // blocks, i % blocks
        out_ref[owner, b] = potential_ref[i]
        out_ref[owner, blocks + b] = value + above_ref[i] + below_ref[i]


def slots_kernel(blocks, panels, chunk, *refs):
    slot_refs, gathered_ref, rest = refs[:4], refs[4], refs[5:]
    potential_ref, adjoint_ref, held, stack, across, *ids, id_sems, sems = rest
    group_blocks = potential_ref.shape[0]

    def prepare():
        potential_ref[...] = jnp.zeros(potential_ref.shape, potential_ref.dtype)
        adjoint_ref[...] = jnp.zeros(adjoint_ref.shape, adjoint_ref.dtype)
        for offset in range(3):
            for i, block in enumerate(part_of(gathered_ref, blocks, panels, offset)):
                stack[offset * group_blocks + i] = jnp.concatenate([block, turned(block)], axis=0)
        for i, block in enumerate(part_of(gathered_ref, blocks, panels, 3)):
            block = block.astype(jnp.float32).T
            across[i] = jnp.concatenate([block, turned_rows(block)], axis=1).astype(jnp.bfloat16)

    def work(slot):
        target, source = place(*ids, slot, group_blocks)
        real, imag = held[slot, 0], held[slot, 1]
        potential_ref[target] += jnp.dot(
            jnp.concatenate([real, imag], axis=1), stack[source], preferred_element_type=jnp.float32
        )
        adjoint_ref[source] += jnp.dot(
            across[target], jnp.concatenate([real, imag], axis=0), preferred_element_type=jnp.float32
        )

    each_slot(chunk, slot_refs, held, ids, id_sems, sems, prepare, work)


def finish_kernel(blocks, parts_ref, potential_ref, adjoint_ref):
    total = parts_ref[0]
    for c in range(1, parts_ref.shape[0]):
        total = total + parts_ref[c]
    panels = total.shape[1]
    for b in range(blocks):
        potential_ref[b * panels : (b + 1) * panels] = total[b]
        adjoint_ref[b * panels : (b + 1) * panels] = total[blocks + b].T


def local(strengths, adjoint_weights, kernels, target_ids, source_ids, live_slots):
    slots, _, panels, _ = kernels.shape
    width = strengths.shape[1]
    blocks = strengths.shape[0] // panels
    clusters = lax.axis_size("clu")
    group_blocks = clusters * blocks
    sources = 3 * group_blocks
    pairs = group_blocks * sources
    chunk = 8 if slots % 8 == 0 else 1
    in_vmem, in_smem, in_hbm = (pl.BlockSpec(memory_space=m) for m in (pltpu.VMEM, pltpu.SMEM, pltpu.HBM))
    f32, bf16 = jnp.float32, jnp.bfloat16
    slot_args = (live_slots,) + tuple(
        pltpu.with_memory_space_constraint(x, pltpu.HBM) for x in (target_ids, source_ids, kernels)
    )
    held = pltpu.VMEM(kernels.shape, bf16)
    fetch = [
        pltpu.SMEM(target_ids.shape, jnp.int32),
        pltpu.SMEM(source_ids.shape, jnp.int32),
        pltpu.SemaphoreType.DMA((2,)),
        pltpu.SemaphoreType.DMA((slots // chunk,)),
    ]

    def call(body, shapes, args, specs=None, scratch=(), mib=8, flops=0):
        single = not isinstance(shapes, tuple)
        return pl.pallas_call(
            body,
            out_shape=shapes,
            in_specs=specs or [in_vmem] * len(args),
            out_specs=in_vmem if single else (in_vmem,) * len(shapes),
            scratch_shapes=scratch,
            compiler_params=pltpu.CompilerParams(vmem_limit_bytes=mib << 20),
            cost_estimate=pl.CostEstimate(flops=flops, bytes_accessed=1 << 20, transcendentals=0),
        )(*args)

    def shape(*dims, kind=f32):
        return jax.ShapeDtypeStruct(dims, kind)

    def with_halo(token):
        from_lower, from_upper = shifted(strengths, "grp", 1), shifted(strengths, "grp", -1)
        mine = call(
            gather_kernel,
            shape(clusters, 4 * blocks * panels, width, kind=bf16),
            (from_lower, strengths, from_upper, adjoint_weights, token),
            [in_vmem] * 4 + [in_hbm],
        )
        return lax.all_to_all(mine, "clu", 0, 0, tiled=True)

    block_sums = shape(group_blocks, panels, width)
    if pairs <= slots:
        pair_blocks = call(
            functools.partial(combine_kernel, group_blocks, chunk),
            pltpu.VMEM((2, pairs, 2 * panels, panels), bf16),
            slot_args,
            [in_smem] + [in_hbm] * 3,
            [held, pltpu.VMEM((pairs, 2 * panels, panels), f32), *fetch],
            mib=28,
            flops=1 << 30,
        )
        gathered = with_halo(pair_blocks)
        kept = pltpu.with_memory_space_constraint(pair_blocks, pltpu.VMEM)
        lower, upper = call(
            functools.partial(outer_kernel, blocks, panels), (block_sums, block_sums), (kept, gathered), flops=1 << 30
        )
        potential = call(
            functools.partial(forward_kernel, blocks, panels), block_sums, (kept, gathered), flops=1 << 30
        )
        above, below = shifted(lower, "grp", -1), shifted(upper, "grp", 1)
        parts = call(
            functools.partial(middle_kernel, blocks, panels),
            shape(clusters, 2 * blocks, panels, width),
            (kept, gathered, potential, above, below),
        )
    else:
        gathered = with_halo(strengths)
        potential, adjoint = call(
            functools.partial(slots_kernel, blocks, panels, chunk),
            (block_sums, shape(sources, width, panels)),
            (*slot_args, gathered),
            [in_smem] + [in_hbm] * 3 + [in_vmem],
            [
                held,
                pltpu.VMEM((sources, 2 * panels, width), bf16),
                pltpu.VMEM((group_blocks, width, 2 * panels), bf16),
                *fetch,
            ],
            mib=40,
        )
        lower, middle, upper = (adjoint[i * group_blocks : (i + 1) * group_blocks] for i in range(3))
        adjoint = middle + shifted(lower, "grp", -1) + shifted(upper, "grp", 1)
        split = (clusters, blocks, panels, width)
        parts = jnp.concatenate([potential.reshape(split), adjoint.reshape(split)], axis=1)

    parts = lax.all_to_all(parts, "clu", 0, 0, tiled=True)
    out = shape(blocks * panels, width)
    return tuple(call(functools.partial(finish_kernel, blocks), (out, out), (parts,)))


def solution(mesh):
    return jax.shard_map(
        local,
        mesh=mesh,
        in_specs=(
            P(("grp", "clu"), None),
            P(("grp", "clu"), None),
            P(("grp", "clu"), None, None, None),
            P(("grp", "clu")),
            P(("grp", "clu")),
            P(("grp", "clu")),
        ),
        out_specs=(P(("grp", "clu"), None), P(("grp", "clu"), None)),
        check_vma=False,
    )
```

time: 269 us -> 47.5 us (0.18)
  the two profiles are of different devices: /device:TPU:0 before, /device:TPU:8 now
where the time goes in v2:
time: 47.5 us; the launch traced here: 47.1 us
  blocking collectives  22.7 us (48%)
  starting transfers between devices  10 us (21%)
  Pallas kernels  9.58 us (20%)
  waiting for transfers between devices  3.4 us (7%)
  between operations  1.4 us (3%)
    all_to_all x1, blocking collectives, with_halo(): return lax.all_to_all(mine, 'clu', 0, 0, tiled=True)  12.2 us
    all_to_all x1, blocking collectives, local(): parts = lax.all_to_all(parts, 'clu', 0, 0, tiled=True)  10.6 us
    ppermute x4, starting transfers between devices, shifted(): lax.ppermute(value, axis, [(source, source + steps) for source in range(f...  10 us
    pallas_call x6, Pallas kernels, call(): pl.pallas_call(body, out_shape=shapes, in_specs=specs or [in_vmem] * len(...  9.58 us
    ppermute x4, waiting for transfers between devices, shifted(): lax.ppermute(value, axis, [(source, source + steps) for source in range(f...  3.4 us
  transfers between devices with their start and end apart: 4, of which 1 were waited for; matrix products, arithmetic and copies ran while one was open for 0% of the time, Pallas kernels for 16%

profile of v2, /device:TPU:8, one launch (start us, length us, event | category | flops | bytes accessed | tf_op | source)
XLA Modules:
  0.0 47.1 jit_solution(11381219925339948472)
XLA Ops:
  0.6 0.0 copy-start
  0.6 0.0 copy-start.1
  0.7 2.1 %collective-permute-start = (bf16[128,128]{1,0:T(8,128)(2,1)}, bf16[128,128]{1,0:T(8,128)(2,1)S(1)}, u32[]{:S(2)}, u32[]{:S(2)}) collective-permute-start(bf16[128,128]{1,0:T(8,128)(2,1)} %middle_ref.1), channel_id=1, source_target_pairs={{0,4},{4,8},{8,12},{12,16},{16,20},{20,24},{24,28},{1,5},{5,9},{9,... | collective-permute-start | bytes 98312 | tf_op jit(solution)/shard_map/ppermute | solution.py:14
  2.7 3.6 %collective-permute-start.1 = (bf16[128,128]{1,0:T(8,128)(2,1)}, bf16[128,128]{1,0:T(8,128)(2,1)S(1)}, u32[]{:S(2)}, u32[]{:S(2)}) collective-permute-start(bf16[128,128]{1,0:T(8,128)(2,1)} %middle_ref.1), channel_id=1, source_target_pairs={{4,0},{8,4},{12,8},{16,12},{20,16},{24,20},{28,24},{5,1},{9,5},{13... | collective-permute-start | bytes 98312 | tf_op jit(solution)/shard_map/ppermute | solution.py:14
  7.0 5.6 %shard_map.77._.pairs_ref = bf16[2,48,256,128]{3,2,1,0:T(8,128)(2,1)S(1)} custom-call(s32[1]{0:T(128)S(6)} %copy.8.refs_0_, s32[192]{0:T(256)} %refs_1_.1, s32[192]{0:T(256)} %refs_2_.1, bf16[192,2,128,128]{3,2,1,0:T(8,128)(2,1)} %refs_3_.1), custom_call_target="tpu_custom_call" | custom-call | flops 1073741824 | bytes 1048576 | tf_op jit(solution)/shard_map/pallas_call | solution.py:233
  12.6 0.0 collective-permute-done.lower_ref
  12.7 0.0 collective-permute-done.1.upper_ref
  12.7 0.0 copy-done
  12.7 0.0 copy-done.1
  12.7 0.1 shard_map.78
  12.8 12.2 %all_to_all.10.gathered_ref = bf16[4,512,128]{2,1,0:T(8,128)(2,1)S(1)} all-to-all(bf16[4,512,128]{2,1,0:T(8,128)(2,1)S(1)} %shard_map.78), channel_id=1, replica_groups=mesh['grp'=8,'clu'=4] {'clu'}, dimensions={0} | all-to-all | bytes 1048576 | tf_op jit(solution)/shard_map/all_to_all | solution.py:254
  24.9 0.8 %shard_map.80 = (f32[4,128,128]{2,1,0:T(8,128)S(1)}, f32[4,128,128]{2,1,0:T(8,128)S(1)}) custom-call(bf16[2,48,256,128]{3,2,1,0:T(8,128)(2,1)S(1)} %shard_map.77._.pairs_ref, bf16[4,512,128]{2,1,0:T(8,128)(2,1)S(1)} %all_to_all.10.gathered_ref), custom_call_target="tpu_custom_call" | custom-call | flops 1073741824 | bytes 1048576 | tf_op jit(solution)/shard_map/pallas_call | solution.py:233
  25.7 1.9 %collective-permute-start.2 = (f32[4,128,128]{2,1,0:T(8,128)S(1)}, f32[4,128,128]{2,1,0:T(8,128)S(1)}, u32[]{:S(2)}, u32[]{:S(2)}) collective-permute-start(f32[4,128,128]{2,1,0:T(8,128)S(1)} %get-tuple-element.4), channel_id=1, source_target_pairs={{4,0},{8,4},{12,8},{16,12},{20,16},{24,20},{28,24},{5,1},{9,5},{13... | collective-permute-start | bytes 786440 | tf_op jit(solution)/shard_map/ppermute | solution.py:14
  27.6 2.4 %collective-permute-start.3 = (f32[4,128,128]{2,1,0:T(8,128)S(1)}, f32[4,128,128]{2,1,0:T(8,128)S(1)}, u32[]{:S(2)}, u32[]{:S(2)}) collective-permute-start(f32[4,128,128]{2,1,0:T(8,128)S(1)} %get-tuple-element.5), channel_id=1, source_target_pairs={{0,4},{4,8},{8,12},{12,16},{16,20},{20,24},{24,28},{1,5},{5,9},{9,... | collective-permute-start | bytes 786440 | tf_op jit(solution)/shard_map/ppermute | solution.py:14
  30.0 1.9 %shard_map.79.potential_ref = f32[4,128,128]{2,1,0:T(8,128)S(1)} custom-call(bf16[2,48,256,128]{3,2,1,0:T(8,128)(2,1)S(1)} %shard_map.77._.pairs_ref, bf16[4,512,128]{2,1,0:T(8,128)(2,1)S(1)} %all_to_all.10.gathered_ref), custom_call_target="tpu_custom_call" | custom-call | flops 1073741824 | bytes 1048576 | tf_op jit(solution)/shard_map/pallas_call | solution.py:233
  31.9 0.0 collective-permute-done.2.above_ref
  31.9 3.4 %collective-permute-done.3.below_ref = f32[4,128,128]{2,1,0:T(8,128)S(1)} collective-permute-done((f32[4,128,128]{2,1,0:T(8,128)S(1)}, f32[4,128,128]{2,1,0:T(8,128)S(1)}, u32[]{:S(2)}, u32[]{:S(2)}) %collective-permute-start.3) | collective-permute-done | bytes 262176 | tf_op jit(solution)/shard_map/ppermute | solution.py:14
  35.3 0.5 %shard_map.81 = f32[4,2,128,128]{3,2,1,0:T(8,128)S(1)} custom-call(bf16[2,48,256,128]{3,2,1,0:T(8,128)(2,1)S(1)} %shard_map.77._.pairs_ref, bf16[4,512,128]{2,1,0:T(8,128)(2,1)S(1)} %all_to_all.10.gathered_ref, f32[4,128,128]{2,1,0:T(8,128)S(1)} %shard_map.79.potential_ref, f32[4,128,128]{2,1,0:T(8,128)S(1)} %collective-permute-done.2.above_ref, ...), custom_call_target="tpu_custom_call" | custom-call | bytes 1048576 | tf_op jit(solution)/shard_map/pallas_call | solution.py:233
  35.8 10.6 %all_to_all.11.parts_ref = f32[4,2,128,128]{3,2,1,0:T(8,128)S(1)} all-to-all(f32[4,2,128,128]{3,2,1,0:T(8,128)S(1)} %shard_map.81), channel_id=1, replica_groups=mesh['grp'=8,'clu'=4] {'clu'}, dimensions={0} | all-to-all | bytes 1048576 | tf_op jit(solution)/shard_map/all_to_all | solution.py:301
  46.4 0.7 %shard_map.82 = (f32[128,128]{1,0:T(8,128)}, f32[128,128]{1,0:T(8,128)}) custom-call(f32[4,2,128,128]{3,2,1,0:T(8,128)S(1)} %all_to_all.11.parts_ref), custom_call_target="tpu_custom_call" | custom-call | bytes 1048576 | tf_op jit(solution)/shard_map/pallas_call | solution.py:233
Async XLA Ops:
  0.6 12.0 %copy-start = (bf16[128,128]{1,0:T(8,128)(2,1)S(1)}, bf16[128,128]{1,0:T(8,128)(2,1)}, u32[]{:S(2)}) copy-start(bf16[128,128]{1,0:T(8,128)(2,1)} %middle_ref.1) | copy-start | bytes 98308
  0.6 12.0 %copy-start.1 = (bf16[128,128]{1,0:T(8,128)(2,1)S(1)}, bf16[128,128]{1,0:T(8,128)(2,1)}, u32[]{:S(2)}) copy-start(bf16[128,128]{1,0:T(8,128)(2,1)} %weights_ref.1) | copy-start | bytes 98308
  0.7 12.0 %collective-permute-start = (bf16[128,128]{1,0:T(8,128)(2,1)}, bf16[128,128]{1,0:T(8,128)(2,1)S(1)}, u32[]{:S(2)}, u32[]{:S(2)}) collective-permute-start(bf16[128,128]{1,0:T(8,128)(2,1)} %middle_ref.1), channel_id=1, source_target_pairs={{0,4},{4,8},{8,12},{12,16},{16,20},{20,24},{24,28},{1,5},{5,9},{9,... | collective-permute-start | bytes 98312 | tf_op jit(solution)/shard_map/ppermute | solution.py:14
  2.7 9.9 %collective-permute-start.1 = (bf16[128,128]{1,0:T(8,128)(2,1)}, bf16[128,128]{1,0:T(8,128)(2,1)S(1)}, u32[]{:S(2)}, u32[]{:S(2)}) collective-permute-start(bf16[128,128]{1,0:T(8,128)(2,1)} %middle_ref.1), channel_id=1, source_target_pairs={{4,0},{8,4},{12,8},{16,12},{20,16},{24,20},{28,24},{5,1},{9,5},{13... | collective-permute-start | bytes 98312 | tf_op jit(solution)/shard_map/ppermute | solution.py:14
  25.7 6.2 %collective-permute-start.2 = (f32[4,128,128]{2,1,0:T(8,128)S(1)}, f32[4,128,128]{2,1,0:T(8,128)S(1)}, u32[]{:S(2)}, u32[]{:S(2)}) collective-permute-start(f32[4,128,128]{2,1,0:T(8,128)S(1)} %get-tuple-element.4), channel_id=1, source_target_pairs={{4,0},{8,4},{12,8},{16,12},{20,16},{24,20},{28,24},{5,1},{9,5},{13... | collective-permute-start | bytes 786440 | tf_op jit(solution)/shard_map/ppermute | solution.py:14
  27.6 7.7 %collective-permute-start.3 = (f32[4,128,128]{2,1,0:T(8,128)S(1)}, f32[4,128,128]{2,1,0:T(8,128)S(1)}, u32[]{:S(2)}, u32[]{:S(2)}) collective-permute-start(f32[4,128,128]{2,1,0:T(8,128)S(1)} %get-tuple-element.5), channel_id=1, source_target_pairs={{0,4},{4,8},{8,12},{12,16},{16,20},{20,24},{24,28},{1,5},{5,9},{9,... | collective-permute-start | bytes 786440 | tf_op jit(solution)/shard_map/ppermute | solution.py:14

commit v3 on v2

v3 whole, which is shorter than its diff:
```python
import functools

import jax
import jax.numpy as jnp
from jax import lax
from jax.experimental import pallas as pl
from jax.experimental.pallas import tpu as pltpu
from jax.sharding import PartitionSpec as P


def exchange(value, axis, step):
    return lax.ppermute(value, axis, [(i, i ^ step) for i in range(lax.axis_size(axis))])


def exchange_beside(value, axis, first):
    pairs = [(i, i + 1) for i in range(first, lax.axis_size(axis) - 1, 2)]
    return lax.ppermute(value, axis, pairs + [(j, i) for i, j in pairs])


def turned(block):
    half = block.shape[1] // 2
    wide = pltpu.roll(block.astype(jnp.float32), half, axis=1)
    lane = lax.broadcasted_iota(jnp.int32, wide.shape, 1)
    return jnp.where(lane < half, -wide, wide).astype(block.dtype)


def turned_rows(block):
    half = block.shape[0] // 2
    return jnp.concatenate([-block[half:], block[:half]], axis=0)


def place(target_ref, source_ref, slot, group_blocks, blocks):
    group, mine = lax.axis_index("grp"), lax.axis_index("clu") * blocks
    target = (target_ref[slot] - group * group_blocks) ^ mine
    source = (source_ref[slot] - (group - 1) * group_blocks) ^ mine
    offset = lax.div(source, group_blocks) - 1
    return target, jnp.where(group % 2 == 0, source - 2 * offset * group_blocks, source)


def each_slot(chunk, refs, held, ids, id_sems, sems, prepare, work):
    live_ref, *id_refs, kernels_ref = refs
    chunks = held.shape[0] // chunk
    copies = [pltpu.make_async_copy(ref, kept, id_sems.at[i]) for i, (ref, kept) in enumerate(zip(id_refs, ids))]

    def fetch(c):
        rows = pl.ds(c * chunk, chunk)
        return pltpu.make_async_copy(kernels_ref.at[rows], held.at[rows], sems.at[c])

    for copy in copies:
        copy.start()
    for c in range(chunks):
        fetch(c).start()
    prepare()
    for copy in copies:
        copy.wait()
    live = live_ref[0]

    @pl.loop(0, chunks)
    def _(c):
        fetch(c).wait()
        first = c * chunk

        @pl.when(first + chunk <= live)
        def _():
            for i in range(chunk):
                work(first + i)

        @pl.when(first + chunk > live)
        def _():
            @pl.loop(first, jnp.maximum(live, first))
            def _(slot):
                work(slot)


def combine_kernel(group_blocks, blocks, chunk, *refs):
    slot_refs, (total, held, *ids, id_sems, sems) = refs[:4], refs[4:]
    sources = 3 * group_blocks

    def clear():
        @pl.loop(0, total.shape[0])
        def _(pair):
            total[pair] = jnp.zeros(total.shape[1:], total.dtype)

    def add(slot):
        target, source = place(*ids, slot, group_blocks, blocks)
        pair = target * sources + source
        total[pair] += held[slot].reshape(total.shape[1:]).astype(jnp.float32)

    each_slot(chunk, slot_refs, held, ids, id_sems, sems, clear, add)


def split_kernel(total, out_ref):
    @pl.loop(0, total.shape[0])
    def _(pair):
        value = total[pair]
        high = value.astype(jnp.bfloat16)
        out_ref[0, pair] = high
        out_ref[1, pair] = (value - high.astype(jnp.float32)).astype(jnp.bfloat16)


def join_kernel(first_ref, own_ref, second_ref, weights_ref, _, out_ref):
    rows = own_ref.shape[0]
    for i, ref in enumerate((first_ref, own_ref, second_ref, weights_ref)):
        out_ref[i * rows : (i + 1) * rows] = ref[...]


def part_of(gathered, blocks, panels, part):
    for ref in gathered:
        for b in range(blocks):
            yield ref[pl.ds((part * blocks + b) * panels, panels), :]


def weights_across(gathered, blocks, panels):
    across = []
    for block in part_of(gathered, blocks, panels, 3):
        block = block.astype(jnp.float32).T
        across += [block, turned_rows(block)]
    return jnp.concatenate(across, axis=1).astype(jnp.bfloat16)


def strengths_stacked(gathered, blocks, panels):
    stack = []
    for offset in range(3):
        for block in part_of(gathered, blocks, panels, offset):
            stack += [block, turned(block)]
    return jnp.concatenate(stack, axis=0)


def adjoint_of(pairs_ref, weights, first, count):
    width = pairs_ref.shape[3]
    targets = weights.shape[1] // pairs_ref.shape[2]
    sources = pairs_ref.shape[1] // targets
    both = jnp.concatenate([weights, weights], axis=1)
    step = 2 if count % 2 == 0 else 1
    for i in range(0, count, step):
        columns = []
        for j in range(step):
            tiles = [pairs_ref[h, t * sources + first + i + j] for h in range(2) for t in range(targets)]
            columns.append(jnp.concatenate(tiles, axis=0))
        product = jnp.dot(both, jnp.concatenate(columns, axis=1), preferred_element_type=jnp.float32)
        for j in range(step):
            yield i + j, product[:, j * width : (j + 1) * width]


def outer_kernel(blocks, panels, pairs_ref, *refs):
    *gathered, first_ref, second_ref = refs
    count = first_ref.shape[0]
    weights = weights_across(gathered, blocks, panels)
    for i, value in adjoint_of(pairs_ref, weights, 0, count):
        first_ref[i] = value
    for i, value in adjoint_of(pairs_ref, weights, 2 * count, count):
        second_ref[i] = value


def forward_kernel(blocks, panels, pairs_ref, *refs):
    *gathered, potential_ref = refs
    targets = potential_ref.shape[0]
    sources = pairs_ref.shape[1] // targets
    stack = strengths_stacked(gathered, blocks, panels)
    for t in range(targets):
        halves = []
        for h in range(2):
            tiles = []
            for s in range(sources):
                tiles += [pairs_ref[h, t * sources + s, :panels], pairs_ref[h, t * sources + s, panels:]]
            halves.append(jnp.concatenate(tiles, axis=1))
        product = jnp.dot(jnp.concatenate(halves, axis=0), stack, preferred_element_type=jnp.float32)
        potential_ref[t] = product[:panels] + product[panels:]


def middle_kernel(blocks, panels, clusters, pairs_ref, *refs):
    gathered, (potential_ref, first_ref, second_ref, *outs) = refs[:clusters], refs[clusters:]
    count = potential_ref.shape[0]
    weights = weights_across(gathered, blocks, panels)
    for i, value in adjoint_of(pairs_ref, weights, count, count):
        out_ref, b = outs[i // blocks], i % blocks
        out_ref[b] = potential_ref[i]
        out_ref[blocks + b] = value + first_ref[i] + second_ref[i]


def slots_kernel(blocks, panels, clusters, chunk, *refs):
    slot_refs, gathered, rest = refs[:4], refs[4 : 4 + clusters], refs[4 + clusters :]
    potential_ref, adjoint_ref, held, stack, across, *ids, id_sems, sems = rest
    group_blocks = potential_ref.shape[0]

    def prepare():
        potential_ref[...] = jnp.zeros(potential_ref.shape, potential_ref.dtype)
        adjoint_ref[...] = jnp.zeros(adjoint_ref.shape, adjoint_ref.dtype)
        for offset in range(3):
            for i, block in enumerate(part_of(gathered, blocks, panels, offset)):
                stack[offset * group_blocks + i] = jnp.concatenate([block, turned(block)], axis=0)
        for i, block in enumerate(part_of(gathered, blocks, panels, 3)):
            block = block.astype(jnp.float32).T
            across[i] = jnp.concatenate([block, turned_rows(block)], axis=1).astype(jnp.bfloat16)

    def work(slot):
        target, source = place(*ids, slot, group_blocks, blocks)
        real, imag = held[slot, 0], held[slot, 1]
        potential_ref[target] += jnp.dot(
            jnp.concatenate([real, imag], axis=1), stack[source], preferred_element_type=jnp.float32
        )
        adjoint_ref[source] += jnp.dot(
            across[target], jnp.concatenate([real, imag], axis=0), preferred_element_type=jnp.float32
        )

    each_slot(chunk, slot_refs, held, ids, id_sems, sems, prepare, work)


def finish_kernel(blocks, *refs):
    *parts, potential_ref, adjoint_ref = refs
    total = parts[0][...]
    for part in parts[1:]:
        total = total + part[...]
    panels = total.shape[1]
    for b in range(blocks):
        potential_ref[b * panels : (b + 1) * panels] = total[b]
        adjoint_ref[b * panels : (b + 1) * panels] = total[blocks + b].T


def local(strengths, adjoint_weights, kernels, target_ids, source_ids, live_slots):
    slots, _, panels, _ = kernels.shape
    width = strengths.shape[1]
    blocks = strengths.shape[0] // panels
    clusters = lax.axis_size("clu")
    group_blocks = clusters * blocks
    sources = 3 * group_blocks
    pairs = group_blocks * sources
    chunk = 8 if slots % 8 == 0 else 1
    in_vmem, in_smem, in_hbm = (pl.BlockSpec(memory_space=m) for m in (pltpu.VMEM, pltpu.SMEM, pltpu.HBM))
    f32, bf16 = jnp.float32, jnp.bfloat16
    slot_args = (live_slots,) + tuple(
        pltpu.with_memory_space_constraint(x, pltpu.HBM) for x in (target_ids, source_ids, kernels)
    )
    held = pltpu.VMEM(kernels.shape, bf16)
    fetch = [
        pltpu.SMEM(target_ids.shape, jnp.int32),
        pltpu.SMEM(source_ids.shape, jnp.int32),
        pltpu.SemaphoreType.DMA((2,)),
        pltpu.SemaphoreType.DMA((slots // chunk,)),
    ]

    def call(body, shapes, args, specs=None, scratch=(), mib=8, flops=0):
        single = not isinstance(shapes, tuple)
        return pl.pallas_call(
            body,
            out_shape=shapes,
            in_specs=specs or [in_vmem] * len(args),
            out_specs=in_vmem if single else (in_vmem,) * len(shapes),
            scratch_shapes=scratch,
            compiler_params=pltpu.CompilerParams(vmem_limit_bytes=mib << 20),
            cost_estimate=pl.CostEstimate(flops=flops, bytes_accessed=1 << 20, transcendentals=0),
        )(*args)

    def shape(*dims, kind=f32):
        return jax.ShapeDtypeStruct(dims, kind)

    def with_halo(token):
        first, second = exchange_beside(strengths, "grp", 0), exchange_beside(strengths, "grp", 1)
        mine = call(
            join_kernel,
            shape(4 * blocks * panels, width, kind=bf16),
            (first, strengths, second, adjoint_weights, token),
            [in_vmem] * 4 + [in_hbm],
        )
        return [mine] + [exchange(mine, "clu", k) for k in range(1, clusters)]

    block_sums = shape(group_blocks, panels, width)
    if pairs <= slots:
        total = call(
            functools.partial(combine_kernel, group_blocks, blocks, chunk),
            pltpu.VMEM((pairs, 2 * panels, panels), f32),
            slot_args,
            [in_smem] + [in_hbm] * 3,
            [held, *fetch],
            mib=20,
            flops=1 << 30,
        )
        gathered = with_halo(total)
        total = pltpu.with_memory_space_constraint(total, pltpu.VMEM)
        kept = call(split_kernel, pltpu.VMEM((2, *total.shape), bf16), (total,), flops=1 << 30)
        kept = pltpu.with_memory_space_constraint(kept, pltpu.VMEM)
        first, second = call(
            functools.partial(outer_kernel, blocks, panels),
            (block_sums, block_sums),
            (kept, *gathered),
            flops=1 << 30,
        )
        potential = call(
            functools.partial(forward_kernel, blocks, panels), block_sums, (kept, *gathered), flops=1 << 30
        )
        first, second = exchange_beside(first, "grp", 0), exchange_beside(second, "grp", 1)
        parts = call(
            functools.partial(middle_kernel, blocks, panels, clusters),
            (shape(2 * blocks, panels, width),) * clusters,
            (kept, *gathered, potential, first, second),
        )
    else:
        gathered = with_halo(strengths)
        potential, adjoint = call(
            functools.partial(slots_kernel, blocks, panels, clusters, chunk),
            (block_sums, shape(sources, width, panels)),
            (*slot_args, *gathered),
            [in_smem] + [in_hbm] * 3 + [in_vmem] * clusters,
            [
                held,
                pltpu.VMEM((sources, 2 * panels, width), bf16),
                pltpu.VMEM((group_blocks, width, 2 * panels), bf16),
                *fetch,
            ],
            mib=40,
        )
        first, middle, second = (adjoint[i * group_blocks : (i + 1) * group_blocks] for i in range(3))
        adjoint = middle + exchange_beside(first, "grp", 0) + exchange_beside(second, "grp", 1)
        owned = [slice(k * blocks, (k + 1) * blocks) for k in range(clusters)]
        parts = [jnp.concatenate([potential[rows], adjoint[rows]], axis=0) for rows in owned]

    parts = [parts[0]] + [exchange(parts[k], "clu", k) for k in range(1, clusters)]
    out = shape(blocks * panels, width)
    return tuple(call(functools.partial(finish_kernel, blocks), (out, out), parts))


def solution(mesh):
    return jax.shard_map(
        local,
        mesh=mesh,
        in_specs=(
            P(("grp", "clu"), None),
            P(("grp", "clu"), None),
            P(("grp", "clu"), None, None, None),
            P(("grp", "clu")),
            P(("grp", "clu")),
            P(("grp", "clu")),
        ),
        out_specs=(P(("grp", "clu"), None), P(("grp", "clu"), None)),
        check_vma=False,
    )
```

time: 47.5 us -> 38.8 us (0.82)
  the two profiles are of different devices: /device:TPU:8 before, /device:TPU:16 now
where the time goes in v3:
time: 38.8 us; the launch traced here: 38.7 us
  waiting for transfers between devices  15.6 us (40%)
  starting transfers between devices  12.1 us (31%)
  Pallas kernels  9.52 us (25%)
  between operations  1.41 us (4%)
    ppermute x6, waiting for transfers between devices, exchange(): lax.ppermute(value, axis, [(i, i ^ step) for i in range(lax.axis_size(axi...  12.1 us
    pallas_call x7, Pallas kernels, call(): pl.pallas_call(body, out_shape=shapes, in_specs=specs or [in_vmem] * len(...  9.52 us
    ppermute x6, starting transfers between devices, exchange(): lax.ppermute(value, axis, [(i, i ^ step) for i in range(lax.axis_size(axi...  7.11 us
    ppermute x4, starting transfers between devices, exchange_beside(): return lax.ppermute(value, axis, pairs + [(j, i) for i, j in pairs])  4.96 us
    ppermute x4, waiting for transfers between devices, exchange_beside(): return lax.ppermute(value, axis, pairs + [(j, i) for i, j in pairs])  3.53 us
  transfers between devices with their start and end apart: 10, of which 5 were waited for; matrix products, arithmetic and copies ran while one was open for 0% of the time, Pallas kernels for 19%

profile of v3, /device:TPU:16, one launch (start us, length us, event | category | flops | bytes accessed | tf_op | source)
XLA Modules:
  0.0 38.7 jit_solution(11232061623266873156)
XLA Ops:
  0.6 0.1 collective-permute-start
  0.7 2.4 %collective-permute-start.1 = (bf16[128,128]{1,0:T(8,128)(2,1)}, bf16[128,128]{1,0:T(8,128)(2,1)S(1)}, u32[]{:S(2)}, u32[]{:S(2)}) collective-permute-start(bf16[128,128]{1,0:T(8,128)(2,1)} %own_ref.1), channel_id=1, source_target_pairs={{4,8},{12,16},{20,24},{8,4},{16,12},{24,20},{5,9},{13,17},{21,25},... | collective-permute-start | bytes 98312 | tf_op jit(solution)/shard_map/ppermute | solution.py:17
  3.8 4.8 %shard_map.77.total._ = f32[48,256,128]{2,1,0:T(8,128)S(1)} custom-call(s32[1]{0:T(128)S(6)} %copy.8.refs_0_, s32[192]{0:T(256)} %refs_1_.1, s32[192]{0:T(256)} %refs_2_.1, bf16[192,2,128,128]{3,2,1,0:T(8,128)(2,1)} %refs_3_.1), custom_call_target="tpu_custom_call" | custom-call | flops 1073741824 | bytes 1048576 | tf_op jit(solution)/shard_map/pallas_call | solution.py:244
  8.6 0.0 collective-permute-done.first_ref
  8.7 2.5 %collective-permute-start.4 = (bf16[512,128]{1,0:T(8,128)(2,1)S(1)}, bf16[512,128]{1,0:T(8,128)(2,1)S(1)}, u32[]{:S(2)}, u32[]{:S(2)}) collective-permute-start(bf16[512,128]{1,0:T(8,128)(2,1)S(1)} %shard_map.79.refs_0_), channel_id=1, source_target_pairs={{0,3},{1,2},{2,1},{3,0},{4,7},{5,6},{6,5},{7,4},{8,11},{9,10},{10,... | collective-permute-start | bytes 393224 | tf_op jit(solution)/shard_map/ppermute | solution.py:12
  11.2 0.5 %collective-permute-start.3 = (bf16[512,128]{1,0:T(8,128)(2,1)S(1)}, bf16[512,128]{1,0:T(8,128)(2,1)S(1)}, u32[]{:S(2)}, u32[]{:S(2)}) collective-permute-start(bf16[512,128]{1,0:T(8,128)(2,1)S(1)} %shard_map.79.refs_0_), channel_id=1, source_target_pairs={{0,2},{1,3},{2,0},{3,1},{4,6},{5,7},{6,4},{7,5},{8,10},{9,11},{10,... | collective-permute-start | bytes 393224 | tf_op jit(solution)/shard_map/ppermute | solution.py:12
  11.7 0.5 %collective-permute-start.2 = (bf16[512,128]{1,0:T(8,128)(2,1)S(1)}, bf16[512,128]{1,0:T(8,128)(2,1)S(1)}, u32[]{:S(2)}, u32[]{:S(2)}) collective-permute-start(bf16[512,128]{1,0:T(8,128)(2,1)S(1)} %shard_map.79.refs_0_), channel_id=1, source_target_pairs={{0,1},{1,0},{2,3},{3,2},{4,5},{5,4},{6,7},{7,6},{8,9},{9,8},{10,11... | collective-permute-start | bytes 393224 | tf_op jit(solution)/shard_map/ppermute | solution.py:12
  12.3 0.8 %shard_map.78.pairs_ref = bf16[2,48,256,128]{3,2,1,0:T(8,128)(2,1)S(1)} custom-call(f32[48,256,128]{2,1,0:T(8,128)S(1)} %shard_map.77.total._), custom_call_target="tpu_custom_call" | custom-call | flops 1073741824 | bytes 1048576 | tf_op jit(solution)/shard_map/pallas_call | solution.py:244
  13.1 2.9 %collective-permute-done.4.refs_3_ = bf16[512,128]{1,0:T(8,128)(2,1)S(1)} collective-permute-done((bf16[512,128]{1,0:T(8,128)(2,1)S(1)}, bf16[512,128]{1,0:T(8,128)(2,1)S(1)}, u32[]{:S(2)}, u32[]{:S(2)}) %collective-permute-start.4) | collective-permute-done | bytes 131104 | tf_op jit(solution)/shard_map/ppermute | solution.py:12
  16.0 2.9 %collective-permute-done.3.refs_2_ = bf16[512,128]{1,0:T(8,128)(2,1)S(1)} collective-permute-done((bf16[512,128]{1,0:T(8,128)(2,1)S(1)}, bf16[512,128]{1,0:T(8,128)(2,1)S(1)}, u32[]{:S(2)}, u32[]{:S(2)}) %collective-permute-start.3) | collective-permute-done | bytes 131104 | tf_op jit(solution)/shard_map/ppermute | solution.py:12
  18.9 0.0 collective-permute-done.2.refs_1_
  18.9 0.8 %shard_map.81 = (f32[4,128,128]{2,1,0:T(8,128)S(1)}, f32[4,128,128]{2,1,0:T(8,128)S(1)}) custom-call(bf16[2,48,256,128]{3,2,1,0:T(8,128)(2,1)S(1)} %shard_map.78.pairs_ref, bf16[512,128]{1,0:T(8,128)(2,1)S(1)} %shard_map.79.refs_0_, bf16[512,128]{1,0:T(8,128)(2,1)S(1)} %collective-permute-done.2.refs_1_, ...), custom_call_target="tpu_custom_call" | custom-call | flops 1073741824 | bytes 1048576 | tf_op jit(solution)/shard_map/pallas_call | solution.py:244
  19.6 0.2 collective-permute-start.5
  19.8 2.3 %collective-permute-start.6 = (f32[4,128,128]{2,1,0:T(8,128)S(1)}, f32[4,128,128]{2,1,0:T(8,128)S(1)}, u32[]{:S(2)}, u32[]{:S(2)}) collective-permute-start(f32[4,128,128]{2,1,0:T(8,128)S(1)} %get-tuple-element.9), channel_id=1, source_target_pairs={{4,8},{12,16},{20,24},{8,4},{16,12},{24,20},{5,9},{13,17},{21,25},... | collective-permute-start | bytes 786440 | tf_op jit(solution)/shard_map/ppermute | solution.py:17
  22.1 1.9 %shard_map.80.refs_4_ = f32[4,128,128]{2,1,0:T(8,128)S(1)} custom-call(bf16[2,48,256,128]{3,2,1,0:T(8,128)(2,1)S(1)} %shard_map.78.pairs_ref, bf16[512,128]{1,0:T(8,128)(2,1)S(1)} %shard_map.79.refs_0_, bf16[512,128]{1,0:T(8,128)(2,1)S(1)} %collective-permute-done.2.refs_1_, bf16[512,128]{1,0:T(8,128)(2,1)S(1)} %collective-permute-done.3.refs_2_, ...), custom_call_target="tpu_custom_call" | custom-call | flops 1073741824 | bytes 1048576 | tf_op jit(solution)/shard_map/pallas_call | solution.py:244
  24.0 0.0 collective-permute-done.5.refs_5_
  24.0 3.5 %collective-permute-done.6.refs_6_ = f32[4,128,128]{2,1,0:T(8,128)S(1)} collective-permute-done((f32[4,128,128]{2,1,0:T(8,128)S(1)}, f32[4,128,128]{2,1,0:T(8,128)S(1)}, u32[]{:S(2)}, u32[]{:S(2)}) %collective-permute-start.6) | collective-permute-done | bytes 262176 | tf_op jit(solution)/shard_map/ppermute | solution.py:17
  27.5 0.5 %shard_map.82 = (f32[2,128,128]{2,1,0:T(8,128)S(1)}, f32[2,128,128]{2,1,0:T(8,128)S(1)}, f32[2,128,128]{2,1,0:T(8,128)S(1)}, f32[2,128,128]{2,1,0:T(8,128)S(1)}) custom-call(bf16[2,48,256,128]{3,2,1,0:T(8,128)(2,1)S(1)} %shard_map.78.pairs_ref, bf16[512,128]{1,0:T(8,128)(2,1)S(1)} %shard_map.79.refs_0_, bf16[512,128]{1,0:T(8,128)(2,1)S(1)} %collective-permute-done.2.refs_1_, ...), custom_call_target="tpu_custom_call" | custom-call | bytes 1048576 | tf_op jit(solution)/shard_map/pallas_call | solution.py:244
  28.0 1.6 %collective-permute-start.7 = (f32[2,128,128]{2,1,0:T(8,128)S(1)}, f32[2,128,128]{2,1,0:T(8,128)S(1)}, u32[]{:S(2)}, u32[]{:S(2)}) collective-permute-start(f32[2,128,128]{2,1,0:T(8,128)S(1)} %get-tuple-element.11), channel_id=1, source_target_pairs={{0,1},{1,0},{2,3},{3,2},{4,5},{5,4},{6,7},{7,6},{8,9},{9,8},{10,11... | collective-permute-start | bytes 393224 | tf_op jit(solution)/shard_map/ppermute | solution.py:12
  29.6 0.9 %collective-permute-start.8 = (f32[2,128,128]{2,1,0:T(8,128)S(1)}, f32[2,128,128]{2,1,0:T(8,128)S(1)}, u32[]{:S(2)}, u32[]{:S(2)}) collective-permute-start(f32[2,128,128]{2,1,0:T(8,128)S(1)} %get-tuple-element.12), channel_id=1, source_target_pairs={{0,2},{1,3},{2,0},{3,1},{4,6},{5,7},{6,4},{7,5},{8,10},{9,11},{10,... | collective-permute-start | bytes 393224 | tf_op jit(solution)/shard_map/ppermute | solution.py:12
  30.5 1.1 %collective-permute-start.9 = (f32[2,128,128]{2,1,0:T(8,128)S(1)}, f32[2,128,128]{2,1,0:T(8,128)S(1)}, u32[]{:S(2)}, u32[]{:S(2)}) collective-permute-start(f32[2,128,128]{2,1,0:T(8,128)S(1)} %get-tuple-element.13), channel_id=1, source_target_pairs={{0,3},{1,2},{2,1},{3,0},{4,7},{5,6},{6,5},{7,4},{8,11},{9,10},{10,... | collective-permute-start | bytes 393224 | tf_op jit(solution)/shard_map/ppermute | solution.py:12
  31.6 2.7 %collective-permute-done.7.refs_1_ = f32[2,128,128]{2,1,0:T(8,128)S(1)} collective-permute-done((f32[2,128,128]{2,1,0:T(8,128)S(1)}, f32[2,128,128]{2,1,0:T(8,128)S(1)}, u32[]{:S(2)}, u32[]{:S(2)}) %collective-permute-start.7) | collective-permute-done | bytes 131104 | tf_op jit(solution)/shard_map/ppermute | solution.py:12
  34.2 3.7 %collective-permute-done.8.refs_2_ = f32[2,128,128]{2,1,0:T(8,128)S(1)} collective-permute-done((f32[2,128,128]{2,1,0:T(8,128)S(1)}, f32[2,128,128]{2,1,0:T(8,128)S(1)}, u32[]{:S(2)}, u32[]{:S(2)}) %collective-permute-start.8) | collective-permute-done | bytes 131104 | tf_op jit(solution)/shard_map/ppermute | solution.py:12
  37.9 0.7 %shard_map.83 = (f32[128,128]{1,0:T(8,128)}, f32[128,128]{1,0:T(8,128)}) custom-call(f32[2,128,128]{2,1,0:T(8,128)S(1)} %get-tuple-element.10.refs_0_, f32[2,128,128]{2,1,0:T(8,128)S(1)} %collective-permute-done.7.refs_1_, f32[2,128,128]{2,1,0:T(8,128)S(1)} %collective-permute-done.8.refs_2_, f32[2,128,128]{2,1,0:T(8,128)S(1)} %collective-permute-done.9.refs_3_), custom_call_target="tpu_custom_call" | custom-call | bytes 1048576 | tf_op jit(solution)/shard_map/pallas_call | solution.py:244
  (7 shorter events, 0.0 us)
Async XLA Ops:
  0.6 8.0 %collective-permute-start = (bf16[128,128]{1,0:T(8,128)(2,1)}, bf16[128,128]{1,0:T(8,128)(2,1)S(1)}, u32[]{:S(2)}, u32[]{:S(2)}) collective-permute-start(bf16[128,128]{1,0:T(8,128)(2,1)} %own_ref.1), channel_id=1, source_target_pairs={{0,4},{8,12},{16,20},{24,28},{4,0},{12,8},{20,16},{28,24},{1,5},{9... | collective-permute-start | bytes 98312 | tf_op jit(solution)/shard_map/ppermute | solution.py:17
  0.7 7.9 %collective-permute-start.1 = (bf16[128,128]{1,0:T(8,128)(2,1)}, bf16[128,128]{1,0:T(8,128)(2,1)S(1)}, u32[]{:S(2)}, u32[]{:S(2)}) collective-permute-start(bf16[128,128]{1,0:T(8,128)(2,1)} %own_ref.1), channel_id=1, source_target_pairs={{4,8},{12,16},{20,24},{8,4},{16,12},{24,20},{5,9},{13,17},{21,25},... | collective-permute-start | bytes 98312 | tf_op jit(solution)/shard_map/ppermute | solution.py:17
  3.8 4.9 %copy-start = (bf16[128,128]{1,0:T(8,128)(2,1)S(1)}, bf16[128,128]{1,0:T(8,128)(2,1)}, u32[]{:S(2)}) copy-start(bf16[128,128]{1,0:T(8,128)(2,1)} %own_ref.1) | copy-start | bytes 98308
  3.8 4.9 %copy-start.1 = (bf16[128,128]{1,0:T(8,128)(2,1)S(1)}, bf16[128,128]{1,0:T(8,128)(2,1)}, u32[]{:S(2)}) copy-start(bf16[128,128]{1,0:T(8,128)(2,1)} %weights_ref.1) | copy-start | bytes 98308
  8.7 7.2 %collective-permute-start.4 = (bf16[512,128]{1,0:T(8,128)(2,1)S(1)}, bf16[512,128]{1,0:T(8,128)(2,1)S(1)}, u32[]{:S(2)}, u32[]{:S(2)}) collective-permute-start(bf16[512,128]{1,0:T(8,128)(2,1)S(1)} %shard_map.79.refs_0_), channel_id=1, source_target_pairs={{0,3},{1,2},{2,1},{3,0},{4,7},{5,6},{6,5},{7,4},{8,11},{9,10},{10,... | collective-permute-start | bytes 393224 | tf_op jit(solution)/shard_map/ppermute | solution.py:12
  11.2 7.6 %collective-permute-start.3 = (bf16[512,128]{1,0:T(8,128)(2,1)S(1)}, bf16[512,128]{1,0:T(8,128)(2,1)S(1)}, u32[]{:S(2)}, u32[]{:S(2)}) collective-permute-start(bf16[512,128]{1,0:T(8,128)(2,1)S(1)} %shard_map.79.refs_0_), channel_id=1, source_target_pairs={{0,2},{1,3},{2,0},{3,1},{4,6},{5,7},{6,4},{7,5},{8,10},{9,11},{10,... | collective-permute-start | bytes 393224 | tf_op jit(solution)/shard_map/ppermute | solution.py:12
  11.7 7.1 %collective-permute-start.2 = (bf16[512,128]{1,0:T(8,128)(2,1)S(1)}, bf16[512,128]{1,0:T(8,128)(2,1)S(1)}, u32[]{:S(2)}, u32[]{:S(2)}) collective-permute-start(bf16[512,128]{1,0:T(8,128)(2,1)S(1)} %shard_map.79.refs_0_), channel_id=1, source_target_pairs={{0,1},{1,0},{2,3},{3,2},{4,5},{5,4},{6,7},{7,6},{8,9},{9,8},{10,11... | collective-permute-start | bytes 393224 | tf_op jit(solution)/shard_map/ppermute | solution.py:12
  19.6 4.3 %collective-permute-start.5 = (f32[4,128,128]{2,1,0:T(8,128)S(1)}, f32[4,128,128]{2,1,0:T(8,128)S(1)}, u32[]{:S(2)}, u32[]{:S(2)}) collective-permute-start(f32[4,128,128]{2,1,0:T(8,128)S(1)} %get-tuple-element.8), channel_id=1, source_target_pairs={{0,4},{8,12},{16,20},{24,28},{4,0},{12,8},{20,16},{28,24},{1,5},{9... | collective-permute-start | bytes 786440 | tf_op jit(solution)/shard_map/ppermute | solution.py:17
  19.8 7.7 %collective-permute-start.6 = (f32[4,128,128]{2,1,0:T(8,128)S(1)}, f32[4,128,128]{2,1,0:T(8,128)S(1)}, u32[]{:S(2)}, u32[]{:S(2)}) collective-permute-start(f32[4,128,128]{2,1,0:T(8,128)S(1)} %get-tuple-element.9), channel_id=1, source_target_pairs={{4,8},{12,16},{20,24},{8,4},{16,12},{24,20},{5,9},{13,17},{21,25},... | collective-permute-start | bytes 786440 | tf_op jit(solution)/shard_map/ppermute | solution.py:17
  28.0 6.2 %collective-permute-start.7 = (f32[2,128,128]{2,1,0:T(8,128)S(1)}, f32[2,128,128]{2,1,0:T(8,128)S(1)}, u32[]{:S(2)}, u32[]{:S(2)}) collective-permute-start(f32[2,128,128]{2,1,0:T(8,128)S(1)} %get-tuple-element.11), channel_id=1, source_target_pairs={{0,1},{1,0},{2,3},{3,2},{4,5},{5,4},{6,7},{7,6},{8,9},{9,8},{10,11... | collective-permute-start | bytes 393224 | tf_op jit(solution)/shard_map/ppermute | solution.py:12
  29.6 8.4 %collective-permute-start.8 = (f32[2,128,128]{2,1,0:T(8,128)S(1)}, f32[2,128,128]{2,1,0:T(8,128)S(1)}, u32[]{:S(2)}, u32[]{:S(2)}) collective-permute-start(f32[2,128,128]{2,1,0:T(8,128)S(1)} %get-tuple-element.12), channel_id=1, source_target_pairs={{0,2},{1,3},{2,0},{3,1},{4,6},{5,7},{6,4},{7,5},{8,10},{9,11},{10,... | collective-permute-start | bytes 393224 | tf_op jit(solution)/shard_map/ppermute | solution.py:12
  30.5 7.5 %collective-permute-start.9 = (f32[2,128,128]{2,1,0:T(8,128)S(1)}, f32[2,128,128]{2,1,0:T(8,128)S(1)}, u32[]{:S(2)}, u32[]{:S(2)}) collective-permute-start(f32[2,128,128]{2,1,0:T(8,128)S(1)} %get-tuple-element.13), channel_id=1, source_target_pairs={{0,3},{1,2},{2,1},{3,0},{4,7},{5,6},{6,5},{7,4},{8,11},{9,10},{10,... | collective-permute-start | bytes 393224 | tf_op jit(solution)/shard_map/ppermute | solution.py:12

commit v4 on v3

--- a/solution.py
+++ b/solution.py
@@ -89,7 +89,9 @@
     each_slot(chunk, slot_refs, held, ids, id_sems, sems, clear, add)
 
 
-def split_kernel(total, out_ref):
+def split_kernel(blocks, panels, _, total, *refs):
+    *gathered, out_ref, across_ref = refs
+
     @pl.loop(0, total.shape[0])
     def _(pair):
         value = total[pair]
@@ -97,11 +99,26 @@
         out_ref[0, pair] = high
         out_ref[1, pair] = (value - high.astype(jnp.float32)).astype(jnp.bfloat16)
 
-
-def join_kernel(first_ref, own_ref, second_ref, weights_ref, _, out_ref):
-    rows = own_ref.shape[0]
-    for i, ref in enumerate((first_ref, own_ref, second_ref, weights_ref)):
-        out_ref[i * rows : (i + 1) * rows] = ref[...]
+    for i, block in enumerate(part_of(gathered, blocks, panels, 1)):
+        across_ref[:, 2 * i * panels : 2 * (i + 1) * panels] = crossed(block)
+
+
+def pack_kernel(strengths_ref, weights_ref, out_ref, sems):
+    rows = strengths_ref.shape[0]
+    copies = [
+        pltpu.make_async_copy(ref, out_ref.at[pl.ds(i * rows, rows)], sems.at[i])
+        for i, ref in enumerate((strengths_ref, weights_ref))
+    ]
+    for copy in copies:
+        copy.start()
+    for copy in copies:
+        copy.wait()
+
+
+def group_kernel(blocks, panels, *refs):
+    *gathered, _, out_ref = refs
+    for i, block in enumerate(part_of(gathered, blocks, panels, 0)):
+        out_ref[i * panels : (i + 1) * panels] = block
 
 
 def part_of(gathered, blocks, panels, part):
@@ -110,24 +127,18 @@
             yield ref[pl.ds((part * blocks + b) * panels, panels), :]
 
 
-def weights_across(gathered, blocks, panels):
-    across = []
-    for block in part_of(gathered, blocks, panels, 3):
-        block = block.astype(jnp.float32).T
-        across += [block, turned_rows(block)]
-    return jnp.concatenate(across, axis=1).astype(jnp.bfloat16)
-
-
-def strengths_stacked(gathered, blocks, panels):
-    stack = []
-    for offset in range(3):
-        for block in part_of(gathered, blocks, panels, offset):
-            stack += [block, turned(block)]
-    return jnp.concatenate(stack, axis=0)
-
-
-def adjoint_of(pairs_ref, weights, first, count):
+def crossed(block):
+    block = block.astype(jnp.float32).T
+    return jnp.concatenate([block, turned_rows(block)], axis=1).astype(jnp.bfloat16)
+
+
+def stacked(block):
+    return jnp.concatenate([block, turned(block)], axis=0)
+
+
+def adjoint_of(pairs_ref, across_ref, first, count):
     width = pairs_ref.shape[3]
+    weights = across_ref[...]
     targets = weights.shape[1] // pairs_ref.shape[2]
     sources = pairs_ref.shape[1] // targets
     both = jnp.concatenate([weights, weights], axis=1)
@@ -142,21 +153,22 @@
             yield i + j, product[:, j * width : (j + 1) * width]
 
 
-def outer_kernel(blocks, panels, pairs_ref, *refs):
-    *gathered, first_ref, second_ref = refs
+def outer_kernel(pairs_ref, across_ref, first_ref, second_ref):
     count = first_ref.shape[0]
-    weights = weights_across(gathered, blocks, panels)
-    for i, value in adjoint_of(pairs_ref, weights, 0, count):
+    for i, value in adjoint_of(pairs_ref, across_ref, 0, count):
         first_ref[i] = value
-    for i, value in adjoint_of(pairs_ref, weights, 2 * count, count):
+    for i, value in adjoint_of(pairs_ref, across_ref, 2 * count, count):
         second_ref[i] = value
 
 
-def forward_kernel(blocks, panels, pairs_ref, *refs):
-    *gathered, potential_ref = refs
-    targets = potential_ref.shape[0]
+def forward_kernel(pairs_ref, *refs):
+    *strengths, potential_ref = refs
+    targets, panels = potential_ref.shape[:2]
     sources = pairs_ref.shape[1] // targets
-    stack = strengths_stacked(gathered, blocks, panels)
+    stack = []
+    for ref in strengths:
+        stack += [stacked(ref[i : i + panels]) for i in range(0, ref.shape[0], panels)]
+    stack = jnp.concatenate(stack, axis=0)
     for t in range(targets):
         halves = []
         for h in range(2):
@@ -168,30 +180,27 @@
         potential_ref[t] = product[:panels] + product[panels:]
 
 
-def middle_kernel(blocks, panels, clusters, pairs_ref, *refs):
-    gathered, (potential_ref, first_ref, second_ref, *outs) = refs[:clusters], refs[clusters:]
+def middle_kernel(blocks, pairs_ref, across_ref, potential_ref, first_ref, second_ref, *outs):
     count = potential_ref.shape[0]
-    weights = weights_across(gathered, blocks, panels)
-    for i, value in adjoint_of(pairs_ref, weights, count, count):
+    for i, value in adjoint_of(pairs_ref, across_ref, count, count):
         out_ref, b = outs[i // blocks], i % blocks
         out_ref[b] = potential_ref[i]
         out_ref[blocks + b] = value + first_ref[i] + second_ref[i]
 
 
 def slots_kernel(blocks, panels, clusters, chunk, *refs):
-    slot_refs, gathered, rest = refs[:4], refs[4 : 4 + clusters], refs[4 + clusters :]
-    potential_ref, adjoint_ref, held, stack, across, *ids, id_sems, sems = rest
+    slot_refs, gathered, refs = refs[:4], refs[4 : 4 + clusters], refs[4 + clusters :]
+    strengths, (potential_ref, adjoint_ref, held, stack, across, *ids, id_sems, sems) = refs[:3], refs[3:]
     group_blocks = potential_ref.shape[0]
 
     def prepare():
         potential_ref[...] = jnp.zeros(potential_ref.shape, potential_ref.dtype)
         adjoint_ref[...] = jnp.zeros(adjoint_ref.shape, adjoint_ref.dtype)
-        for offset in range(3):
-            for i, block in enumerate(part_of(gathered, blocks, panels, offset)):
-                stack[offset * group_blocks + i] = jnp.concatenate([block, turned(block)], axis=0)
-        for i, block in enumerate(part_of(gathered, blocks, panels, 3)):
-            block = block.astype(jnp.float32).T
-            across[i] = jnp.concatenate([block, turned_rows(block)], axis=1).astype(jnp.bfloat16)
+        for offset, ref in enumerate(strengths):
+            for i in range(group_blocks):
+                stack[offset * group_blocks + i] = stacked(ref[i * panels : (i + 1) * panels])
+        for i, block in enumerate(part_of(gathered, blocks, panels, 1)):
+            across[i] = crossed(block)
 
     def work(slot):
         target, source = place(*ids, slot, group_blocks, blocks)
@@ -254,15 +263,23 @@
     def shape(*dims, kind=f32):
         return jax.ShapeDtypeStruct(dims, kind)
 
-    def with_halo(token):
-        first, second = exchange_beside(strengths, "grp", 0), exchange_beside(strengths, "grp", 1)
-        mine = call(
-            join_kernel,
-            shape(4 * blocks * panels, width, kind=bf16),
-            (first, strengths, second, adjoint_weights, token),
-            [in_vmem] * 4 + [in_hbm],
-        )
-        return [mine] + [exchange(mine, "clu", k) for k in range(1, clusters)]
+    mine = call(
+        pack_kernel,
+        shape(2 * blocks * panels, width, kind=bf16),
+        [pltpu.with_memory_space_constraint(x, pltpu.HBM) for x in (strengths, adjoint_weights)],
+        [in_hbm] * 2,
+        [pltpu.SemaphoreType.DMA((2,))],
+    )
+    gathered = [mine] + [exchange(mine, "clu", k) for k in range(1, clusters)]
+
+    def group_strengths(token):
+        own = call(
+            functools.partial(group_kernel, blocks, panels),
+            shape(group_blocks * panels, width, kind=bf16),
+            (*gathered, token),
+            [in_vmem] * clusters + [in_hbm],
+        )
+        return exchange_beside(own, "grp", 0), own, exchange_beside(own, "grp", 1)
 
     block_sums = shape(group_blocks, panels, width)
     if pairs <= slots:
@@ -273,34 +290,32 @@
             [in_smem] + [in_hbm] * 3,
             [held, *fetch],
             mib=20,
-            flops=1 << 30,
-        )
-        gathered = with_halo(total)
+            flops=1 << 33,
+        )
+        first, own, second = group_strengths(total)
         total = pltpu.with_memory_space_constraint(total, pltpu.VMEM)
-        kept = call(split_kernel, pltpu.VMEM((2, *total.shape), bf16), (total,), flops=1 << 30)
+        kept, across = call(
+            functools.partial(split_kernel, blocks, panels),
+            (pltpu.VMEM((2, *total.shape), bf16), shape(width, 2 * group_blocks * panels, kind=bf16)),
+            (own, total, *gathered),
+            [in_hbm] + [in_vmem] * (1 + clusters),
+            flops=1 << 33,
+        )
         kept = pltpu.with_memory_space_constraint(kept, pltpu.VMEM)
-        first, second = call(
-            functools.partial(outer_kernel, blocks, panels),
-            (block_sums, block_sums),
-            (kept, *gathered),
-            flops=1 << 30,
-        )
-        potential = call(
-            functools.partial(forward_kernel, blocks, panels), block_sums, (kept, *gathered), flops=1 << 30
-        )
-        first, second = exchange_beside(first, "grp", 0), exchange_beside(second, "grp", 1)
+        lower, upper = call(outer_kernel, (block_sums, block_sums), (kept, across), flops=1 << 33)
+        potential = call(forward_kernel, block_sums, (kept, first, own, second), flops=1 << 33)
+        lower, upper = exchange_beside(lower, "grp", 0), exchange_beside(upper, "grp", 1)
         parts = call(
-            functools.partial(middle_kernel, blocks, panels, clusters),
+            functools.partial(middle_kernel, blocks),
             (shape(2 * blocks, panels, width),) * clusters,
-            (kept, *gathered, potential, first, second),
+            (kept, across, potential, lower, upper),
         )
     else:
-        gathered = with_halo(strengths)
         potential, adjoint = call(
             functools.partial(slots_kernel, blocks, panels, clusters, chunk),
             (block_sums, shape(sources, width, panels)),
-            (*slot_args, *gathered),
-            [in_smem] + [in_hbm] * 3 + [in_vmem] * clusters,
+            (*slot_args, *gathered, *group_strengths(strengths)),
+            [in_smem] + [in_hbm] * 3 + [in_vmem] * (clusters + 3),
             [
                 held,
                 pltpu.VMEM((sources, 2 * panels, width), bf16),

time: 38.8 us -> 35 us (0.902)
  the two profiles are of different devices: /device:TPU:16 before, /device:TPU:12 now
where the time goes in v4:
time: 35 us; the launch traced here: 34.8 us
  starting transfers between devices  13.3 us (38%)
  Pallas kernels  10.3 us (29%)
  waiting for transfers between devices  9.77 us (28%)
  between operations  1.4 us (4%)
    pallas_call x8, Pallas kernels, call(): pl.pallas_call(body, out_shape=shapes, in_specs=specs or [in_vmem] * len(...  10.3 us
    ppermute x6, starting transfers between devices, exchange(): lax.ppermute(value, axis, [(i, i ^ step) for i in range(lax.axis_size(axi...  7.11 us
    ppermute x6, waiting for transfers between devices, exchange(): lax.ppermute(value, axis, [(i, i ^ step) for i in range(lax.axis_size(axi...  6.43 us
    ppermute x4, starting transfers between devices, exchange_beside(): return lax.ppermute(value, axis, pairs + [(j, i) for i, j in pairs])  6.19 us
    ppermute x4, waiting for transfers between devices, exchange_beside(): return lax.ppermute(value, axis, pairs + [(j, i) for i, j in pairs])  3.34 us
  transfers between devices with their start and end apart: 10, of which 3 were waited for; matrix products, arithmetic and copies ran while one was open for 0% of the time, Pallas kernels for 24%

profile of v4, /device:TPU:12, one launch (start us, length us, event | category | flops | bytes accessed | tf_op | source)
XLA Modules:
  0.0 34.8 jit_solution(8993442786103576873)
XLA Ops:
  0.6 0.8 %shard_map.77.refs_0_ = bf16[256,128]{1,0:T(8,128)(2,1)S(1)} custom-call(bf16[128,128]{1,0:T(8,128)(2,1)} %strengths_ref.1, bf16[128,128]{1,0:T(8,128)(2,1)} %weights_ref.1), custom_call_target="tpu_custom_call" | custom-call | bytes 1048576 | tf_op jit(solution)/shard_map/pallas_call | solution.py:253
  1.4 1.5 %collective-permute-start.2 = (bf16[256,128]{1,0:T(8,128)(2,1)S(1)}, bf16[256,128]{1,0:T(8,128)(2,1)S(1)}, u32[]{:S(2)}, u32[]{:S(2)}) collective-permute-start(bf16[256,128]{1,0:T(8,128)(2,1)S(1)} %shard_map.77.refs_0_), channel_id=1, source_target_pairs={{0,3},{1,2},{2,1},{3,0},{4,7},{5,6},{6,5},{7,4},{8,11},{9,10},{10,... | collective-permute-start | bytes 196616 | tf_op jit(solution)/shard_map/ppermute | solution.py:12
  2.9 1.5 %collective-permute-start.1 = (bf16[256,128]{1,0:T(8,128)(2,1)S(1)}, bf16[256,128]{1,0:T(8,128)(2,1)S(1)}, u32[]{:S(2)}, u32[]{:S(2)}) collective-permute-start(bf16[256,128]{1,0:T(8,128)(2,1)S(1)} %shard_map.77.refs_0_), channel_id=1, source_target_pairs={{0,2},{1,3},{2,0},{3,1},{4,6},{5,7},{6,4},{7,5},{8,10},{9,11},{10,... | collective-permute-start | bytes 196616 | tf_op jit(solution)/shard_map/ppermute | solution.py:12
  4.4 0.5 %collective-permute-start = (bf16[256,128]{1,0:T(8,128)(2,1)S(1)}, bf16[256,128]{1,0:T(8,128)(2,1)S(1)}, u32[]{:S(2)}, u32[]{:S(2)}) collective-permute-start(bf16[256,128]{1,0:T(8,128)(2,1)S(1)} %shard_map.77.refs_0_), channel_id=1, source_target_pairs={{0,1},{1,0},{2,3},{3,2},{4,5},{5,4},{6,7},{7,6},{8,9},{9,8},{10,11... | collective-permute-start | bytes 196616 | tf_op jit(solution)/shard_map/ppermute | solution.py:12
  5.6 4.8 %shard_map.78.refs_4_.total = f32[48,256,128]{2,1,0:T(8,128)S(1)} custom-call(s32[1]{0:T(128)S(6)} %copy.8.refs_0_, s32[192]{0:T(256)} %refs_1_.1, s32[192]{0:T(256)} %refs_2_.1, bf16[192,2,128,128]{3,2,1,0:T(8,128)(2,1)} %refs_3_.1), custom_call_target="tpu_custom_call" | custom-call | flops 8589934592 | bytes 1048576 | tf_op jit(solution)/shard_map/pallas_call | solution.py:253
  10.5 0.0 collective-permute-done.1.refs_2_
  10.5 0.0 collective-permute-done.refs_1_
  10.5 1.9 %collective-permute-start.4 = (bf16[512,128]{1,0:T(8,128)(2,1)S(1)}, bf16[512,128]{1,0:T(8,128)(2,1)S(1)}, u32[]{:S(2)}, u32[]{:S(2)}) collective-permute-start(bf16[512,128]{1,0:T(8,128)(2,1)S(1)} %shard_map.79._.refs_1_), channel_id=1, source_target_pairs={{4,8},{12,16},{20,24},{8,4},{16,12},{24,20},{5,9},{13,17},{21,25},... | collective-permute-start | bytes 393224 | tf_op jit(solution)/shard_map/ppermute | solution.py:17
  12.4 1.7 %collective-permute-start.3 = (bf16[512,128]{1,0:T(8,128)(2,1)S(1)}, bf16[512,128]{1,0:T(8,128)(2,1)S(1)}, u32[]{:S(2)}, u32[]{:S(2)}) collective-permute-start(bf16[512,128]{1,0:T(8,128)(2,1)S(1)} %shard_map.79._.refs_1_), channel_id=1, source_target_pairs={{0,4},{8,12},{16,20},{24,28},{4,0},{12,8},{20,16},{28,24},{1,5},{9... | collective-permute-start | bytes 393224 | tf_op jit(solution)/shard_map/ppermute | solution.py:17
  14.2 0.9 %shard_map.80 = (bf16[2,48,256,128]{3,2,1,0:T(8,128)(2,1)S(1)}, bf16[128,1024]{1,0:T(8,128)(2,1)S(1)}) custom-call(bf16[512,128]{1,0:T(8,128)(2,1)S(1)} %shard_map.79._.refs_1_, f32[48,256,128]{2,1,0:T(8,128)S(1)} %shard_map.78.refs_4_.total, bf16[256,128]{1,0:T(8,128)(2,1)S(1)} %shard_map.77.refs_0_, bf16[256,128]{1,0:T(8,128)(2,1)S(1)} %collective-permute-done.refs_1_, ...), custom_call_target="tpu_custom_call" | custom-call | flops 8589934592 | bytes 1048576 | tf_op jit(solution)/shard_map/pallas_call | solution.py:253
  15.1 0.7 %shard_map.82 = (f32[4,128,128]{2,1,0:T(8,128)S(1)}, f32[4,128,128]{2,1,0:T(8,128)S(1)}) custom-call(bf16[2,48,256,128]{3,2,1,0:T(8,128)(2,1)S(1)} %get-tuple-element.10.pairs_ref, bf16[128,1024]{1,0:T(8,128)(2,1)S(1)} %get-tuple-element.11.across_ref), custom_call_target="tpu_custom_call" | custom-call | flops 8589934592 | bytes 1048576 | tf_op jit(solution)/shard_map/pallas_call | solution.py:253
  15.8 0.1 collective-permute-start.5
  15.9 2.4 %collective-permute-start.6 = (f32[4,128,128]{2,1,0:T(8,128)S(1)}, f32[4,128,128]{2,1,0:T(8,128)S(1)}, u32[]{:S(2)}, u32[]{:S(2)}) collective-permute-start(f32[4,128,128]{2,1,0:T(8,128)S(1)} %get-tuple-element.13), channel_id=1, source_target_pairs={{4,8},{12,16},{20,24},{8,4},{16,12},{24,20},{5,9},{13,17},{21,25},... | collective-permute-start | bytes 786440 | tf_op jit(solution)/shard_map/ppermute | solution.py:17
  18.4 0.0 collective-permute-done.4.refs_2_
  18.4 0.0 collective-permute-done.3.refs_0_
  18.4 1.9 %shard_map.81.potential_ref = f32[4,128,128]{2,1,0:T(8,128)S(1)} custom-call(bf16[2,48,256,128]{3,2,1,0:T(8,128)(2,1)S(1)} %get-tuple-element.10.pairs_ref, bf16[512,128]{1,0:T(8,128)(2,1)S(1)} %collective-permute-done.3.refs_0_, bf16[512,128]{1,0:T(8,128)(2,1)S(1)} %shard_map.79._.refs_1_, bf16[512,128]{1,0:T(8,128)(2,1)S(1)} %collective-permute-done.4.refs_2_), custom_call_target="tpu_custom_call" | custom-call | flops 8589934592 | bytes 1048576 | tf_op jit(solution)/shard_map/pallas_call | solution.py:253
  20.3 3.3 %collective-permute-done.6.second_ref = f32[4,128,128]{2,1,0:T(8,128)S(1)} collective-permute-done((f32[4,128,128]{2,1,0:T(8,128)S(1)}, f32[4,128,128]{2,1,0:T(8,128)S(1)}, u32[]{:S(2)}, u32[]{:S(2)}) %collective-permute-start.6) | collective-permute-done | bytes 262176 | tf_op jit(solution)/shard_map/ppermute | solution.py:17
  23.6 0.4 %shard_map.83 = (f32[2,128,128]{2,1,0:T(8,128)S(1)}, f32[2,128,128]{2,1,0:T(8,128)S(1)}, f32[2,128,128]{2,1,0:T(8,128)S(1)}, f32[2,128,128]{2,1,0:T(8,128)S(1)}) custom-call(bf16[2,48,256,128]{3,2,1,0:T(8,128)(2,1)S(1)} %get-tuple-element.10.pairs_ref, bf16[128,1024]{1,0:T(8,128)(2,1)S(1)} %get-tuple-element.11.across_ref, ...), custom_call_target="tpu_custom_call" | custom-call | bytes 1048576 | tf_op jit(solution)/shard_map/pallas_call | solution.py:253
  24.1 1.6 %collective-permute-start.7 = (f32[2,128,128]{2,1,0:T(8,128)S(1)}, f32[2,128,128]{2,1,0:T(8,128)S(1)}, u32[]{:S(2)}, u32[]{:S(2)}) collective-permute-start(f32[2,128,128]{2,1,0:T(8,128)S(1)} %get-tuple-element.15), channel_id=1, source_target_pairs={{0,1},{1,0},{2,3},{3,2},{4,5},{5,4},{6,7},{7,6},{8,9},{9,8},{10,11... | collective-permute-start | bytes 393224 | tf_op jit(solution)/shard_map/ppermute | solution.py:12
  25.6 0.5 %collective-permute-start.8 = (f32[2,128,128]{2,1,0:T(8,128)S(1)}, f32[2,128,128]{2,1,0:T(8,128)S(1)}, u32[]{:S(2)}, u32[]{:S(2)}) collective-permute-start(f32[2,128,128]{2,1,0:T(8,128)S(1)} %get-tuple-element.16), channel_id=1, source_target_pairs={{0,2},{1,3},{2,0},{3,1},{4,6},{5,7},{6,4},{7,5},{8,10},{9,11},{10,... | collective-permute-start | bytes 393224 | tf_op jit(solution)/shard_map/ppermute | solution.py:12
  26.1 1.5 %collective-permute-start.9 = (f32[2,128,128]{2,1,0:T(8,128)S(1)}, f32[2,128,128]{2,1,0:T(8,128)S(1)}, u32[]{:S(2)}, u32[]{:S(2)}) collective-permute-start(f32[2,128,128]{2,1,0:T(8,128)S(1)} %get-tuple-element.17), channel_id=1, source_target_pairs={{0,3},{1,2},{2,1},{3,0},{4,7},{5,6},{6,5},{7,4},{8,11},{9,10},{10,... | collective-permute-start | bytes 393224 | tf_op jit(solution)/shard_map/ppermute | solution.py:12
  27.6 2.7 %collective-permute-done.7.refs_1_ = f32[2,128,128]{2,1,0:T(8,128)S(1)} collective-permute-done((f32[2,128,128]{2,1,0:T(8,128)S(1)}, f32[2,128,128]{2,1,0:T(8,128)S(1)}, u32[]{:S(2)}, u32[]{:S(2)}) %collective-permute-start.7) | collective-permute-done | bytes 131104 | tf_op jit(solution)/shard_map/ppermute | solution.py:12
  30.3 3.7 %collective-permute-done.8.refs_2_ = f32[2,128,128]{2,1,0:T(8,128)S(1)} collective-permute-done((f32[2,128,128]{2,1,0:T(8,128)S(1)}, f32[2,128,128]{2,1,0:T(8,128)S(1)}, u32[]{:S(2)}, u32[]{:S(2)}) %collective-permute-start.8) | collective-permute-done | bytes 131104 | tf_op jit(solution)/shard_map/ppermute | solution.py:12
  34.0 0.7 %shard_map.84 = (f32[128,128]{1,0:T(8,128)}, f32[128,128]{1,0:T(8,128)}) custom-call(f32[2,128,128]{2,1,0:T(8,128)S(1)} %get-tuple-element.14.refs_0_, f32[2,128,128]{2,1,0:T(8,128)S(1)} %collective-permute-done.7.refs_1_, f32[2,128,128]{2,1,0:T(8,128)S(1)} %collective-permute-done.8.refs_2_, f32[2,128,128]{2,1,0:T(8,128)S(1)} %collective-permute-done.9.refs_3_), custom_call_target="tpu_custom_call" | custom-call | bytes 1048576 | tf_op jit(solution)/shard_map/pallas_call | solution.py:253
  (4 shorter events, 0.0 us)
Async XLA Ops:
  1.4 9.0 %collective-permute-start.2 = (bf16[256,128]{1,0:T(8,128)(2,1)S(1)}, bf16[256,128]{1,0:T(8,128)(2,1)S(1)}, u32[]{:S(2)}, u32[]{:S(2)}) collective-permute-start(bf16[256,128]{1,0:T(8,128)(2,1)S(1)} %shard_map.77.refs_0_), channel_id=1, source_target_pairs={{0,3},{1,2},{2,1},{3,0},{4,7},{5,6},{6,5},{7,4},{8,11},{9,10},{10,... | collective-permute-start | bytes 196616 | tf_op jit(solution)/shard_map/ppermute | solution.py:12
  2.9 7.5 %collective-permute-start.1 = (bf16[256,128]{1,0:T(8,128)(2,1)S(1)}, bf16[256,128]{1,0:T(8,128)(2,1)S(1)}, u32[]{:S(2)}, u32[]{:S(2)}) collective-permute-start(bf16[256,128]{1,0:T(8,128)(2,1)S(1)} %shard_map.77.refs_0_), channel_id=1, source_target_pairs={{0,2},{1,3},{2,0},{3,1},{4,6},{5,7},{6,4},{7,5},{8,10},{9,11},{10,... | collective-permute-start | bytes 196616 | tf_op jit(solution)/shard_map/ppermute | solution.py:12
  4.4 6.0 %collective-permute-start = (bf16[256,128]{1,0:T(8,128)(2,1)S(1)}, bf16[256,128]{1,0:T(8,128)(2,1)S(1)}, u32[]{:S(2)}, u32[]{:S(2)}) collective-permute-start(bf16[256,128]{1,0:T(8,128)(2,1)S(1)} %shard_map.77.refs_0_), channel_id=1, source_target_pairs={{0,1},{1,0},{2,3},{3,2},{4,5},{5,4},{6,7},{7,6},{8,9},{9,8},{10,11... | collective-permute-start | bytes 196616 | tf_op jit(solution)/shard_map/ppermute | solution.py:12
  10.5 7.9 %collective-permute-start.4 = (bf16[512,128]{1,0:T(8,128)(2,1)S(1)}, bf16[512,128]{1,0:T(8,128)(2,1)S(1)}, u32[]{:S(2)}, u32[]{:S(2)}) collective-permute-start(bf16[512,128]{1,0:T(8,128)(2,1)S(1)} %shard_map.79._.refs_1_), channel_id=1, source_target_pairs={{4,8},{12,16},{20,24},{8,4},{16,12},{24,20},{5,9},{13,17},{21,25},... | collective-permute-start | bytes 393224 | tf_op jit(solution)/shard_map/ppermute | solution.py:17
  12.4 6.0 %collective-permute-start.3 = (bf16[512,128]{1,0:T(8,128)(2,1)S(1)}, bf16[512,128]{1,0:T(8,128)(2,1)S(1)}, u32[]{:S(2)}, u32[]{:S(2)}) collective-permute-start(bf16[512,128]{1,0:T(8,128)(2,1)S(1)} %shard_map.79._.refs_1_), channel_id=1, source_target_pairs={{0,4},{8,12},{16,20},{24,28},{4,0},{12,8},{20,16},{28,24},{1,5},{9... | collective-permute-start | bytes 393224 | tf_op jit(solution)/shard_map/ppermute | solution.py:17
  15.8 4.4 %collective-permute-start.5 = (f32[4,128,128]{2,1,0:T(8,128)S(1)}, f32[4,128,128]{2,1,0:T(8,128)S(1)}, u32[]{:S(2)}, u32[]{:S(2)}) collective-permute-start(f32[4,128,128]{2,1,0:T(8,128)S(1)} %get-tuple-element.12), channel_id=1, source_target_pairs={{0,4},{8,12},{16,20},{24,28},{4,0},{12,8},{20,16},{28,24},{1,5},{9... | collective-permute-start | bytes 786440 | tf_op jit(solution)/shard_map/ppermute | solution.py:17
  15.9 7.7 %collective-permute-start.6 = (f32[4,128,128]{2,1,0:T(8,128)S(1)}, f32[4,128,128]{2,1,0:T(8,128)S(1)}, u32[]{:S(2)}, u32[]{:S(2)}) collective-permute-start(f32[4,128,128]{2,1,0:T(8,128)S(1)} %get-tuple-element.13), channel_id=1, source_target_pairs={{4,8},{12,16},{20,24},{8,4},{16,12},{24,20},{5,9},{13,17},{21,25},... | collective-permute-start | bytes 786440 | tf_op jit(solution)/shard_map/ppermute | solution.py:17
  24.1 6.3 %collective-permute-start.7 = (f32[2,128,128]{2,1,0:T(8,128)S(1)}, f32[2,128,128]{2,1,0:T(8,128)S(1)}, u32[]{:S(2)}, u32[]{:S(2)}) collective-permute-start(f32[2,128,128]{2,1,0:T(8,128)S(1)} %get-tuple-element.15), channel_id=1, source_target_pairs={{0,1},{1,0},{2,3},{3,2},{4,5},{5,4},{6,7},{7,6},{8,9},{9,8},{10,11... | collective-permute-start | bytes 393224 | tf_op jit(solution)/shard_map/ppermute | solution.py:12
  25.6 8.4 %collective-permute-start.8 = (f32[2,128,128]{2,1,0:T(8,128)S(1)}, f32[2,128,128]{2,1,0:T(8,128)S(1)}, u32[]{:S(2)}, u32[]{:S(2)}) collective-permute-start(f32[2,128,128]{2,1,0:T(8,128)S(1)} %get-tuple-element.16), channel_id=1, source_target_pairs={{0,2},{1,3},{2,0},{3,1},{4,6},{5,7},{6,4},{7,5},{8,10},{9,11},{10,... | collective-permute-start | bytes 393224 | tf_op jit(solution)/shard_map/ppermute | solution.py:12
  26.1 7.9 %collective-permute-start.9 = (f32[2,128,128]{2,1,0:T(8,128)S(1)}, f32[2,128,128]{2,1,0:T(8,128)S(1)}, u32[]{:S(2)}, u32[]{:S(2)}) collective-permute-start(f32[2,128,128]{2,1,0:T(8,128)S(1)} %get-tuple-element.17), channel_id=1, source_target_pairs={{0,3},{1,2},{2,1},{3,0},{4,7},{5,6},{6,5},{7,4},{8,11},{9,10},{10,... | collective-permute-start | bytes 393224 | tf_op jit(solution)/shard_map/ppermute | solution.py:12

commit v5 on v4

v5 whole, which is shorter than its diff:
```python
import functools

import jax
import jax.numpy as jnp
from jax import lax
from jax.experimental import pallas as pl
from jax.experimental.pallas import tpu as pltpu
from jax.sharding import PartitionSpec as P


def exchange(value, axis, step):
    return lax.ppermute(value, axis, [(i, i ^ step) for i in range(lax.axis_size(axis))])


def exchange_beside(value, axis, first):
    pairs = [(i, i + 1) for i in range(first, lax.axis_size(axis) - 1, 2)]
    return lax.ppermute(value, axis, pairs + [(j, i) for i, j in pairs])


def turned(block):
    half = block.shape[1] // 2
    wide = pltpu.roll(block.astype(jnp.float32), half, axis=1)
    lane = lax.broadcasted_iota(jnp.int32, wide.shape, 1)
    return jnp.where(lane < half, -wide, wide).astype(block.dtype)


def turned_rows(block):
    half = block.shape[0] // 2
    return jnp.concatenate([-block[half:], block[:half]], axis=0)


def place(target_ref, source_ref, slot, group_blocks, blocks):
    group, mine = lax.axis_index("grp"), lax.axis_index("clu") * blocks
    target = (target_ref[slot] - group * group_blocks) ^ mine
    source = (source_ref[slot] - (group - 1) * group_blocks) ^ mine
    offset = lax.div(source, group_blocks) - 1
    return target, jnp.where(group % 2 == 0, source - 2 * offset * group_blocks, source)


def each_slot(start, chunk, refs, held, ids, id_sems, sems, prepare, work):
    live_ref, *id_refs, kernels_ref = refs
    chunks = held.shape[0] // chunk
    copies = [pltpu.make_async_copy(ref, kept, id_sems.at[i]) for i, (ref, kept) in enumerate(zip(id_refs, ids))]

    def fetch(c):
        return pltpu.make_async_copy(
            kernels_ref.at[pl.ds(start + c * chunk, chunk)], held.at[pl.ds(c * chunk, chunk)], sems.at[c]
        )

    for copy in copies:
        copy.start()
    for c in range(chunks):
        fetch(c).start()
    prepare()
    for copy in copies:
        copy.wait()
    live = live_ref[0] - start

    @pl.loop(0, chunks)
    def _(c):
        fetch(c).wait()
        first = c * chunk

        @pl.when(first + chunk <= live)
        def _():
            for i in range(chunk):
                work(start + first + i, held.at[first + i])

        @pl.when(first + chunk > live)
        def _():
            @pl.loop(first, jnp.maximum(live, first))
            def _(i):
                work(start + i, held.at[i])


def combine_kernel(group_blocks, blocks, start, chunk, *refs):
    slot_refs, (_, total, held, *ids, id_sems, sems) = refs[:4], refs[4:]
    sources = 3 * group_blocks

    def clear():
        @pl.loop(0, total.shape[0])
        def _(pair):
            total[pair] = jnp.zeros(total.shape[1:], total.dtype)

    def add(slot, block):
        target, source = place(*ids, slot, group_blocks, blocks)
        pair = target * sources + source
        total[pair] += block[...].reshape(total.shape[1:]).astype(jnp.float32)

    each_slot(start, chunk, slot_refs, held, ids, id_sems, sems, clear, add)


def split_kernel(blocks, panels, _, early, late, *refs):
    *gathered, out_ref, across_ref = refs

    @pl.loop(0, early.shape[0])
    def _(pair):
        value = early[pair] + late[pair]
        high = value.astype(jnp.bfloat16)
        out_ref[0, pair] = high
        out_ref[1, pair] = (value - high.astype(jnp.float32)).astype(jnp.bfloat16)

    for i, block in enumerate(part_of(gathered, blocks, panels, 1)):
        across_ref[:, 2 * i * panels : 2 * (i + 1) * panels] = crossed(block)


def join_kernel(_, *refs):
    *parts, out_ref = refs
    rows = parts[0].shape[0]
    for i, ref in enumerate(parts):
        out_ref[i * rows : (i + 1) * rows] = ref[...]


def group_kernel(blocks, panels, _, *refs):
    *gathered, out_ref = refs
    for i, block in enumerate(part_of(gathered, blocks, panels, 0)):
        out_ref[i * panels : (i + 1) * panels] = block


def part_of(gathered, blocks, panels, part):
    for ref in gathered:
        for b in range(blocks):
            yield ref[pl.ds((part * blocks + b) * panels, panels), :]


def strengths_of(first_ref, gathered, blocks, panels):
    for i in range(0, first_ref.shape[0], panels):
        yield first_ref[i : i + panels]
    yield from part_of(gathered, blocks, panels, 0)
    yield from part_of(gathered, blocks, panels, 2)


def crossed(block):
    block = block.astype(jnp.float32).T
    return jnp.concatenate([block, turned_rows(block)], axis=1).astype(jnp.bfloat16)


def stacked(block):
    return jnp.concatenate([block, turned(block)], axis=0)


def adjoint_of(pairs_ref, across_ref, first, count):
    width = pairs_ref.shape[3]
    weights = across_ref[...]
    targets = weights.shape[1] // pairs_ref.shape[2]
    sources = pairs_ref.shape[1] // targets
    both = jnp.concatenate([weights, weights], axis=1)
    step = 2 if count % 2 == 0 else 1
    for i in range(0, count, step):
        columns = []
        for j in range(step):
            tiles = [pairs_ref[h, t * sources + first + i + j] for h in range(2) for t in range(targets)]
            columns.append(jnp.concatenate(tiles, axis=0))
        product = jnp.dot(both, jnp.concatenate(columns, axis=1), preferred_element_type=jnp.float32)
        for j in range(step):
            yield i + j, product[:, j * width : (j + 1) * width]


def outer_kernel(pairs_ref, across_ref, first_ref, second_ref):
    count = first_ref.shape[0]
    for i, value in adjoint_of(pairs_ref, across_ref, 0, count):
        first_ref[i] = value
    for i, value in adjoint_of(pairs_ref, across_ref, 2 * count, count):
        second_ref[i] = value


def inner_kernel(blocks, pairs_ref, across_ref, first_ref, *refs):
    *gathered, potential_ref, middle_ref = refs
    targets, panels = potential_ref.shape[:2]
    sources = pairs_ref.shape[1] // targets
    stack = jnp.concatenate([stacked(x) for x in strengths_of(first_ref, gathered, blocks, panels)], axis=0)
    for t in range(targets):
        halves = []
        for h in range(2):
            tiles = []
            for s in range(sources):
                tiles += [pairs_ref[h, t * sources + s, :panels], pairs_ref[h, t * sources + s, panels:]]
            halves.append(jnp.concatenate(tiles, axis=1))
        product = jnp.dot(jnp.concatenate(halves, axis=0), stack, preferred_element_type=jnp.float32)
        potential_ref[t] = product[:panels] + product[panels:]
    for i, value in adjoint_of(pairs_ref, across_ref, targets, targets):
        middle_ref[i] = value


def parts_kernel(blocks, potential_ref, middle_ref, first_ref, second_ref, *outs):
    for i in range(potential_ref.shape[0]):
        out_ref, b = outs[i // blocks], i % blocks
        out_ref[b] = potential_ref[i]
        out_ref[blocks + b] = middle_ref[i] + first_ref[i] + second_ref[i]


def slots_kernel(blocks, panels, chunk, *refs):
    slot_refs, (first_ref, *gathered), refs = refs[:4], refs[4:-9], refs[-9:]
    potential_ref, adjoint_ref, held, stack, across, *ids, id_sems, sems = refs
    group_blocks = potential_ref.shape[0]

    def prepare():
        potential_ref[...] = jnp.zeros(potential_ref.shape, potential_ref.dtype)
        adjoint_ref[...] = jnp.zeros(adjoint_ref.shape, adjoint_ref.dtype)
        for i, block in enumerate(strengths_of(first_ref, gathered, blocks, panels)):
            stack[i] = stacked(block)
        for i, block in enumerate(part_of(gathered, blocks, panels, 1)):
            across[i] = crossed(block)

    def work(slot, block):
        target, source = place(*ids, slot, group_blocks, blocks)
        real, imag = block[0], block[1]
        potential_ref[target] += jnp.dot(
            jnp.concatenate([real, imag], axis=1), stack[source], preferred_element_type=jnp.float32
        )
        adjoint_ref[source] += jnp.dot(
            across[target], jnp.concatenate([real, imag], axis=0), preferred_element_type=jnp.float32
        )

    each_slot(0, chunk, slot_refs, held, ids, id_sems, sems, prepare, work)


def finish_kernel(blocks, *refs):
    *parts, potential_ref, adjoint_ref = refs
    total = parts[0][...]
    for part in parts[1:]:
        total = total + part[...]
    panels = total.shape[1]
    for b in range(blocks):
        potential_ref[b * panels : (b + 1) * panels] = total[b]
        adjoint_ref[b * panels : (b + 1) * panels] = total[blocks + b].T


def local(strengths, adjoint_weights, kernels, target_ids, source_ids, live_slots):
    slots, _, panels, _ = kernels.shape
    width = strengths.shape[1]
    blocks = strengths.shape[0] // panels
    clusters = lax.axis_size("clu")
    group_blocks = clusters * blocks
    sources = 3 * group_blocks
    pairs = group_blocks * sources
    chunk = 8 if slots % 8 == 0 else 1
    in_vmem, in_smem, in_hbm = (pl.BlockSpec(memory_space=m) for m in (pltpu.VMEM, pltpu.SMEM, pltpu.HBM))
    f32, bf16 = jnp.float32, jnp.bfloat16
    slot_args = (live_slots,) + tuple(
        pltpu.with_memory_space_constraint(x, pltpu.HBM) for x in (target_ids, source_ids, kernels)
    )

    def fetched(count):
        return [
            pltpu.VMEM((count, *kernels.shape[1:]), bf16),
            pltpu.SMEM(target_ids.shape, jnp.int32),
            pltpu.SMEM(source_ids.shape, jnp.int32),
            pltpu.SemaphoreType.DMA((2,)),
            pltpu.SemaphoreType.DMA((count // chunk,)),
        ]

    def call(body, shapes, args, specs=None, scratch=(), mib=8, flops=0):
        single = not isinstance(shapes, tuple)
        return pl.pallas_call(
            body,
            out_shape=shapes,
            in_specs=specs or [in_vmem] * len(args),
            out_specs=in_vmem if single else (in_vmem,) * len(shapes),
            scratch_shapes=scratch,
            compiler_params=pltpu.CompilerParams(vmem_limit_bytes=mib << 20),
            cost_estimate=pl.CostEstimate(flops=flops, bytes_accessed=1 << 20, transcendentals=0),
        )(*args)

    def shape(*dims, kind=f32):
        return jax.ShapeDtypeStruct(dims, kind)

    def gather(token):
        mine = call(
            join_kernel,
            shape(3 * blocks * panels, width, kind=bf16),
            (token, strengths, adjoint_weights, beside),
            [in_hbm] + [in_vmem] * 3,
        )
        return [mine] + [exchange(mine, "clu", k) for k in range(1, clusters)]

    def group_strengths(token):
        return call(
            functools.partial(group_kernel, blocks, panels),
            shape(group_blocks * panels, width, kind=bf16),
            (token, *gathered),
            [in_hbm] + [in_vmem] * clusters,
        )

    def combine(start, count, token):
        total = call(
            functools.partial(combine_kernel, group_blocks, blocks, start, chunk),
            pltpu.VMEM((pairs, 2 * panels, panels), f32),
            (*slot_args, token),
            [in_smem] + [in_hbm] * 4,
            fetched(count),
            mib=20,
            flops=1 << 33,
        )
        return total, pltpu.with_memory_space_constraint(total, pltpu.VMEM)

    beside = exchange_beside(strengths, "grp", 1)
    block_sums = shape(group_blocks, panels, width)
    if pairs <= slots:
        early_slots = max(slots // chunk // 3, 1) * chunk
        token, early = combine(0, early_slots, slot_args[1])
        gathered = gather(token)
        token, late = combine(early_slots, slots - early_slots, gathered[0])
        own = group_strengths(token)
        first = exchange_beside(own, "grp", 0)
        kept, across = call(
            functools.partial(split_kernel, blocks, panels),
            (pltpu.VMEM((2, pairs, 2 * panels, panels), bf16), shape(width, 2 * group_blocks * panels, kind=bf16)),
            (own, early, late, *gathered),
            [in_hbm] + [in_vmem] * (2 + clusters),
            flops=1 << 33,
        )
        kept = pltpu.with_memory_space_constraint(kept, pltpu.VMEM)
        lower, upper = call(outer_kernel, (block_sums, block_sums), (kept, across), flops=1 << 33)
        potential, middle = call(
            functools.partial(inner_kernel, blocks),
            (block_sums, block_sums),
            (kept, across, first, *gathered),
            flops=1 << 33,
        )
        lower, upper = exchange_beside(lower, "grp", 0), exchange_beside(upper, "grp", 1)
        parts = call(
            functools.partial(parts_kernel, blocks),
            (shape(2 * blocks, panels, width),) * clusters,
            (potential, middle, lower, upper),
        )
    else:
        gathered = gather(strengths)
        first = exchange_beside(group_strengths(strengths), "grp", 0)
        potential, adjoint = call(
            functools.partial(slots_kernel, blocks, panels, chunk),
            (block_sums, shape(sources, width, panels)),
            (*slot_args, first, *gathered),
            [in_smem] + [in_hbm] * 3 + [in_vmem] * (1 + clusters),
            [
                *fetched(slots)[:1],
                pltpu.VMEM((sources, 2 * panels, width), bf16),
                pltpu.VMEM((group_blocks, width, 2 * panels), bf16),
                *fetched(slots)[1:],
            ],
            mib=40,
        )
        lower, middle, upper = (adjoint[i * group_blocks : (i + 1) * group_blocks] for i in range(3))
        adjoint = middle + exchange_beside(lower, "grp", 0) + exchange_beside(upper, "grp", 1)
        owned = [slice(k * blocks, (k + 1) * blocks) for k in range(clusters)]
        parts = [jnp.concatenate([potential[rows], adjoint[rows]], axis=0) for rows in owned]

    parts = [parts[0]] + [exchange(parts[k], "clu", k) for k in range(1, clusters)]
    out = shape(blocks * panels, width)
    return tuple(call(functools.partial(finish_kernel, blocks), (out, out), parts))


def solution(mesh):
    return jax.shard_map(
        local,
        mesh=mesh,
        in_specs=(
            P(("grp", "clu"), None),
            P(("grp", "clu"), None),
            P(("grp", "clu"), None, None, None),
            P(("grp", "clu")),
            P(("grp", "clu")),
            P(("grp", "clu")),
        ),
        out_specs=(P(("grp", "clu"), None), P(("grp", "clu"), None)),
        check_vma=False,
    )
```

time: 35 us -> 35.6 us (1.017)
  the two profiles are of different devices: /device:TPU:12 before, /device:TPU:8 now
where the time goes in v5:
time: 35.6 us; the launch traced here: 35.5 us
  waiting for transfers between devices  11.9 us (33%)
  starting transfers between devices  11.6 us (33%)
  Pallas kernels  10.6 us (30%)
  between operations  1.39 us (4%)
    pallas_call x9, Pallas kernels, call(): pl.pallas_call(body, out_shape=shapes, in_specs=specs or [in_vmem] * len(...  10.6 us
    ppermute x6, waiting for transfers between devices, exchange(): lax.ppermute(value, axis, [(i, i ^ step) for i in range(lax.axis_size(axi...  7.69 us
    ppermute x6, starting transfers between devices, exchange(): lax.ppermute(value, axis, [(i, i ^ step) for i in range(lax.axis_size(axi...  7.11 us
    ppermute x4, starting transfers between devices, exchange_beside(): return lax.ppermute(value, axis, pairs + [(j, i) for i, j in pairs])  4.47 us
    ppermute x4, waiting for transfers between devices, exchange_beside(): return lax.ppermute(value, axis, pairs + [(j, i) for i, j in pairs])  4.16 us
  transfers between devices with their start and end apart: 10, of which 5 were waited for; matrix products, arithmetic and copies ran while one was open for 0% of the time, Pallas kernels for 28%

profile of v5, /device:TPU:8, one launch (start us, length us, event | category | flops | bytes accessed | tf_op | source)
XLA Modules:
  0.0 35.5 jit_solution(1800595304904489044)
XLA Ops:
  0.6 1.9 %collective-permute-start = (bf16[128,128]{1,0:T(8,128)(2,1)}, bf16[128,128]{1,0:T(8,128)(2,1)S(1)}, u32[]{:S(2)}, u32[]{:S(2)}) collective-permute-start(bf16[128,128]{1,0:T(8,128)(2,1)} %refs_0_.3), channel_id=1, source_target_pairs={{4,8},{12,16},{20,24},{8,4},{16,12},{24,20},{5,9},{13,17},{21,25},... | collective-permute-start | bytes 98312 | tf_op jit(solution)/shard_map/ppermute | solution.py:17
  3.2 2.3 %shard_map.77._.early = f32[48,256,128]{2,1,0:T(8,128)S(1)} custom-call(s32[1]{0:T(128)S(6)} %copy.8.refs_0_, s32[192]{0:T(256)} %refs_1_.5, s32[192]{0:T(256)} %refs_2_.3, bf16[192,2,128,128]{3,2,1,0:T(8,128)(2,1)} %refs_3_.3, s32[192]{0:T(256)} %refs_1_.5), custom_call_target="tpu_custom_call" | custom-call | flops 8589934592 | bytes 1048576 | tf_op jit(solution)/shard_map/pallas_call | solution.py:255
  5.5 0.6 %collective-permute-done.refs_2_ = bf16[128,128]{1,0:T(8,128)(2,1)S(1)} collective-permute-done((bf16[128,128]{1,0:T(8,128)(2,1)}, bf16[128,128]{1,0:T(8,128)(2,1)S(1)}, u32[]{:S(2)}, u32[]{:S(2)}) %collective-permute-start) | collective-permute-done | bytes 32800 | tf_op jit(solution)/shard_map/ppermute | solution.py:17
  6.1 2.5 %collective-permute-start.3 = (bf16[384,128]{1,0:T(8,128)(2,1)S(1)}, bf16[384,128]{1,0:T(8,128)(2,1)S(1)}, u32[]{:S(2)}, u32[]{:S(2)}) collective-permute-start(bf16[384,128]{1,0:T(8,128)(2,1)S(1)} %shard_map.78.refs_4_.refs_0_), channel_id=1, source_target_pairs={{0,3},{1,2},{2,1},{3,0},{4,7},{5,6},{6,5},{7,4},{8,11},{9,10},{10,... | collective-permute-start | bytes 294920 | tf_op jit(solution)/shard_map/ppermute | solution.py:12
  8.6 0.5 %collective-permute-start.2 = (bf16[384,128]{1,0:T(8,128)(2,1)S(1)}, bf16[384,128]{1,0:T(8,128)(2,1)S(1)}, u32[]{:S(2)}, u32[]{:S(2)}) collective-permute-start(bf16[384,128]{1,0:T(8,128)(2,1)S(1)} %shard_map.78.refs_4_.refs_0_), channel_id=1, source_target_pairs={{0,2},{1,3},{2,0},{3,1},{4,6},{5,7},{6,4},{7,5},{8,10},{9,11},{10,... | collective-permute-start | bytes 294920 | tf_op jit(solution)/shard_map/ppermute | solution.py:12
  9.1 0.5 %collective-permute-start.1 = (bf16[384,128]{1,0:T(8,128)(2,1)S(1)}, bf16[384,128]{1,0:T(8,128)(2,1)S(1)}, u32[]{:S(2)}, u32[]{:S(2)}) collective-permute-start(bf16[384,128]{1,0:T(8,128)(2,1)S(1)} %shard_map.78.refs_4_.refs_0_), channel_id=1, source_target_pairs={{0,1},{1,0},{2,3},{3,2},{4,5},{5,4},{6,7},{7,6},{8,9},{9,8},{10,11... | collective-permute-start | bytes 294920 | tf_op jit(solution)/shard_map/ppermute | solution.py:12
  9.6 3.5 %shard_map.79._.late = f32[48,256,128]{2,1,0:T(8,128)S(1)} custom-call(s32[1]{0:T(128)S(6)} %copy.8.refs_0_, s32[192]{0:T(256)} %refs_1_.5, s32[192]{0:T(256)} %refs_2_.3, bf16[192,2,128,128]{3,2,1,0:T(8,128)(2,1)} %refs_3_.3, bf16[384,128]{1,0:T(8,128)(2,1)S(1)} %shard_map.78.refs_4_.refs_0_), custom_call_target="tpu_custom_call" | custom-call | flops 8589934592 | bytes 1048576 | tf_op jit(solution)/shard_map/pallas_call | solution.py:255
  13.2 0.0 collective-permute-done.3.refs_3_
  13.2 1.6 %collective-permute-done.2.refs_2_ = bf16[384,128]{1,0:T(8,128)(2,1)S(1)} collective-permute-done((bf16[384,128]{1,0:T(8,128)(2,1)S(1)}, bf16[384,128]{1,0:T(8,128)(2,1)S(1)}, u32[]{:S(2)}, u32[]{:S(2)}) %collective-permute-start.2) | collective-permute-done | bytes 98336 | tf_op jit(solution)/shard_map/ppermute | solution.py:12
  14.8 0.0 collective-permute-done.1.refs_1_
  14.9 0.2 collective-permute-start.4
  15.1 1.2 %shard_map.81 = (bf16[2,48,256,128]{3,2,1,0:T(8,128)(2,1)S(1)}, bf16[128,1024]{1,0:T(8,128)(2,1)S(1)}) custom-call(bf16[512,128]{1,0:T(8,128)(2,1)S(1)} %shard_map.80._, f32[48,256,128]{2,1,0:T(8,128)S(1)} %shard_map.77._.early, f32[48,256,128]{2,1,0:T(8,128)S(1)} %shard_map.79._.late, bf16[384,128]{1,0:T(8,128)(2,1)S(1)} %shard_map.78.refs_4_.refs_0_, ...), custom_call_target="tpu_custom_call" | custom-call | flops 8589934592 | bytes 1048576 | tf_op jit(solution)/shard_map/pallas_call | solution.py:255
  16.2 0.7 %shard_map.83 = (f32[4,128,128]{2,1,0:T(8,128)S(1)}, f32[4,128,128]{2,1,0:T(8,128)S(1)}) custom-call(bf16[2,48,256,128]{3,2,1,0:T(8,128)(2,1)S(1)} %get-tuple-element.12.pairs_ref, bf16[128,1024]{1,0:T(8,128)(2,1)S(1)} %get-tuple-element.13.across_ref), custom_call_target="tpu_custom_call" | custom-call | flops 8589934592 | bytes 1048576 | tf_op jit(solution)/shard_map/pallas_call | solution.py:255
  16.9 0.5 %collective-permute-start.5 = (f32[4,128,128]{2,1,0:T(8,128)S(1)}, f32[4,128,128]{2,1,0:T(8,128)S(1)}, u32[]{:S(2)}, u32[]{:S(2)}) collective-permute-start(f32[4,128,128]{2,1,0:T(8,128)S(1)} %get-tuple-element.16), channel_id=1, source_target_pairs={{0,4},{8,12},{16,20},{24,28},{4,0},{12,8},{20,16},{28,24},{1,5},{9... | collective-permute-start | bytes 786440 | tf_op jit(solution)/shard_map/ppermute | solution.py:17
  17.4 1.9 %collective-permute-start.6 = (f32[4,128,128]{2,1,0:T(8,128)S(1)}, f32[4,128,128]{2,1,0:T(8,128)S(1)}, u32[]{:S(2)}, u32[]{:S(2)}) collective-permute-start(f32[4,128,128]{2,1,0:T(8,128)S(1)} %get-tuple-element.17), channel_id=1, source_target_pairs={{4,8},{12,16},{20,24},{8,4},{16,12},{24,20},{5,9},{13,17},{21,25},... | collective-permute-start | bytes 786440 | tf_op jit(solution)/shard_map/ppermute | solution.py:17
  19.3 2.1 %shard_map.82 = (f32[4,128,128]{2,1,0:T(8,128)S(1)}, f32[4,128,128]{2,1,0:T(8,128)S(1)}) custom-call(bf16[2,48,256,128]{3,2,1,0:T(8,128)(2,1)S(1)} %get-tuple-element.12.pairs_ref, bf16[128,1024]{1,0:T(8,128)(2,1)S(1)} %get-tuple-element.13.across_ref, bf16[512,128]{1,0:T(8,128)(2,1)S(1)} %collective-permute-done.4.first_ref, ...), custom_call_target="tpu_custom_call" | custom-call | flops 8589934592 | bytes 1048576 | tf_op jit(solution)/shard_map/pallas_call | solution.py:255
  21.5 3.6 %collective-permute-done.6.second_ref = f32[4,128,128]{2,1,0:T(8,128)S(1)} collective-permute-done((f32[4,128,128]{2,1,0:T(8,128)S(1)}, f32[4,128,128]{2,1,0:T(8,128)S(1)}, u32[]{:S(2)}, u32[]{:S(2)}) %collective-permute-start.6) | collective-permute-done | bytes 262176 | tf_op jit(solution)/shard_map/ppermute | solution.py:17
  25.1 0.1 shard_map.84
  25.1 1.5 %collective-permute-start.7 = (f32[2,128,128]{2,1,0:T(8,128)S(1)}, f32[2,128,128]{2,1,0:T(8,128)S(1)}, u32[]{:S(2)}, u32[]{:S(2)}) collective-permute-start(f32[2,128,128]{2,1,0:T(8,128)S(1)} %get-tuple-element.19), channel_id=1, source_target_pairs={{0,1},{1,0},{2,3},{3,2},{4,5},{5,4},{6,7},{7,6},{8,9},{9,8},{10,11... | collective-permute-start | bytes 393224 | tf_op jit(solution)/shard_map/ppermute | solution.py:12
  26.7 1.1 %collective-permute-start.8 = (f32[2,128,128]{2,1,0:T(8,128)S(1)}, f32[2,128,128]{2,1,0:T(8,128)S(1)}, u32[]{:S(2)}, u32[]{:S(2)}) collective-permute-start(f32[2,128,128]{2,1,0:T(8,128)S(1)} %get-tuple-element.20), channel_id=1, source_target_pairs={{0,2},{1,3},{2,0},{3,1},{4,6},{5,7},{6,4},{7,5},{8,10},{9,11},{10,... | collective-permute-start | bytes 393224 | tf_op jit(solution)/shard_map/ppermute | solution.py:12
  27.7 0.9 %collective-permute-start.9 = (f32[2,128,128]{2,1,0:T(8,128)S(1)}, f32[2,128,128]{2,1,0:T(8,128)S(1)}, u32[]{:S(2)}, u32[]{:S(2)}) collective-permute-start(f32[2,128,128]{2,1,0:T(8,128)S(1)} %get-tuple-element.21), channel_id=1, source_target_pairs={{0,3},{1,2},{2,1},{3,0},{4,7},{5,6},{6,5},{7,4},{8,11},{9,10},{10,... | collective-permute-start | bytes 393224 | tf_op jit(solution)/shard_map/ppermute | solution.py:12
  28.7 2.4 %collective-permute-done.7.refs_1_ = f32[2,128,128]{2,1,0:T(8,128)S(1)} collective-permute-done((f32[2,128,128]{2,1,0:T(8,128)S(1)}, f32[2,128,128]{2,1,0:T(8,128)S(1)}, u32[]{:S(2)}, u32[]{:S(2)}) %collective-permute-start.7) | collective-permute-done | bytes 131104 | tf_op jit(solution)/shard_map/ppermute | solution.py:12
  31.1 3.6 %collective-permute-done.8.refs_2_ = f32[2,128,128]{2,1,0:T(8,128)S(1)} collective-permute-done((f32[2,128,128]{2,1,0:T(8,128)S(1)}, f32[2,128,128]{2,1,0:T(8,128)S(1)}, u32[]{:S(2)}, u32[]{:S(2)}) %collective-permute-start.8) | collective-permute-done | bytes 131104 | tf_op jit(solution)/shard_map/ppermute | solution.py:12
  34.7 0.7 %shard_map.85 = (f32[128,128]{1,0:T(8,128)}, f32[128,128]{1,0:T(8,128)}) custom-call(f32[2,128,128]{2,1,0:T(8,128)S(1)} %get-tuple-element.18.refs_0_, f32[2,128,128]{2,1,0:T(8,128)S(1)} %collective-permute-done.7.refs_1_, f32[2,128,128]{2,1,0:T(8,128)S(1)} %collective-permute-done.8.refs_2_, f32[2,128,128]{2,1,0:T(8,128)S(1)} %collective-permute-done.9.refs_3_), custom_call_target="tpu_custom_call" | custom-call | bytes 1048576 | tf_op jit(solution)/shard_map/pallas_call | solution.py:255
  (9 shorter events, 0.0 us)
Async XLA Ops:
  0.6 5.4 %collective-permute-start = (bf16[128,128]{1,0:T(8,128)(2,1)}, bf16[128,128]{1,0:T(8,128)(2,1)S(1)}, u32[]{:S(2)}, u32[]{:S(2)}) collective-permute-start(bf16[128,128]{1,0:T(8,128)(2,1)} %refs_0_.3), channel_id=1, source_target_pairs={{4,8},{12,16},{20,24},{8,4},{16,12},{24,20},{5,9},{13,17},{21,25},... | collective-permute-start | bytes 98312 | tf_op jit(solution)/shard_map/ppermute | solution.py:17
  3.2 2.9 %copy-start = (bf16[128,128]{1,0:T(8,128)(2,1)S(1)}, bf16[128,128]{1,0:T(8,128)(2,1)}, u32[]{:S(2)}) copy-start(bf16[128,128]{1,0:T(8,128)(2,1)} %refs_0_.3) | copy-start | bytes 98308
  3.2 2.9 %copy-start.1 = (bf16[128,128]{1,0:T(8,128)(2,1)S(1)}, bf16[128,128]{1,0:T(8,128)(2,1)}, u32[]{:S(2)}) copy-start(bf16[128,128]{1,0:T(8,128)(2,1)} %refs_1_.4) | copy-start | bytes 98308
  6.1 7.1 %collective-permute-start.3 = (bf16[384,128]{1,0:T(8,128)(2,1)S(1)}, bf16[384,128]{1,0:T(8,128)(2,1)S(1)}, u32[]{:S(2)}, u32[]{:S(2)}) collective-permute-start(bf16[384,128]{1,0:T(8,128)(2,1)S(1)} %shard_map.78.refs_4_.refs_0_), channel_id=1, source_target_pairs={{0,3},{1,2},{2,1},{3,0},{4,7},{5,6},{6,5},{7,4},{8,11},{9,10},{10,... | collective-permute-start | bytes 294920 | tf_op jit(solution)/shard_map/ppermute | solution.py:12
  8.6 6.2 %collective-permute-start.2 = (bf16[384,128]{1,0:T(8,128)(2,1)S(1)}, bf16[384,128]{1,0:T(8,128)(2,1)S(1)}, u32[]{:S(2)}, u32[]{:S(2)}) collective-permute-start(bf16[384,128]{1,0:T(8,128)(2,1)S(1)} %shard_map.78.refs_4_.refs_0_), channel_id=1, source_target_pairs={{0,2},{1,3},{2,0},{3,1},{4,6},{5,7},{6,4},{7,5},{8,10},{9,11},{10,... | collective-permute-start | bytes 294920 | tf_op jit(solution)/shard_map/ppermute | solution.py:12
  9.1 5.7 %collective-permute-start.1 = (bf16[384,128]{1,0:T(8,128)(2,1)S(1)}, bf16[384,128]{1,0:T(8,128)(2,1)S(1)}, u32[]{:S(2)}, u32[]{:S(2)}) collective-permute-start(bf16[384,128]{1,0:T(8,128)(2,1)S(1)} %shard_map.78.refs_4_.refs_0_), channel_id=1, source_target_pairs={{0,1},{1,0},{2,3},{3,2},{4,5},{5,4},{6,7},{7,6},{8,9},{9,8},{10,11... | collective-permute-start | bytes 294920 | tf_op jit(solution)/shard_map/ppermute | solution.py:12
  14.9 4.4 %collective-permute-start.4 = (bf16[512,128]{1,0:T(8,128)(2,1)S(1)}, bf16[512,128]{1,0:T(8,128)(2,1)S(1)}, u32[]{:S(2)}, u32[]{:S(2)}) collective-permute-start(bf16[512,128]{1,0:T(8,128)(2,1)S(1)} %shard_map.80._), channel_id=1, source_target_pairs={{0,4},{8,12},{16,20},{24,28},{4,0},{12,8},{20,16},{28,24},{1,5},{9... | collective-permute-start | bytes 393224 | tf_op jit(solution)/shard_map/ppermute | solution.py:17
  16.9 4.5 %collective-permute-start.5 = (f32[4,128,128]{2,1,0:T(8,128)S(1)}, f32[4,128,128]{2,1,0:T(8,128)S(1)}, u32[]{:S(2)}, u32[]{:S(2)}) collective-permute-start(f32[4,128,128]{2,1,0:T(8,128)S(1)} %get-tuple-element.16), channel_id=1, source_target_pairs={{0,4},{8,12},{16,20},{24,28},{4,0},{12,8},{20,16},{28,24},{1,5},{9... | collective-permute-start | bytes 786440 | tf_op jit(solution)/shard_map/ppermute | solution.py:17
  17.4 7.7 %collective-permute-start.6 = (f32[4,128,128]{2,1,0:T(8,128)S(1)}, f32[4,128,128]{2,1,0:T(8,128)S(1)}, u32[]{:S(2)}, u32[]{:S(2)}) collective-permute-start(f32[4,128,128]{2,1,0:T(8,128)S(1)} %get-tuple-element.17), channel_id=1, source_target_pairs={{4,8},{12,16},{20,24},{8,4},{16,12},{24,20},{5,9},{13,17},{21,25},... | collective-permute-start | bytes 786440 | tf_op jit(solution)/shard_map/ppermute | solution.py:17
  25.1 6.0 %collective-permute-start.7 = (f32[2,128,128]{2,1,0:T(8,128)S(1)}, f32[2,128,128]{2,1,0:T(8,128)S(1)}, u32[]{:S(2)}, u32[]{:S(2)}) collective-permute-start(f32[2,128,128]{2,1,0:T(8,128)S(1)} %get-tuple-element.19), channel_id=1, source_target_pairs={{0,1},{1,0},{2,3},{3,2},{4,5},{5,4},{6,7},{7,6},{8,9},{9,8},{10,11... | collective-permute-start | bytes 393224 | tf_op jit(solution)/shard_map/ppermute | solution.py:12
  26.7 8.0 %collective-permute-start.8 = (f32[2,128,128]{2,1,0:T(8,128)S(1)}, f32[2,128,128]{2,1,0:T(8,128)S(1)}, u32[]{:S(2)}, u32[]{:S(2)}) collective-permute-start(f32[2,128,128]{2,1,0:T(8,128)S(1)} %get-tuple-element.20), channel_id=1, source_target_pairs={{0,2},{1,3},{2,0},{3,1},{4,6},{5,7},{6,4},{7,5},{8,10},{9,11},{10,... | collective-permute-start | bytes 393224 | tf_op jit(solution)/shard_map/ppermute | solution.py:12
  27.7 7.0 %collective-permute-start.9 = (f32[2,128,128]{2,1,0:T(8,128)S(1)}, f32[2,128,128]{2,1,0:T(8,128)S(1)}, u32[]{:S(2)}, u32[]{:S(2)}) collective-permute-start(f32[2,128,128]{2,1,0:T(8,128)S(1)} %get-tuple-element.21), channel_id=1, source_target_pairs={{0,3},{1,2},{2,1},{3,0},{4,7},{5,6},{6,5},{7,4},{8,11},{9,10},{10,... | collective-permute-start | bytes 393224 | tf_op jit(solution)/shard_map/ppermute | solution.py:12

commit v6 on v4

--- a/solution.py
+++ b/solution.py
@@ -12,9 +12,12 @@
     return lax.ppermute(value, axis, [(i, i ^ step) for i in range(lax.axis_size(axis))])
 
 
-def exchange_beside(value, axis, first):
-    pairs = [(i, i + 1) for i in range(first, lax.axis_size(axis) - 1, 2)]
-    return lax.ppermute(value, axis, pairs + [(j, i) for i, j in pairs])
+def exchange_beside(value, first, step=0):
+    groups, clusters = lax.axis_size("grp"), lax.axis_size("clu")
+    pairs = [(i, i + 1) for i in range(first, groups - 1, 2)]
+    pairs += [(j, i) for i, j in pairs]
+    moves = [(i * clusters + c, j * clusters + (c ^ step)) for i, j in pairs for c in range(clusters)]
+    return lax.ppermute(value, ("grp", "clu"), moves)
 
 
 def turned(block):
@@ -115,8 +118,8 @@
         copy.wait()
 
 
-def group_kernel(blocks, panels, *refs):
-    *gathered, _, out_ref = refs
+def group_kernel(blocks, panels, _, *refs):
+    *gathered, out_ref = refs
     for i, block in enumerate(part_of(gathered, blocks, panels, 0)):
         out_ref[i * panels : (i + 1) * panels] = block
 
@@ -125,6 +128,13 @@
     for ref in gathered:
         for b in range(blocks):
             yield ref[pl.ds((part * blocks + b) * panels, panels), :]
+
+
+def strengths_of(first_ref, gathered, second, blocks, panels):
+    for i in range(0, first_ref.shape[0], panels):
+        yield first_ref[i : i + panels]
+    yield from part_of(gathered, blocks, panels, 0)
+    yield from part_of(second, blocks, panels, 0)
 
 
 def crossed(block):
@@ -161,14 +171,12 @@
         second_ref[i] = value
 
 
-def forward_kernel(pairs_ref, *refs):
-    *strengths, potential_ref = refs
+def inner_kernel(blocks, pairs_ref, across_ref, first_ref, *refs):
+    *others, potential_ref, middle_ref = refs
+    gathered, second = others[: len(others) // 2], others[len(others) // 2 :]
     targets, panels = potential_ref.shape[:2]
     sources = pairs_ref.shape[1] // targets
-    stack = []
-    for ref in strengths:
-        stack += [stacked(ref[i : i + panels]) for i in range(0, ref.shape[0], panels)]
-    stack = jnp.concatenate(stack, axis=0)
+    stack = jnp.concatenate([stacked(x) for x in strengths_of(first_ref, gathered, second, blocks, panels)], axis=0)
     for t in range(targets):
         halves = []
         for h in range(2):
@@ -178,27 +186,28 @@
             halves.append(jnp.concatenate(tiles, axis=1))
         product = jnp.dot(jnp.concatenate(halves, axis=0), stack, preferred_element_type=jnp.float32)
         potential_ref[t] = product[:panels] + product[panels:]
-
-
-def middle_kernel(blocks, pairs_ref, across_ref, potential_ref, first_ref, second_ref, *outs):
-    count = potential_ref.shape[0]
-    for i, value in adjoint_of(pairs_ref, across_ref, count, count):
+    for i, value in adjoint_of(pairs_ref, across_ref, targets, targets):
+        middle_ref[i] = value
+
+
+def parts_kernel(blocks, potential_ref, middle_ref, first_ref, second_ref, *outs):
+    for i in range(potential_ref.shape[0]):
         out_ref, b = outs[i // blocks], i % blocks
         out_ref[b] = potential_ref[i]
-        out_ref[blocks + b] = value + first_ref[i] + second_ref[i]
-
-
-def slots_kernel(blocks, panels, clusters, chunk, *refs):
-    slot_refs, gathered, refs = refs[:4], refs[4 : 4 + clusters], refs[4 + clusters :]
-    strengths, (potential_ref, adjoint_ref, held, stack, across, *ids, id_sems, sems) = refs[:3], refs[3:]
+        out_ref[blocks + b] = middle_ref[i] + first_ref[i] + second_ref[i]
+
+
+def slots_kernel(blocks, panels, chunk, *refs):
+    slot_refs, (first_ref, *others), refs = refs[:4], refs[4:-9], refs[-9:]
+    gathered, second = others[: len(others) // 2], others[len(others) // 2 :]
+    potential_ref, adjoint_ref, held, stack, across, *ids, id_sems, sems = refs
     group_blocks = potential_ref.shape[0]
 
     def prepare():
         potential_ref[...] = jnp.zeros(potential_ref.shape, potential_ref.dtype)
         adjoint_ref[...] = jnp.zeros(adjoint_ref.shape, adjoint_ref.dtype)
-        for offset, ref in enumerate(strengths):
-            for i in range(group_blocks):
-                stack[offset * group_blocks + i] = stacked(ref[i * panels : (i + 1) * panels])
+        for i, block in enumerate(strengths_of(first_ref, gathered, second, blocks, panels)):
+            stack[i] = stacked(block)
         for i, block in enumerate(part_of(gathered, blocks, panels, 1)):
             across[i] = crossed(block)
 
@@ -263,6 +272,7 @@
     def shape(*dims, kind=f32):
         return jax.ShapeDtypeStruct(dims, kind)
 
+    second = [exchange_beside(strengths, 1, k) for k in range(clusters)]
     mine = call(
         pack_kernel,
         shape(2 * blocks * panels, width, kind=bf16),
@@ -273,13 +283,12 @@
     gathered = [mine] + [exchange(mine, "clu", k) for k in range(1, clusters)]
 
     def group_strengths(token):
-        own = call(
+        return call(
             functools.partial(group_kernel, blocks, panels),
             shape(group_blocks * panels, width, kind=bf16),
-            (*gathered, token),
-            [in_vmem] * clusters + [in_hbm],
-        )
-        return exchange_beside(own, "grp", 0), own, exchange_beside(own, "grp", 1)
+            (token, *gathered),
+            [in_hbm] + [in_vmem] * clusters,
+        )
 
     block_sums = shape(group_blocks, panels, width)
     if pairs <= slots:
@@ -292,30 +301,37 @@
             mib=20,
             flops=1 << 33,
         )
-        first, own, second = group_strengths(total)
+        own = group_strengths(total)
+        first = exchange_beside(own, 0)
         total = pltpu.with_memory_space_constraint(total, pltpu.VMEM)
         kept, across = call(
             functools.partial(split_kernel, blocks, panels),
-            (pltpu.VMEM((2, *total.shape), bf16), shape(width, 2 * group_blocks * panels, kind=bf16)),
+            (pltpu.VMEM((2, pairs, 2 * panels, panels), bf16), shape(width, 2 * group_blocks * panels, kind=bf16)),
             (own, total, *gathered),
             [in_hbm] + [in_vmem] * (1 + clusters),
             flops=1 << 33,
         )
         kept = pltpu.with_memory_space_constraint(kept, pltpu.VMEM)
         lower, upper = call(outer_kernel, (block_sums, block_sums), (kept, across), flops=1 << 33)
-        potential = call(forward_kernel, block_sums, (kept, first, own, second), flops=1 << 33)
-        lower, upper = exchange_beside(lower, "grp", 0), exchange_beside(upper, "grp", 1)
+        potential, middle = call(
+            functools.partial(inner_kernel, blocks),
+            (block_sums, block_sums),
+            (kept, across, first, *gathered, *second),
+            flops=1 << 33,
+        )
+        lower, upper = exchange_beside(lower, 0), exchange_beside(upper, 1)
         parts = call(
-            functools.partial(middle_kernel, blocks),
+            functools.partial(parts_kernel, blocks),
             (shape(2 * blocks, panels, width),) * clusters,
-            (kept, across, potential, lower, upper),
+            (potential, middle, lower, upper),
         )
     else:
+        first = exchange_beside(group_strengths(mine), 0)
         potential, adjoint = call(
-            functools.partial(slots_kernel, blocks, panels, clusters, chunk),
+            functools.partial(slots_kernel, blocks, panels, chunk),
             (block_sums, shape(sources, width, panels)),
-            (*slot_args, *gathered, *group_strengths(strengths)),
-            [in_smem] + [in_hbm] * 3 + [in_vmem] * (clusters + 3),
+            (*slot_args, first, *gathered, *second),
+            [in_smem] + [in_hbm] * 3 + [in_vmem] * (1 + 2 * clusters),
             [
                 held,
                 pltpu.VMEM((sources, 2 * panels, width), bf16),
@@ -324,8 +340,8 @@
             ],
             mib=40,
         )
-        first, middle, second = (adjoint[i * group_blocks : (i + 1) * group_blocks] for i in range(3))
-        adjoint = middle + exchange_beside(first, "grp", 0) + exchange_beside(second, "grp", 1)
+        lower, middle, upper = (adjoint[i * group_blocks : (i + 1) * group_blocks] for i in range(3))
+        adjoint = middle + exchange_beside(lower, 0) + exchange_beside(upper, 1)
         owned = [slice(k * blocks, (k + 1) * blocks) for k in range(clusters)]
         parts = [jnp.concatenate([potential[rows], adjoint[rows]], axis=0) for rows in owned]
 

time: 35 us -> 44.2 us (1.26)
  the two profiles are of different devices: /device:TPU:12 before, /device:TPU:8 now
where the time goes in v6:
time: 44.2 us; the launch traced here: 43.9 us
  starting transfers between devices  22.7 us (51%)
  Pallas kernels  10.2 us (23%)
  waiting for transfers between devices  9.57 us (22%)
  between operations  1.45 us (3%)
    ppermute x7, starting transfers between devices, exchange_beside(): return lax.ppermute(value, ('grp', 'clu'), moves)  15.6 us
    pallas_call x8, Pallas kernels, call(): pl.pallas_call(body, out_shape=shapes, in_specs=specs or [in_vmem] * len(...  10.2 us
    ppermute x6, starting transfers between devices, exchange(): lax.ppermute(value, axis, [(i, i ^ step) for i in range(lax.axis_size(axi...  7.11 us
    ppermute x6, waiting for transfers between devices, exchange(): lax.ppermute(value, axis, [(i, i ^ step) for i in range(lax.axis_size(axi...  6.06 us
    ppermute x7, waiting for transfers between devices, exchange_beside(): return lax.ppermute(value, ('grp', 'clu'), moves)  3.51 us
  transfers between devices with their start and end apart: 13, of which 3 were waited for; matrix products, arithmetic and copies ran while one was open for 0% of the time, Pallas kernels for 20%

profile of v6, /device:TPU:8, one launch (start us, length us, event | category | flops | bytes accessed | tf_op | source)
XLA Modules:
  0.0 43.9 jit_solution(13752639781996090376)
XLA Ops:
  0.6 0.8 %shard_map.78.refs_0_ = bf16[256,128]{1,0:T(8,128)(2,1)S(1)} custom-call(bf16[128,128]{1,0:T(8,128)(2,1)} %strengths_ref.1, bf16[128,128]{1,0:T(8,128)(2,1)} %weights_ref.1), custom_call_target="tpu_custom_call" | custom-call | bytes 1048576 | tf_op jit(solution)/shard_map/pallas_call | solution.py:262
  1.4 1.6 %collective-permute-start = (bf16[256,128]{1,0:T(8,128)(2,1)S(1)}, bf16[256,128]{1,0:T(8,128)(2,1)S(1)}, u32[]{:S(2)}, u32[]{:S(2)}) collective-permute-start(bf16[256,128]{1,0:T(8,128)(2,1)S(1)} %shard_map.78.refs_0_), channel_id=1, source_target_pairs={{0,1},{1,0},{2,3},{3,2},{4,5},{5,4},{6,7},{7,6},{8,9},{9,8},{10,11... | collective-permute-start | bytes 196616 | tf_op jit(solution)/shard_map/ppermute | solution.py:12
  3.0 1.5 %collective-permute-start.1 = (bf16[256,128]{1,0:T(8,128)(2,1)S(1)}, bf16[256,128]{1,0:T(8,128)(2,1)S(1)}, u32[]{:S(2)}, u32[]{:S(2)}) collective-permute-start(bf16[256,128]{1,0:T(8,128)(2,1)S(1)} %shard_map.78.refs_0_), channel_id=1, source_target_pairs={{0,2},{1,3},{2,0},{3,1},{4,6},{5,7},{6,4},{7,5},{8,10},{9,11},{10,... | collective-permute-start | bytes 196616 | tf_op jit(solution)/shard_map/ppermute | solution.py:12
  4.5 0.5 %collective-permute-start.2 = (bf16[256,128]{1,0:T(8,128)(2,1)S(1)}, bf16[256,128]{1,0:T(8,128)(2,1)S(1)}, u32[]{:S(2)}, u32[]{:S(2)}) collective-permute-start(bf16[256,128]{1,0:T(8,128)(2,1)S(1)} %shard_map.78.refs_0_), channel_id=1, source_target_pairs={{0,3},{1,2},{2,1},{3,0},{4,7},{5,6},{6,5},{7,4},{8,11},{9,10},{10,... | collective-permute-start | bytes 196616 | tf_op jit(solution)/shard_map/ppermute | solution.py:12
  5.0 1.9 %collective-permute-start.4 = (bf16[128,128]{1,0:T(8,128)(2,1)}, bf16[128,128]{1,0:T(8,128)(2,1)S(1)}, u32[]{:S(2)}, u32[]{:S(2)}) collective-permute-start(bf16[128,128]{1,0:T(8,128)(2,1)} %strengths_ref.1), channel_id=1, source_target_pairs={{4,8},{5,9},{6,10},{7,11},{12,16},{13,17},{14,18},{15,19},{20,24},... | collective-permute-start | bytes 98312 | tf_op jit(solution)/shard_map/ppermute | solution.py:20
  6.9 4.6 %collective-permute-start.5 = (bf16[128,128]{1,0:T(8,128)(2,1)}, bf16[128,128]{1,0:T(8,128)(2,1)S(1)}, u32[]{:S(2)}, u32[]{:S(2)}) collective-permute-start(bf16[128,128]{1,0:T(8,128)(2,1)} %strengths_ref.1), channel_id=1, source_target_pairs={{4,9},{5,8},{6,11},{7,10},{12,17},{13,16},{14,19},{15,18},{20,25},... | collective-permute-start | bytes 98312 | tf_op jit(solution)/shard_map/ppermute | solution.py:20
  12.1 0.0 copy-start
  12.1 4.8 %shard_map.77._.total = f32[48,256,128]{2,1,0:T(8,128)S(1)} custom-call(s32[1]{0:T(128)S(6)} %copy.8.refs_0_, s32[192]{0:T(256)} %refs_1_.1, s32[192]{0:T(256)} %refs_2_.1, bf16[192,2,128,128]{3,2,1,0:T(8,128)(2,1)} %refs_3_.1), custom_call_target="tpu_custom_call" | custom-call | flops 8589934592 | bytes 1048576 | tf_op jit(solution)/shard_map/pallas_call | solution.py:262
  17.0 2.9 %collective-permute-start.6 = (bf16[128,128]{1,0:T(8,128)(2,1)S(1)}, bf16[128,128]{1,0:T(8,128)(2,1)S(1)}, u32[]{:S(2)}, u32[]{:S(2)}) collective-permute-start(bf16[128,128]{1,0:T(8,128)(2,1)S(1)} %copy-done), channel_id=1, source_target_pairs={{4,10},{5,11},{6,8},{7,9},{12,18},{13,19},{14,16},{15,17},{20,26},... | collective-permute-start | bytes 98312 | tf_op jit(solution)/shard_map/ppermute | solution.py:20
  19.9 3.6 %collective-permute-start.7 = (bf16[128,128]{1,0:T(8,128)(2,1)S(1)}, bf16[128,128]{1,0:T(8,128)(2,1)S(1)}, u32[]{:S(2)}, u32[]{:S(2)}) collective-permute-start(bf16[128,128]{1,0:T(8,128)(2,1)S(1)} %copy-done), channel_id=1, source_target_pairs={{4,11},{5,10},{6,9},{7,8},{12,19},{13,18},{14,17},{15,16},{20,27},... | collective-permute-start | bytes 98312 | tf_op jit(solution)/shard_map/ppermute | solution.py:20
  23.5 0.2 collective-permute-start.3
  23.7 0.9 %shard_map.80 = (bf16[2,48,256,128]{3,2,1,0:T(8,128)(2,1)S(1)}, bf16[128,1024]{1,0:T(8,128)(2,1)S(1)}) custom-call(bf16[512,128]{1,0:T(8,128)(2,1)S(1)} %shard_map.79._, f32[48,256,128]{2,1,0:T(8,128)S(1)} %shard_map.77._.total, bf16[256,128]{1,0:T(8,128)(2,1)S(1)} %shard_map.78.refs_0_, bf16[256,128]{1,0:T(8,128)(2,1)S(1)} %collective-permute-done.refs_1_, ...), custom_call_target="tpu_custom_call" | custom-call | flops 8589934592 | bytes 1048576 | tf_op jit(solution)/shard_map/pallas_call | solution.py:262
  24.6 0.7 %shard_map.82 = (f32[4,128,128]{2,1,0:T(8,128)S(1)}, f32[4,128,128]{2,1,0:T(8,128)S(1)}) custom-call(bf16[2,48,256,128]{3,2,1,0:T(8,128)(2,1)S(1)} %get-tuple-element.12.pairs_ref, bf16[128,1024]{1,0:T(8,128)(2,1)S(1)} %get-tuple-element.13.across_ref), custom_call_target="tpu_custom_call" | custom-call | flops 8589934592 | bytes 1048576 | tf_op jit(solution)/shard_map/pallas_call | solution.py:262
  25.4 0.4 collective-permute-start.8
  25.8 2.0 %collective-permute-start.9 = (f32[4,128,128]{2,1,0:T(8,128)S(1)}, f32[4,128,128]{2,1,0:T(8,128)S(1)}, u32[]{:S(2)}, u32[]{:S(2)}) collective-permute-start(f32[4,128,128]{2,1,0:T(8,128)S(1)} %get-tuple-element.17), channel_id=1, source_target_pairs={{4,8},{5,9},{6,10},{7,11},{12,16},{13,17},{14,18},{15,19},{20,24},... | collective-permute-start | bytes 786440 | tf_op jit(solution)/shard_map/ppermute | solution.py:20
  27.8 2.1 %shard_map.81 = (f32[4,128,128]{2,1,0:T(8,128)S(1)}, f32[4,128,128]{2,1,0:T(8,128)S(1)}) custom-call(bf16[2,48,256,128]{3,2,1,0:T(8,128)(2,1)S(1)} %get-tuple-element.12.pairs_ref, bf16[128,1024]{1,0:T(8,128)(2,1)S(1)} %get-tuple-element.13.across_ref, bf16[512,128]{1,0:T(8,128)(2,1)S(1)} %collective-permute-done.3.first_ref, ...), custom_call_target="tpu_custom_call" | custom-call | flops 8589934592 | bytes 1048576 | tf_op jit(solution)/shard_map/pallas_call | solution.py:262
  30.0 3.5 %collective-permute-done.9.second_ref = f32[4,128,128]{2,1,0:T(8,128)S(1)} collective-permute-done((f32[4,128,128]{2,1,0:T(8,128)S(1)}, f32[4,128,128]{2,1,0:T(8,128)S(1)}, u32[]{:S(2)}, u32[]{:S(2)}) %collective-permute-start.9) | collective-permute-done | bytes 262176 | tf_op jit(solution)/shard_map/ppermute | solution.py:20
  33.5 0.1 shard_map.83
  33.5 1.6 %collective-permute-start.10 = (f32[2,128,128]{2,1,0:T(8,128)S(1)}, f32[2,128,128]{2,1,0:T(8,128)S(1)}, u32[]{:S(2)}, u32[]{:S(2)}) collective-permute-start(f32[2,128,128]{2,1,0:T(8,128)S(1)} %get-tuple-element.19), channel_id=1, source_target_pairs={{0,1},{1,0},{2,3},{3,2},{4,5},{5,4},{6,7},{7,6},{8,9},{9,8},{10,11... | collective-permute-start | bytes 393224 | tf_op jit(solution)/shard_map/ppermute | solution.py:12
  35.1 1.5 %collective-permute-start.11 = (f32[2,128,128]{2,1,0:T(8,128)S(1)}, f32[2,128,128]{2,1,0:T(8,128)S(1)}, u32[]{:S(2)}, u32[]{:S(2)}) collective-permute-start(f32[2,128,128]{2,1,0:T(8,128)S(1)} %get-tuple-element.20), channel_id=1, source_target_pairs={{0,2},{1,3},{2,0},{3,1},{4,6},{5,7},{6,4},{7,5},{8,10},{9,11},{10,... | collective-permute-start | bytes 393224 | tf_op jit(solution)/shard_map/ppermute | solution.py:12
  36.6 0.5 %collective-permute-start.12 = (f32[2,128,128]{2,1,0:T(8,128)S(1)}, f32[2,128,128]{2,1,0:T(8,128)S(1)}, u32[]{:S(2)}, u32[]{:S(2)}) collective-permute-start(f32[2,128,128]{2,1,0:T(8,128)S(1)} %get-tuple-element.21), channel_id=1, source_target_pairs={{0,3},{1,2},{2,1},{3,0},{4,7},{5,6},{6,5},{7,4},{8,11},{9,10},{10,... | collective-permute-start | bytes 393224 | tf_op jit(solution)/shard_map/ppermute | solution.py:12
  37.1 2.5 %collective-permute-done.10.refs_1_ = f32[2,128,128]{2,1,0:T(8,128)S(1)} collective-permute-done((f32[2,128,128]{2,1,0:T(8,128)S(1)}, f32[2,128,128]{2,1,0:T(8,128)S(1)}, u32[]{:S(2)}, u32[]{:S(2)}) %collective-permute-start.10) | collective-permute-done | bytes 131104 | tf_op jit(solution)/shard_map/ppermute | solution.py:12
  39.6 3.6 %collective-permute-done.11.refs_2_ = f32[2,128,128]{2,1,0:T(8,128)S(1)} collective-permute-done((f32[2,128,128]{2,1,0:T(8,128)S(1)}, f32[2,128,128]{2,1,0:T(8,128)S(1)}, u32[]{:S(2)}, u32[]{:S(2)}) %collective-permute-start.11) | collective-permute-done | bytes 131104 | tf_op jit(solution)/shard_map/ppermute | solution.py:12
  43.1 0.7 %shard_map.84 = (f32[128,128]{1,0:T(8,128)}, f32[128,128]{1,0:T(8,128)}) custom-call(f32[2,128,128]{2,1,0:T(8,128)S(1)} %get-tuple-element.18.refs_0_, f32[2,128,128]{2,1,0:T(8,128)S(1)} %collective-permute-done.10.refs_1_, f32[2,128,128]{2,1,0:T(8,128)S(1)} %collective-permute-done.11.refs_2_, f32[2,128,128]{2,1,0:T(8,128)S(1)} %collective-permute-done.12.refs_3_), custom_call_target="tpu_custom_call" | custom-call | bytes 1048576 | tf_op jit(solution)/shard_map/pallas_call | solution.py:262
  (12 shorter events, 0.0 us)
Async XLA Ops:
  1.4 15.5 %collective-permute-start = (bf16[256,128]{1,0:T(8,128)(2,1)S(1)}, bf16[256,128]{1,0:T(8,128)(2,1)S(1)}, u32[]{:S(2)}, u32[]{:S(2)}) collective-permute-start(bf16[256,128]{1,0:T(8,128)(2,1)S(1)} %shard_map.78.refs_0_), channel_id=1, source_target_pairs={{0,1},{1,0},{2,3},{3,2},{4,5},{5,4},{6,7},{7,6},{8,9},{9,8},{10,11... | collective-permute-start | bytes 196616 | tf_op jit(solution)/shard_map/ppermute | solution.py:12
  3.0 16.9 %collective-permute-start.1 = (bf16[256,128]{1,0:T(8,128)(2,1)S(1)}, bf16[256,128]{1,0:T(8,128)(2,1)S(1)}, u32[]{:S(2)}, u32[]{:S(2)}) collective-permute-start(bf16[256,128]{1,0:T(8,128)(2,1)S(1)} %shard_map.78.refs_0_), channel_id=1, source_target_pairs={{0,2},{1,3},{2,0},{3,1},{4,6},{5,7},{6,4},{7,5},{8,10},{9,11},{10,... | collective-permute-start | bytes 196616 | tf_op jit(solution)/shard_map/ppermute | solution.py:12
  4.5 18.9 %collective-permute-start.2 = (bf16[256,128]{1,0:T(8,128)(2,1)S(1)}, bf16[256,128]{1,0:T(8,128)(2,1)S(1)}, u32[]{:S(2)}, u32[]{:S(2)}) collective-permute-start(bf16[256,128]{1,0:T(8,128)(2,1)S(1)} %shard_map.78.refs_0_), channel_id=1, source_target_pairs={{0,3},{1,2},{2,1},{3,0},{4,7},{5,6},{6,5},{7,4},{8,11},{9,10},{10,... | collective-permute-start | bytes 196616 | tf_op jit(solution)/shard_map/ppermute | solution.py:12
  5.0 20.4 %collective-permute-start.4 = (bf16[128,128]{1,0:T(8,128)(2,1)}, bf16[128,128]{1,0:T(8,128)(2,1)S(1)}, u32[]{:S(2)}, u32[]{:S(2)}) collective-permute-start(bf16[128,128]{1,0:T(8,128)(2,1)} %strengths_ref.1), channel_id=1, source_target_pairs={{4,8},{5,9},{6,10},{7,11},{12,16},{13,17},{14,18},{15,19},{20,24},... | collective-permute-start | bytes 98312 | tf_op jit(solution)/shard_map/ppermute | solution.py:20
  6.9 18.9 %collective-permute-start.5 = (bf16[128,128]{1,0:T(8,128)(2,1)}, bf16[128,128]{1,0:T(8,128)(2,1)S(1)}, u32[]{:S(2)}, u32[]{:S(2)}) collective-permute-start(bf16[128,128]{1,0:T(8,128)(2,1)} %strengths_ref.1), channel_id=1, source_target_pairs={{4,9},{5,8},{6,11},{7,10},{12,17},{13,16},{14,19},{15,18},{20,25},... | collective-permute-start | bytes 98312 | tf_op jit(solution)/shard_map/ppermute | solution.py:20
  12.1 4.8 %copy-start = (bf16[128,128]{1,0:T(8,128)(2,1)S(1)}, bf16[128,128]{1,0:T(8,128)(2,1)}, u32[]{:S(2)}) copy-start(bf16[128,128]{1,0:T(8,128)(2,1)} %strengths_ref.1) | copy-start | bytes 98308
  17.0 10.8 %collective-permute-start.6 = (bf16[128,128]{1,0:T(8,128)(2,1)S(1)}, bf16[128,128]{1,0:T(8,128)(2,1)S(1)}, u32[]{:S(2)}, u32[]{:S(2)}) collective-permute-start(bf16[128,128]{1,0:T(8,128)(2,1)S(1)} %copy-done), channel_id=1, source_target_pairs={{4,10},{5,11},{6,8},{7,9},{12,18},{13,19},{14,16},{15,17},{20,26},... | collective-permute-start | bytes 98312 | tf_op jit(solution)/shard_map/ppermute | solution.py:20
  19.9 7.9 %collective-permute-start.7 = (bf16[128,128]{1,0:T(8,128)(2,1)S(1)}, bf16[128,128]{1,0:T(8,128)(2,1)S(1)}, u32[]{:S(2)}, u32[]{:S(2)}) collective-permute-start(bf16[128,128]{1,0:T(8,128)(2,1)S(1)} %copy-done), channel_id=1, source_target_pairs={{4,11},{5,10},{6,9},{7,8},{12,19},{13,18},{14,17},{15,16},{20,27},... | collective-permute-start | bytes 98312 | tf_op jit(solution)/shard_map/ppermute | solution.py:20
  23.5 4.3 %collective-permute-start.3 = (bf16[512,128]{1,0:T(8,128)(2,1)S(1)}, bf16[512,128]{1,0:T(8,128)(2,1)S(1)}, u32[]{:S(2)}, u32[]{:S(2)}) collective-permute-start(bf16[512,128]{1,0:T(8,128)(2,1)S(1)} %shard_map.79._), channel_id=1, source_target_pairs={{0,4},{1,5},{2,6},{3,7},{8,12},{9,13},{10,14},{11,15},{16,20},{17,... | collective-permute-start | bytes 393224 | tf_op jit(solution)/shard_map/ppermute | solution.py:20
  25.4 4.6 %collective-permute-start.8 = (f32[4,128,128]{2,1,0:T(8,128)S(1)}, f32[4,128,128]{2,1,0:T(8,128)S(1)}, u32[]{:S(2)}, u32[]{:S(2)}) collective-permute-start(f32[4,128,128]{2,1,0:T(8,128)S(1)} %get-tuple-element.16), channel_id=1, source_target_pairs={{0,4},{1,5},{2,6},{3,7},{8,12},{9,13},{10,14},{11,15},{16,20},{17,... | collective-permute-start | bytes 786440 | tf_op jit(solution)/shard_map/ppermute | solution.py:20
  25.8 7.7 %collective-permute-start.9 = (f32[4,128,128]{2,1,0:T(8,128)S(1)}, f32[4,128,128]{2,1,0:T(8,128)S(1)}, u32[]{:S(2)}, u32[]{:S(2)}) collective-permute-start(f32[4,128,128]{2,1,0:T(8,128)S(1)} %get-tuple-element.17), channel_id=1, source_target_pairs={{4,8},{5,9},{6,10},{7,11},{12,16},{13,17},{14,18},{15,19},{20,24},... | collective-permute-start | bytes 786440 | tf_op jit(solution)/shard_map/ppermute | solution.py:20
  33.5 6.0 %collective-permute-start.10 = (f32[2,128,128]{2,1,0:T(8,128)S(1)}, f32[2,128,128]{2,1,0:T(8,128)S(1)}, u32[]{:S(2)}, u32[]{:S(2)}) collective-permute-start(f32[2,128,128]{2,1,0:T(8,128)S(1)} %get-tuple-element.19), channel_id=1, source_target_pairs={{0,1},{1,0},{2,3},{3,2},{4,5},{5,4},{6,7},{7,6},{8,9},{9,8},{10,11... | collective-permute-start | bytes 393224 | tf_op jit(solution)/shard_map/ppermute | solution.py:12
  35.1 8.0 %collective-permute-start.11 = (f32[2,128,128]{2,1,0:T(8,128)S(1)}, f32[2,128,128]{2,1,0:T(8,128)S(1)}, u32[]{:S(2)}, u32[]{:S(2)}) collective-permute-start(f32[2,128,128]{2,1,0:T(8,128)S(1)} %get-tuple-element.20), channel_id=1, source_target_pairs={{0,2},{1,3},{2,0},{3,1},{4,6},{5,7},{6,4},{7,5},{8,10},{9,11},{10,... | collective-permute-start | bytes 393224 | tf_op jit(solution)/shard_map/ppermute | solution.py:12
  36.6 6.5 %collective-permute-start.12 = (f32[2,128,128]{2,1,0:T(8,128)S(1)}, f32[2,128,128]{2,1,0:T(8,128)S(1)}, u32[]{:S(2)}, u32[]{:S(2)}) collective-permute-start(f32[2,128,128]{2,1,0:T(8,128)S(1)} %get-tuple-element.21), channel_id=1, source_target_pairs={{0,3},{1,2},{2,1},{3,0},{4,7},{5,6},{6,5},{7,4},{8,11},{9,10},{10,... | collective-permute-start | bytes 393224 | tf_op jit(solution)/shard_map/ppermute | solution.py:12

commit v7 on v6

--- a/solution.py
+++ b/solution.py
@@ -7,17 +7,44 @@
 from jax.experimental.pallas import tpu as pltpu
 from jax.sharding import PartitionSpec as P
 
+EXPONENT_ROWS = 16
+TINY = 2.0**-100
+
 
 def exchange(value, axis, step):
     return lax.ppermute(value, axis, [(i, i ^ step) for i in range(lax.axis_size(axis))])
 
 
-def exchange_beside(value, first, step=0):
-    groups, clusters = lax.axis_size("grp"), lax.axis_size("clu")
-    pairs = [(i, i + 1) for i in range(first, groups - 1, 2)]
-    pairs += [(j, i) for i, j in pairs]
-    moves = [(i * clusters + c, j * clusters + (c ^ step)) for i, j in pairs for c in range(clusters)]
-    return lax.ppermute(value, ("grp", "clu"), moves)
+def exchange_beside(value, first):
+    groups = lax.axis_size("grp")
+    partner = [i + 1 if (i - first) % 2 == 0 else i - 1 for i in range(groups)]
+    return lax.ppermute(value, "grp", [(i, j if 0 <= j < groups else i) for i, j in enumerate(partner)])
+
+
+def rows_of(index, panels):
+    return pl.ds(index * panels, panels)
+
+
+def encode(values, out_ref):
+    exponents = []
+    for i, value in enumerate(values):
+        largest = jnp.max(jnp.abs(value), axis=0, keepdims=True)
+        exponent = jnp.floor(jnp.log2(jnp.maximum(largest, TINY))) + 1.0
+        scaled = jnp.round(value * jnp.exp2(15.0 - exponent))
+        scaled = jnp.minimum(jnp.maximum(scaled, -32767.0), 32767.0)
+        out_ref[rows_of(i, value.shape[0])] = scaled.astype(jnp.int32).astype(jnp.int16)
+        exponents.append(exponent)
+    last = out_ref.shape[0] - EXPONENT_ROWS * pl.cdiv(len(values), EXPONENT_ROWS)
+    exponents += [jnp.zeros_like(exponents[0])] * (out_ref.shape[0] - last - len(exponents))
+    table = jnp.concatenate(exponents, axis=0)
+    out_ref[last:] = table.astype(jnp.int32).astype(jnp.int16)
+
+
+def decode(ref, count, panels):
+    table = ref[count * panels :].astype(jnp.int32).astype(jnp.float32)
+    for i in range(count):
+        value = ref[rows_of(i, panels)].astype(jnp.int32).astype(jnp.float32)
+        yield value * jnp.exp2(table[i : i + 1] - 15.0)
 
 
 def turned(block):
@@ -130,11 +157,12 @@
             yield ref[pl.ds((part * blocks + b) * panels, panels), :]
 
 
-def strengths_of(first_ref, gathered, second, blocks, panels):
-    for i in range(0, first_ref.shape[0], panels):
-        yield first_ref[i : i + panels]
+def strengths_of(first_ref, gathered, second_ref, blocks, panels):
+    for i in range(first_ref.shape[0] // panels):
+        yield first_ref[rows_of(i, panels)]
     yield from part_of(gathered, blocks, panels, 0)
-    yield from part_of(second, blocks, panels, 0)
+    for i in range(second_ref.shape[0] // panels):
+        yield second_ref[rows_of(i, panels)]
 
 
 def crossed(block):
@@ -163,20 +191,16 @@
             yield i + j, product[:, j * width : (j + 1) * width]
 
 
-def outer_kernel(pairs_ref, across_ref, first_ref, second_ref):
-    count = first_ref.shape[0]
-    for i, value in adjoint_of(pairs_ref, across_ref, 0, count):
-        first_ref[i] = value
-    for i, value in adjoint_of(pairs_ref, across_ref, 2 * count, count):
-        second_ref[i] = value
-
-
-def inner_kernel(blocks, pairs_ref, across_ref, first_ref, *refs):
-    *others, potential_ref, middle_ref = refs
-    gathered, second = others[: len(others) // 2], others[len(others) // 2 :]
+def outer_kernel(count, pairs_ref, across_ref, first_ref, second_ref):
+    encode([value for _, value in adjoint_of(pairs_ref, across_ref, 0, count)], first_ref)
+    encode([value for _, value in adjoint_of(pairs_ref, across_ref, 2 * count, count)], second_ref)
+
+
+def inner_kernel(blocks, pairs_ref, across_ref, first_ref, second_ref, *refs):
+    *gathered, potential_ref, middle_ref = refs
     targets, panels = potential_ref.shape[:2]
     sources = pairs_ref.shape[1] // targets
-    stack = jnp.concatenate([stacked(x) for x in strengths_of(first_ref, gathered, second, blocks, panels)], axis=0)
+    stack = jnp.concatenate([stacked(x) for x in strengths_of(first_ref, gathered, second_ref, blocks, panels)], axis=0)
     for t in range(targets):
         halves = []
         for h in range(2):
@@ -190,23 +214,28 @@
         middle_ref[i] = value
 
 
-def parts_kernel(blocks, potential_ref, middle_ref, first_ref, second_ref, *outs):
-    for i in range(potential_ref.shape[0]):
-        out_ref, b = outs[i // blocks], i % blocks
-        out_ref[b] = potential_ref[i]
-        out_ref[blocks + b] = middle_ref[i] + first_ref[i] + second_ref[i]
+def parts_kernel(blocks, potential_ref, middle_ref, first_ref, second_ref, own_ref, *outs):
+    count, panels = potential_ref.shape[:2]
+    potential = [potential_ref[i] for i in range(count)]
+    others = zip(decode(first_ref, count, panels), decode(second_ref, count, panels))
+    adjoint = [middle_ref[i] + first + second for i, (first, second) in enumerate(others)]
+    for i in range(blocks):
+        own_ref[rows_of(i, panels)] = potential[i]
+        own_ref[rows_of(blocks + i, panels)] = adjoint[i]
+    for k, out_ref in enumerate(outs, 1):
+        rows = slice(k * blocks, (k + 1) * blocks)
+        encode(potential[rows] + adjoint[rows], out_ref)
 
 
 def slots_kernel(blocks, panels, chunk, *refs):
-    slot_refs, (first_ref, *others), refs = refs[:4], refs[4:-9], refs[-9:]
-    gathered, second = others[: len(others) // 2], others[len(others) // 2 :]
+    slot_refs, (first_ref, second_ref, *gathered), refs = refs[:4], refs[4:-9], refs[-9:]
     potential_ref, adjoint_ref, held, stack, across, *ids, id_sems, sems = refs
     group_blocks = potential_ref.shape[0]
 
     def prepare():
         potential_ref[...] = jnp.zeros(potential_ref.shape, potential_ref.dtype)
         adjoint_ref[...] = jnp.zeros(adjoint_ref.shape, adjoint_ref.dtype)
-        for i, block in enumerate(strengths_of(first_ref, gathered, second, blocks, panels)):
+        for i, block in enumerate(strengths_of(first_ref, gathered, second_ref, blocks, panels)):
             stack[i] = stacked(block)
         for i, block in enumerate(part_of(gathered, blocks, panels, 1)):
             across[i] = crossed(block)
@@ -224,15 +253,19 @@
     each_slot(chunk, slot_refs, held, ids, id_sems, sems, prepare, work)
 
 
-def finish_kernel(blocks, *refs):
+def code_kernel(*refs):
+    for ref, out_ref in zip(refs[:2], refs[2:]):
+        encode([ref[i] for i in range(ref.shape[0])], out_ref)
+
+
+def finish_kernel(blocks, panels, own_ref, *refs):
     *parts, potential_ref, adjoint_ref = refs
-    total = parts[0][...]
-    for part in parts[1:]:
-        total = total + part[...]
-    panels = total.shape[1]
+    total = [own_ref[rows_of(i, panels)] for i in range(2 * blocks)]
+    for ref in parts:
+        total = [a + b for a, b in zip(total, decode(ref, 2 * blocks, panels))]
     for b in range(blocks):
-        potential_ref[b * panels : (b + 1) * panels] = total[b]
-        adjoint_ref[b * panels : (b + 1) * panels] = total[blocks + b].T
+        potential_ref[rows_of(b, panels)] = total[b]
+        adjoint_ref[rows_of(b, panels)] = total[blocks + b].T
 
 
 def local(strengths, adjoint_weights, kernels, target_ids, source_ids, live_slots):
@@ -272,7 +305,6 @@
     def shape(*dims, kind=f32):
         return jax.ShapeDtypeStruct(dims, kind)
 
-    second = [exchange_beside(strengths, 1, k) for k in range(clusters)]
     mine = call(
         pack_kernel,
         shape(2 * blocks * panels, width, kind=bf16),
@@ -289,6 +321,9 @@
             (token, *gathered),
             [in_hbm] + [in_vmem] * clusters,
         )
+
+    def coded(count):
+        return shape(count * panels + EXPONENT_ROWS * pl.cdiv(count, EXPONENT_ROWS), width, kind=jnp.int16)
 
     block_sums = shape(group_blocks, panels, width)
     if pairs <= slots:
@@ -302,7 +337,7 @@
             flops=1 << 33,
         )
         own = group_strengths(total)
-        first = exchange_beside(own, 0)
+        first, second = exchange_beside(own, 0), exchange_beside(own, 1)
         total = pltpu.with_memory_space_constraint(total, pltpu.VMEM)
         kept, across = call(
             functools.partial(split_kernel, blocks, panels),
@@ -312,26 +347,23 @@
             flops=1 << 33,
         )
         kept = pltpu.with_memory_space_constraint(kept, pltpu.VMEM)
-        lower, upper = call(outer_kernel, (block_sums, block_sums), (kept, across), flops=1 << 33)
+        lower, upper = call(
+            functools.partial(outer_kernel, group_blocks), (coded(group_blocks),) * 2, (kept, across), flops=1 << 33
+        )
         potential, middle = call(
             functools.partial(inner_kernel, blocks),
             (block_sums, block_sums),
-            (kept, across, first, *gathered, *second),
+            (kept, across, first, second, *gathered),
             flops=1 << 33,
         )
-        lower, upper = exchange_beside(lower, 0), exchange_beside(upper, 1)
-        parts = call(
-            functools.partial(parts_kernel, blocks),
-            (shape(2 * blocks, panels, width),) * clusters,
-            (potential, middle, lower, upper),
-        )
     else:
-        first = exchange_beside(group_strengths(mine), 0)
+        own = group_strengths(mine)
+        first, second = exchange_beside(own, 0), exchange_beside(own, 1)
         potential, adjoint = call(
             functools.partial(slots_kernel, blocks, panels, chunk),
             (block_sums, shape(sources, width, panels)),
-            (*slot_args, first, *gathered, *second),
-            [in_smem] + [in_hbm] * 3 + [in_vmem] * (1 + 2 * clusters),
+            (*slot_args, first, second, *gathered),
+            [in_smem] + [in_hbm] * 3 + [in_vmem] * (2 + clusters),
             [
                 held,
                 pltpu.VMEM((sources, 2 * panels, width), bf16),
@@ -341,13 +373,16 @@
             mib=40,
         )
         lower, middle, upper = (adjoint[i * group_blocks : (i + 1) * group_blocks] for i in range(3))
-        adjoint = middle + exchange_beside(lower, 0) + exchange_beside(upper, 1)
-        owned = [slice(k * blocks, (k + 1) * blocks) for k in range(clusters)]
-        parts = [jnp.concatenate([potential[rows], adjoint[rows]], axis=0) for rows in owned]
-
-    parts = [parts[0]] + [exchange(parts[k], "clu", k) for k in range(1, clusters)]
+        lower, upper = call(code_kernel, (coded(group_blocks),) * 2, (lower, upper))
+    lower, upper = exchange_beside(lower, 0), exchange_beside(upper, 1)
+    mine, *parts = call(
+        functools.partial(parts_kernel, blocks),
+        (shape(2 * blocks * panels, width),) + (coded(2 * blocks),) * (clusters - 1),
+        (potential, middle, lower, upper),
+    )
+    parts = [exchange(part, "clu", k) for k, part in enumerate(parts, 1)]
     out = shape(blocks * panels, width)
-    return tuple(call(functools.partial(finish_kernel, blocks), (out, out), parts))
+    return tuple(call(functools.partial(finish_kernel, blocks, panels), (out, out), (mine, *parts)))
 
 
 def solution(mesh):

time: 44.2 us -> 31.8 us (0.72)
  starting transfers between devices: 22.7 us -> 12.8 us
  waiting for transfers between devices: 9.57 us -> 6.91 us
    ppermute x7 -> x4, starting transfers between devices: 15.6 us -> 5.71 us  [exchange_beside(): lax.ppermute(value, 'grp', [(i, j if 0 <= j < groups else i) for i, j in...]
    ppermute x7 -> x4, waiting for transfers between devices: 3.51 us -> 2.17 us  [exchange_beside(): lax.ppermute(value, 'grp', [(i, j if 0 <= j < groups else i) for i, j in...]
    ppermute x6, waiting for transfers between devices: 6.06 us -> 4.74 us  [exchange(): lax.ppermute(value, axis, [(i, i ^ step) for i in range(lax.axis_size(axi...]
  transfers between devices with their start and end apart: 13 -> 10, of which waited for: 3 -> 4; matrix products, arithmetic and copies ran while one was open for 0% -> 0% of each run, Pallas kernels for 20% -> 28%
where the time goes in v7:
time: 31.8 us; the launch traced here: 31.6 us
  starting transfers between devices  12.8 us (40%)
  Pallas kernels  10.4 us (33%)
  waiting for transfers between devices  6.91 us (22%)
  between operations  1.41 us (4%)
    pallas_call x8, Pallas kernels, call(): pl.pallas_call(body, out_shape=shapes, in_specs=specs or [in_vmem] * len(...  10.4 us
    ppermute x6, starting transfers between devices, exchange(): lax.ppermute(value, axis, [(i, i ^ step) for i in range(lax.axis_size(axi...  7.11 us
    ppermute x4, starting transfers between devices, exchange_beside(): lax.ppermute(value, 'grp', [(i, j if 0 <= j < groups else i) for i, j in...  5.71 us
    ppermute x6, waiting for transfers between devices, exchange(): lax.ppermute(value, axis, [(i, i ^ step) for i in range(lax.axis_size(axi...  4.74 us
    ppermute x4, waiting for transfers between devices, exchange_beside(): lax.ppermute(value, 'grp', [(i, j if 0 <= j < groups else i) for i, j in...  2.17 us
  transfers between devices with their start and end apart: 10, of which 4 were waited for; matrix products, arithmetic and copies ran while one was open for 0% of the time, Pallas kernels for 28%

profile of v7, /device:TPU:8, one launch (start us, length us, event | category | flops | bytes accessed | tf_op | source)
XLA Modules:
  0.0 31.6 jit_solution(11407399788116381181)
XLA Ops:
  0.6 0.8 %shard_map.78.refs_0_ = bf16[256,128]{1,0:T(8,128)(2,1)S(1)} custom-call(bf16[128,128]{1,0:T(8,128)(2,1)} %strengths_ref.1, bf16[128,128]{1,0:T(8,128)(2,1)} %weights_ref.1), custom_call_target="tpu_custom_call" | custom-call | bytes 1048576 | tf_op jit(solution)/shard_map/pallas_call | solution.py:295
  1.4 1.6 %collective-permute-start = (bf16[256,128]{1,0:T(8,128)(2,1)S(1)}, bf16[256,128]{1,0:T(8,128)(2,1)S(1)}, u32[]{:S(2)}, u32[]{:S(2)}) collective-permute-start(bf16[256,128]{1,0:T(8,128)(2,1)S(1)} %shard_map.78.refs_0_), channel_id=1, source_target_pairs={{0,1},{1,0},{2,3},{3,2},{4,5},{5,4},{6,7},{7,6},{8,9},{9,8},{10,11... | collective-permute-start | bytes 196616 | tf_op jit(solution)/shard_map/ppermute | solution.py:15
  3.0 1.5 %collective-permute-start.1 = (bf16[256,128]{1,0:T(8,128)(2,1)S(1)}, bf16[256,128]{1,0:T(8,128)(2,1)S(1)}, u32[]{:S(2)}, u32[]{:S(2)}) collective-permute-start(bf16[256,128]{1,0:T(8,128)(2,1)S(1)} %shard_map.78.refs_0_), channel_id=1, source_target_pairs={{0,2},{1,3},{2,0},{3,1},{4,6},{5,7},{6,4},{7,5},{8,10},{9,11},{10,... | collective-permute-start | bytes 196616 | tf_op jit(solution)/shard_map/ppermute | solution.py:15
  4.5 0.5 %collective-permute-start.2 = (bf16[256,128]{1,0:T(8,128)(2,1)S(1)}, bf16[256,128]{1,0:T(8,128)(2,1)S(1)}, u32[]{:S(2)}, u32[]{:S(2)}) collective-permute-start(bf16[256,128]{1,0:T(8,128)(2,1)S(1)} %shard_map.78.refs_0_), channel_id=1, source_target_pairs={{0,3},{1,2},{2,1},{3,0},{4,7},{5,6},{6,5},{7,4},{8,11},{9,10},{10,... | collective-permute-start | bytes 196616 | tf_op jit(solution)/shard_map/ppermute | solution.py:15
  5.6 4.8 %shard_map.77._.total = f32[48,256,128]{2,1,0:T(8,128)S(1)} custom-call(s32[1]{0:T(128)S(6)} %copy.8.refs_0_, s32[192]{0:T(256)} %refs_1_.1, s32[192]{0:T(256)} %refs_2_.1, bf16[192,2,128,128]{3,2,1,0:T(8,128)(2,1)} %refs_3_.1), custom_call_target="tpu_custom_call" | custom-call | flops 8589934592 | bytes 1048576 | tf_op jit(solution)/shard_map/pallas_call | solution.py:295
  10.4 0.0 collective-permute-done.refs_1_
  10.5 0.0 collective-permute-done.2.refs_3_
  10.5 0.1 collective-permute-start.3
  10.6 2.0 %collective-permute-start.4 = (bf16[512,128]{1,0:T(8,128)(2,1)S(1)}, bf16[512,128]{1,0:T(8,128)(2,1)S(1)}, u32[]{:S(2)}, u32[]{:S(2)}) collective-permute-start(bf16[512,128]{1,0:T(8,128)(2,1)S(1)} %shard_map.79._), channel_id=1, source_target_pairs={{0,0},{4,8},{8,4},{12,16},{16,12},{20,24},{24,20},{28,28},{1,1},{5... | collective-permute-start | bytes 393224 | tf_op jit(solution)/shard_map/ppermute | solution.py:21
  12.6 0.9 %shard_map.80 = (bf16[2,48,256,128]{3,2,1,0:T(8,128)(2,1)S(1)}, bf16[128,1024]{1,0:T(8,128)(2,1)S(1)}) custom-call(bf16[512,128]{1,0:T(8,128)(2,1)S(1)} %shard_map.79._, f32[48,256,128]{2,1,0:T(8,128)S(1)} %shard_map.77._.total, bf16[256,128]{1,0:T(8,128)(2,1)S(1)} %shard_map.78.refs_0_, bf16[256,128]{1,0:T(8,128)(2,1)S(1)} %collective-permute-done.refs_1_, ...), custom_call_target="tpu_custom_call" | custom-call | flops 8589934592 | bytes 1048576 | tf_op jit(solution)/shard_map/pallas_call | solution.py:295
  13.5 0.9 %shard_map.82 = (s16[528,128]{1,0:T(8,128)(2,1)S(1)}, s16[528,128]{1,0:T(8,128)(2,1)S(1)}) custom-call(bf16[2,48,256,128]{3,2,1,0:T(8,128)(2,1)S(1)} %get-tuple-element.12.pairs_ref, bf16[128,1024]{1,0:T(8,128)(2,1)S(1)} %get-tuple-element.13.across_ref), custom_call_target="tpu_custom_call" | custom-call | flops 8589934592 | bytes 1048576 | tf_op jit(solution)/shard_map/pallas_call | solution.py:295
  14.4 1.7 %collective-permute-start.5 = (s16[528,128]{1,0:T(8,128)(2,1)S(1)}, s16[528,128]{1,0:T(8,128)(2,1)S(1)}, u32[]{:S(2)}, u32[]{:S(2)}) collective-permute-start(s16[528,128]{1,0:T(8,128)(2,1)S(1)} %get-tuple-element.16), channel_id=1, source_target_pairs={{0,4},{4,0},{8,12},{12,8},{16,20},{20,16},{24,28},{28,24},{1,5},{5... | collective-permute-start | bytes 405512 | tf_op jit(solution)/shard_map/ppermute | solution.py:21
  16.0 2.0 %collective-permute-start.6 = (s16[528,128]{1,0:T(8,128)(2,1)S(1)}, s16[528,128]{1,0:T(8,128)(2,1)S(1)}, u32[]{:S(2)}, u32[]{:S(2)}) collective-permute-start(s16[528,128]{1,0:T(8,128)(2,1)S(1)} %get-tuple-element.17), channel_id=1, source_target_pairs={{0,0},{4,8},{8,4},{12,16},{16,12},{20,24},{24,20},{28,28},{1,1},{5... | collective-permute-start | bytes 405512 | tf_op jit(solution)/shard_map/ppermute | solution.py:21
  18.0 0.0 collective-permute-done.3.first_ref
  18.1 2.1 %shard_map.81 = (f32[4,128,128]{2,1,0:T(8,128)S(1)}, f32[4,128,128]{2,1,0:T(8,128)S(1)}) custom-call(bf16[2,48,256,128]{3,2,1,0:T(8,128)(2,1)S(1)} %get-tuple-element.12.pairs_ref, bf16[128,1024]{1,0:T(8,128)(2,1)S(1)} %get-tuple-element.13.across_ref, bf16[512,128]{1,0:T(8,128)(2,1)S(1)} %collective-permute-done.3.first_ref, ...), custom_call_target="tpu_custom_call" | custom-call | flops 8589934592 | bytes 1048576 | tf_op jit(solution)/shard_map/pallas_call | solution.py:295
  20.2 2.2 %collective-permute-done.6.second_ref = s16[528,128]{1,0:T(8,128)(2,1)S(1)} collective-permute-done((s16[528,128]{1,0:T(8,128)(2,1)S(1)}, s16[528,128]{1,0:T(8,128)(2,1)S(1)}, u32[]{:S(2)}, u32[]{:S(2)}) %collective-permute-start.6) | collective-permute-done | bytes 135200 | tf_op jit(solution)/shard_map/ppermute | solution.py:21
  22.4 0.2 shard_map.83
  22.5 1.6 %collective-permute-start.7 = (s16[272,128]{1,0:T(8,128)(2,1)S(1)}, s16[272,128]{1,0:T(8,128)(2,1)S(1)}, u32[]{:S(2)}, u32[]{:S(2)}) collective-permute-start(s16[272,128]{1,0:T(8,128)(2,1)S(1)} %get-tuple-element.19), channel_id=1, source_target_pairs={{0,1},{1,0},{2,3},{3,2},{4,5},{5,4},{6,7},{7,6},{8,9},{9,8},{10,11... | collective-permute-start | bytes 208904 | tf_op jit(solution)/shard_map/ppermute | solution.py:15
  24.1 1.5 %collective-permute-start.8 = (s16[272,128]{1,0:T(8,128)(2,1)S(1)}, s16[272,128]{1,0:T(8,128)(2,1)S(1)}, u32[]{:S(2)}, u32[]{:S(2)}) collective-permute-start(s16[272,128]{1,0:T(8,128)(2,1)S(1)} %get-tuple-element.20), channel_id=1, source_target_pairs={{0,2},{1,3},{2,0},{3,1},{4,6},{5,7},{6,4},{7,5},{8,10},{9,11},{10,... | collective-permute-start | bytes 208904 | tf_op jit(solution)/shard_map/ppermute | solution.py:15
  25.6 0.5 %collective-permute-start.9 = (s16[272,128]{1,0:T(8,128)(2,1)S(1)}, s16[272,128]{1,0:T(8,128)(2,1)S(1)}, u32[]{:S(2)}, u32[]{:S(2)}) collective-permute-start(s16[272,128]{1,0:T(8,128)(2,1)S(1)} %get-tuple-element.21), channel_id=1, source_target_pairs={{0,3},{1,2},{2,1},{3,0},{4,7},{5,6},{6,5},{7,4},{8,11},{9,10},{10,... | collective-permute-start | bytes 208904 | tf_op jit(solution)/shard_map/ppermute | solution.py:15
  26.1 0.8 %collective-permute-done.7.refs_0_ = s16[272,128]{1,0:T(8,128)(2,1)S(1)} collective-permute-done((s16[272,128]{1,0:T(8,128)(2,1)S(1)}, s16[272,128]{1,0:T(8,128)(2,1)S(1)}, u32[]{:S(2)}, u32[]{:S(2)}) %collective-permute-start.7) | collective-permute-done | bytes 69664 | tf_op jit(solution)/shard_map/ppermute | solution.py:15
  26.9 1.5 %collective-permute-done.8.refs_1_ = s16[272,128]{1,0:T(8,128)(2,1)S(1)} collective-permute-done((s16[272,128]{1,0:T(8,128)(2,1)S(1)}, s16[272,128]{1,0:T(8,128)(2,1)S(1)}, u32[]{:S(2)}, u32[]{:S(2)}) %collective-permute-start.8) | collective-permute-done | bytes 69664 | tf_op jit(solution)/shard_map/ppermute | solution.py:15
  28.4 2.4 %collective-permute-done.9.refs_2_ = s16[272,128]{1,0:T(8,128)(2,1)S(1)} collective-permute-done((s16[272,128]{1,0:T(8,128)(2,1)S(1)}, s16[272,128]{1,0:T(8,128)(2,1)S(1)}, u32[]{:S(2)}, u32[]{:S(2)}) %collective-permute-start.9) | collective-permute-done | bytes 69664 | tf_op jit(solution)/shard_map/ppermute | solution.py:15
  30.8 0.7 %shard_map.84 = (f32[128,128]{1,0:T(8,128)}, f32[128,128]{1,0:T(8,128)}) custom-call(f32[256,128]{1,0:T(8,128)S(1)} %get-tuple-element.18.own_ref, s16[272,128]{1,0:T(8,128)(2,1)S(1)} %collective-permute-done.7.refs_0_, s16[272,128]{1,0:T(8,128)(2,1)S(1)} %collective-permute-done.8.refs_1_, s16[272,128]{1,0:T(8,128)(2,1)S(1)} %collective-permute-done.9.refs_2_), custom_call_target="tpu_custom_call" | custom-call | bytes 1048576 | tf_op jit(solution)/shard_map/pallas_call | solution.py:295
  (4 shorter events, 0.0 us)
Async XLA Ops:
  1.4 9.0 %collective-permute-start = (bf16[256,128]{1,0:T(8,128)(2,1)S(1)}, bf16[256,128]{1,0:T(8,128)(2,1)S(1)}, u32[]{:S(2)}, u32[]{:S(2)}) collective-permute-start(bf16[256,128]{1,0:T(8,128)(2,1)S(1)} %shard_map.78.refs_0_), channel_id=1, source_target_pairs={{0,1},{1,0},{2,3},{3,2},{4,5},{5,4},{6,7},{7,6},{8,9},{9,8},{10,11... | collective-permute-start | bytes 196616 | tf_op jit(solution)/shard_map/ppermute | solution.py:15
  3.0 7.5 %collective-permute-start.1 = (bf16[256,128]{1,0:T(8,128)(2,1)S(1)}, bf16[256,128]{1,0:T(8,128)(2,1)S(1)}, u32[]{:S(2)}, u32[]{:S(2)}) collective-permute-start(bf16[256,128]{1,0:T(8,128)(2,1)S(1)} %shard_map.78.refs_0_), channel_id=1, source_target_pairs={{0,2},{1,3},{2,0},{3,1},{4,6},{5,7},{6,4},{7,5},{8,10},{9,11},{10,... | collective-permute-start | bytes 196616 | tf_op jit(solution)/shard_map/ppermute | solution.py:15
  4.5 6.0 %collective-permute-start.2 = (bf16[256,128]{1,0:T(8,128)(2,1)S(1)}, bf16[256,128]{1,0:T(8,128)(2,1)S(1)}, u32[]{:S(2)}, u32[]{:S(2)}) collective-permute-start(bf16[256,128]{1,0:T(8,128)(2,1)S(1)} %shard_map.78.refs_0_), channel_id=1, source_target_pairs={{0,3},{1,2},{2,1},{3,0},{4,7},{5,6},{6,5},{7,4},{8,11},{9,10},{10,... | collective-permute-start | bytes 196616 | tf_op jit(solution)/shard_map/ppermute | solution.py:15
  10.5 7.5 %collective-permute-start.3 = (bf16[512,128]{1,0:T(8,128)(2,1)S(1)}, bf16[512,128]{1,0:T(8,128)(2,1)S(1)}, u32[]{:S(2)}, u32[]{:S(2)}) collective-permute-start(bf16[512,128]{1,0:T(8,128)(2,1)S(1)} %shard_map.79._), channel_id=1, source_target_pairs={{0,4},{4,0},{8,12},{12,8},{16,20},{20,16},{24,28},{28,24},{1,5},{5... | collective-permute-start | bytes 393224 | tf_op jit(solution)/shard_map/ppermute | solution.py:21
  10.6 7.5 %collective-permute-start.4 = (bf16[512,128]{1,0:T(8,128)(2,1)S(1)}, bf16[512,128]{1,0:T(8,128)(2,1)S(1)}, u32[]{:S(2)}, u32[]{:S(2)}) collective-permute-start(bf16[512,128]{1,0:T(8,128)(2,1)S(1)} %shard_map.79._), channel_id=1, source_target_pairs={{0,0},{4,8},{8,4},{12,16},{16,12},{20,24},{24,20},{28,28},{1,1},{5... | collective-permute-start | bytes 393224 | tf_op jit(solution)/shard_map/ppermute | solution.py:21
  14.4 5.8 %collective-permute-start.5 = (s16[528,128]{1,0:T(8,128)(2,1)S(1)}, s16[528,128]{1,0:T(8,128)(2,1)S(1)}, u32[]{:S(2)}, u32[]{:S(2)}) collective-permute-start(s16[528,128]{1,0:T(8,128)(2,1)S(1)} %get-tuple-element.16), channel_id=1, source_target_pairs={{0,4},{4,0},{8,12},{12,8},{16,20},{20,16},{24,28},{28,24},{1,5},{5... | collective-permute-start | bytes 405512 | tf_op jit(solution)/shard_map/ppermute | solution.py:21
  16.0 6.3 %collective-permute-start.6 = (s16[528,128]{1,0:T(8,128)(2,1)S(1)}, s16[528,128]{1,0:T(8,128)(2,1)S(1)}, u32[]{:S(2)}, u32[]{:S(2)}) collective-permute-start(s16[528,128]{1,0:T(8,128)(2,1)S(1)} %get-tuple-element.17), channel_id=1, source_target_pairs={{0,0},{4,8},{8,4},{12,16},{16,12},{20,24},{24,20},{28,28},{1,1},{5... | collective-permute-start | bytes 405512 | tf_op jit(solution)/shard_map/ppermute | solution.py:21
  22.5 4.4 %collective-permute-start.7 = (s16[272,128]{1,0:T(8,128)(2,1)S(1)}, s16[272,128]{1,0:T(8,128)(2,1)S(1)}, u32[]{:S(2)}, u32[]{:S(2)}) collective-permute-start(s16[272,128]{1,0:T(8,128)(2,1)S(1)} %get-tuple-element.19), channel_id=1, source_target_pairs={{0,1},{1,0},{2,3},{3,2},{4,5},{5,4},{6,7},{7,6},{8,9},{9,8},{10,11... | collective-permute-start | bytes 208904 | tf_op jit(solution)/shard_map/ppermute | solution.py:15
  24.1 4.3 %collective-permute-start.8 = (s16[272,128]{1,0:T(8,128)(2,1)S(1)}, s16[272,128]{1,0:T(8,128)(2,1)S(1)}, u32[]{:S(2)}, u32[]{:S(2)}) collective-permute-start(s16[272,128]{1,0:T(8,128)(2,1)S(1)} %get-tuple-element.20), channel_id=1, source_target_pairs={{0,2},{1,3},{2,0},{3,1},{4,6},{5,7},{6,4},{7,5},{8,10},{9,11},{10,... | collective-permute-start | bytes 208904 | tf_op jit(solution)/shard_map/ppermute | solution.py:15
  25.6 5.2 %collective-permute-start.9 = (s16[272,128]{1,0:T(8,128)(2,1)S(1)}, s16[272,128]{1,0:T(8,128)(2,1)S(1)}, u32[]{:S(2)}, u32[]{:S(2)}) collective-permute-start(s16[272,128]{1,0:T(8,128)(2,1)S(1)} %get-tuple-element.21), channel_id=1, source_target_pairs={{0,3},{1,2},{2,1},{3,0},{4,7},{5,6},{6,5},{7,4},{8,11},{9,10},{10,... | collective-permute-start | bytes 208904 | tf_op jit(solution)/shard_map/ppermute | solution.py:15

commit v8 on v7

--- a/solution.py
+++ b/solution.py
@@ -67,27 +67,18 @@
     return target, jnp.where(group % 2 == 0, source - 2 * offset * group_blocks, source)
 
 
-def each_slot(chunk, refs, held, ids, id_sems, sems, prepare, work):
-    live_ref, *id_refs, kernels_ref = refs
-    chunks = held.shape[0] // chunk
+def each_slot(chunk, live_ref, id_refs, ids, id_sems, prepare, wait, work):
     copies = [pltpu.make_async_copy(ref, kept, id_sems.at[i]) for i, (ref, kept) in enumerate(zip(id_refs, ids))]
-
-    def fetch(c):
-        rows = pl.ds(c * chunk, chunk)
-        return pltpu.make_async_copy(kernels_ref.at[rows], held.at[rows], sems.at[c])
-
     for copy in copies:
         copy.start()
-    for c in range(chunks):
-        fetch(c).start()
     prepare()
     for copy in copies:
         copy.wait()
     live = live_ref[0]
 
-    @pl.loop(0, chunks)
+    @pl.loop(0, ids[0].shape[0] // chunk)
     def _(c):
-        fetch(c).wait()
+        wait(c)
         first = c * chunk
 
         @pl.when(first + chunk <= live)
@@ -102,8 +93,8 @@
                 work(slot)
 
 
-def combine_kernel(group_blocks, blocks, chunk, *refs):
-    slot_refs, (total, held, *ids, id_sems, sems) = refs[:4], refs[4:]
+def combine_kernel(group_blocks, blocks, chunk, live_ref, target_ref, source_ref, kernels_ref, total, *scratch):
+    *ids, id_sems = scratch
     sources = 3 * group_blocks
 
     def clear():
@@ -114,9 +105,9 @@
     def add(slot):
         target, source = place(*ids, slot, group_blocks, blocks)
         pair = target * sources + source
-        total[pair] += held[slot].reshape(total.shape[1:]).astype(jnp.float32)
-
-    each_slot(chunk, slot_refs, held, ids, id_sems, sems, clear, add)
+        total[pair] += kernels_ref[slot].reshape(total.shape[1:]).astype(jnp.float32)
+
+    each_slot(chunk, live_ref, (target_ref, source_ref), ids, id_sems, clear, lambda c: None, add)
 
 
 def split_kernel(blocks, panels, _, total, *refs):
@@ -228,11 +219,17 @@
 
 
 def slots_kernel(blocks, panels, chunk, *refs):
-    slot_refs, (first_ref, second_ref, *gathered), refs = refs[:4], refs[4:-9], refs[-9:]
-    potential_ref, adjoint_ref, held, stack, across, *ids, id_sems, sems = refs
+    (live_ref, *id_refs, kernels_ref), (first_ref, second_ref, *gathered) = refs[:4], refs[4:-9]
+    potential_ref, adjoint_ref, held, stack, across, *ids, id_sems, sems = refs[-9:]
     group_blocks = potential_ref.shape[0]
 
+    def fetch(c):
+        rows = pl.ds(c * chunk, chunk)
+        return pltpu.make_async_copy(kernels_ref.at[rows], held.at[rows], sems.at[c])
+
     def prepare():
+        for c in range(held.shape[0] // chunk):
+            fetch(c).start()
         potential_ref[...] = jnp.zeros(potential_ref.shape, potential_ref.dtype)
         adjoint_ref[...] = jnp.zeros(adjoint_ref.shape, adjoint_ref.dtype)
         for i, block in enumerate(strengths_of(first_ref, gathered, second_ref, blocks, panels)):
@@ -250,7 +247,7 @@
             across[target], jnp.concatenate([real, imag], axis=0), preferred_element_type=jnp.float32
         )
 
-    each_slot(chunk, slot_refs, held, ids, id_sems, sems, prepare, work)
+    each_slot(chunk, live_ref, id_refs, ids, id_sems, prepare, lambda c: fetch(c).wait(), work)
 
 
 def code_kernel(*refs):
@@ -279,16 +276,8 @@
     chunk = 8 if slots % 8 == 0 else 1
     in_vmem, in_smem, in_hbm = (pl.BlockSpec(memory_space=m) for m in (pltpu.VMEM, pltpu.SMEM, pltpu.HBM))
     f32, bf16 = jnp.float32, jnp.bfloat16
-    slot_args = (live_slots,) + tuple(
-        pltpu.with_memory_space_constraint(x, pltpu.HBM) for x in (target_ids, source_ids, kernels)
-    )
-    held = pltpu.VMEM(kernels.shape, bf16)
-    fetch = [
-        pltpu.SMEM(target_ids.shape, jnp.int32),
-        pltpu.SMEM(source_ids.shape, jnp.int32),
-        pltpu.SemaphoreType.DMA((2,)),
-        pltpu.SemaphoreType.DMA((slots // chunk,)),
-    ]
+    slot_args = (live_slots,) + tuple(pltpu.with_memory_space_constraint(x, pltpu.HBM) for x in (target_ids, source_ids))
+    ids = [pltpu.SMEM(x.shape, x.dtype) for x in (target_ids, source_ids)] + [pltpu.SemaphoreType.DMA((2,))]
 
     def call(body, shapes, args, specs=None, scratch=(), mib=8, flops=0):
         single = not isinstance(shapes, tuple)
@@ -311,6 +300,7 @@
         [pltpu.with_memory_space_constraint(x, pltpu.HBM) for x in (strengths, adjoint_weights)],
         [in_hbm] * 2,
         [pltpu.SemaphoreType.DMA((2,))],
+        flops=1 << 34,
     )
     gathered = [mine] + [exchange(mine, "clu", k) for k in range(1, clusters)]
 
@@ -330,10 +320,9 @@
         total = call(
             functools.partial(combine_kernel, group_blocks, blocks, chunk),
             pltpu.VMEM((pairs, 2 * panels, panels), f32),
-            slot_args,
-            [in_smem] + [in_hbm] * 3,
-            [held, *fetch],
-            mib=20,
+            (*slot_args, pltpu.with_memory_space_constraint(kernels, pltpu.VMEM)),
+            [in_smem] + [in_hbm] * 2 + [in_vmem],
+            ids,
             flops=1 << 33,
         )
         own = group_strengths(total)
@@ -362,13 +351,14 @@
         potential, adjoint = call(
             functools.partial(slots_kernel, blocks, panels, chunk),
             (block_sums, shape(sources, width, panels)),
-            (*slot_args, first, second, *gathered),
+            (*slot_args, pltpu.with_memory_space_constraint(kernels, pltpu.HBM), first, second, *gathered),
             [in_smem] + [in_hbm] * 3 + [in_vmem] * (2 + clusters),
             [
-                held,
+                pltpu.VMEM(kernels.shape, bf16),
                 pltpu.VMEM((sources, 2 * panels, width), bf16),
                 pltpu.VMEM((group_blocks, width, 2 * panels), bf16),
-                *fetch,
+                *ids,
+                pltpu.SemaphoreType.DMA((slots // chunk,)),
             ],
             mib=40,
         )
@@ -380,7 +370,7 @@
         (shape(2 * blocks * panels, width),) + (coded(2 * blocks),) * (clusters - 1),
         (potential, middle, lower, upper),
     )
-    parts = [exchange(part, "clu", k) for k, part in enumerate(parts, 1)]
+    parts = [exchange(parts[k - 1], "clu", k) for k in range(clusters - 1, 0, -1)]
     out = shape(blocks * panels, width)
     return tuple(call(functools.partial(finish_kernel, blocks, panels), (out, out), (mine, *parts)))
 

time: 31.8 us -> 29.9 us (0.940)
  Pallas kernels: 10.4 us -> 8.71 us
    pallas_call x8, Pallas kernels: 10.4 us -> 8.71 us  [call(): pl.pallas_call(body, out_shape=shapes, in_specs=specs or [in_vmem] * len(...]
  transfers between devices with their start and end apart: 10 -> 10, of which waited for: 4 -> 5; matrix products, arithmetic and copies ran while one was open for 0% -> 0% of each run, Pallas kernels for 28% -> 23%
where the time goes in v8:
time: 29.9 us; the launch traced here: 29.8 us
  starting transfers between devices  12.8 us (43%)
  Pallas kernels  8.71 us (29%)
  waiting for transfers between devices  6.87 us (23%)
  between operations  1.41 us (5%)
    pallas_call x8, Pallas kernels, call(): pl.pallas_call(body, out_shape=shapes, in_specs=specs or [in_vmem] * len(...  8.71 us
    ppermute x6, starting transfers between devices, exchange(): lax.ppermute(value, axis, [(i, i ^ step) for i in range(lax.axis_size(axi...  7.11 us
    ppermute x4, starting transfers between devices, exchange_beside(): lax.ppermute(value, 'grp', [(i, j if 0 <= j < groups else i) for i, j in...  5.71 us
    ppermute x6, waiting for transfers between devices, exchange(): lax.ppermute(value, axis, [(i, i ^ step) for i in range(lax.axis_size(axi...  4.7 us
    ppermute x4, waiting for transfers between devices, exchange_beside(): lax.ppermute(value, 'grp', [(i, j if 0 <= j < groups else i) for i, j in...  2.17 us
  transfers between devices with their start and end apart: 10, of which 5 were waited for; matrix products, arithmetic and copies ran while one was open for 0% of the time, Pallas kernels for 23%

profile of v8, /device:TPU:8, one launch (start us, length us, event | category | flops | bytes accessed | tf_op | source)
XLA Modules:
  0.0 29.8 jit_solution(14258046899681366315)
XLA Ops:
  0.6 0.9 %shard_map.78.refs_0_ = bf16[256,128]{1,0:T(8,128)(2,1)S(1)} custom-call(bf16[128,128]{1,0:T(8,128)(2,1)} %strengths_ref.1, bf16[128,128]{1,0:T(8,128)(2,1)} %weights_ref.1), custom_call_target="tpu_custom_call" | custom-call | flops 17179869184 | bytes 1048576 | tf_op jit(solution)/shard_map/pallas_call | solution.py:284
  1.6 1.6 %collective-permute-start = (bf16[256,128]{1,0:T(8,128)(2,1)S(1)}, bf16[256,128]{1,0:T(8,128)(2,1)S(1)}, u32[]{:S(2)}, u32[]{:S(2)}) collective-permute-start(bf16[256,128]{1,0:T(8,128)(2,1)S(1)} %shard_map.78.refs_0_), channel_id=1, source_target_pairs={{0,1},{1,0},{2,3},{3,2},{4,5},{5,4},{6,7},{7,6},{8,9},{9,8},{10,11... | collective-permute-start | bytes 196616 | tf_op jit(solution)/shard_map/ppermute | solution.py:15
  3.1 1.5 %collective-permute-start.1 = (bf16[256,128]{1,0:T(8,128)(2,1)S(1)}, bf16[256,128]{1,0:T(8,128)(2,1)S(1)}, u32[]{:S(2)}, u32[]{:S(2)}) collective-permute-start(bf16[256,128]{1,0:T(8,128)(2,1)S(1)} %shard_map.78.refs_0_), channel_id=1, source_target_pairs={{0,2},{1,3},{2,0},{3,1},{4,6},{5,7},{6,4},{7,5},{8,10},{9,11},{10,... | collective-permute-start | bytes 196616 | tf_op jit(solution)/shard_map/ppermute | solution.py:15
  4.7 0.5 %collective-permute-start.2 = (bf16[256,128]{1,0:T(8,128)(2,1)S(1)}, bf16[256,128]{1,0:T(8,128)(2,1)S(1)}, u32[]{:S(2)}, u32[]{:S(2)}) collective-permute-start(bf16[256,128]{1,0:T(8,128)(2,1)S(1)} %shard_map.78.refs_0_), channel_id=1, source_target_pairs={{0,3},{1,2},{2,1},{3,0},{4,7},{5,6},{6,5},{7,4},{8,11},{9,10},{10,... | collective-permute-start | bytes 196616 | tf_op jit(solution)/shard_map/ppermute | solution.py:15
  5.8 2.9 %shard_map.77._.total = f32[48,256,128]{2,1,0:T(8,128)S(1)} custom-call(s32[1]{0:T(128)S(6)} %copy.8.live_ref, s32[192]{0:T(256)} %target_ref.1, s32[192]{0:T(256)} %source_ref.1, bf16[192,2,128,128]{3,2,1,0:T(8,128)(2,1)S(1)} %copy-done), custom_call_target="tpu_custom_call" | custom-call | flops 8589934592 | bytes 1048576 | tf_op jit(solution)/shard_map/pallas_call | solution.py:284
  8.7 0.0 collective-permute-done.refs_1_
  8.7 0.0 collective-permute-done.1.refs_2_
  8.8 1.1 %collective-permute-done.2.refs_3_ = bf16[256,128]{1,0:T(8,128)(2,1)S(1)} collective-permute-done((bf16[256,128]{1,0:T(8,128)(2,1)S(1)}, bf16[256,128]{1,0:T(8,128)(2,1)S(1)}, u32[]{:S(2)}, u32[]{:S(2)}) %collective-permute-start.2) | collective-permute-done | bytes 65568 | tf_op jit(solution)/shard_map/ppermute | solution.py:15
  9.8 0.1 collective-permute-start.3
  9.9 2.4 %collective-permute-start.4 = (bf16[512,128]{1,0:T(8,128)(2,1)S(1)}, bf16[512,128]{1,0:T(8,128)(2,1)S(1)}, u32[]{:S(2)}, u32[]{:S(2)}) collective-permute-start(bf16[512,128]{1,0:T(8,128)(2,1)S(1)} %shard_map.79._), channel_id=1, source_target_pairs={{0,0},{4,8},{8,4},{12,16},{16,12},{20,24},{24,20},{28,28},{1,1},{5... | collective-permute-start | bytes 393224 | tf_op jit(solution)/shard_map/ppermute | solution.py:21
  12.4 0.9 %shard_map.80 = (bf16[2,48,256,128]{3,2,1,0:T(8,128)(2,1)S(1)}, bf16[128,1024]{1,0:T(8,128)(2,1)S(1)}) custom-call(bf16[512,128]{1,0:T(8,128)(2,1)S(1)} %shard_map.79._, f32[48,256,128]{2,1,0:T(8,128)S(1)} %shard_map.77._.total, bf16[256,128]{1,0:T(8,128)(2,1)S(1)} %shard_map.78.refs_0_, bf16[256,128]{1,0:T(8,128)(2,1)S(1)} %collective-permute-done.refs_1_, ...), custom_call_target="tpu_custom_call" | custom-call | flops 8589934592 | bytes 1048576 | tf_op jit(solution)/shard_map/pallas_call | solution.py:284
  13.3 0.9 %shard_map.82 = (s16[528,128]{1,0:T(8,128)(2,1)S(1)}, s16[528,128]{1,0:T(8,128)(2,1)S(1)}) custom-call(bf16[2,48,256,128]{3,2,1,0:T(8,128)(2,1)S(1)} %get-tuple-element.12.pairs_ref, bf16[128,1024]{1,0:T(8,128)(2,1)S(1)} %get-tuple-element.13.across_ref), custom_call_target="tpu_custom_call" | custom-call | flops 8589934592 | bytes 1048576 | tf_op jit(solution)/shard_map/pallas_call | solution.py:284
  14.2 1.2 %collective-permute-start.5 = (s16[528,128]{1,0:T(8,128)(2,1)S(1)}, s16[528,128]{1,0:T(8,128)(2,1)S(1)}, u32[]{:S(2)}, u32[]{:S(2)}) collective-permute-start(s16[528,128]{1,0:T(8,128)(2,1)S(1)} %get-tuple-element.16), channel_id=1, source_target_pairs={{0,4},{4,0},{8,12},{12,8},{16,20},{20,16},{24,28},{28,24},{1,5},{5... | collective-permute-start | bytes 405512 | tf_op jit(solution)/shard_map/ppermute | solution.py:21
  15.4 2.0 %collective-permute-start.6 = (s16[528,128]{1,0:T(8,128)(2,1)S(1)}, s16[528,128]{1,0:T(8,128)(2,1)S(1)}, u32[]{:S(2)}, u32[]{:S(2)}) collective-permute-start(s16[528,128]{1,0:T(8,128)(2,1)S(1)} %get-tuple-element.17), channel_id=1, source_target_pairs={{0,0},{4,8},{8,4},{12,16},{16,12},{20,24},{24,20},{28,28},{1,1},{5... | collective-permute-start | bytes 405512 | tf_op jit(solution)/shard_map/ppermute | solution.py:21
  17.4 2.1 %shard_map.81 = (f32[4,128,128]{2,1,0:T(8,128)S(1)}, f32[4,128,128]{2,1,0:T(8,128)S(1)}) custom-call(bf16[2,48,256,128]{3,2,1,0:T(8,128)(2,1)S(1)} %get-tuple-element.12.pairs_ref, bf16[128,1024]{1,0:T(8,128)(2,1)S(1)} %get-tuple-element.13.across_ref, bf16[512,128]{1,0:T(8,128)(2,1)S(1)} %collective-permute-done.3.first_ref, ...), custom_call_target="tpu_custom_call" | custom-call | flops 8589934592 | bytes 1048576 | tf_op jit(solution)/shard_map/pallas_call | solution.py:284
  19.6 2.2 %collective-permute-done.6.second_ref = s16[528,128]{1,0:T(8,128)(2,1)S(1)} collective-permute-done((s16[528,128]{1,0:T(8,128)(2,1)S(1)}, s16[528,128]{1,0:T(8,128)(2,1)S(1)}, u32[]{:S(2)}, u32[]{:S(2)}) %collective-permute-start.6) | collective-permute-done | bytes 135200 | tf_op jit(solution)/shard_map/ppermute | solution.py:21
  21.7 0.2 shard_map.83
  21.9 2.2 %collective-permute-start.7 = (s16[272,128]{1,0:T(8,128)(2,1)S(1)}, s16[272,128]{1,0:T(8,128)(2,1)S(1)}, u32[]{:S(2)}, u32[]{:S(2)}) collective-permute-start(s16[272,128]{1,0:T(8,128)(2,1)S(1)} %get-tuple-element.19), channel_id=1, source_target_pairs={{0,3},{1,2},{2,1},{3,0},{4,7},{5,6},{6,5},{7,4},{8,11},{9,10},{10,... | collective-permute-start | bytes 208904 | tf_op jit(solution)/shard_map/ppermute | solution.py:15
  24.1 0.6 %collective-permute-start.8 = (s16[272,128]{1,0:T(8,128)(2,1)S(1)}, s16[272,128]{1,0:T(8,128)(2,1)S(1)}, u32[]{:S(2)}, u32[]{:S(2)}) collective-permute-start(s16[272,128]{1,0:T(8,128)(2,1)S(1)} %get-tuple-element.20), channel_id=1, source_target_pairs={{0,2},{1,3},{2,0},{3,1},{4,6},{5,7},{6,4},{7,5},{8,10},{9,11},{10,... | collective-permute-start | bytes 208904 | tf_op jit(solution)/shard_map/ppermute | solution.py:15
  24.8 0.7 %collective-permute-start.9 = (s16[272,128]{1,0:T(8,128)(2,1)S(1)}, s16[272,128]{1,0:T(8,128)(2,1)S(1)}, u32[]{:S(2)}, u32[]{:S(2)}) collective-permute-start(s16[272,128]{1,0:T(8,128)(2,1)S(1)} %get-tuple-element.21), channel_id=1, source_target_pairs={{0,1},{1,0},{2,3},{3,2},{4,5},{5,4},{6,7},{7,6},{8,9},{9,8},{10,11... | collective-permute-start | bytes 208904 | tf_op jit(solution)/shard_map/ppermute | solution.py:15
  25.4 1.8 %collective-permute-done.7.refs_0_ = s16[272,128]{1,0:T(8,128)(2,1)S(1)} collective-permute-done((s16[272,128]{1,0:T(8,128)(2,1)S(1)}, s16[272,128]{1,0:T(8,128)(2,1)S(1)}, u32[]{:S(2)}, u32[]{:S(2)}) %collective-permute-start.7) | collective-permute-done | bytes 69664 | tf_op jit(solution)/shard_map/ppermute | solution.py:15
  27.2 1.4 %collective-permute-done.8.refs_1_ = s16[272,128]{1,0:T(8,128)(2,1)S(1)} collective-permute-done((s16[272,128]{1,0:T(8,128)(2,1)S(1)}, s16[272,128]{1,0:T(8,128)(2,1)S(1)}, u32[]{:S(2)}, u32[]{:S(2)}) %collective-permute-start.8) | collective-permute-done | bytes 69664 | tf_op jit(solution)/shard_map/ppermute | solution.py:15
  28.7 0.4 %collective-permute-done.9.refs_2_ = s16[272,128]{1,0:T(8,128)(2,1)S(1)} collective-permute-done((s16[272,128]{1,0:T(8,128)(2,1)S(1)}, s16[272,128]{1,0:T(8,128)(2,1)S(1)}, u32[]{:S(2)}, u32[]{:S(2)}) %collective-permute-start.9) | collective-permute-done | bytes 69664 | tf_op jit(solution)/shard_map/ppermute | solution.py:15
  29.1 0.7 %shard_map.84 = (f32[128,128]{1,0:T(8,128)}, f32[128,128]{1,0:T(8,128)}) custom-call(f32[256,128]{1,0:T(8,128)S(1)} %get-tuple-element.18.own_ref, s16[272,128]{1,0:T(8,128)(2,1)S(1)} %collective-permute-done.7.refs_0_, s16[272,128]{1,0:T(8,128)(2,1)S(1)} %collective-permute-done.8.refs_1_, s16[272,128]{1,0:T(8,128)(2,1)S(1)} %collective-permute-done.9.refs_2_), custom_call_target="tpu_custom_call" | custom-call | bytes 1048576 | tf_op jit(solution)/shard_map/pallas_call | solution.py:284
  (6 shorter events, 0.0 us)
Async XLA Ops:
  0.6 5.2 %copy-start = (bf16[192,2,128,128]{3,2,1,0:T(8,128)(2,1)S(1)}, bf16[192,2,128,128]{3,2,1,0:T(8,128)(2,1)}, u32[]{:S(2)}) copy-start(bf16[192,2,128,128]{3,2,1,0:T(8,128)(2,1)} %kernels_ref.1) | copy-start | bytes 37748740
  1.6 7.1 %collective-permute-start = (bf16[256,128]{1,0:T(8,128)(2,1)S(1)}, bf16[256,128]{1,0:T(8,128)(2,1)S(1)}, u32[]{:S(2)}, u32[]{:S(2)}) collective-permute-start(bf16[256,128]{1,0:T(8,128)(2,1)S(1)} %shard_map.78.refs_0_), channel_id=1, source_target_pairs={{0,1},{1,0},{2,3},{3,2},{4,5},{5,4},{6,7},{7,6},{8,9},{9,8},{10,11... | collective-permute-start | bytes 196616 | tf_op jit(solution)/shard_map/ppermute | solution.py:15
  3.1 5.6 %collective-permute-start.1 = (bf16[256,128]{1,0:T(8,128)(2,1)S(1)}, bf16[256,128]{1,0:T(8,128)(2,1)S(1)}, u32[]{:S(2)}, u32[]{:S(2)}) collective-permute-start(bf16[256,128]{1,0:T(8,128)(2,1)S(1)} %shard_map.78.refs_0_), channel_id=1, source_target_pairs={{0,2},{1,3},{2,0},{3,1},{4,6},{5,7},{6,4},{7,5},{8,10},{9,11},{10,... | collective-permute-start | bytes 196616 | tf_op jit(solution)/shard_map/ppermute | solution.py:15
  4.7 5.2 %collective-permute-start.2 = (bf16[256,128]{1,0:T(8,128)(2,1)S(1)}, bf16[256,128]{1,0:T(8,128)(2,1)S(1)}, u32[]{:S(2)}, u32[]{:S(2)}) collective-permute-start(bf16[256,128]{1,0:T(8,128)(2,1)S(1)} %shard_map.78.refs_0_), channel_id=1, source_target_pairs={{0,3},{1,2},{2,1},{3,0},{4,7},{5,6},{6,5},{7,4},{8,11},{9,10},{10,... | collective-permute-start | bytes 196616 | tf_op jit(solution)/shard_map/ppermute | solution.py:15
  9.8 7.5 %collective-permute-start.3 = (bf16[512,128]{1,0:T(8,128)(2,1)S(1)}, bf16[512,128]{1,0:T(8,128)(2,1)S(1)}, u32[]{:S(2)}, u32[]{:S(2)}) collective-permute-start(bf16[512,128]{1,0:T(8,128)(2,1)S(1)} %shard_map.79._), channel_id=1, source_target_pairs={{0,4},{4,0},{8,12},{12,8},{16,20},{20,16},{24,28},{28,24},{1,5},{5... | collective-permute-start | bytes 393224 | tf_op jit(solution)/shard_map/ppermute | solution.py:21
  9.9 7.5 %collective-permute-start.4 = (bf16[512,128]{1,0:T(8,128)(2,1)S(1)}, bf16[512,128]{1,0:T(8,128)(2,1)S(1)}, u32[]{:S(2)}, u32[]{:S(2)}) collective-permute-start(bf16[512,128]{1,0:T(8,128)(2,1)S(1)} %shard_map.79._), channel_id=1, source_target_pairs={{0,0},{4,8},{8,4},{12,16},{16,12},{20,24},{24,20},{28,28},{1,1},{5... | collective-permute-start | bytes 393224 | tf_op jit(solution)/shard_map/ppermute | solution.py:21
  14.2 5.4 %collective-permute-start.5 = (s16[528,128]{1,0:T(8,128)(2,1)S(1)}, s16[528,128]{1,0:T(8,128)(2,1)S(1)}, u32[]{:S(2)}, u32[]{:S(2)}) collective-permute-start(s16[528,128]{1,0:T(8,128)(2,1)S(1)} %get-tuple-element.16), channel_id=1, source_target_pairs={{0,4},{4,0},{8,12},{12,8},{16,20},{20,16},{24,28},{28,24},{1,5},{5... | collective-permute-start | bytes 405512 | tf_op jit(solution)/shard_map/ppermute | solution.py:21
  15.4 6.3 %collective-permute-start.6 = (s16[528,128]{1,0:T(8,128)(2,1)S(1)}, s16[528,128]{1,0:T(8,128)(2,1)S(1)}, u32[]{:S(2)}, u32[]{:S(2)}) collective-permute-start(s16[528,128]{1,0:T(8,128)(2,1)S(1)} %get-tuple-element.17), channel_id=1, source_target_pairs={{0,0},{4,8},{8,4},{12,16},{16,12},{20,24},{24,20},{28,28},{1,1},{5... | collective-permute-start | bytes 405512 | tf_op jit(solution)/shard_map/ppermute | solution.py:21
  21.9 5.3 %collective-permute-start.7 = (s16[272,128]{1,0:T(8,128)(2,1)S(1)}, s16[272,128]{1,0:T(8,128)(2,1)S(1)}, u32[]{:S(2)}, u32[]{:S(2)}) collective-permute-start(s16[272,128]{1,0:T(8,128)(2,1)S(1)} %get-tuple-element.19), channel_id=1, source_target_pairs={{0,3},{1,2},{2,1},{3,0},{4,7},{5,6},{6,5},{7,4},{8,11},{9,10},{10,... | collective-permute-start | bytes 208904 | tf_op jit(solution)/shard_map/ppermute | solution.py:15
  24.1 4.5 %collective-permute-start.8 = (s16[272,128]{1,0:T(8,128)(2,1)S(1)}, s16[272,128]{1,0:T(8,128)(2,1)S(1)}, u32[]{:S(2)}, u32[]{:S(2)}) collective-permute-start(s16[272,128]{1,0:T(8,128)(2,1)S(1)} %get-tuple-element.20), channel_id=1, source_target_pairs={{0,2},{1,3},{2,0},{3,1},{4,6},{5,7},{6,4},{7,5},{8,10},{9,11},{10,... | collective-permute-start | bytes 208904 | tf_op jit(solution)/shard_map/ppermute | solution.py:15
  24.8 4.3 %collective-permute-start.9 = (s16[272,128]{1,0:T(8,128)(2,1)S(1)}, s16[272,128]{1,0:T(8,128)(2,1)S(1)}, u32[]{:S(2)}, u32[]{:S(2)}) collective-permute-start(s16[272,128]{1,0:T(8,128)(2,1)S(1)} %get-tuple-element.21), channel_id=1, source_target_pairs={{0,1},{1,0},{2,3},{3,2},{4,5},{5,4},{6,7},{7,6},{8,9},{9,8},{10,11... | collective-permute-start | bytes 208904 | tf_op jit(solution)/shard_map/ppermute | solution.py:15

commit v9 on v8

--- a/solution.py
+++ b/solution.py
@@ -95,7 +95,6 @@
 
 def combine_kernel(group_blocks, blocks, chunk, live_ref, target_ref, source_ref, kernels_ref, total, *scratch):
     *ids, id_sems = scratch
-    sources = 3 * group_blocks
 
     def clear():
         @pl.loop(0, total.shape[0])
@@ -104,24 +103,19 @@
 
     def add(slot):
         target, source = place(*ids, slot, group_blocks, blocks)
-        pair = target * sources + source
+        pair = source * group_blocks + target
         total[pair] += kernels_ref[slot].reshape(total.shape[1:]).astype(jnp.float32)
 
     each_slot(chunk, live_ref, (target_ref, source_ref), ids, id_sems, clear, lambda c: None, add)
 
 
-def split_kernel(blocks, panels, _, total, *refs):
-    *gathered, out_ref, across_ref = refs
-
-    @pl.loop(0, total.shape[0])
+def split(total, first, out_ref):
+    @pl.loop(0, out_ref.shape[1])
     def _(pair):
-        value = total[pair]
+        value = total[first + pair]
         high = value.astype(jnp.bfloat16)
         out_ref[0, pair] = high
         out_ref[1, pair] = (value - high.astype(jnp.float32)).astype(jnp.bfloat16)
-
-    for i, block in enumerate(part_of(gathered, blocks, panels, 1)):
-        across_ref[:, 2 * i * panels : 2 * (i + 1) * panels] = crossed(block)
 
 
 def pack_kernel(strengths_ref, weights_ref, out_ref, sems):
@@ -169,40 +163,47 @@
     width = pairs_ref.shape[3]
     weights = across_ref[...]
     targets = weights.shape[1] // pairs_ref.shape[2]
-    sources = pairs_ref.shape[1] // targets
     both = jnp.concatenate([weights, weights], axis=1)
     step = 2 if count % 2 == 0 else 1
     for i in range(0, count, step):
         columns = []
-        for j in range(step):
-            tiles = [pairs_ref[h, t * sources + first + i + j] for h in range(2) for t in range(targets)]
+        for j in range(first + i, first + i + step):
+            tiles = [pairs_ref[h, j * targets + t] for h in range(2) for t in range(targets)]
             columns.append(jnp.concatenate(tiles, axis=0))
         product = jnp.dot(both, jnp.concatenate(columns, axis=1), preferred_element_type=jnp.float32)
         for j in range(step):
-            yield i + j, product[:, j * width : (j + 1) * width]
-
-
-def outer_kernel(count, pairs_ref, across_ref, first_ref, second_ref):
-    encode([value for _, value in adjoint_of(pairs_ref, across_ref, 0, count)], first_ref)
-    encode([value for _, value in adjoint_of(pairs_ref, across_ref, 2 * count, count)], second_ref)
-
-
-def inner_kernel(blocks, pairs_ref, across_ref, first_ref, second_ref, *refs):
-    *gathered, potential_ref, middle_ref = refs
+            yield product[:, j * width : (j + 1) * width]
+
+
+def second_kernel(blocks, panels, count, _, total, *refs):
+    *gathered, pairs_ref, across_ref, out_ref = refs
+    split(total, total.shape[0] - pairs_ref.shape[1], pairs_ref)
+    for i, block in enumerate(part_of(gathered, blocks, panels, 1)):
+        across_ref[:, 2 * i * panels : 2 * (i + 1) * panels] = crossed(block)
+    encode(list(adjoint_of(pairs_ref, across_ref, 0, count)), out_ref)
+
+
+def first_kernel(count, _first, _second, total, across_ref, pairs_ref, middle_ref, out_ref):
+    split(total, 0, pairs_ref)
+    encode(list(adjoint_of(pairs_ref, across_ref, 0, count)), out_ref)
+    for i, value in enumerate(adjoint_of(pairs_ref, across_ref, count, count)):
+        middle_ref[i] = value
+
+
+def forward_kernel(blocks, pairs_ref, second_pairs_ref, first_ref, second_ref, *refs):
+    *gathered, potential_ref = refs
     targets, panels = potential_ref.shape[:2]
-    sources = pairs_ref.shape[1] // targets
     stack = jnp.concatenate([stacked(x) for x in strengths_of(first_ref, gathered, second_ref, blocks, panels)], axis=0)
     for t in range(targets):
         halves = []
         for h in range(2):
             tiles = []
-            for s in range(sources):
-                tiles += [pairs_ref[h, t * sources + s, :panels], pairs_ref[h, t * sources + s, panels:]]
+            for ref in (pairs_ref, second_pairs_ref):
+                for pair in range(t, ref.shape[1], targets):
+                    tiles += [ref[h, pair, :panels], ref[h, pair, panels:]]
             halves.append(jnp.concatenate(tiles, axis=1))
         product = jnp.dot(jnp.concatenate(halves, axis=0), stack, preferred_element_type=jnp.float32)
         potential_ref[t] = product[:panels] + product[panels:]
-    for i, value in adjoint_of(pairs_ref, across_ref, targets, targets):
-        middle_ref[i] = value
 
 
 def parts_kernel(blocks, potential_ref, middle_ref, first_ref, second_ref, own_ref, *outs):
@@ -302,7 +303,8 @@
         [pltpu.SemaphoreType.DMA((2,))],
         flops=1 << 34,
     )
-    gathered = [mine] + [exchange(mine, "clu", k) for k in range(1, clusters)]
+    gathered = [exchange(mine, "clu", k) for k in range(clusters - 1, 0, -1)]
+    gathered = [mine] + gathered[::-1]
 
     def group_strengths(token):
         return call(
@@ -326,24 +328,32 @@
             flops=1 << 33,
         )
         own = group_strengths(total)
-        first, second = exchange_beside(own, 0), exchange_beside(own, 1)
+        second, first = exchange_beside(own, 1), exchange_beside(own, 0)
         total = pltpu.with_memory_space_constraint(total, pltpu.VMEM)
-        kept, across = call(
-            functools.partial(split_kernel, blocks, panels),
-            (pltpu.VMEM((2, pairs, 2 * panels, panels), bf16), shape(width, 2 * group_blocks * panels, kind=bf16)),
+        second_pairs = pairs // 3
+        kept_second, across, upper = call(
+            functools.partial(second_kernel, blocks, panels, group_blocks),
+            (
+                pltpu.VMEM((2, second_pairs, 2 * panels, panels), bf16),
+                shape(width, 2 * group_blocks * panels, kind=bf16),
+                coded(group_blocks),
+            ),
             (own, total, *gathered),
             [in_hbm] + [in_vmem] * (1 + clusters),
             flops=1 << 33,
         )
-        kept = pltpu.with_memory_space_constraint(kept, pltpu.VMEM)
-        lower, upper = call(
-            functools.partial(outer_kernel, group_blocks), (coded(group_blocks),) * 2, (kept, across), flops=1 << 33
-        )
-        potential, middle = call(
-            functools.partial(inner_kernel, blocks),
-            (block_sums, block_sums),
-            (kept, across, first, second, *gathered),
+        kept, middle, lower = call(
+            functools.partial(first_kernel, group_blocks),
+            (pltpu.VMEM((2, pairs - second_pairs, 2 * panels, panels), bf16), block_sums, coded(group_blocks)),
+            (first, second, total, across),
+            [in_hbm] * 2 + [in_vmem] * 2,
             flops=1 << 33,
+        )
+        kept, kept_second = (pltpu.with_memory_space_constraint(x, pltpu.VMEM) for x in (kept, kept_second))
+        potential = call(
+            functools.partial(forward_kernel, blocks),
+            block_sums,
+            (kept, kept_second, first, second, *gathered),
         )
     else:
         own = group_strengths(mine)
@@ -364,7 +374,7 @@
         )
         lower, middle, upper = (adjoint[i * group_blocks : (i + 1) * group_blocks] for i in range(3))
         lower, upper = call(code_kernel, (coded(group_blocks),) * 2, (lower, upper))
-    lower, upper = exchange_beside(lower, 0), exchange_beside(upper, 1)
+    upper, lower = exchange_beside(upper, 1), exchange_beside(lower, 0)
     mine, *parts = call(
         functools.partial(parts_kernel, blocks),
         (shape(2 * blocks * panels, width),) + (coded(2 * blocks),) * (clusters - 1),

time: 29.9 us -> 30.3 us (1.013)
  the two profiles are of different devices: /device:TPU:8 before, /device:TPU:0 now
where the time goes in v9:
time: 30.3 us; the launch traced here: 30.4 us
  starting transfers between devices  15.6 us (51%)
  Pallas kernels  8.91 us (29%)
  waiting for transfers between devices  4.5 us (15%)
  between operations  1.41 us (5%)
    pallas_call x8, Pallas kernels, call(): pl.pallas_call(body, out_shape=shapes, in_specs=specs or [in_vmem] * len(...  8.91 us
    ppermute x6, starting transfers between devices, exchange(): lax.ppermute(value, axis, [(i, i ^ step) for i in range(lax.axis_size(axi...  8.16 us
    ppermute x4, starting transfers between devices, exchange_beside(): lax.ppermute(value, 'grp', [(i, j if 0 <= j < groups else i) for i, j in...  7.43 us
    ppermute x6, waiting for transfers between devices, exchange(): lax.ppermute(value, axis, [(i, i ^ step) for i in range(lax.axis_size(axi...  4.49 us
  transfers between devices with their start and end apart: 10, of which 4 were waited for; matrix products, arithmetic and copies ran while one was open for 0% of the time, Pallas kernels for 23%

profile of v9, /device:TPU:0, one launch (start us, length us, event | category | flops | bytes accessed | tf_op | source)
XLA Modules:
  0.0 30.4 jit_solution(17629174388036160839)
XLA Ops:
  0.6 0.9 %shard_map.78.refs_0_ = bf16[256,128]{1,0:T(8,128)(2,1)S(1)} custom-call(bf16[128,128]{1,0:T(8,128)(2,1)} %strengths_ref.1, bf16[128,128]{1,0:T(8,128)(2,1)} %weights_ref.1), custom_call_target="tpu_custom_call" | custom-call | flops 17179869184 | bytes 1048576 | tf_op jit(solution)/shard_map/pallas_call | solution.py:285
  1.6 4.0 %collective-permute-start.2 = (bf16[256,128]{1,0:T(8,128)(2,1)S(1)}, bf16[256,128]{1,0:T(8,128)(2,1)S(1)}, u32[]{:S(2)}, u32[]{:S(2)}) collective-permute-start(bf16[256,128]{1,0:T(8,128)(2,1)S(1)} %shard_map.78.refs_0_), channel_id=1, source_target_pairs={{0,3},{1,2},{2,1},{3,0},{4,7},{5,6},{6,5},{7,4},{8,11},{9,10},{10,... | collective-permute-start | bytes 196616 | tf_op jit(solution)/shard_map/ppermute | solution.py:15
  5.5 0.5 %collective-permute-start.1 = (bf16[256,128]{1,0:T(8,128)(2,1)S(1)}, bf16[256,128]{1,0:T(8,128)(2,1)S(1)}, u32[]{:S(2)}, u32[]{:S(2)}) collective-permute-start(bf16[256,128]{1,0:T(8,128)(2,1)S(1)} %shard_map.78.refs_0_), channel_id=1, source_target_pairs={{0,2},{1,3},{2,0},{3,1},{4,6},{5,7},{6,4},{7,5},{8,10},{9,11},{10,... | collective-permute-start | bytes 196616 | tf_op jit(solution)/shard_map/ppermute | solution.py:15
  6.1 0.1 collective-permute-start
  6.9 3.0 %shard_map.77._.total = f32[48,256,128]{2,1,0:T(8,128)S(1)} custom-call(s32[1]{0:T(128)S(6)} %copy.8.live_ref, s32[192]{0:T(256)} %target_ref.1, s32[192]{0:T(256)} %source_ref.1, bf16[192,2,128,128]{3,2,1,0:T(8,128)(2,1)S(1)} %copy-done), custom_call_target="tpu_custom_call" | custom-call | flops 8589934592 | bytes 1048576 | tf_op jit(solution)/shard_map/pallas_call | solution.py:285
  9.9 0.0 collective-permute-done.1.refs_2_
  9.9 0.5 %collective-permute-done.refs_1_ = bf16[256,128]{1,0:T(8,128)(2,1)S(1)} collective-permute-done((bf16[256,128]{1,0:T(8,128)(2,1)S(1)}, bf16[256,128]{1,0:T(8,128)(2,1)S(1)}, u32[]{:S(2)}, u32[]{:S(2)}) %collective-permute-start) | collective-permute-done | bytes 65568 | tf_op jit(solution)/shard_map/ppermute | solution.py:15
  10.3 0.7 %collective-permute-start.4 = (bf16[512,128]{1,0:T(8,128)(2,1)S(1)}, bf16[512,128]{1,0:T(8,128)(2,1)S(1)}, u32[]{:S(2)}, u32[]{:S(2)}) collective-permute-start(bf16[512,128]{1,0:T(8,128)(2,1)S(1)} %shard_map.79._), channel_id=1, source_target_pairs={{0,0},{4,8},{8,4},{12,16},{16,12},{20,24},{24,20},{28,28},{1,1},{5... | collective-permute-start | bytes 393224 | tf_op jit(solution)/shard_map/ppermute | solution.py:21
  11.0 3.0 %collective-permute-start.3 = (bf16[512,128]{1,0:T(8,128)(2,1)S(1)}, bf16[512,128]{1,0:T(8,128)(2,1)S(1)}, u32[]{:S(2)}, u32[]{:S(2)}) collective-permute-start(bf16[512,128]{1,0:T(8,128)(2,1)S(1)} %shard_map.79._), channel_id=1, source_target_pairs={{0,4},{4,0},{8,12},{12,8},{16,20},{20,16},{24,28},{28,24},{1,5},{5... | collective-permute-start | bytes 393224 | tf_op jit(solution)/shard_map/ppermute | solution.py:21
  14.0 0.8 %shard_map.80 = (bf16[2,16,256,128]{3,2,1,0:T(8,128)(2,1)S(1)}, bf16[128,1024]{1,0:T(8,128)(2,1)S(1)}, s16[528,128]{1,0:T(8,128)(2,1)S(1)}) custom-call(bf16[512,128]{1,0:T(8,128)(2,1)S(1)} %shard_map.79._, f32[48,256,128]{2,1,0:T(8,128)S(1)} %shard_map.77._.total, bf16[256,128]{1,0:T(8,128)(2,1)S(1)} %shard_map.78.refs_0_, ...), custom_call_target="tpu_custom_call" | custom-call | flops 8589934592 | bytes 1048576 | tf_op jit(solution)/shard_map/pallas_call | solution.py:285
  14.8 0.7 %collective-permute-start.6 = (s16[528,128]{1,0:T(8,128)(2,1)S(1)}, s16[528,128]{1,0:T(8,128)(2,1)S(1)}, u32[]{:S(2)}, u32[]{:S(2)}) collective-permute-start(s16[528,128]{1,0:T(8,128)(2,1)S(1)} %get-tuple-element.17), channel_id=1, source_target_pairs={{0,0},{4,8},{8,4},{12,16},{16,12},{20,24},{24,20},{28,28},{1,1},{5... | collective-permute-start | bytes 405512 | tf_op jit(solution)/shard_map/ppermute | solution.py:21
  15.5 0.0 collective-permute-done.3._first.first_ref
  15.5 1.4 %shard_map.81 = (bf16[2,32,256,128]{3,2,1,0:T(8,128)(2,1)S(1)}, f32[4,128,128]{2,1,0:T(8,128)S(1)}, s16[528,128]{1,0:T(8,128)(2,1)S(1)}) custom-call(bf16[512,128]{1,0:T(8,128)(2,1)S(1)} %collective-permute-done.3._first.first_ref, bf16[512,128]{1,0:T(8,128)(2,1)S(1)} %collective-permute-done.4._second.second_ref, f32[48,256,128]{2,1,0:T(8,128)S(1)} %shard_map.77._.total, ...), custom_call_target="tpu_custom_call" | custom-call | flops 8589934592 | bytes 1048576 | tf_op jit(solution)/shard_map/pallas_call | solution.py:285
  16.9 3.1 %collective-permute-start.5 = (s16[528,128]{1,0:T(8,128)(2,1)S(1)}, s16[528,128]{1,0:T(8,128)(2,1)S(1)}, u32[]{:S(2)}, u32[]{:S(2)}) collective-permute-start(s16[528,128]{1,0:T(8,128)(2,1)S(1)} %get-tuple-element.16), channel_id=1, source_target_pairs={{0,4},{4,0},{8,12},{12,8},{16,20},{20,16},{24,28},{28,24},{1,5},{5... | collective-permute-start | bytes 405512 | tf_op jit(solution)/shard_map/ppermute | solution.py:21
  20.0 1.9 %shard_map.82.potential_ref = f32[4,128,128]{2,1,0:T(8,128)S(1)} custom-call(bf16[2,32,256,128]{3,2,1,0:T(8,128)(2,1)S(1)} %get-tuple-element.13.pairs_ref, bf16[2,16,256,128]{3,2,1,0:T(8,128)(2,1)S(1)} %get-tuple-element.14.second_pairs_ref, bf16[512,128]{1,0:T(8,128)(2,1)S(1)} %collective-permute-done.3._first.first_ref, ...), custom_call_target="tpu_custom_call" | custom-call | bytes 1048576 | tf_op jit(solution)/shard_map/pallas_call | solution.py:285
  21.9 0.0 collective-permute-done.5.first_ref
  21.9 0.2 shard_map.83
  22.1 2.8 %collective-permute-start.7 = (s16[272,128]{1,0:T(8,128)(2,1)S(1)}, s16[272,128]{1,0:T(8,128)(2,1)S(1)}, u32[]{:S(2)}, u32[]{:S(2)}) collective-permute-start(s16[272,128]{1,0:T(8,128)(2,1)S(1)} %get-tuple-element.19), channel_id=1, source_target_pairs={{0,3},{1,2},{2,1},{3,0},{4,7},{5,6},{6,5},{7,4},{8,11},{9,10},{10,... | collective-permute-start | bytes 208904 | tf_op jit(solution)/shard_map/ppermute | solution.py:15
  24.9 0.5 %collective-permute-start.8 = (s16[272,128]{1,0:T(8,128)(2,1)S(1)}, s16[272,128]{1,0:T(8,128)(2,1)S(1)}, u32[]{:S(2)}, u32[]{:S(2)}) collective-permute-start(s16[272,128]{1,0:T(8,128)(2,1)S(1)} %get-tuple-element.20), channel_id=1, source_target_pairs={{0,2},{1,3},{2,0},{3,1},{4,6},{5,7},{6,4},{7,5},{8,10},{9,11},{10,... | collective-permute-start | bytes 208904 | tf_op jit(solution)/shard_map/ppermute | solution.py:15
  25.4 0.3 collective-permute-start.9
  25.6 1.7 %collective-permute-done.7.refs_0_ = s16[272,128]{1,0:T(8,128)(2,1)S(1)} collective-permute-done((s16[272,128]{1,0:T(8,128)(2,1)S(1)}, s16[272,128]{1,0:T(8,128)(2,1)S(1)}, u32[]{:S(2)}, u32[]{:S(2)}) %collective-permute-start.7) | collective-permute-done | bytes 69664 | tf_op jit(solution)/shard_map/ppermute | solution.py:15
  27.4 1.8 %collective-permute-done.8.refs_1_ = s16[272,128]{1,0:T(8,128)(2,1)S(1)} collective-permute-done((s16[272,128]{1,0:T(8,128)(2,1)S(1)}, s16[272,128]{1,0:T(8,128)(2,1)S(1)}, u32[]{:S(2)}, u32[]{:S(2)}) %collective-permute-start.8) | collective-permute-done | bytes 69664 | tf_op jit(solution)/shard_map/ppermute | solution.py:15
  29.2 0.5 %collective-permute-done.9.refs_2_ = s16[272,128]{1,0:T(8,128)(2,1)S(1)} collective-permute-done((s16[272,128]{1,0:T(8,128)(2,1)S(1)}, s16[272,128]{1,0:T(8,128)(2,1)S(1)}, u32[]{:S(2)}, u32[]{:S(2)}) %collective-permute-start.9) | collective-permute-done | bytes 69664 | tf_op jit(solution)/shard_map/ppermute | solution.py:15
  29.7 0.7 %shard_map.84 = (f32[128,128]{1,0:T(8,128)}, f32[128,128]{1,0:T(8,128)}) custom-call(f32[256,128]{1,0:T(8,128)S(1)} %get-tuple-element.18.own_ref, s16[272,128]{1,0:T(8,128)(2,1)S(1)} %collective-permute-done.7.refs_0_, s16[272,128]{1,0:T(8,128)(2,1)S(1)} %collective-permute-done.8.refs_1_, s16[272,128]{1,0:T(8,128)(2,1)S(1)} %collective-permute-done.9.refs_2_), custom_call_target="tpu_custom_call" | custom-call | bytes 1048576 | tf_op jit(solution)/shard_map/pallas_call | solution.py:285
  (6 shorter events, 0.0 us)
Async XLA Ops:
  0.6 6.2 %copy-start = (bf16[192,2,128,128]{3,2,1,0:T(8,128)(2,1)S(1)}, bf16[192,2,128,128]{3,2,1,0:T(8,128)(2,1)}, u32[]{:S(2)}) copy-start(bf16[192,2,128,128]{3,2,1,0:T(8,128)(2,1)} %kernels_ref.1) | copy-start | bytes 37748740
  1.6 8.3 %collective-permute-start.2 = (bf16[256,128]{1,0:T(8,128)(2,1)S(1)}, bf16[256,128]{1,0:T(8,128)(2,1)S(1)}, u32[]{:S(2)}, u32[]{:S(2)}) collective-permute-start(bf16[256,128]{1,0:T(8,128)(2,1)S(1)} %shard_map.78.refs_0_), channel_id=1, source_target_pairs={{0,3},{1,2},{2,1},{3,0},{4,7},{5,6},{6,5},{7,4},{8,11},{9,10},{10,... | collective-permute-start | bytes 196616 | tf_op jit(solution)/shard_map/ppermute | solution.py:15
  5.5 4.3 %collective-permute-start.1 = (bf16[256,128]{1,0:T(8,128)(2,1)S(1)}, bf16[256,128]{1,0:T(8,128)(2,1)S(1)}, u32[]{:S(2)}, u32[]{:S(2)}) collective-permute-start(bf16[256,128]{1,0:T(8,128)(2,1)S(1)} %shard_map.78.refs_0_), channel_id=1, source_target_pairs={{0,2},{1,3},{2,0},{3,1},{4,6},{5,7},{6,4},{7,5},{8,10},{9,11},{10,... | collective-permute-start | bytes 196616 | tf_op jit(solution)/shard_map/ppermute | solution.py:15
  6.1 4.3 %collective-permute-start = (bf16[256,128]{1,0:T(8,128)(2,1)S(1)}, bf16[256,128]{1,0:T(8,128)(2,1)S(1)}, u32[]{:S(2)}, u32[]{:S(2)}) collective-permute-start(bf16[256,128]{1,0:T(8,128)(2,1)S(1)} %shard_map.78.refs_0_), channel_id=1, source_target_pairs={{0,1},{1,0},{2,3},{3,2},{4,5},{5,4},{6,7},{7,6},{8,9},{9,8},{10,11... | collective-permute-start | bytes 196616 | tf_op jit(solution)/shard_map/ppermute | solution.py:15
  10.3 5.2 %collective-permute-start.4 = (bf16[512,128]{1,0:T(8,128)(2,1)S(1)}, bf16[512,128]{1,0:T(8,128)(2,1)S(1)}, u32[]{:S(2)}, u32[]{:S(2)}) collective-permute-start(bf16[512,128]{1,0:T(8,128)(2,1)S(1)} %shard_map.79._), channel_id=1, source_target_pairs={{0,0},{4,8},{8,4},{12,16},{16,12},{20,24},{24,20},{28,28},{1,1},{5... | collective-permute-start | bytes 393224 | tf_op jit(solution)/shard_map/ppermute | solution.py:21
  11.0 4.5 %collective-permute-start.3 = (bf16[512,128]{1,0:T(8,128)(2,1)S(1)}, bf16[512,128]{1,0:T(8,128)(2,1)S(1)}, u32[]{:S(2)}, u32[]{:S(2)}) collective-permute-start(bf16[512,128]{1,0:T(8,128)(2,1)S(1)} %shard_map.79._), channel_id=1, source_target_pairs={{0,4},{4,0},{8,12},{12,8},{16,20},{20,16},{24,28},{28,24},{1,5},{5... | collective-permute-start | bytes 393224 | tf_op jit(solution)/shard_map/ppermute | solution.py:21
  14.8 7.0 %collective-permute-start.6 = (s16[528,128]{1,0:T(8,128)(2,1)S(1)}, s16[528,128]{1,0:T(8,128)(2,1)S(1)}, u32[]{:S(2)}, u32[]{:S(2)}) collective-permute-start(s16[528,128]{1,0:T(8,128)(2,1)S(1)} %get-tuple-element.17), channel_id=1, source_target_pairs={{0,0},{4,8},{8,4},{12,16},{16,12},{20,24},{24,20},{28,28},{1,1},{5... | collective-permute-start | bytes 405512 | tf_op jit(solution)/shard_map/ppermute | solution.py:21
  16.9 5.0 %collective-permute-start.5 = (s16[528,128]{1,0:T(8,128)(2,1)S(1)}, s16[528,128]{1,0:T(8,128)(2,1)S(1)}, u32[]{:S(2)}, u32[]{:S(2)}) collective-permute-start(s16[528,128]{1,0:T(8,128)(2,1)S(1)} %get-tuple-element.16), channel_id=1, source_target_pairs={{0,4},{4,0},{8,12},{12,8},{16,20},{20,16},{24,28},{28,24},{1,5},{5... | collective-permute-start | bytes 405512 | tf_op jit(solution)/shard_map/ppermute | solution.py:21
  22.1 5.3 %collective-permute-start.7 = (s16[272,128]{1,0:T(8,128)(2,1)S(1)}, s16[272,128]{1,0:T(8,128)(2,1)S(1)}, u32[]{:S(2)}, u32[]{:S(2)}) collective-permute-start(s16[272,128]{1,0:T(8,128)(2,1)S(1)} %get-tuple-element.19), channel_id=1, source_target_pairs={{0,3},{1,2},{2,1},{3,0},{4,7},{5,6},{6,5},{7,4},{8,11},{9,10},{10,... | collective-permute-start | bytes 208904 | tf_op jit(solution)/shard_map/ppermute | solution.py:15
  24.9 4.3 %collective-permute-start.8 = (s16[272,128]{1,0:T(8,128)(2,1)S(1)}, s16[272,128]{1,0:T(8,128)(2,1)S(1)}, u32[]{:S(2)}, u32[]{:S(2)}) collective-permute-start(s16[272,128]{1,0:T(8,128)(2,1)S(1)} %get-tuple-element.20), channel_id=1, source_target_pairs={{0,2},{1,3},{2,0},{3,1},{4,6},{5,7},{6,4},{7,5},{8,10},{9,11},{10,... | collective-permute-start | bytes 208904 | tf_op jit(solution)/shard_map/ppermute | solution.py:15
  25.4 4.3 %collective-permute-start.9 = (s16[272,128]{1,0:T(8,128)(2,1)S(1)}, s16[272,128]{1,0:T(8,128)(2,1)S(1)}, u32[]{:S(2)}, u32[]{:S(2)}) collective-permute-start(s16[272,128]{1,0:T(8,128)(2,1)S(1)} %get-tuple-element.21), channel_id=1, source_target_pairs={{0,1},{1,0},{2,3},{3,2},{4,5},{5,4},{6,7},{7,6},{8,9},{9,8},{10,11... | collective-permute-start | bytes 208904 | tf_op jit(solution)/shard_map/ppermute | solution.py:15

commit v10 on v9

--- a/solution.py
+++ b/solution.py
@@ -183,7 +183,7 @@
     encode(list(adjoint_of(pairs_ref, across_ref, 0, count)), out_ref)
 
 
-def first_kernel(count, _first, _second, total, across_ref, pairs_ref, middle_ref, out_ref):
+def first_kernel(count, _second, _first, total, across_ref, pairs_ref, middle_ref, out_ref):
     split(total, 0, pairs_ref)
     encode(list(adjoint_of(pairs_ref, across_ref, 0, count)), out_ref)
     for i, value in enumerate(adjoint_of(pairs_ref, across_ref, count, count)):
@@ -328,7 +328,7 @@
             flops=1 << 33,
         )
         own = group_strengths(total)
-        second, first = exchange_beside(own, 1), exchange_beside(own, 0)
+        first, second = exchange_beside(own, 0), exchange_beside(own, 1)
         total = pltpu.with_memory_space_constraint(total, pltpu.VMEM)
         second_pairs = pairs // 3
         kept_second, across, upper = call(
@@ -345,7 +345,7 @@
         kept, middle, lower = call(
             functools.partial(first_kernel, group_blocks),
             (pltpu.VMEM((2, pairs - second_pairs, 2 * panels, panels), bf16), block_sums, coded(group_blocks)),
-            (first, second, total, across),
+            (second, first, total, across),
             [in_hbm] * 2 + [in_vmem] * 2,
             flops=1 << 33,
         )

time: 30.3 us -> 29.4 us (0.970); the launches traced: 30.4 us -> 29 us
  starting transfers between devices: 15.6 us -> 14.3 us
  Pallas kernels: 8.91 us -> 8.04 us
  waiting for transfers between devices: 4.5 us -> 5.18 us
    ppermute x4, starting transfers between devices: 7.43 us -> 6.19 us  [exchange_beside(): lax.ppermute(value, 'grp', [(i, j if 0 <= j < groups else i) for i, j in...]
    pallas_call x8, Pallas kernels: 8.91 us -> 8.04 us  [call(): pl.pallas_call(body, out_shape=shapes, in_specs=specs or [in_vmem] * len(...]
    ppermute x6, waiting for transfers between devices: 4.49 us -> 5.17 us  [exchange(): lax.ppermute(value, axis, [(i, i ^ step) for i in range(lax.axis_size(axi...]
  transfers between devices with their start and end apart: 10 -> 10, of which waited for: 4 -> 4; matrix products, arithmetic and copies ran while one was open for 0% -> 0% of each run, Pallas kernels for 23% -> 21%
where the time goes in v10:
time: 29.4 us; the launch traced here: 29 us
  starting transfers between devices  14.3 us (49%)
  Pallas kernels  8.04 us (27%)
  waiting for transfers between devices  5.18 us (18%)
  between operations  1.41 us (5%)
    ppermute x6, starting transfers between devices, exchange(): lax.ppermute(value, axis, [(i, i ^ step) for i in range(lax.axis_size(axi...  8.16 us
    pallas_call x8, Pallas kernels, call(): pl.pallas_call(body, out_shape=shapes, in_specs=specs or [in_vmem] * len(...  8.04 us
    ppermute x4, starting transfers between devices, exchange_beside(): lax.ppermute(value, 'grp', [(i, j if 0 <= j < groups else i) for i, j in...  6.19 us
    ppermute x6, waiting for transfers between devices, exchange(): lax.ppermute(value, axis, [(i, i ^ step) for i in range(lax.axis_size(axi...  5.17 us
  transfers between devices with their start and end apart: 10, of which 4 were waited for; matrix products, arithmetic and copies ran while one was open for 0% of the time, Pallas kernels for 21%

profile of v10, /device:TPU:0, one launch (start us, length us, event | category | flops | bytes accessed | tf_op | source)
XLA Modules:
  0.0 29.0 jit_solution(13454646892538799561)
XLA Ops:
  0.6 0.9 %shard_map.78.refs_0_ = bf16[256,128]{1,0:T(8,128)(2,1)S(1)} custom-call(bf16[128,128]{1,0:T(8,128)(2,1)} %strengths_ref.1, bf16[128,128]{1,0:T(8,128)(2,1)} %weights_ref.1), custom_call_target="tpu_custom_call" | custom-call | flops 17179869184 | bytes 1048576 | tf_op jit(solution)/shard_map/pallas_call | solution.py:285
  1.6 4.0 %collective-permute-start.2 = (bf16[256,128]{1,0:T(8,128)(2,1)S(1)}, bf16[256,128]{1,0:T(8,128)(2,1)S(1)}, u32[]{:S(2)}, u32[]{:S(2)}) collective-permute-start(bf16[256,128]{1,0:T(8,128)(2,1)S(1)} %shard_map.78.refs_0_), channel_id=1, source_target_pairs={{0,3},{1,2},{2,1},{3,0},{4,7},{5,6},{6,5},{7,4},{8,11},{9,10},{10,... | collective-permute-start | bytes 196616 | tf_op jit(solution)/shard_map/ppermute | solution.py:15
  5.5 0.5 %collective-permute-start.1 = (bf16[256,128]{1,0:T(8,128)(2,1)S(1)}, bf16[256,128]{1,0:T(8,128)(2,1)S(1)}, u32[]{:S(2)}, u32[]{:S(2)}) collective-permute-start(bf16[256,128]{1,0:T(8,128)(2,1)S(1)} %shard_map.78.refs_0_), channel_id=1, source_target_pairs={{0,2},{1,3},{2,0},{3,1},{4,6},{5,7},{6,4},{7,5},{8,10},{9,11},{10,... | collective-permute-start | bytes 196616 | tf_op jit(solution)/shard_map/ppermute | solution.py:15
  6.1 0.1 collective-permute-start
  6.9 2.1 %shard_map.77._.total = f32[48,256,128]{2,1,0:T(8,128)S(1)} custom-call(s32[1]{0:T(128)S(6)} %copy.8.live_ref, s32[192]{0:T(256)} %target_ref.1, s32[192]{0:T(256)} %source_ref.1, bf16[192,2,128,128]{3,2,1,0:T(8,128)(2,1)S(1)} %copy-done), custom_call_target="tpu_custom_call" | custom-call | flops 8589934592 | bytes 1048576 | tf_op jit(solution)/shard_map/pallas_call | solution.py:285
  9.0 0.8 %collective-permute-done.1.refs_2_ = bf16[256,128]{1,0:T(8,128)(2,1)S(1)} collective-permute-done((bf16[256,128]{1,0:T(8,128)(2,1)S(1)}, bf16[256,128]{1,0:T(8,128)(2,1)S(1)}, u32[]{:S(2)}, u32[]{:S(2)}) %collective-permute-start.1) | collective-permute-done | bytes 65568 | tf_op jit(solution)/shard_map/ppermute | solution.py:15
  9.8 0.5 %collective-permute-done.refs_1_ = bf16[256,128]{1,0:T(8,128)(2,1)S(1)} collective-permute-done((bf16[256,128]{1,0:T(8,128)(2,1)S(1)}, bf16[256,128]{1,0:T(8,128)(2,1)S(1)}, u32[]{:S(2)}, u32[]{:S(2)}) %collective-permute-start) | collective-permute-done | bytes 65568 | tf_op jit(solution)/shard_map/ppermute | solution.py:15
  10.3 0.1 collective-permute-start.4
  10.4 0.7 %collective-permute-start.3 = (bf16[512,128]{1,0:T(8,128)(2,1)S(1)}, bf16[512,128]{1,0:T(8,128)(2,1)S(1)}, u32[]{:S(2)}, u32[]{:S(2)}) collective-permute-start(bf16[512,128]{1,0:T(8,128)(2,1)S(1)} %shard_map.79._), channel_id=1, source_target_pairs={{0,0},{4,8},{8,4},{12,16},{16,12},{20,24},{24,20},{28,28},{1,1},{5... | collective-permute-start | bytes 393224 | tf_op jit(solution)/shard_map/ppermute | solution.py:21
  11.1 0.8 %shard_map.80 = (bf16[2,16,256,128]{3,2,1,0:T(8,128)(2,1)S(1)}, bf16[128,1024]{1,0:T(8,128)(2,1)S(1)}, s16[528,128]{1,0:T(8,128)(2,1)S(1)}) custom-call(bf16[512,128]{1,0:T(8,128)(2,1)S(1)} %shard_map.79._, f32[48,256,128]{2,1,0:T(8,128)S(1)} %shard_map.77._.total, bf16[256,128]{1,0:T(8,128)(2,1)S(1)} %shard_map.78.refs_0_, ...), custom_call_target="tpu_custom_call" | custom-call | flops 8589934592 | bytes 1048576 | tf_op jit(solution)/shard_map/pallas_call | solution.py:285
  11.9 0.7 %collective-permute-start.6 = (s16[528,128]{1,0:T(8,128)(2,1)S(1)}, s16[528,128]{1,0:T(8,128)(2,1)S(1)}, u32[]{:S(2)}, u32[]{:S(2)}) collective-permute-start(s16[528,128]{1,0:T(8,128)(2,1)S(1)} %get-tuple-element.17), channel_id=1, source_target_pairs={{0,0},{4,8},{8,4},{12,16},{16,12},{20,24},{24,20},{28,28},{1,1},{5... | collective-permute-start | bytes 405512 | tf_op jit(solution)/shard_map/ppermute | solution.py:21
  12.6 0.0 collective-permute-done.3._second.second_ref
  12.6 1.4 %shard_map.81 = (bf16[2,32,256,128]{3,2,1,0:T(8,128)(2,1)S(1)}, f32[4,128,128]{2,1,0:T(8,128)S(1)}, s16[528,128]{1,0:T(8,128)(2,1)S(1)}) custom-call(bf16[512,128]{1,0:T(8,128)(2,1)S(1)} %collective-permute-done.3._second.second_ref, bf16[512,128]{1,0:T(8,128)(2,1)S(1)} %collective-permute-done.4._first.first_ref, f32[48,256,128]{2,1,0:T(8,128)S(1)} %shard_map.77._.total, ...), custom_call_target="tpu_custom_call" | custom-call | flops 8589934592 | bytes 1048576 | tf_op jit(solution)/shard_map/pallas_call | solution.py:285
  14.0 4.8 %collective-permute-start.5 = (s16[528,128]{1,0:T(8,128)(2,1)S(1)}, s16[528,128]{1,0:T(8,128)(2,1)S(1)}, u32[]{:S(2)}, u32[]{:S(2)}) collective-permute-start(s16[528,128]{1,0:T(8,128)(2,1)S(1)} %get-tuple-element.16), channel_id=1, source_target_pairs={{0,4},{4,0},{8,12},{12,8},{16,20},{20,16},{24,28},{28,24},{1,5},{5... | collective-permute-start | bytes 405512 | tf_op jit(solution)/shard_map/ppermute | solution.py:21
  18.8 1.9 %shard_map.82.potential_ref = f32[4,128,128]{2,1,0:T(8,128)S(1)} custom-call(bf16[2,32,256,128]{3,2,1,0:T(8,128)(2,1)S(1)} %get-tuple-element.13.pairs_ref, bf16[2,16,256,128]{3,2,1,0:T(8,128)(2,1)S(1)} %get-tuple-element.14.second_pairs_ref, bf16[512,128]{1,0:T(8,128)(2,1)S(1)} %collective-permute-done.4._first.first_ref, ...), custom_call_target="tpu_custom_call" | custom-call | bytes 1048576 | tf_op jit(solution)/shard_map/pallas_call | solution.py:285
  20.7 0.0 collective-permute-done.6.second_ref
  20.7 0.0 collective-permute-done.5.first_ref
  20.7 0.2 shard_map.83
  20.9 2.0 %collective-permute-start.7 = (s16[272,128]{1,0:T(8,128)(2,1)S(1)}, s16[272,128]{1,0:T(8,128)(2,1)S(1)}, u32[]{:S(2)}, u32[]{:S(2)}) collective-permute-start(s16[272,128]{1,0:T(8,128)(2,1)S(1)} %get-tuple-element.19), channel_id=1, source_target_pairs={{0,3},{1,2},{2,1},{3,0},{4,7},{5,6},{6,5},{7,4},{8,11},{9,10},{10,... | collective-permute-start | bytes 208904 | tf_op jit(solution)/shard_map/ppermute | solution.py:15
  22.8 0.8 %collective-permute-start.8 = (s16[272,128]{1,0:T(8,128)(2,1)S(1)}, s16[272,128]{1,0:T(8,128)(2,1)S(1)}, u32[]{:S(2)}, u32[]{:S(2)}) collective-permute-start(s16[272,128]{1,0:T(8,128)(2,1)S(1)} %get-tuple-element.20), channel_id=1, source_target_pairs={{0,2},{1,3},{2,0},{3,1},{4,6},{5,7},{6,4},{7,5},{8,10},{9,11},{10,... | collective-permute-start | bytes 208904 | tf_op jit(solution)/shard_map/ppermute | solution.py:15
  23.6 0.8 %collective-permute-start.9 = (s16[272,128]{1,0:T(8,128)(2,1)S(1)}, s16[272,128]{1,0:T(8,128)(2,1)S(1)}, u32[]{:S(2)}, u32[]{:S(2)}) collective-permute-start(s16[272,128]{1,0:T(8,128)(2,1)S(1)} %get-tuple-element.21), channel_id=1, source_target_pairs={{0,1},{1,0},{2,3},{3,2},{4,5},{5,4},{6,7},{7,6},{8,9},{9,8},{10,11... | collective-permute-start | bytes 208904 | tf_op jit(solution)/shard_map/ppermute | solution.py:15
  24.4 2.4 %collective-permute-done.7.refs_0_ = s16[272,128]{1,0:T(8,128)(2,1)S(1)} collective-permute-done((s16[272,128]{1,0:T(8,128)(2,1)S(1)}, s16[272,128]{1,0:T(8,128)(2,1)S(1)}, u32[]{:S(2)}, u32[]{:S(2)}) %collective-permute-start.7) | collective-permute-done | bytes 69664 | tf_op jit(solution)/shard_map/ppermute | solution.py:15
  26.8 1.4 %collective-permute-done.8.refs_1_ = s16[272,128]{1,0:T(8,128)(2,1)S(1)} collective-permute-done((s16[272,128]{1,0:T(8,128)(2,1)S(1)}, s16[272,128]{1,0:T(8,128)(2,1)S(1)}, u32[]{:S(2)}, u32[]{:S(2)}) %collective-permute-start.8) | collective-permute-done | bytes 69664 | tf_op jit(solution)/shard_map/ppermute | solution.py:15
  28.2 0.7 %shard_map.84 = (f32[128,128]{1,0:T(8,128)}, f32[128,128]{1,0:T(8,128)}) custom-call(f32[256,128]{1,0:T(8,128)S(1)} %get-tuple-element.18.own_ref, s16[272,128]{1,0:T(8,128)(2,1)S(1)} %collective-permute-done.7.refs_0_, s16[272,128]{1,0:T(8,128)(2,1)S(1)} %collective-permute-done.8.refs_1_, s16[272,128]{1,0:T(8,128)(2,1)S(1)} %collective-permute-done.9.refs_2_), custom_call_target="tpu_custom_call" | custom-call | bytes 1048576 | tf_op jit(solution)/shard_map/pallas_call | solution.py:285
  (6 shorter events, 0.0 us)
Async XLA Ops:
  0.6 6.2 %copy-start = (bf16[192,2,128,128]{3,2,1,0:T(8,128)(2,1)S(1)}, bf16[192,2,128,128]{3,2,1,0:T(8,128)(2,1)}, u32[]{:S(2)}) copy-start(bf16[192,2,128,128]{3,2,1,0:T(8,128)(2,1)} %kernels_ref.1) | copy-start | bytes 37748740
  1.6 7.4 %collective-permute-start.2 = (bf16[256,128]{1,0:T(8,128)(2,1)S(1)}, bf16[256,128]{1,0:T(8,128)(2,1)S(1)}, u32[]{:S(2)}, u32[]{:S(2)}) collective-permute-start(bf16[256,128]{1,0:T(8,128)(2,1)S(1)} %shard_map.78.refs_0_), channel_id=1, source_target_pairs={{0,3},{1,2},{2,1},{3,0},{4,7},{5,6},{6,5},{7,4},{8,11},{9,10},{10,... | collective-permute-start | bytes 196616 | tf_op jit(solution)/shard_map/ppermute | solution.py:15
  5.5 4.3 %collective-permute-start.1 = (bf16[256,128]{1,0:T(8,128)(2,1)S(1)}, bf16[256,128]{1,0:T(8,128)(2,1)S(1)}, u32[]{:S(2)}, u32[]{:S(2)}) collective-permute-start(bf16[256,128]{1,0:T(8,128)(2,1)S(1)} %shard_map.78.refs_0_), channel_id=1, source_target_pairs={{0,2},{1,3},{2,0},{3,1},{4,6},{5,7},{6,4},{7,5},{8,10},{9,11},{10,... | collective-permute-start | bytes 196616 | tf_op jit(solution)/shard_map/ppermute | solution.py:15
  6.1 4.3 %collective-permute-start = (bf16[256,128]{1,0:T(8,128)(2,1)S(1)}, bf16[256,128]{1,0:T(8,128)(2,1)S(1)}, u32[]{:S(2)}, u32[]{:S(2)}) collective-permute-start(bf16[256,128]{1,0:T(8,128)(2,1)S(1)} %shard_map.78.refs_0_), channel_id=1, source_target_pairs={{0,1},{1,0},{2,3},{3,2},{4,5},{5,4},{6,7},{7,6},{8,9},{9,8},{10,11... | collective-permute-start | bytes 196616 | tf_op jit(solution)/shard_map/ppermute | solution.py:15
  10.3 2.3 %collective-permute-start.4 = (bf16[512,128]{1,0:T(8,128)(2,1)S(1)}, bf16[512,128]{1,0:T(8,128)(2,1)S(1)}, u32[]{:S(2)}, u32[]{:S(2)}) collective-permute-start(bf16[512,128]{1,0:T(8,128)(2,1)S(1)} %shard_map.79._), channel_id=1, source_target_pairs={{0,4},{4,0},{8,12},{12,8},{16,20},{20,16},{24,28},{28,24},{1,5},{5... | collective-permute-start | bytes 393224 | tf_op jit(solution)/shard_map/ppermute | solution.py:21
  10.4 2.2 %collective-permute-start.3 = (bf16[512,128]{1,0:T(8,128)(2,1)S(1)}, bf16[512,128]{1,0:T(8,128)(2,1)S(1)}, u32[]{:S(2)}, u32[]{:S(2)}) collective-permute-start(bf16[512,128]{1,0:T(8,128)(2,1)S(1)} %shard_map.79._), channel_id=1, source_target_pairs={{0,0},{4,8},{8,4},{12,16},{16,12},{20,24},{24,20},{28,28},{1,1},{5... | collective-permute-start | bytes 393224 | tf_op jit(solution)/shard_map/ppermute | solution.py:21
  11.9 8.7 %collective-permute-start.6 = (s16[528,128]{1,0:T(8,128)(2,1)S(1)}, s16[528,128]{1,0:T(8,128)(2,1)S(1)}, u32[]{:S(2)}, u32[]{:S(2)}) collective-permute-start(s16[528,128]{1,0:T(8,128)(2,1)S(1)} %get-tuple-element.17), channel_id=1, source_target_pairs={{0,0},{4,8},{8,4},{12,16},{16,12},{20,24},{24,20},{28,28},{1,1},{5... | collective-permute-start | bytes 405512 | tf_op jit(solution)/shard_map/ppermute | solution.py:21
  14.0 6.7 %collective-permute-start.5 = (s16[528,128]{1,0:T(8,128)(2,1)S(1)}, s16[528,128]{1,0:T(8,128)(2,1)S(1)}, u32[]{:S(2)}, u32[]{:S(2)}) collective-permute-start(s16[528,128]{1,0:T(8,128)(2,1)S(1)} %get-tuple-element.16), channel_id=1, source_target_pairs={{0,4},{4,0},{8,12},{12,8},{16,20},{20,16},{24,28},{28,24},{1,5},{5... | collective-permute-start | bytes 405512 | tf_op jit(solution)/shard_map/ppermute | solution.py:21
  20.9 6.0 %collective-permute-start.7 = (s16[272,128]{1,0:T(8,128)(2,1)S(1)}, s16[272,128]{1,0:T(8,128)(2,1)S(1)}, u32[]{:S(2)}, u32[]{:S(2)}) collective-permute-start(s16[272,128]{1,0:T(8,128)(2,1)S(1)} %get-tuple-element.19), channel_id=1, source_target_pairs={{0,3},{1,2},{2,1},{3,0},{4,7},{5,6},{6,5},{7,4},{8,11},{9,10},{10,... | collective-permute-start | bytes 208904 | tf_op jit(solution)/shard_map/ppermute | solution.py:15
  22.8 5.4 %collective-permute-start.8 = (s16[272,128]{1,0:T(8,128)(2,1)S(1)}, s16[272,128]{1,0:T(8,128)(2,1)S(1)}, u32[]{:S(2)}, u32[]{:S(2)}) collective-permute-start(s16[272,128]{1,0:T(8,128)(2,1)S(1)} %get-tuple-element.20), channel_id=1, source_target_pairs={{0,2},{1,3},{2,0},{3,1},{4,6},{5,7},{6,4},{7,5},{8,10},{9,11},{10,... | collective-permute-start | bytes 208904 | tf_op jit(solution)/shard_map/ppermute | solution.py:15
  23.6 4.6 %collective-permute-start.9 = (s16[272,128]{1,0:T(8,128)(2,1)S(1)}, s16[272,128]{1,0:T(8,128)(2,1)S(1)}, u32[]{:S(2)}, u32[]{:S(2)}) collective-permute-start(s16[272,128]{1,0:T(8,128)(2,1)S(1)} %get-tuple-element.21), channel_id=1, source_target_pairs={{0,1},{1,0},{2,3},{3,2},{4,5},{5,4},{6,7},{7,6},{8,9},{9,8},{10,11... | collective-permute-start | bytes 208904 | tf_op jit(solution)/shard_map/ppermute | solution.py:15

commit v11 on v10

--- a/solution.py
+++ b/solution.py
@@ -180,43 +180,66 @@
     split(total, total.shape[0] - pairs_ref.shape[1], pairs_ref)
     for i, block in enumerate(part_of(gathered, blocks, panels, 1)):
         across_ref[:, 2 * i * panels : 2 * (i + 1) * panels] = crossed(block)
-    encode(list(adjoint_of(pairs_ref, across_ref, 0, count)), out_ref)
-
-
-def first_kernel(count, _second, _first, total, across_ref, pairs_ref, middle_ref, out_ref):
+    strengths = [block.astype(jnp.float32) for block in part_of(gathered, blocks, panels, 0)]
+    encode(strengths + list(adjoint_of(pairs_ref, across_ref, 0, count)), out_ref)
+
+
+def first_kernel(count, _, total, across_ref, pairs_ref, middle_ref, out_ref):
     split(total, 0, pairs_ref)
     encode(list(adjoint_of(pairs_ref, across_ref, 0, count)), out_ref)
     for i, value in enumerate(adjoint_of(pairs_ref, across_ref, count, count)):
         middle_ref[i] = value
 
 
-def forward_kernel(blocks, pairs_ref, second_pairs_ref, first_ref, second_ref, *refs):
-    *gathered, potential_ref = refs
-    targets, panels = potential_ref.shape[:2]
-    stack = jnp.concatenate([stacked(x) for x in strengths_of(first_ref, gathered, second_ref, blocks, panels)], axis=0)
+def forward_of(pairs_ref, strengths, targets):
+    panels = pairs_ref.shape[2] // 2
+    stack = jnp.concatenate([stacked(x) for x in strengths], axis=0)
     for t in range(targets):
         halves = []
         for h in range(2):
             tiles = []
-            for ref in (pairs_ref, second_pairs_ref):
-                for pair in range(t, ref.shape[1], targets):
-                    tiles += [ref[h, pair, :panels], ref[h, pair, panels:]]
+            for pair in range(t, pairs_ref.shape[1], targets):
+                tiles += [pairs_ref[h, pair, :panels], pairs_ref[h, pair, panels:]]
             halves.append(jnp.concatenate(tiles, axis=1))
         product = jnp.dot(jnp.concatenate(halves, axis=0), stack, preferred_element_type=jnp.float32)
-        potential_ref[t] = product[:panels] + product[panels:]
-
-
-def parts_kernel(blocks, potential_ref, middle_ref, first_ref, second_ref, own_ref, *outs):
-    count, panels = potential_ref.shape[:2]
-    potential = [potential_ref[i] for i in range(count)]
-    others = zip(decode(first_ref, count, panels), decode(second_ref, count, panels))
-    adjoint = [middle_ref[i] + first + second for i, (first, second) in enumerate(others)]
+        yield product[:panels] + product[panels:]
+
+
+def forward_kernel(blocks, pairs_ref, first_ref, *refs):
+    *gathered, potential_ref = refs
+    targets, panels = potential_ref.shape[:2]
+    strengths = [first_ref[rows_of(i, panels)] for i in range(targets)]
+    strengths += part_of(gathered, blocks, panels, 0)
+    for t, value in enumerate(forward_of(pairs_ref, strengths, targets)):
+        potential_ref[t] = value
+
+
+def parts_of(blocks, potential, adjoint, own_ref, *outs):
+    panels = potential[0].shape[0]
     for i in range(blocks):
         own_ref[rows_of(i, panels)] = potential[i]
         own_ref[rows_of(blocks + i, panels)] = adjoint[i]
     for k, out_ref in enumerate(outs, 1):
         rows = slice(k * blocks, (k + 1) * blocks)
         encode(potential[rows] + adjoint[rows], out_ref)
+
+
+def parts_kernel(blocks, pairs_ref, potential_ref, middle_ref, first_ref, second_ref, *outs):
+    count, panels = potential_ref.shape[:2]
+    received = list(decode(second_ref, 2 * count, panels))
+    strengths = [block.astype(jnp.bfloat16) for block in received[:count]]
+    forward = forward_of(pairs_ref, strengths, count)
+    potential = [potential_ref[i] + value for i, value in enumerate(forward)]
+    others = zip(decode(first_ref, count, panels), received[count:])
+    adjoint = [middle_ref[i] + first + second for i, (first, second) in enumerate(others)]
+    parts_of(blocks, potential, adjoint, *outs)
+
+
+def slots_parts_kernel(blocks, potential_ref, adjoint_ref, first_ref, second_ref, *outs):
+    count, panels = potential_ref.shape[:2]
+    others = zip(decode(first_ref, count, panels), decode(second_ref, count, panels))
+    adjoint = [adjoint_ref[count + i] + first + second for i, (first, second) in enumerate(others)]
+    parts_of(blocks, [potential_ref[i] for i in range(count)], adjoint, *outs)
 
 
 def slots_kernel(blocks, panels, chunk, *refs):
@@ -251,9 +274,10 @@
     each_slot(chunk, live_ref, id_refs, ids, id_sems, prepare, lambda c: fetch(c).wait(), work)
 
 
-def code_kernel(*refs):
-    for ref, out_ref in zip(refs[:2], refs[2:]):
-        encode([ref[i] for i in range(ref.shape[0])], out_ref)
+def code_kernel(adjoint_ref, *outs):
+    count = adjoint_ref.shape[0] // 3
+    for first, out_ref in zip((0, 2 * count), outs):
+        encode([adjoint_ref[first + i] for i in range(count)], out_ref)
 
 
 def finish_kernel(blocks, panels, own_ref, *refs):
@@ -328,7 +352,7 @@
             flops=1 << 33,
         )
         own = group_strengths(total)
-        first, second = exchange_beside(own, 0), exchange_beside(own, 1)
+        first = exchange_beside(own, 0)
         total = pltpu.with_memory_space_constraint(total, pltpu.VMEM)
         second_pairs = pairs // 3
         kept_second, across, upper = call(
@@ -336,7 +360,7 @@
             (
                 pltpu.VMEM((2, second_pairs, 2 * panels, panels), bf16),
                 shape(width, 2 * group_blocks * panels, kind=bf16),
-                coded(group_blocks),
+                coded(2 * group_blocks),
             ),
             (own, total, *gathered),
             [in_hbm] + [in_vmem] * (1 + clusters),
@@ -345,16 +369,14 @@
         kept, middle, lower = call(
             functools.partial(first_kernel, group_blocks),
             (pltpu.VMEM((2, pairs - second_pairs, 2 * panels, panels), bf16), block_sums, coded(group_blocks)),
-            (second, first, total, across),
-            [in_hbm] * 2 + [in_vmem] * 2,
+            (first, total, across),
+            [in_hbm] + [in_vmem] * 2,
             flops=1 << 33,
         )
         kept, kept_second = (pltpu.with_memory_space_constraint(x, pltpu.VMEM) for x in (kept, kept_second))
-        potential = call(
-            functools.partial(forward_kernel, blocks),
-            block_sums,
-            (kept, kept_second, first, second, *gathered),
-        )
+        potential = call(functools.partial(forward_kernel, blocks), block_sums, (kept, first, *gathered))
+        upper, lower = exchange_beside(upper, 1), exchange_beside(lower, 0)
+        parts_body, parts_args = parts_kernel, (kept_second, potential, middle, lower, upper)
     else:
         own = group_strengths(mine)
         first, second = exchange_beside(own, 0), exchange_beside(own, 1)
@@ -372,13 +394,13 @@
             ],
             mib=40,
         )
-        lower, middle, upper = (adjoint[i * group_blocks : (i + 1) * group_blocks] for i in range(3))
-        lower, upper = call(code_kernel, (coded(group_blocks),) * 2, (lower, upper))
-    upper, lower = exchange_beside(upper, 1), exchange_beside(lower, 0)
+        lower, upper = call(code_kernel, (coded(group_blocks),) * 2, (adjoint,))
+        upper, lower = exchange_beside(upper, 1), exchange_beside(lower, 0)
+        parts_body, parts_args = slots_parts_kernel, (potential, adjoint, lower, upper)
     mine, *parts = call(
-        functools.partial(parts_kernel, blocks),
+        functools.partial(parts_body, blocks),
         (shape(2 * blocks * panels, width),) + (coded(2 * blocks),) * (clusters - 1),
-        (potential, middle, lower, upper),
+        parts_args,
     )
     parts = [exchange(parts[k - 1], "clu", k) for k in range(clusters - 1, 0, -1)]
     out = shape(blocks * panels, width)

time: 29.4 us -> 27.5 us (0.935)
  starting transfers between devices: 14.3 us -> 12.3 us
  Pallas kernels: 8.04 us -> 8.79 us
  waiting for transfers between devices: 5.18 us -> 4.55 us
    ppermute x4 -> x3, starting transfers between devices: 6.19 us -> 3.74 us  [exchange_beside(): lax.ppermute(value, 'grp', [(i, j if 0 <= j < groups else i) for i, j in...]
    pallas_call x8, Pallas kernels: 8.04 us -> 8.79 us  [call(): pl.pallas_call(body, out_shape=shapes, in_specs=specs or [in_vmem] * len(...]
    ppermute x6, waiting for transfers between devices: 5.17 us -> 4.54 us  [exchange(): lax.ppermute(value, axis, [(i, i ^ step) for i in range(lax.axis_size(axi...]
    ppermute x6, starting transfers between devices: 8.16 us -> 8.58 us  [exchange(): lax.ppermute(value, axis, [(i, i ^ step) for i in range(lax.axis_size(axi...]
  transfers between devices with their start and end apart: 10 -> 9, of which waited for: 4 -> 5; matrix products, arithmetic and copies ran while one was open for 0% -> 0% of each run, Pallas kernels for 21% -> 23%
where the time goes in v11:
time: 27.5 us; the launch traced here: 27.1 us
  starting transfers between devices  12.3 us (45%)
  Pallas kernels  8.79 us (32%)
  waiting for transfers between devices  4.55 us (17%)
  between operations  1.4 us (5%)
    pallas_call x8, Pallas kernels, call(): pl.pallas_call(body, out_shape=shapes, in_specs=specs or [in_vmem] * len(...  8.79 us
    ppermute x6, starting transfers between devices, exchange(): lax.ppermute(value, axis, [(i, i ^ step) for i in range(lax.axis_size(axi...  8.58 us
    ppermute x6, waiting for transfers between devices, exchange(): lax.ppermute(value, axis, [(i, i ^ step) for i in range(lax.axis_size(axi...  4.54 us
    ppermute x3, starting transfers between devices, exchange_beside(): lax.ppermute(value, 'grp', [(i, j if 0 <= j < groups else i) for i, j in...  3.74 us
  transfers between devices with their start and end apart: 9, of which 5 were waited for; matrix products, arithmetic and copies ran while one was open for 0% of the time, Pallas kernels for 23%

profile of v11, /device:TPU:0, one launch (start us, length us, event | category | flops | bytes accessed | tf_op | source)
XLA Modules:
  0.0 27.1 jit_solution(15203483076288618078)
XLA Ops:
  0.6 0.9 %shard_map.78.refs_0_ = bf16[256,128]{1,0:T(8,128)(2,1)S(1)} custom-call(bf16[128,128]{1,0:T(8,128)(2,1)} %strengths_ref.1, bf16[128,128]{1,0:T(8,128)(2,1)} %weights_ref.1), custom_call_target="tpu_custom_call" | custom-call | flops 17179869184 | bytes 1048576 | tf_op jit(solution)/shard_map/pallas_call | solution.py:309
  1.6 4.0 %collective-permute-start.2 = (bf16[256,128]{1,0:T(8,128)(2,1)S(1)}, bf16[256,128]{1,0:T(8,128)(2,1)S(1)}, u32[]{:S(2)}, u32[]{:S(2)}) collective-permute-start(bf16[256,128]{1,0:T(8,128)(2,1)S(1)} %shard_map.78.refs_0_), channel_id=1, source_target_pairs={{0,3},{1,2},{2,1},{3,0},{4,7},{5,6},{6,5},{7,4},{8,11},{9,10},{10,... | collective-permute-start | bytes 196616 | tf_op jit(solution)/shard_map/ppermute | solution.py:15
  5.5 0.5 %collective-permute-start.1 = (bf16[256,128]{1,0:T(8,128)(2,1)S(1)}, bf16[256,128]{1,0:T(8,128)(2,1)S(1)}, u32[]{:S(2)}, u32[]{:S(2)}) collective-permute-start(bf16[256,128]{1,0:T(8,128)(2,1)S(1)} %shard_map.78.refs_0_), channel_id=1, source_target_pairs={{0,2},{1,3},{2,0},{3,1},{4,6},{5,7},{6,4},{7,5},{8,10},{9,11},{10,... | collective-permute-start | bytes 196616 | tf_op jit(solution)/shard_map/ppermute | solution.py:15
  6.1 0.1 collective-permute-start
  6.9 2.7 %shard_map.77._.total = f32[48,256,128]{2,1,0:T(8,128)S(1)} custom-call(s32[1]{0:T(128)S(6)} %copy.8.live_ref, s32[192]{0:T(256)} %target_ref.1, s32[192]{0:T(256)} %source_ref.1, bf16[192,2,128,128]{3,2,1,0:T(8,128)(2,1)S(1)} %copy-done), custom_call_target="tpu_custom_call" | custom-call | flops 8589934592 | bytes 1048576 | tf_op jit(solution)/shard_map/pallas_call | solution.py:309
  9.6 0.0 collective-permute-done.2.refs_3_
  9.6 0.2 collective-permute-done.1.refs_2_
  9.8 0.5 %collective-permute-done.refs_1_ = bf16[256,128]{1,0:T(8,128)(2,1)S(1)} collective-permute-done((bf16[256,128]{1,0:T(8,128)(2,1)S(1)}, bf16[256,128]{1,0:T(8,128)(2,1)S(1)}, u32[]{:S(2)}, u32[]{:S(2)}) %collective-permute-start) | collective-permute-done | bytes 65568 | tf_op jit(solution)/shard_map/ppermute | solution.py:15
  10.3 0.1 collective-permute-start.3
  10.4 0.8 %shard_map.80 = (bf16[2,16,256,128]{3,2,1,0:T(8,128)(2,1)S(1)}, bf16[128,1024]{1,0:T(8,128)(2,1)S(1)}, s16[1040,128]{1,0:T(8,128)(2,1)S(1)}) custom-call(bf16[512,128]{1,0:T(8,128)(2,1)S(1)} %shard_map.79._, f32[48,256,128]{2,1,0:T(8,128)S(1)} %shard_map.77._.total, bf16[256,128]{1,0:T(8,128)(2,1)S(1)} %shard_map.78.refs_0_, ...), custom_call_target="tpu_custom_call" | custom-call | flops 8589934592 | bytes 1048576 | tf_op jit(solution)/shard_map/pallas_call | solution.py:309
  11.3 0.7 %collective-permute-start.5 = (s16[1040,128]{1,0:T(8,128)(2,1)S(1)}, s16[1040,128]{1,0:T(8,128)(2,1)S(1)}, u32[]{:S(2)}, u32[]{:S(2)}) collective-permute-start(s16[1040,128]{1,0:T(8,128)(2,1)S(1)} %get-tuple-element.17), channel_id=1, source_target_pairs={{0,0},{4,8},{8,4},{12,16},{16,12},{20,24},{24,20},{28,28},{1,1},{5... | collective-permute-start | bytes 798728 | tf_op jit(solution)/shard_map/ppermute | solution.py:21
  11.9 0.0 collective-permute-done.3._.first_ref
  12.0 1.3 %shard_map.81 = (bf16[2,32,256,128]{3,2,1,0:T(8,128)(2,1)S(1)}, f32[4,128,128]{2,1,0:T(8,128)S(1)}, s16[528,128]{1,0:T(8,128)(2,1)S(1)}) custom-call(bf16[512,128]{1,0:T(8,128)(2,1)S(1)} %collective-permute-done.3._.first_ref, f32[48,256,128]{2,1,0:T(8,128)S(1)} %shard_map.77._.total, bf16[128,1024]{1,0:T(8,128)(2,1)S(1)} %get-tuple-element.13.across_ref), custom_call_target="tpu_custom_call" | custom-call | flops 8589934592 | bytes 1048576 | tf_op jit(solution)/shard_map/pallas_call | solution.py:309
  13.3 3.0 %collective-permute-start.4 = (s16[528,128]{1,0:T(8,128)(2,1)S(1)}, s16[528,128]{1,0:T(8,128)(2,1)S(1)}, u32[]{:S(2)}, u32[]{:S(2)}) collective-permute-start(s16[528,128]{1,0:T(8,128)(2,1)S(1)} %get-tuple-element.16), channel_id=1, source_target_pairs={{0,4},{4,0},{8,12},{12,8},{16,20},{20,16},{24,28},{28,24},{1,5},{5... | collective-permute-start | bytes 405512 | tf_op jit(solution)/shard_map/ppermute | solution.py:21
  16.3 1.3 %shard_map.82.potential_ref = f32[4,128,128]{2,1,0:T(8,128)S(1)} custom-call(bf16[2,32,256,128]{3,2,1,0:T(8,128)(2,1)S(1)} %get-tuple-element.14.pairs_ref, bf16[512,128]{1,0:T(8,128)(2,1)S(1)} %collective-permute-done.3._.first_ref, bf16[256,128]{1,0:T(8,128)(2,1)S(1)} %shard_map.78.refs_0_, bf16[256,128]{1,0:T(8,128)(2,1)S(1)} %collective-permute-done.refs_1_, ...), custom_call_target="tpu_custom_call" | custom-call | bytes 1048576 | tf_op jit(solution)/shard_map/pallas_call | solution.py:309
  17.6 0.0 collective-permute-done.4.first_ref
  17.6 0.9 %shard_map.83 = (f32[256,128]{1,0:T(8,128)S(1)}, s16[272,128]{1,0:T(8,128)(2,1)S(1)}, s16[272,128]{1,0:T(8,128)(2,1)S(1)}, s16[272,128]{1,0:T(8,128)(2,1)S(1)}) custom-call(bf16[2,16,256,128]{3,2,1,0:T(8,128)(2,1)S(1)} %get-tuple-element.12.pairs_ref, f32[4,128,128]{2,1,0:T(8,128)S(1)} %shard_map.82.potential_ref, ...), custom_call_target="tpu_custom_call" | custom-call | bytes 1048576 | tf_op jit(solution)/shard_map/pallas_call | solution.py:309
  18.5 2.5 %collective-permute-start.6 = (s16[272,128]{1,0:T(8,128)(2,1)S(1)}, s16[272,128]{1,0:T(8,128)(2,1)S(1)}, u32[]{:S(2)}, u32[]{:S(2)}) collective-permute-start(s16[272,128]{1,0:T(8,128)(2,1)S(1)} %get-tuple-element.19), channel_id=1, source_target_pairs={{0,3},{1,2},{2,1},{3,0},{4,7},{5,6},{6,5},{7,4},{8,11},{9,10},{10,... | collective-permute-start | bytes 208904 | tf_op jit(solution)/shard_map/ppermute | solution.py:15
  21.1 0.4 %collective-permute-start.7 = (s16[272,128]{1,0:T(8,128)(2,1)S(1)}, s16[272,128]{1,0:T(8,128)(2,1)S(1)}, u32[]{:S(2)}, u32[]{:S(2)}) collective-permute-start(s16[272,128]{1,0:T(8,128)(2,1)S(1)} %get-tuple-element.20), channel_id=1, source_target_pairs={{0,2},{1,3},{2,0},{3,1},{4,6},{5,7},{6,4},{7,5},{8,10},{9,11},{10,... | collective-permute-start | bytes 208904 | tf_op jit(solution)/shard_map/ppermute | solution.py:15
  21.5 1.0 %collective-permute-start.8 = (s16[272,128]{1,0:T(8,128)(2,1)S(1)}, s16[272,128]{1,0:T(8,128)(2,1)S(1)}, u32[]{:S(2)}, u32[]{:S(2)}) collective-permute-start(s16[272,128]{1,0:T(8,128)(2,1)S(1)} %get-tuple-element.21), channel_id=1, source_target_pairs={{0,1},{1,0},{2,3},{3,2},{4,5},{5,4},{6,7},{7,6},{8,9},{9,8},{10,11... | collective-permute-start | bytes 208904 | tf_op jit(solution)/shard_map/ppermute | solution.py:15
  22.5 1.3 %collective-permute-done.6.refs_0_ = s16[272,128]{1,0:T(8,128)(2,1)S(1)} collective-permute-done((s16[272,128]{1,0:T(8,128)(2,1)S(1)}, s16[272,128]{1,0:T(8,128)(2,1)S(1)}, u32[]{:S(2)}, u32[]{:S(2)}) %collective-permute-start.6) | collective-permute-done | bytes 69664 | tf_op jit(solution)/shard_map/ppermute | solution.py:15
  23.8 2.1 %collective-permute-done.7.refs_1_ = s16[272,128]{1,0:T(8,128)(2,1)S(1)} collective-permute-done((s16[272,128]{1,0:T(8,128)(2,1)S(1)}, s16[272,128]{1,0:T(8,128)(2,1)S(1)}, u32[]{:S(2)}, u32[]{:S(2)}) %collective-permute-start.7) | collective-permute-done | bytes 69664 | tf_op jit(solution)/shard_map/ppermute | solution.py:15
  25.9 0.5 %collective-permute-done.8.refs_2_ = s16[272,128]{1,0:T(8,128)(2,1)S(1)} collective-permute-done((s16[272,128]{1,0:T(8,128)(2,1)S(1)}, s16[272,128]{1,0:T(8,128)(2,1)S(1)}, u32[]{:S(2)}, u32[]{:S(2)}) %collective-permute-start.8) | collective-permute-done | bytes 69664 | tf_op jit(solution)/shard_map/ppermute | solution.py:15
  26.3 0.7 %shard_map.84 = (f32[128,128]{1,0:T(8,128)}, f32[128,128]{1,0:T(8,128)}) custom-call(f32[256,128]{1,0:T(8,128)S(1)} %get-tuple-element.18.own_ref, s16[272,128]{1,0:T(8,128)(2,1)S(1)} %collective-permute-done.6.refs_0_, s16[272,128]{1,0:T(8,128)(2,1)S(1)} %collective-permute-done.7.refs_1_, s16[272,128]{1,0:T(8,128)(2,1)S(1)} %collective-permute-done.8.refs_2_), custom_call_target="tpu_custom_call" | custom-call | bytes 1048576 | tf_op jit(solution)/shard_map/pallas_call | solution.py:309
  (4 shorter events, 0.0 us)
Async XLA Ops:
  0.6 6.2 %copy-start = (bf16[192,2,128,128]{3,2,1,0:T(8,128)(2,1)S(1)}, bf16[192,2,128,128]{3,2,1,0:T(8,128)(2,1)}, u32[]{:S(2)}) copy-start(bf16[192,2,128,128]{3,2,1,0:T(8,128)(2,1)} %kernels_ref.1) | copy-start | bytes 37748740
  1.6 8.0 %collective-permute-start.2 = (bf16[256,128]{1,0:T(8,128)(2,1)S(1)}, bf16[256,128]{1,0:T(8,128)(2,1)S(1)}, u32[]{:S(2)}, u32[]{:S(2)}) collective-permute-start(bf16[256,128]{1,0:T(8,128)(2,1)S(1)} %shard_map.78.refs_0_), channel_id=1, source_target_pairs={{0,3},{1,2},{2,1},{3,0},{4,7},{5,6},{6,5},{7,4},{8,11},{9,10},{10,... | collective-permute-start | bytes 196616 | tf_op jit(solution)/shard_map/ppermute | solution.py:15
  5.5 4.3 %collective-permute-start.1 = (bf16[256,128]{1,0:T(8,128)(2,1)S(1)}, bf16[256,128]{1,0:T(8,128)(2,1)S(1)}, u32[]{:S(2)}, u32[]{:S(2)}) collective-permute-start(bf16[256,128]{1,0:T(8,128)(2,1)S(1)} %shard_map.78.refs_0_), channel_id=1, source_target_pairs={{0,2},{1,3},{2,0},{3,1},{4,6},{5,7},{6,4},{7,5},{8,10},{9,11},{10,... | collective-permute-start | bytes 196616 | tf_op jit(solution)/shard_map/ppermute | solution.py:15
  6.1 4.3 %collective-permute-start = (bf16[256,128]{1,0:T(8,128)(2,1)S(1)}, bf16[256,128]{1,0:T(8,128)(2,1)S(1)}, u32[]{:S(2)}, u32[]{:S(2)}) collective-permute-start(bf16[256,128]{1,0:T(8,128)(2,1)S(1)} %shard_map.78.refs_0_), channel_id=1, source_target_pairs={{0,1},{1,0},{2,3},{3,2},{4,5},{5,4},{6,7},{7,6},{8,9},{9,8},{10,11... | collective-permute-start | bytes 196616 | tf_op jit(solution)/shard_map/ppermute | solution.py:15
  10.3 1.6 %collective-permute-start.3 = (bf16[512,128]{1,0:T(8,128)(2,1)S(1)}, bf16[512,128]{1,0:T(8,128)(2,1)S(1)}, u32[]{:S(2)}, u32[]{:S(2)}) collective-permute-start(bf16[512,128]{1,0:T(8,128)(2,1)S(1)} %shard_map.79._), channel_id=1, source_target_pairs={{0,4},{4,0},{8,12},{12,8},{16,20},{20,16},{24,28},{28,24},{1,5},{5... | collective-permute-start | bytes 393224 | tf_op jit(solution)/shard_map/ppermute | solution.py:21
  11.3 6.4 %collective-permute-start.5 = (s16[1040,128]{1,0:T(8,128)(2,1)S(1)}, s16[1040,128]{1,0:T(8,128)(2,1)S(1)}, u32[]{:S(2)}, u32[]{:S(2)}) collective-permute-start(s16[1040,128]{1,0:T(8,128)(2,1)S(1)} %get-tuple-element.17), channel_id=1, source_target_pairs={{0,0},{4,8},{8,4},{12,16},{16,12},{20,24},{24,20},{28,28},{1,1},{5... | collective-permute-start | bytes 798728 | tf_op jit(solution)/shard_map/ppermute | solution.py:21
  13.3 4.3 %collective-permute-start.4 = (s16[528,128]{1,0:T(8,128)(2,1)S(1)}, s16[528,128]{1,0:T(8,128)(2,1)S(1)}, u32[]{:S(2)}, u32[]{:S(2)}) collective-permute-start(s16[528,128]{1,0:T(8,128)(2,1)S(1)} %get-tuple-element.16), channel_id=1, source_target_pairs={{0,4},{4,0},{8,12},{12,8},{16,20},{20,16},{24,28},{28,24},{1,5},{5... | collective-permute-start | bytes 405512 | tf_op jit(solution)/shard_map/ppermute | solution.py:21
  18.5 5.3 %collective-permute-start.6 = (s16[272,128]{1,0:T(8,128)(2,1)S(1)}, s16[272,128]{1,0:T(8,128)(2,1)S(1)}, u32[]{:S(2)}, u32[]{:S(2)}) collective-permute-start(s16[272,128]{1,0:T(8,128)(2,1)S(1)} %get-tuple-element.19), channel_id=1, source_target_pairs={{0,3},{1,2},{2,1},{3,0},{4,7},{5,6},{6,5},{7,4},{8,11},{9,10},{10,... | collective-permute-start | bytes 208904 | tf_op jit(solution)/shard_map/ppermute | solution.py:15
  21.1 4.8 %collective-permute-start.7 = (s16[272,128]{1,0:T(8,128)(2,1)S(1)}, s16[272,128]{1,0:T(8,128)(2,1)S(1)}, u32[]{:S(2)}, u32[]{:S(2)}) collective-permute-start(s16[272,128]{1,0:T(8,128)(2,1)S(1)} %get-tuple-element.20), channel_id=1, source_target_pairs={{0,2},{1,3},{2,0},{3,1},{4,6},{5,7},{6,4},{7,5},{8,10},{9,11},{10,... | collective-permute-start | bytes 208904 | tf_op jit(solution)/shard_map/ppermute | solution.py:15
  21.5 4.8 %collective-permute-start.8 = (s16[272,128]{1,0:T(8,128)(2,1)S(1)}, s16[272,128]{1,0:T(8,128)(2,1)S(1)}, u32[]{:S(2)}, u32[]{:S(2)}) collective-permute-start(s16[272,128]{1,0:T(8,128)(2,1)S(1)} %get-tuple-element.21), channel_id=1, source_target_pairs={{0,1},{1,0},{2,3},{3,2},{4,5},{5,4},{6,7},{7,6},{8,9},{9,8},{10,11... | collective-permute-start | bytes 208904 | tf_op jit(solution)/shard_map/ppermute | solution.py:15

commit v12 on v11

--- a/solution.py
+++ b/solution.py
@@ -93,20 +93,15 @@
                 work(slot)
 
 
-def combine_kernel(group_blocks, blocks, chunk, live_ref, target_ref, source_ref, kernels_ref, total, *scratch):
+def combine_kernel(group_blocks, blocks, chunk, live_ref, target_ref, source_ref, kernels_ref, _, total, *scratch):
     *ids, id_sems = scratch
-
-    def clear():
-        @pl.loop(0, total.shape[0])
-        def _(pair):
-            total[pair] = jnp.zeros(total.shape[1:], total.dtype)
 
     def add(slot):
         target, source = place(*ids, slot, group_blocks, blocks)
         pair = source * group_blocks + target
         total[pair] += kernels_ref[slot].reshape(total.shape[1:]).astype(jnp.float32)
 
-    each_slot(chunk, live_ref, (target_ref, source_ref), ids, id_sems, clear, lambda c: None, add)
+    each_slot(chunk, live_ref, (target_ref, source_ref), ids, id_sems, lambda: None, lambda c: None, add)
 
 
 def split(total, first, out_ref):
@@ -118,7 +113,8 @@
         out_ref[1, pair] = (value - high.astype(jnp.float32)).astype(jnp.bfloat16)
 
 
-def pack_kernel(strengths_ref, weights_ref, out_ref, sems):
+def pack_kernel(strengths_ref, weights_ref, out_ref, *rest):
+    *zeros, sems = rest
     rows = strengths_ref.shape[0]
     copies = [
         pltpu.make_async_copy(ref, out_ref.at[pl.ds(i * rows, rows)], sems.at[i])
@@ -126,6 +122,12 @@
     ]
     for copy in copies:
         copy.start()
+    for ref in zeros:
+
+        @pl.loop(0, ref.shape[0])
+        def _(i):
+            ref[i] = jnp.zeros(ref.shape[1:], ref.dtype)
+
     for copy in copies:
         copy.wait()
 
@@ -175,7 +177,7 @@
             yield product[:, j * width : (j + 1) * width]
 
 
-def second_kernel(blocks, panels, count, _, total, *refs):
+def second_kernel(blocks, panels, count, total, *refs):
     *gathered, pairs_ref, across_ref, out_ref = refs
     split(total, total.shape[0] - pairs_ref.shape[1], pairs_ref)
     for i, block in enumerate(part_of(gathered, blocks, panels, 1)):
@@ -301,14 +303,15 @@
     chunk = 8 if slots % 8 == 0 else 1
     in_vmem, in_smem, in_hbm = (pl.BlockSpec(memory_space=m) for m in (pltpu.VMEM, pltpu.SMEM, pltpu.HBM))
     f32, bf16 = jnp.float32, jnp.bfloat16
-    slot_args = (live_slots,) + tuple(pltpu.with_memory_space_constraint(x, pltpu.HBM) for x in (target_ids, source_ids))
+    slot_args = (live_slots,) + tuple(pltpu.with_memory_space_constraint(x, pltpu.VMEM) for x in (target_ids, source_ids))
     ids = [pltpu.SMEM(x.shape, x.dtype) for x in (target_ids, source_ids)] + [pltpu.SemaphoreType.DMA((2,))]
 
-    def call(body, shapes, args, specs=None, scratch=(), mib=8, flops=0):
+    def call(body, shapes, args, specs=None, scratch=(), mib=8, flops=0, aliases=()):
         single = not isinstance(shapes, tuple)
         return pl.pallas_call(
             body,
             out_shape=shapes,
+            input_output_aliases=dict(aliases),
             in_specs=specs or [in_vmem] * len(args),
             out_specs=in_vmem if single else (in_vmem,) * len(shapes),
             scratch_shapes=scratch,
@@ -319,9 +322,10 @@
     def shape(*dims, kind=f32):
         return jax.ShapeDtypeStruct(dims, kind)
 
-    mine = call(
+    zeros = [pltpu.VMEM((pairs, 2 * panels, panels), f32)] if pairs <= slots else []
+    mine, *zeros = call(
         pack_kernel,
-        shape(2 * blocks * panels, width, kind=bf16),
+        (shape(2 * blocks * panels, width, kind=bf16), *zeros),
         [pltpu.with_memory_space_constraint(x, pltpu.HBM) for x in (strengths, adjoint_weights)],
         [in_hbm] * 2,
         [pltpu.SemaphoreType.DMA((2,))],
@@ -346,13 +350,12 @@
         total = call(
             functools.partial(combine_kernel, group_blocks, blocks, chunk),
             pltpu.VMEM((pairs, 2 * panels, panels), f32),
-            (*slot_args, pltpu.with_memory_space_constraint(kernels, pltpu.VMEM)),
-            [in_smem] + [in_hbm] * 2 + [in_vmem],
+            (*slot_args, *(pltpu.with_memory_space_constraint(x, pltpu.VMEM) for x in (kernels, *zeros))),
+            [in_smem] + [in_vmem] * 4,
             ids,
             flops=1 << 33,
-        )
-        own = group_strengths(total)
-        first = exchange_beside(own, 0)
+            aliases=[(4, 0)],
+        )
         total = pltpu.with_memory_space_constraint(total, pltpu.VMEM)
         second_pairs = pairs // 3
         kept_second, across, upper = call(
@@ -362,10 +365,10 @@
                 shape(width, 2 * group_blocks * panels, kind=bf16),
                 coded(2 * group_blocks),
             ),
-            (own, total, *gathered),
-            [in_hbm] + [in_vmem] * (1 + clusters),
+            (total, *gathered),
             flops=1 << 33,
         )
+        first = exchange_beside(group_strengths(across), 0)
         kept, middle, lower = call(
             functools.partial(first_kernel, group_blocks),
             (pltpu.VMEM((2, pairs - second_pairs, 2 * panels, panels), bf16), block_sums, coded(group_blocks)),
@@ -384,7 +387,7 @@
             functools.partial(slots_kernel, blocks, panels, chunk),
             (block_sums, shape(sources, width, panels)),
             (*slot_args, pltpu.with_memory_space_constraint(kernels, pltpu.HBM), first, second, *gathered),
-            [in_smem] + [in_hbm] * 3 + [in_vmem] * (2 + clusters),
+            [in_smem] + [in_vmem] * 2 + [in_hbm] + [in_vmem] * (2 + clusters),
             [
                 pltpu.VMEM(kernels.shape, bf16),
                 pltpu.VMEM((sources, 2 * panels, width), bf16),

time: 27.5 us -> 27.8 us (1.011)
  waiting for transfers between devices: 4.55 us -> 6.06 us
  Pallas kernels: 8.79 us -> 8.11 us
  starting transfers between devices: 12.3 us -> 12 us
    ppermute x6, waiting for transfers between devices: 4.54 us -> 5.4 us  [exchange(): lax.ppermute(value, axis, [(i, i ^ step) for i in range(lax.axis_size(axi...]
    pallas_call x8, Pallas kernels: 8.79 us -> 8.11 us  [call(): pl.pallas_call(body, out_shape=shapes, input_output_aliases=dict(aliases)...]
    ppermute x3, waiting for transfers between devices: 0.01 us -> 0.65 us  [exchange_beside(): lax.ppermute(value, 'grp', [(i, j if 0 <= j < groups else i) for i, j in...]
    ppermute x6, starting transfers between devices: 8.58 us -> 8.16 us  [exchange(): lax.ppermute(value, axis, [(i, i ^ step) for i in range(lax.axis_size(axi...]
  transfers between devices with their start and end apart: 9 -> 9, of which waited for: 5 -> 6; matrix products, arithmetic and copies ran while one was open for 0% -> 0% of each run, Pallas kernels for 23% -> 17%
where the time goes in v12:
time: 27.8 us; the launch traced here: 27.6 us
  starting transfers between devices  12 us (43%)
  Pallas kernels  8.11 us (29%)
  waiting for transfers between devices  6.06 us (22%)
  between operations  1.43 us (5%)
    ppermute x6, starting transfers between devices, exchange(): lax.ppermute(value, axis, [(i, i ^ step) for i in range(lax.axis_size(axi...  8.16 us
    pallas_call x8, Pallas kernels, call(): pl.pallas_call(body, out_shape=shapes, input_output_aliases=dict(aliases)...  8.11 us
    ppermute x6, waiting for transfers between devices, exchange(): lax.ppermute(value, axis, [(i, i ^ step) for i in range(lax.axis_size(axi...  5.4 us
    ppermute x3, starting transfers between devices, exchange_beside(): lax.ppermute(value, 'grp', [(i, j if 0 <= j < groups else i) for i, j in...  3.85 us
    ppermute x3, waiting for transfers between devices, exchange_beside(): lax.ppermute(value, 'grp', [(i, j if 0 <= j < groups else i) for i, j in...  0.65 us
  transfers between devices with their start and end apart: 9, of which 6 were waited for; matrix products, arithmetic and copies ran while one was open for 0% of the time, Pallas kernels for 17%

profile of v12, /device:TPU:0, one launch (start us, length us, event | category | flops | bytes accessed | tf_op | source)
XLA Modules:
  0.0 27.6 jit_solution(18354376525834371775)
XLA Ops:
  0.7 0.9 %shard_map.77 = (bf16[256,128]{1,0:T(8,128)(2,1)S(1)}, f32[48,256,128]{2,1,0:T(8,128)S(1)}) custom-call(bf16[128,128]{1,0:T(8,128)(2,1)} %strengths_ref.1, bf16[128,128]{1,0:T(8,128)(2,1)} %weights_ref.1), custom_call_target="tpu_custom_call" | custom-call | flops 17179869184 | bytes 1048576 | tf_op jit(solution)/shard_map/pallas_call | solution.py:311
  1.6 4.0 %collective-permute-start.2 = (bf16[256,128]{1,0:T(8,128)(2,1)S(1)}, bf16[256,128]{1,0:T(8,128)(2,1)S(1)}, u32[]{:S(2)}, u32[]{:S(2)}) collective-permute-start(bf16[256,128]{1,0:T(8,128)(2,1)S(1)} %get-tuple-element.15.refs_0_), channel_id=1, source_target_pairs={{0,3},{1,2},{2,1},{3,0},{4,7},{5,6},{6,5},{7,4},{8,11},{9,10},{10,... | collective-permute-start | bytes 196616 | tf_op jit(solution)/shard_map/ppermute | solution.py:15
  5.6 0.5 %collective-permute-start.1 = (bf16[256,128]{1,0:T(8,128)(2,1)S(1)}, bf16[256,128]{1,0:T(8,128)(2,1)S(1)}, u32[]{:S(2)}, u32[]{:S(2)}) collective-permute-start(bf16[256,128]{1,0:T(8,128)(2,1)S(1)} %get-tuple-element.15.refs_0_), channel_id=1, source_target_pairs={{0,2},{1,3},{2,0},{3,1},{4,6},{5,7},{6,4},{7,5},{8,10},{9,11},{10,... | collective-permute-start | bytes 196616 | tf_op jit(solution)/shard_map/ppermute | solution.py:15
  6.1 0.1 collective-permute-start
  6.9 2.0 %shard_map.78.total = f32[48,256,128]{2,1,0:T(8,128)S(1)} custom-call(s32[1]{0:T(128)S(6)} %copy.10.live_ref, s32[192]{0:T(256)S(1)} %copy-done.1, s32[192]{0:T(256)S(1)} %copy-done.2, bf16[192,2,128,128]{3,2,1,0:T(8,128)(2,1)S(1)} %copy-done, f32[48,256,128]{2,1,0:T(8,128)S(1)} %get-tuple-element.14._), custom_call_target="tpu_custom_call", output_to_operand_aliasing={{}: (4, {})} | custom-call | flops 8589934592 | bytes 1048576 | tf_op jit(solution)/shard_map/pallas_call | solution.py:311
  8.9 0.0 collective-permute-done.2.refs_3_
  8.9 0.9 %collective-permute-done.1.refs_2_ = bf16[256,128]{1,0:T(8,128)(2,1)S(1)} collective-permute-done((bf16[256,128]{1,0:T(8,128)(2,1)S(1)}, bf16[256,128]{1,0:T(8,128)(2,1)S(1)}, u32[]{:S(2)}, u32[]{:S(2)}) %collective-permute-start.1) | collective-permute-done | bytes 65568 | tf_op jit(solution)/shard_map/ppermute | solution.py:15
  9.8 0.5 %collective-permute-done.refs_1_ = bf16[256,128]{1,0:T(8,128)(2,1)S(1)} collective-permute-done((bf16[256,128]{1,0:T(8,128)(2,1)S(1)}, bf16[256,128]{1,0:T(8,128)(2,1)S(1)}, u32[]{:S(2)}, u32[]{:S(2)}) %collective-permute-start) | collective-permute-done | bytes 65568 | tf_op jit(solution)/shard_map/ppermute | solution.py:15
  10.3 0.8 %shard_map.79 = (bf16[2,16,256,128]{3,2,1,0:T(8,128)(2,1)S(1)}, bf16[128,1024]{1,0:T(8,128)(2,1)S(1)}, s16[1040,128]{1,0:T(8,128)(2,1)S(1)}) custom-call(f32[48,256,128]{2,1,0:T(8,128)S(1)} %shard_map.78.total, bf16[256,128]{1,0:T(8,128)(2,1)S(1)} %get-tuple-element.15.refs_0_, bf16[256,128]{1,0:T(8,128)(2,1)S(1)} %collective-permute-done.refs_1_, ...), custom_call_target="tpu_custom_call" | custom-call | flops 8589934592 | bytes 1048576 | tf_op jit(solution)/shard_map/pallas_call | solution.py:311
  11.2 0.1 collective-permute-start.3
  11.3 0.7 %collective-permute-start.5 = (s16[1040,128]{1,0:T(8,128)(2,1)S(1)}, s16[1040,128]{1,0:T(8,128)(2,1)S(1)}, u32[]{:S(2)}, u32[]{:S(2)}) collective-permute-start(s16[1040,128]{1,0:T(8,128)(2,1)S(1)} %get-tuple-element.21), channel_id=1, source_target_pairs={{0,0},{4,8},{8,4},{12,16},{16,12},{20,24},{24,20},{28,28},{1,1},{5... | collective-permute-start | bytes 798728 | tf_op jit(solution)/shard_map/ppermute | solution.py:21
  12.0 0.6 %collective-permute-done.3._.first_ref = bf16[512,128]{1,0:T(8,128)(2,1)S(1)} collective-permute-done((bf16[512,128]{1,0:T(8,128)(2,1)S(1)}, bf16[512,128]{1,0:T(8,128)(2,1)S(1)}, u32[]{:S(2)}, u32[]{:S(2)}) %collective-permute-start.3) | collective-permute-done | bytes 131104 | tf_op jit(solution)/shard_map/ppermute | solution.py:21
  12.6 1.3 %shard_map.81 = (bf16[2,32,256,128]{3,2,1,0:T(8,128)(2,1)S(1)}, f32[4,128,128]{2,1,0:T(8,128)S(1)}, s16[528,128]{1,0:T(8,128)(2,1)S(1)}) custom-call(bf16[512,128]{1,0:T(8,128)(2,1)S(1)} %collective-permute-done.3._.first_ref, f32[48,256,128]{2,1,0:T(8,128)S(1)} %shard_map.78.total, bf16[128,1024]{1,0:T(8,128)(2,1)S(1)} %get-tuple-element.17._.across_ref), custom_call_target="tpu_custom_call" | custom-call | flops 8589934592 | bytes 1048576 | tf_op jit(solution)/shard_map/pallas_call | solution.py:311
  14.0 3.1 %collective-permute-start.4 = (s16[528,128]{1,0:T(8,128)(2,1)S(1)}, s16[528,128]{1,0:T(8,128)(2,1)S(1)}, u32[]{:S(2)}, u32[]{:S(2)}) collective-permute-start(s16[528,128]{1,0:T(8,128)(2,1)S(1)} %get-tuple-element.20), channel_id=1, source_target_pairs={{0,4},{4,0},{8,12},{12,8},{16,20},{20,16},{24,28},{28,24},{1,5},{5... | collective-permute-start | bytes 405512 | tf_op jit(solution)/shard_map/ppermute | solution.py:21
  17.1 1.3 %shard_map.82.potential_ref = f32[4,128,128]{2,1,0:T(8,128)S(1)} custom-call(bf16[2,32,256,128]{3,2,1,0:T(8,128)(2,1)S(1)} %get-tuple-element.18.pairs_ref, bf16[512,128]{1,0:T(8,128)(2,1)S(1)} %collective-permute-done.3._.first_ref, bf16[256,128]{1,0:T(8,128)(2,1)S(1)} %get-tuple-element.15.refs_0_, bf16[256,128]{1,0:T(8,128)(2,1)S(1)} %collective-permute-done.refs_1_, ...), custom_call_target="tpu_custom_call" | custom-call | bytes 1048576 | tf_op jit(solution)/shard_map/pallas_call | solution.py:311
  18.4 0.0 collective-permute-done.4.first_ref
  18.4 0.9 %shard_map.83 = (f32[256,128]{1,0:T(8,128)S(1)}, s16[272,128]{1,0:T(8,128)(2,1)S(1)}, s16[272,128]{1,0:T(8,128)(2,1)S(1)}, s16[272,128]{1,0:T(8,128)(2,1)S(1)}) custom-call(bf16[2,16,256,128]{3,2,1,0:T(8,128)(2,1)S(1)} %get-tuple-element.16.pairs_ref, f32[4,128,128]{2,1,0:T(8,128)S(1)} %shard_map.82.potential_ref, ...), custom_call_target="tpu_custom_call" | custom-call | bytes 1048576 | tf_op jit(solution)/shard_map/pallas_call | solution.py:311
  19.3 1.4 %collective-permute-start.6 = (s16[272,128]{1,0:T(8,128)(2,1)S(1)}, s16[272,128]{1,0:T(8,128)(2,1)S(1)}, u32[]{:S(2)}, u32[]{:S(2)}) collective-permute-start(s16[272,128]{1,0:T(8,128)(2,1)S(1)} %get-tuple-element.23), channel_id=1, source_target_pairs={{0,3},{1,2},{2,1},{3,0},{4,7},{5,6},{6,5},{7,4},{8,11},{9,10},{10,... | collective-permute-start | bytes 208904 | tf_op jit(solution)/shard_map/ppermute | solution.py:15
  20.7 1.6 %collective-permute-start.7 = (s16[272,128]{1,0:T(8,128)(2,1)S(1)}, s16[272,128]{1,0:T(8,128)(2,1)S(1)}, u32[]{:S(2)}, u32[]{:S(2)}) collective-permute-start(s16[272,128]{1,0:T(8,128)(2,1)S(1)} %get-tuple-element.24), channel_id=1, source_target_pairs={{0,2},{1,3},{2,0},{3,1},{4,6},{5,7},{6,4},{7,5},{8,10},{9,11},{10,... | collective-permute-start | bytes 208904 | tf_op jit(solution)/shard_map/ppermute | solution.py:15
  22.2 0.6 %collective-permute-start.8 = (s16[272,128]{1,0:T(8,128)(2,1)S(1)}, s16[272,128]{1,0:T(8,128)(2,1)S(1)}, u32[]{:S(2)}, u32[]{:S(2)}) collective-permute-start(s16[272,128]{1,0:T(8,128)(2,1)S(1)} %get-tuple-element.25), channel_id=1, source_target_pairs={{0,1},{1,0},{2,3},{3,2},{4,5},{5,4},{6,7},{7,6},{8,9},{9,8},{10,11... | collective-permute-start | bytes 208904 | tf_op jit(solution)/shard_map/ppermute | solution.py:15
  22.9 1.8 %collective-permute-done.6.refs_0_ = s16[272,128]{1,0:T(8,128)(2,1)S(1)} collective-permute-done((s16[272,128]{1,0:T(8,128)(2,1)S(1)}, s16[272,128]{1,0:T(8,128)(2,1)S(1)}, u32[]{:S(2)}, u32[]{:S(2)}) %collective-permute-start.6) | collective-permute-done | bytes 69664 | tf_op jit(solution)/shard_map/ppermute | solution.py:15
  24.7 1.4 %collective-permute-done.7.refs_1_ = s16[272,128]{1,0:T(8,128)(2,1)S(1)} collective-permute-done((s16[272,128]{1,0:T(8,128)(2,1)S(1)}, s16[272,128]{1,0:T(8,128)(2,1)S(1)}, u32[]{:S(2)}, u32[]{:S(2)}) %collective-permute-start.7) | collective-permute-done | bytes 69664 | tf_op jit(solution)/shard_map/ppermute | solution.py:15
  26.1 0.8 %collective-permute-done.8.refs_2_ = s16[272,128]{1,0:T(8,128)(2,1)S(1)} collective-permute-done((s16[272,128]{1,0:T(8,128)(2,1)S(1)}, s16[272,128]{1,0:T(8,128)(2,1)S(1)}, u32[]{:S(2)}, u32[]{:S(2)}) %collective-permute-start.8) | collective-permute-done | bytes 69664 | tf_op jit(solution)/shard_map/ppermute | solution.py:15
  26.9 0.7 %shard_map.84 = (f32[128,128]{1,0:T(8,128)}, f32[128,128]{1,0:T(8,128)}) custom-call(f32[256,128]{1,0:T(8,128)S(1)} %get-tuple-element.22.own_ref, s16[272,128]{1,0:T(8,128)(2,1)S(1)} %collective-permute-done.6.refs_0_, s16[272,128]{1,0:T(8,128)(2,1)S(1)} %collective-permute-done.7.refs_1_, s16[272,128]{1,0:T(8,128)(2,1)S(1)} %collective-permute-done.8.refs_2_), custom_call_target="tpu_custom_call" | custom-call | bytes 1048576 | tf_op jit(solution)/shard_map/pallas_call | solution.py:311
  (8 shorter events, 0.0 us)
Async XLA Ops:
  0.6 6.2 %copy-start.2 = (s32[192]{0:T(256)S(1)}, s32[192]{0:T(256)}, u32[]{:S(2)}) copy-start(s32[192]{0:T(256)} %source_ref.1) | copy-start | bytes 2308
  0.6 6.2 %copy-start.1 = (s32[192]{0:T(256)S(1)}, s32[192]{0:T(256)}, u32[]{:S(2)}) copy-start(s32[192]{0:T(256)} %target_ref.1) | copy-start | bytes 2308
  0.7 6.2 %copy-start = (bf16[192,2,128,128]{3,2,1,0:T(8,128)(2,1)S(1)}, bf16[192,2,128,128]{3,2,1,0:T(8,128)(2,1)}, u32[]{:S(2)}) copy-start(bf16[192,2,128,128]{3,2,1,0:T(8,128)(2,1)} %kernels_ref.1) | copy-start | bytes 37748740
  1.6 7.3 %collective-permute-start.2 = (bf16[256,128]{1,0:T(8,128)(2,1)S(1)}, bf16[256,128]{1,0:T(8,128)(2,1)S(1)}, u32[]{:S(2)}, u32[]{:S(2)}) collective-permute-start(bf16[256,128]{1,0:T(8,128)(2,1)S(1)} %get-tuple-element.15.refs_0_), channel_id=1, source_target_pairs={{0,3},{1,2},{2,1},{3,0},{4,7},{5,6},{6,5},{7,4},{8,11},{9,10},{10,... | collective-permute-start | bytes 196616 | tf_op jit(solution)/shard_map/ppermute | solution.py:15
  5.6 4.3 %collective-permute-start.1 = (bf16[256,128]{1,0:T(8,128)(2,1)S(1)}, bf16[256,128]{1,0:T(8,128)(2,1)S(1)}, u32[]{:S(2)}, u32[]{:S(2)}) collective-permute-start(bf16[256,128]{1,0:T(8,128)(2,1)S(1)} %get-tuple-element.15.refs_0_), channel_id=1, source_target_pairs={{0,2},{1,3},{2,0},{3,1},{4,6},{5,7},{6,4},{7,5},{8,10},{9,11},{10,... | collective-permute-start | bytes 196616 | tf_op jit(solution)/shard_map/ppermute | solution.py:15
  6.1 4.3 %collective-permute-start = (bf16[256,128]{1,0:T(8,128)(2,1)S(1)}, bf16[256,128]{1,0:T(8,128)(2,1)S(1)}, u32[]{:S(2)}, u32[]{:S(2)}) collective-permute-start(bf16[256,128]{1,0:T(8,128)(2,1)S(1)} %get-tuple-element.15.refs_0_), channel_id=1, source_target_pairs={{0,1},{1,0},{2,3},{3,2},{4,5},{5,4},{6,7},{7,6},{8,9},{9,8},{10,11... | collective-permute-start | bytes 196616 | tf_op jit(solution)/shard_map/ppermute | solution.py:15
  11.2 1.4 %collective-permute-start.3 = (bf16[512,128]{1,0:T(8,128)(2,1)S(1)}, bf16[512,128]{1,0:T(8,128)(2,1)S(1)}, u32[]{:S(2)}, u32[]{:S(2)}) collective-permute-start(bf16[512,128]{1,0:T(8,128)(2,1)S(1)} %shard_map.80), channel_id=1, source_target_pairs={{0,4},{4,0},{8,12},{12,8},{16,20},{20,16},{24,28},{28,24},{1,5},{5... | collective-permute-start | bytes 393224 | tf_op jit(solution)/shard_map/ppermute | solution.py:21
  11.3 7.1 %collective-permute-start.5 = (s16[1040,128]{1,0:T(8,128)(2,1)S(1)}, s16[1040,128]{1,0:T(8,128)(2,1)S(1)}, u32[]{:S(2)}, u32[]{:S(2)}) collective-permute-start(s16[1040,128]{1,0:T(8,128)(2,1)S(1)} %get-tuple-element.21), channel_id=1, source_target_pairs={{0,0},{4,8},{8,4},{12,16},{16,12},{20,24},{24,20},{28,28},{1,1},{5... | collective-permute-start | bytes 798728 | tf_op jit(solution)/shard_map/ppermute | solution.py:21
  14.0 4.4 %collective-permute-start.4 = (s16[528,128]{1,0:T(8,128)(2,1)S(1)}, s16[528,128]{1,0:T(8,128)(2,1)S(1)}, u32[]{:S(2)}, u32[]{:S(2)}) collective-permute-start(s16[528,128]{1,0:T(8,128)(2,1)S(1)} %get-tuple-element.20), channel_id=1, source_target_pairs={{0,4},{4,0},{8,12},{12,8},{16,20},{20,16},{24,28},{28,24},{1,5},{5... | collective-permute-start | bytes 405512 | tf_op jit(solution)/shard_map/ppermute | solution.py:21
  19.3 5.4 %collective-permute-start.6 = (s16[272,128]{1,0:T(8,128)(2,1)S(1)}, s16[272,128]{1,0:T(8,128)(2,1)S(1)}, u32[]{:S(2)}, u32[]{:S(2)}) collective-permute-start(s16[272,128]{1,0:T(8,128)(2,1)S(1)} %get-tuple-element.23), channel_id=1, source_target_pairs={{0,3},{1,2},{2,1},{3,0},{4,7},{5,6},{6,5},{7,4},{8,11},{9,10},{10,... | collective-permute-start | bytes 208904 | tf_op jit(solution)/shard_map/ppermute | solution.py:15
  20.7 5.4 %collective-permute-start.7 = (s16[272,128]{1,0:T(8,128)(2,1)S(1)}, s16[272,128]{1,0:T(8,128)(2,1)S(1)}, u32[]{:S(2)}, u32[]{:S(2)}) collective-permute-start(s16[272,128]{1,0:T(8,128)(2,1)S(1)} %get-tuple-element.24), channel_id=1, source_target_pairs={{0,2},{1,3},{2,0},{3,1},{4,6},{5,7},{6,4},{7,5},{8,10},{9,11},{10,... | collective-permute-start | bytes 208904 | tf_op jit(solution)/shard_map/ppermute | solution.py:15
  22.2 4.6 %collective-permute-start.8 = (s16[272,128]{1,0:T(8,128)(2,1)S(1)}, s16[272,128]{1,0:T(8,128)(2,1)S(1)}, u32[]{:S(2)}, u32[]{:S(2)}) collective-permute-start(s16[272,128]{1,0:T(8,128)(2,1)S(1)} %get-tuple-element.25), channel_id=1, source_target_pairs={{0,1},{1,0},{2,3},{3,2},{4,5},{5,4},{6,7},{7,6},{8,9},{9,8},{10,11... | collective-permute-start | bytes 208904 | tf_op jit(solution)/shard_map/ppermute | solution.py:15

commit v13 on v12

--- a/solution.py
+++ b/solution.py
@@ -67,18 +67,13 @@
     return target, jnp.where(group % 2 == 0, source - 2 * offset * group_blocks, source)
 
 
-def each_slot(chunk, live_ref, id_refs, ids, id_sems, prepare, wait, work):
-    copies = [pltpu.make_async_copy(ref, kept, id_sems.at[i]) for i, (ref, kept) in enumerate(zip(id_refs, ids))]
-    for copy in copies:
-        copy.start()
-    prepare()
-    for copy in copies:
-        copy.wait()
+def each_slot(chunk, live_ref, slots, work, wait=None):
     live = live_ref[0]
 
-    @pl.loop(0, ids[0].shape[0] // chunk)
+    @pl.loop(0, slots // chunk if wait else pl.cdiv(live, chunk))
     def _(c):
-        wait(c)
+        if wait:
+            wait(c)
         first = c * chunk
 
         @pl.when(first + chunk <= live)
@@ -93,15 +88,13 @@
                 work(slot)
 
 
-def combine_kernel(group_blocks, blocks, chunk, live_ref, target_ref, source_ref, kernels_ref, _, total, *scratch):
-    *ids, id_sems = scratch
-
+def combine_kernel(group_blocks, blocks, chunk, live_ref, target_ref, source_ref, kernels_ref, _, total):
     def add(slot):
-        target, source = place(*ids, slot, group_blocks, blocks)
+        target, source = place(target_ref, source_ref, slot, group_blocks, blocks)
         pair = source * group_blocks + target
         total[pair] += kernels_ref[slot].reshape(total.shape[1:]).astype(jnp.float32)
 
-    each_slot(chunk, live_ref, (target_ref, source_ref), ids, id_sems, lambda: None, lambda c: None, add)
+    each_slot(chunk, live_ref, kernels_ref.shape[0], add)
 
 
 def split(total, first, out_ref):
@@ -113,13 +106,13 @@
         out_ref[1, pair] = (value - high.astype(jnp.float32)).astype(jnp.bfloat16)
 
 
-def pack_kernel(strengths_ref, weights_ref, out_ref, *rest):
-    *zeros, sems = rest
+def pack_kernel(strengths_ref, weights_ref, target_ref, source_ref, out_ref, *rest):
+    *kept, sems = rest
+    ids, zeros = kept[:2], kept[2:]
     rows = strengths_ref.shape[0]
-    copies = [
-        pltpu.make_async_copy(ref, out_ref.at[pl.ds(i * rows, rows)], sems.at[i])
-        for i, ref in enumerate((strengths_ref, weights_ref))
-    ]
+    moves = [(ref, out_ref.at[pl.ds(i * rows, rows)]) for i, ref in enumerate((strengths_ref, weights_ref))]
+    moves += zip((target_ref, source_ref), ids)
+    copies = [pltpu.make_async_copy(ref, to, sems.at[i]) for i, (ref, to) in enumerate(moves)]
     for copy in copies:
         copy.start()
     for ref in zeros:
@@ -177,7 +170,7 @@
             yield product[:, j * width : (j + 1) * width]
 
 
-def second_kernel(blocks, panels, count, total, *refs):
+def second_kernel(blocks, panels, count, _, total, *refs):
     *gathered, pairs_ref, across_ref, out_ref = refs
     split(total, total.shape[0] - pairs_ref.shape[1], pairs_ref)
     for i, block in enumerate(part_of(gathered, blocks, panels, 1)):
@@ -245,8 +238,8 @@
 
 
 def slots_kernel(blocks, panels, chunk, *refs):
-    (live_ref, *id_refs, kernels_ref), (first_ref, second_ref, *gathered) = refs[:4], refs[4:-9]
-    potential_ref, adjoint_ref, held, stack, across, *ids, id_sems, sems = refs[-9:]
+    (live_ref, *ids, kernels_ref), (first_ref, second_ref, *gathered) = refs[:4], refs[4:-6]
+    potential_ref, adjoint_ref, held, stack, across, sems = refs[-6:]
     group_blocks = potential_ref.shape[0]
 
     def fetch(c):
@@ -273,7 +266,8 @@
             across[target], jnp.concatenate([real, imag], axis=0), preferred_element_type=jnp.float32
         )
 
-    each_slot(chunk, live_ref, id_refs, ids, id_sems, prepare, lambda c: fetch(c).wait(), work)
+    prepare()
+    each_slot(chunk, live_ref, held.shape[0], work, lambda c: fetch(c).wait())
 
 
 def code_kernel(adjoint_ref, *outs):
@@ -303,17 +297,15 @@
     chunk = 8 if slots % 8 == 0 else 1
     in_vmem, in_smem, in_hbm = (pl.BlockSpec(memory_space=m) for m in (pltpu.VMEM, pltpu.SMEM, pltpu.HBM))
     f32, bf16 = jnp.float32, jnp.bfloat16
-    slot_args = (live_slots,) + tuple(pltpu.with_memory_space_constraint(x, pltpu.VMEM) for x in (target_ids, source_ids))
-    ids = [pltpu.SMEM(x.shape, x.dtype) for x in (target_ids, source_ids)] + [pltpu.SemaphoreType.DMA((2,))]
-
-    def call(body, shapes, args, specs=None, scratch=(), mib=8, flops=0, aliases=()):
+
+    def call(body, shapes, args, specs=None, scratch=(), mib=8, flops=0, aliases=(), out_specs=None):
         single = not isinstance(shapes, tuple)
         return pl.pallas_call(
             body,
             out_shape=shapes,
             input_output_aliases=dict(aliases),
             in_specs=specs or [in_vmem] * len(args),
-            out_specs=in_vmem if single else (in_vmem,) * len(shapes),
+            out_specs=out_specs or (in_vmem if single else (in_vmem,) * len(shapes)),
             scratch_shapes=scratch,
             compiler_params=pltpu.CompilerParams(vmem_limit_bytes=mib << 20),
             cost_estimate=pl.CostEstimate(flops=flops, bytes_accessed=1 << 20, transcendentals=0),
@@ -323,14 +315,18 @@
         return jax.ShapeDtypeStruct(dims, kind)
 
     zeros = [pltpu.VMEM((pairs, 2 * panels, panels), f32)] if pairs <= slots else []
-    mine, *zeros = call(
+    kept_ids = [pltpu.SMEM(x.shape, x.dtype) for x in (target_ids, source_ids)]
+    mine, *ids = call(
         pack_kernel,
-        (shape(2 * blocks * panels, width, kind=bf16), *zeros),
-        [pltpu.with_memory_space_constraint(x, pltpu.HBM) for x in (strengths, adjoint_weights)],
-        [in_hbm] * 2,
-        [pltpu.SemaphoreType.DMA((2,))],
+        (shape(2 * blocks * panels, width, kind=bf16), *kept_ids, *zeros),
+        [pltpu.with_memory_space_constraint(x, pltpu.HBM) for x in (strengths, adjoint_weights, target_ids, source_ids)],
+        [in_hbm] * 4,
+        [pltpu.SemaphoreType.DMA((4,))],
+        out_specs=(in_vmem, in_smem, in_smem) + (in_vmem,) * len(zeros),
         flops=1 << 34,
     )
+    ids, zeros = ids[:2], ids[2:]
+    slot_args = (live_slots, *(pltpu.with_memory_space_constraint(x, pltpu.SMEM) for x in ids))
     gathered = [exchange(mine, "clu", k) for k in range(clusters - 1, 0, -1)]
     gathered = [mine] + gathered[::-1]
 
@@ -351,11 +347,12 @@
             functools.partial(combine_kernel, group_blocks, blocks, chunk),
             pltpu.VMEM((pairs, 2 * panels, panels), f32),
             (*slot_args, *(pltpu.with_memory_space_constraint(x, pltpu.VMEM) for x in (kernels, *zeros))),
-            [in_smem] + [in_vmem] * 4,
-            ids,
+            [in_smem] * 3 + [in_vmem] * 2,
             flops=1 << 33,
             aliases=[(4, 0)],
         )
+        own = group_strengths(total)
+        first = exchange_beside(own, 0)
         total = pltpu.with_memory_space_constraint(total, pltpu.VMEM)
         second_pairs = pairs // 3
         kept_second, across, upper = call(
@@ -365,10 +362,10 @@
                 shape(width, 2 * group_blocks * panels, kind=bf16),
                 coded(2 * group_blocks),
             ),
-            (total, *gathered),
+            (own, total, *gathered),
+            [in_hbm] + [in_vmem] * (1 + clusters),
             flops=1 << 33,
         )
-        first = exchange_beside(group_strengths(across), 0)
         kept, middle, lower = call(
             functools.partial(first_kernel, group_blocks),
             (pltpu.VMEM((2, pairs - second_pairs, 2 * panels, panels), bf16), block_sums, coded(group_blocks)),
@@ -387,12 +384,11 @@
             functools.partial(slots_kernel, blocks, panels, chunk),
             (block_sums, shape(sources, width, panels)),
             (*slot_args, pltpu.with_memory_space_constraint(kernels, pltpu.HBM), first, second, *gathered),
-            [in_smem] + [in_vmem] * 2 + [in_hbm] + [in_vmem] * (2 + clusters),
+            [in_smem] * 3 + [in_hbm] + [in_vmem] * (2 + clusters),
             [
                 pltpu.VMEM(kernels.shape, bf16),
                 pltpu.VMEM((sources, 2 * panels, width), bf16),
                 pltpu.VMEM((group_blocks, width, 2 * panels), bf16),
-                *ids,
                 pltpu.SemaphoreType.DMA((slots // chunk,)),
             ],
             mib=40,

time: 27.8 us -> 27.3 us (0.982)
  waiting for transfers between devices: 6.06 us -> 4.95 us
  Pallas kernels: 8.11 us -> 9.07 us
    pallas_call x8, Pallas kernels: 8.11 us -> 9.07 us  [call(): pl.pallas_call(body, out_shape=shapes, input_output_aliases=dict(aliases)...]
    ppermute x3, waiting for transfers between devices: 0.65 us -> 0.01 us  [exchange_beside(): lax.ppermute(value, 'grp', [(i, j if 0 <= j < groups else i) for i, j in...]
    ppermute x6, waiting for transfers between devices: 5.4 us -> 4.94 us  [exchange(): lax.ppermute(value, axis, [(i, i ^ step) for i in range(lax.axis_size(axi...]
  transfers between devices with their start and end apart: 9 -> 9, of which waited for: 6 -> 4; matrix products, arithmetic and copies ran while one was open for 0% -> 0% of each run, Pallas kernels for 17% -> 24%
where the time goes in v13:
time: 27.3 us
  starting transfers between devices  11.9 us (44%)
  Pallas kernels  9.07 us (33%)
  waiting for transfers between devices  4.95 us (18%)
  between operations  1.41 us (5%)
    pallas_call x8, Pallas kernels, call(): pl.pallas_call(body, out_shape=shapes, input_output_aliases=dict(aliases)...  9.07 us
    ppermute x6, starting transfers between devices, exchange(): lax.ppermute(value, axis, [(i, i ^ step) for i in range(lax.axis_size(axi...  8.16 us
    ppermute x6, waiting for transfers between devices, exchange(): lax.ppermute(value, axis, [(i, i ^ step) for i in range(lax.axis_size(axi...  4.94 us
    ppermute x3, starting transfers between devices, exchange_beside(): lax.ppermute(value, 'grp', [(i, j if 0 <= j < groups else i) for i, j in...  3.74 us
  transfers between devices with their start and end apart: 9, of which 4 were waited for; matrix products, arithmetic and copies ran while one was open for 0% of the time, Pallas kernels for 24%

profile of v13, /device:TPU:0, one launch (start us, length us, event | category | flops | bytes accessed | tf_op | source)
XLA Modules:
  0.0 27.3 jit_solution(10156551611370260707)
XLA Ops:
  0.6 1.0 %shard_map.77 = (bf16[256,128]{1,0:T(8,128)(2,1)S(1)}, s32[192]{0:T(256)S(4)}, s32[192]{0:T(256)S(4)}, f32[48,256,128]{2,1,0:T(8,128)S(1)}) custom-call(bf16[128,128]{1,0:T(8,128)(2,1)} %strengths_ref.1, bf16[128,128]{1,0:T(8,128)(2,1)} %weights_ref.1, s32[192]{0:T(256)} %target_ref.1, s32[192]{0:T(256)} %source_ref.1), custom_call_target="tpu_custom_call" | custom-call | flops 17179869184 | bytes 1048576 | tf_op jit(solution)/shard_map/pallas_call | solution.py:303
  1.6 4.0 %collective-permute-start.2 = (bf16[256,128]{1,0:T(8,128)(2,1)S(1)}, bf16[256,128]{1,0:T(8,128)(2,1)S(1)}, u32[]{:S(2)}, u32[]{:S(2)}) collective-permute-start(bf16[256,128]{1,0:T(8,128)(2,1)S(1)} %get-tuple-element.19.refs_0_), channel_id=1, source_target_pairs={{0,3},{1,2},{2,1},{3,0},{4,7},{5,6},{6,5},{7,4},{8,11},{9,10},{10,... | collective-permute-start | bytes 196616 | tf_op jit(solution)/shard_map/ppermute | solution.py:15
  5.6 0.5 %collective-permute-start.1 = (bf16[256,128]{1,0:T(8,128)(2,1)S(1)}, bf16[256,128]{1,0:T(8,128)(2,1)S(1)}, u32[]{:S(2)}, u32[]{:S(2)}) collective-permute-start(bf16[256,128]{1,0:T(8,128)(2,1)S(1)} %get-tuple-element.19.refs_0_), channel_id=1, source_target_pairs={{0,2},{1,3},{2,0},{3,1},{4,6},{5,7},{6,4},{7,5},{8,10},{9,11},{10,... | collective-permute-start | bytes 196616 | tf_op jit(solution)/shard_map/ppermute | solution.py:15
  6.1 0.1 collective-permute-start
  6.9 2.9 %shard_map.78._.total = f32[48,256,128]{2,1,0:T(8,128)S(1)} custom-call(s32[1]{0:T(128)S(6)} %copy.10.live_ref, s32[192]{0:T(256)S(4)} %get-tuple-element.16.target_ref, s32[192]{0:T(256)S(4)} %get-tuple-element.17.source_ref, bf16[192,2,128,128]{3,2,1,0:T(8,128)(2,1)S(1)} %copy-done, ...), custom_call_target="tpu_custom_call", output_to_operand_aliasing={{}: (4, {})} | custom-call | flops 8589934592 | bytes 1048576 | tf_op jit(solution)/shard_map/pallas_call | solution.py:303
  9.8 0.0 collective-permute-done.2.refs_3_
  9.9 0.0 collective-permute-done.1.refs_2_
  9.9 0.5 %collective-permute-done.refs_1_ = bf16[256,128]{1,0:T(8,128)(2,1)S(1)} collective-permute-done((bf16[256,128]{1,0:T(8,128)(2,1)S(1)}, bf16[256,128]{1,0:T(8,128)(2,1)S(1)}, u32[]{:S(2)}, u32[]{:S(2)}) %collective-permute-start) | collective-permute-done | bytes 65568 | tf_op jit(solution)/shard_map/ppermute | solution.py:15
  10.4 0.1 collective-permute-start.3
  10.5 0.8 %shard_map.80 = (bf16[2,16,256,128]{3,2,1,0:T(8,128)(2,1)S(1)}, bf16[128,1024]{1,0:T(8,128)(2,1)S(1)}, s16[1040,128]{1,0:T(8,128)(2,1)S(1)}) custom-call(bf16[512,128]{1,0:T(8,128)(2,1)S(1)} %shard_map.79._, f32[48,256,128]{2,1,0:T(8,128)S(1)} %shard_map.78._.total, bf16[256,128]{1,0:T(8,128)(2,1)S(1)} %get-tuple-element.19.refs_0_, ...), custom_call_target="tpu_custom_call" | custom-call | flops 8589934592 | bytes 1048576 | tf_op jit(solution)/shard_map/pallas_call | solution.py:303
  11.3 0.7 %collective-permute-start.5 = (s16[1040,128]{1,0:T(8,128)(2,1)S(1)}, s16[1040,128]{1,0:T(8,128)(2,1)S(1)}, u32[]{:S(2)}, u32[]{:S(2)}) collective-permute-start(s16[1040,128]{1,0:T(8,128)(2,1)S(1)} %get-tuple-element.25), channel_id=1, source_target_pairs={{0,0},{4,8},{8,4},{12,16},{16,12},{20,24},{24,20},{28,28},{1,1},{5... | collective-permute-start | bytes 798728 | tf_op jit(solution)/shard_map/ppermute | solution.py:21
  12.0 0.0 collective-permute-done.3._.first_ref
  12.0 1.3 %shard_map.81 = (bf16[2,32,256,128]{3,2,1,0:T(8,128)(2,1)S(1)}, f32[4,128,128]{2,1,0:T(8,128)S(1)}, s16[528,128]{1,0:T(8,128)(2,1)S(1)}) custom-call(bf16[512,128]{1,0:T(8,128)(2,1)S(1)} %collective-permute-done.3._.first_ref, f32[48,256,128]{2,1,0:T(8,128)S(1)} %shard_map.78._.total, bf16[128,1024]{1,0:T(8,128)(2,1)S(1)} %get-tuple-element.21.across_ref), custom_call_target="tpu_custom_call" | custom-call | flops 8589934592 | bytes 1048576 | tf_op jit(solution)/shard_map/pallas_call | solution.py:303
  13.4 3.0 %collective-permute-start.4 = (s16[528,128]{1,0:T(8,128)(2,1)S(1)}, s16[528,128]{1,0:T(8,128)(2,1)S(1)}, u32[]{:S(2)}, u32[]{:S(2)}) collective-permute-start(s16[528,128]{1,0:T(8,128)(2,1)S(1)} %get-tuple-element.24), channel_id=1, source_target_pairs={{0,4},{4,0},{8,12},{12,8},{16,20},{20,16},{24,28},{28,24},{1,5},{5... | collective-permute-start | bytes 405512 | tf_op jit(solution)/shard_map/ppermute | solution.py:21
  16.3 1.3 %shard_map.82.potential_ref = f32[4,128,128]{2,1,0:T(8,128)S(1)} custom-call(bf16[2,32,256,128]{3,2,1,0:T(8,128)(2,1)S(1)} %get-tuple-element.22.pairs_ref, bf16[512,128]{1,0:T(8,128)(2,1)S(1)} %collective-permute-done.3._.first_ref, bf16[256,128]{1,0:T(8,128)(2,1)S(1)} %get-tuple-element.19.refs_0_, bf16[256,128]{1,0:T(8,128)(2,1)S(1)} %collective-permute-done.refs_1_, ...), custom_call_target="tpu_custom_call" | custom-call | bytes 1048576 | tf_op jit(solution)/shard_map/pallas_call | solution.py:303
  17.7 0.0 collective-permute-done.4.first_ref
  17.7 0.9 %shard_map.83 = (f32[256,128]{1,0:T(8,128)S(1)}, s16[272,128]{1,0:T(8,128)(2,1)S(1)}, s16[272,128]{1,0:T(8,128)(2,1)S(1)}, s16[272,128]{1,0:T(8,128)(2,1)S(1)}) custom-call(bf16[2,16,256,128]{3,2,1,0:T(8,128)(2,1)S(1)} %get-tuple-element.20.pairs_ref, f32[4,128,128]{2,1,0:T(8,128)S(1)} %shard_map.82.potential_ref, ...), custom_call_target="tpu_custom_call" | custom-call | bytes 1048576 | tf_op jit(solution)/shard_map/pallas_call | solution.py:303
  18.6 1.8 %collective-permute-start.6 = (s16[272,128]{1,0:T(8,128)(2,1)S(1)}, s16[272,128]{1,0:T(8,128)(2,1)S(1)}, u32[]{:S(2)}, u32[]{:S(2)}) collective-permute-start(s16[272,128]{1,0:T(8,128)(2,1)S(1)} %get-tuple-element.27), channel_id=1, source_target_pairs={{0,3},{1,2},{2,1},{3,0},{4,7},{5,6},{6,5},{7,4},{8,11},{9,10},{10,... | collective-permute-start | bytes 208904 | tf_op jit(solution)/shard_map/ppermute | solution.py:15
  20.4 1.4 %collective-permute-start.7 = (s16[272,128]{1,0:T(8,128)(2,1)S(1)}, s16[272,128]{1,0:T(8,128)(2,1)S(1)}, u32[]{:S(2)}, u32[]{:S(2)}) collective-permute-start(s16[272,128]{1,0:T(8,128)(2,1)S(1)} %get-tuple-element.28), channel_id=1, source_target_pairs={{0,2},{1,3},{2,0},{3,1},{4,6},{5,7},{6,4},{7,5},{8,10},{9,11},{10,... | collective-permute-start | bytes 208904 | tf_op jit(solution)/shard_map/ppermute | solution.py:15
  21.8 0.3 %collective-permute-start.8 = (s16[272,128]{1,0:T(8,128)(2,1)S(1)}, s16[272,128]{1,0:T(8,128)(2,1)S(1)}, u32[]{:S(2)}, u32[]{:S(2)}) collective-permute-start(s16[272,128]{1,0:T(8,128)(2,1)S(1)} %get-tuple-element.29), channel_id=1, source_target_pairs={{0,1},{1,0},{2,3},{3,2},{4,5},{5,4},{6,7},{7,6},{8,9},{9,8},{10,11... | collective-permute-start | bytes 208904 | tf_op jit(solution)/shard_map/ppermute | solution.py:15
  22.1 1.7 %collective-permute-done.6.refs_0_ = s16[272,128]{1,0:T(8,128)(2,1)S(1)} collective-permute-done((s16[272,128]{1,0:T(8,128)(2,1)S(1)}, s16[272,128]{1,0:T(8,128)(2,1)S(1)}, u32[]{:S(2)}, u32[]{:S(2)}) %collective-permute-start.6) | collective-permute-done | bytes 69664 | tf_op jit(solution)/shard_map/ppermute | solution.py:15
  23.8 2.2 %collective-permute-done.7.refs_1_ = s16[272,128]{1,0:T(8,128)(2,1)S(1)} collective-permute-done((s16[272,128]{1,0:T(8,128)(2,1)S(1)}, s16[272,128]{1,0:T(8,128)(2,1)S(1)}, u32[]{:S(2)}, u32[]{:S(2)}) %collective-permute-start.7) | collective-permute-done | bytes 69664 | tf_op jit(solution)/shard_map/ppermute | solution.py:15
  26.0 0.5 %collective-permute-done.8.refs_2_ = s16[272,128]{1,0:T(8,128)(2,1)S(1)} collective-permute-done((s16[272,128]{1,0:T(8,128)(2,1)S(1)}, s16[272,128]{1,0:T(8,128)(2,1)S(1)}, u32[]{:S(2)}, u32[]{:S(2)}) %collective-permute-start.8) | collective-permute-done | bytes 69664 | tf_op jit(solution)/shard_map/ppermute | solution.py:15
  26.6 0.7 %shard_map.84 = (f32[128,128]{1,0:T(8,128)}, f32[128,128]{1,0:T(8,128)}) custom-call(f32[256,128]{1,0:T(8,128)S(1)} %get-tuple-element.26.own_ref, s16[272,128]{1,0:T(8,128)(2,1)S(1)} %collective-permute-done.6.refs_0_, s16[272,128]{1,0:T(8,128)(2,1)S(1)} %collective-permute-done.7.refs_1_, s16[272,128]{1,0:T(8,128)(2,1)S(1)} %collective-permute-done.8.refs_2_), custom_call_target="tpu_custom_call" | custom-call | bytes 1048576 | tf_op jit(solution)/shard_map/pallas_call | solution.py:303
  (4 shorter events, 0.0 us)
Async XLA Ops:
  0.6 6.3 %copy-start = (bf16[192,2,128,128]{3,2,1,0:T(8,128)(2,1)S(1)}, bf16[192,2,128,128]{3,2,1,0:T(8,128)(2,1)}, u32[]{:S(2)}) copy-start(bf16[192,2,128,128]{3,2,1,0:T(8,128)(2,1)} %kernels_ref.1) | copy-start | bytes 37748740
  1.6 8.2 %collective-permute-start.2 = (bf16[256,128]{1,0:T(8,128)(2,1)S(1)}, bf16[256,128]{1,0:T(8,128)(2,1)S(1)}, u32[]{:S(2)}, u32[]{:S(2)}) collective-permute-start(bf16[256,128]{1,0:T(8,128)(2,1)S(1)} %get-tuple-element.19.refs_0_), channel_id=1, source_target_pairs={{0,3},{1,2},{2,1},{3,0},{4,7},{5,6},{6,5},{7,4},{8,11},{9,10},{10,... | collective-permute-start | bytes 196616 | tf_op jit(solution)/shard_map/ppermute | solution.py:15
  5.6 4.3 %collective-permute-start.1 = (bf16[256,128]{1,0:T(8,128)(2,1)S(1)}, bf16[256,128]{1,0:T(8,128)(2,1)S(1)}, u32[]{:S(2)}, u32[]{:S(2)}) collective-permute-start(bf16[256,128]{1,0:T(8,128)(2,1)S(1)} %get-tuple-element.19.refs_0_), channel_id=1, source_target_pairs={{0,2},{1,3},{2,0},{3,1},{4,6},{5,7},{6,4},{7,5},{8,10},{9,11},{10,... | collective-permute-start | bytes 196616 | tf_op jit(solution)/shard_map/ppermute | solution.py:15
  6.1 4.3 %collective-permute-start = (bf16[256,128]{1,0:T(8,128)(2,1)S(1)}, bf16[256,128]{1,0:T(8,128)(2,1)S(1)}, u32[]{:S(2)}, u32[]{:S(2)}) collective-permute-start(bf16[256,128]{1,0:T(8,128)(2,1)S(1)} %get-tuple-element.19.refs_0_), channel_id=1, source_target_pairs={{0,1},{1,0},{2,3},{3,2},{4,5},{5,4},{6,7},{7,6},{8,9},{9,8},{10,11... | collective-permute-start | bytes 196616 | tf_op jit(solution)/shard_map/ppermute | solution.py:15
  10.4 1.6 %collective-permute-start.3 = (bf16[512,128]{1,0:T(8,128)(2,1)S(1)}, bf16[512,128]{1,0:T(8,128)(2,1)S(1)}, u32[]{:S(2)}, u32[]{:S(2)}) collective-permute-start(bf16[512,128]{1,0:T(8,128)(2,1)S(1)} %shard_map.79._), channel_id=1, source_target_pairs={{0,4},{4,0},{8,12},{12,8},{16,20},{20,16},{24,28},{28,24},{1,5},{5... | collective-permute-start | bytes 393224 | tf_op jit(solution)/shard_map/ppermute | solution.py:21
  11.3 6.4 %collective-permute-start.5 = (s16[1040,128]{1,0:T(8,128)(2,1)S(1)}, s16[1040,128]{1,0:T(8,128)(2,1)S(1)}, u32[]{:S(2)}, u32[]{:S(2)}) collective-permute-start(s16[1040,128]{1,0:T(8,128)(2,1)S(1)} %get-tuple-element.25), channel_id=1, source_target_pairs={{0,0},{4,8},{8,4},{12,16},{16,12},{20,24},{24,20},{28,28},{1,1},{5... | collective-permute-start | bytes 798728 | tf_op jit(solution)/shard_map/ppermute | solution.py:21
  13.4 4.3 %collective-permute-start.4 = (s16[528,128]{1,0:T(8,128)(2,1)S(1)}, s16[528,128]{1,0:T(8,128)(2,1)S(1)}, u32[]{:S(2)}, u32[]{:S(2)}) collective-permute-start(s16[528,128]{1,0:T(8,128)(2,1)S(1)} %get-tuple-element.24), channel_id=1, source_target_pairs={{0,4},{4,0},{8,12},{12,8},{16,20},{20,16},{24,28},{28,24},{1,5},{5... | collective-permute-start | bytes 405512 | tf_op jit(solution)/shard_map/ppermute | solution.py:21
  18.6 5.3 %collective-permute-start.6 = (s16[272,128]{1,0:T(8,128)(2,1)S(1)}, s16[272,128]{1,0:T(8,128)(2,1)S(1)}, u32[]{:S(2)}, u32[]{:S(2)}) collective-permute-start(s16[272,128]{1,0:T(8,128)(2,1)S(1)} %get-tuple-element.27), channel_id=1, source_target_pairs={{0,3},{1,2},{2,1},{3,0},{4,7},{5,6},{6,5},{7,4},{8,11},{9,10},{10,... | collective-permute-start | bytes 208904 | tf_op jit(solution)/shard_map/ppermute | solution.py:15
  20.4 5.7 %collective-permute-start.7 = (s16[272,128]{1,0:T(8,128)(2,1)S(1)}, s16[272,128]{1,0:T(8,128)(2,1)S(1)}, u32[]{:S(2)}, u32[]{:S(2)}) collective-permute-start(s16[272,128]{1,0:T(8,128)(2,1)S(1)} %get-tuple-element.28), channel_id=1, source_target_pairs={{0,2},{1,3},{2,0},{3,1},{4,6},{5,7},{6,4},{7,5},{8,10},{9,11},{10,... | collective-permute-start | bytes 208904 | tf_op jit(solution)/shard_map/ppermute | solution.py:15
  21.8 4.8 %collective-permute-start.8 = (s16[272,128]{1,0:T(8,128)(2,1)S(1)}, s16[272,128]{1,0:T(8,128)(2,1)S(1)}, u32[]{:S(2)}, u32[]{:S(2)}) collective-permute-start(s16[272,128]{1,0:T(8,128)(2,1)S(1)} %get-tuple-element.29), channel_id=1, source_target_pairs={{0,1},{1,0},{2,3},{3,2},{4,5},{5,4},{6,7},{7,6},{8,9},{9,8},{10,11... | collective-permute-start | bytes 208904 | tf_op jit(solution)/shard_map/ppermute | solution.py:15

commit v14 on v13

--- a/solution.py
+++ b/solution.py
@@ -8,7 +8,7 @@
 from jax.sharding import PartitionSpec as P
 
 EXPONENT_ROWS = 16
-TINY = 2.0**-100
+TINY = 2.0**-110
 
 
 def exchange(value, axis, step):
@@ -209,14 +209,16 @@
         potential_ref[t] = value
 
 
-def parts_of(blocks, potential, adjoint, own_ref, *outs):
+def parts_of(blocks, potential, adjoint, own_ref, out_ref):
     panels = potential[0].shape[0]
+    me = lax.axis_index("clu")
     for i in range(blocks):
         own_ref[rows_of(i, panels)] = potential[i]
         own_ref[rows_of(blocks + i, panels)] = adjoint[i]
-    for k, out_ref in enumerate(outs, 1):
+    out_ref[me] = jnp.zeros(out_ref.shape[1:], out_ref.dtype)
+    for k in range(1, out_ref.shape[0]):
         rows = slice(k * blocks, (k + 1) * blocks)
-        encode(potential[rows] + adjoint[rows], out_ref)
+        encode(potential[rows] + adjoint[rows], out_ref.at[me ^ k])
 
 
 def parts_kernel(blocks, pairs_ref, potential_ref, middle_ref, first_ref, second_ref, *outs):
@@ -276,11 +278,11 @@
         encode([adjoint_ref[first + i] for i in range(count)], out_ref)
 
 
-def finish_kernel(blocks, panels, own_ref, *refs):
-    *parts, potential_ref, adjoint_ref = refs
+def finish_kernel(blocks, panels, own_ref, parts_ref, potential_ref, adjoint_ref):
+    me = lax.axis_index("clu")
     total = [own_ref[rows_of(i, panels)] for i in range(2 * blocks)]
-    for ref in parts:
-        total = [a + b for a, b in zip(total, decode(ref, 2 * blocks, panels))]
+    for k in range(1, parts_ref.shape[0]):
+        total = [a + b for a, b in zip(total, decode(parts_ref.at[me ^ k], 2 * blocks, panels))]
     for b in range(blocks):
         potential_ref[rows_of(b, panels)] = total[b]
         adjoint_ref[rows_of(b, panels)] = total[blocks + b].T
@@ -396,14 +398,14 @@
         lower, upper = call(code_kernel, (coded(group_blocks),) * 2, (adjoint,))
         upper, lower = exchange_beside(upper, 1), exchange_beside(lower, 0)
         parts_body, parts_args = slots_parts_kernel, (potential, adjoint, lower, upper)
-    mine, *parts = call(
+    mine, parts = call(
         functools.partial(parts_body, blocks),
-        (shape(2 * blocks * panels, width),) + (coded(2 * blocks),) * (clusters - 1),
+        (shape(2 * blocks * panels, width), shape(clusters, *coded(2 * blocks).shape, kind=jnp.int16)),
         parts_args,
     )
-    parts = [exchange(parts[k - 1], "clu", k) for k in range(clusters - 1, 0, -1)]
+    parts = lax.all_to_all(parts, "clu", 0, 0, tiled=True)
     out = shape(blocks * panels, width)
-    return tuple(call(functools.partial(finish_kernel, blocks, panels), (out, out), (mine, *parts)))
+    return tuple(call(functools.partial(finish_kernel, blocks, panels), (out, out), (mine, parts)))
 
 
 def solution(mesh):

time: 27.3 us -> 30.1 us (1.10); the launches traced: 27.3 us -> 30.5 us
  blocking collectives: 0 us -> 11.3 us
  waiting for transfers between devices: 4.95 us -> 0.18 us
  starting transfers between devices: 11.9 us -> 8.34 us
    all_to_all x0 -> x1, blocking collectives: none -> 11.3 us  [local(): parts = lax.all_to_all(parts, 'clu', 0, 0, tiled=True)]
    ppermute x6 -> x3, waiting for transfers between devices: 4.94 us -> 0.18 us  [exchange(): lax.ppermute(value, axis, [(i, i ^ step) for i in range(lax.axis_size(axi...]
    ppermute x6 -> x3, starting transfers between devices: 8.16 us -> 4.6 us  [exchange(): lax.ppermute(value, axis, [(i, i ^ step) for i in range(lax.axis_size(axi...]
  transfers between devices with their start and end apart: 9 -> 6, of which waited for: 4 -> 1; matrix products, arithmetic and copies ran while one was open for 0% -> 0% of each run, Pallas kernels for 24% -> 22%
where the time goes in v14:
time: 30.1 us; the launch traced here: 30.5 us
  blocking collectives  11.3 us (38%)
  Pallas kernels  9.34 us (31%)
  starting transfers between devices  8.34 us (28%)
  between operations  1.41 us (5%)
    all_to_all x1, blocking collectives, local(): parts = lax.all_to_all(parts, 'clu', 0, 0, tiled=True)  11.3 us
    pallas_call x8, Pallas kernels, call(): pl.pallas_call(body, out_shape=shapes, input_output_aliases=dict(aliases)...  9.34 us
    ppermute x3, starting transfers between devices, exchange(): lax.ppermute(value, axis, [(i, i ^ step) for i in range(lax.axis_size(axi...  4.6 us
    ppermute x3, starting transfers between devices, exchange_beside(): lax.ppermute(value, 'grp', [(i, j if 0 <= j < groups else i) for i, j in...  3.74 us
  transfers between devices with their start and end apart: 6, of which 1 were waited for; matrix products, arithmetic and copies ran while one was open for 0% of the time, Pallas kernels for 22%

profile of v14, /device:TPU:0, one launch (start us, length us, event | category | flops | bytes accessed | tf_op | source)
XLA Modules:
  0.0 30.5 jit_solution(4637452532183728235)
XLA Ops:
  0.6 0.0 copy-start
  0.6 1.0 %shard_map.77 = (bf16[256,128]{1,0:T(8,128)(2,1)S(1)}, s32[192]{0:T(256)S(4)}, s32[192]{0:T(256)S(4)}, f32[48,256,128]{2,1,0:T(8,128)S(1)}) custom-call(bf16[128,128]{1,0:T(8,128)(2,1)} %strengths_ref.1, bf16[128,128]{1,0:T(8,128)(2,1)} %weights_ref.1, s32[192]{0:T(256)} %target_ref.1, s32[192]{0:T(256)} %source_ref.1), custom_call_target="tpu_custom_call" | custom-call | flops 17179869184 | bytes 1048576 | tf_op jit(solution)/shard_map/pallas_call | solution.py:305
  1.6 4.0 %collective-permute-start.2 = (bf16[256,128]{1,0:T(8,128)(2,1)S(1)}, bf16[256,128]{1,0:T(8,128)(2,1)S(1)}, u32[]{:S(2)}, u32[]{:S(2)}) collective-permute-start(bf16[256,128]{1,0:T(8,128)(2,1)S(1)} %get-tuple-element.17.refs_0_), channel_id=1, source_target_pairs={{0,3},{1,2},{2,1},{3,0},{4,7},{5,6},{6,5},{7,4},{8,11},{9,10},{10,... | collective-permute-start | bytes 196616 | tf_op jit(solution)/shard_map/ppermute | solution.py:15
  5.6 0.5 %collective-permute-start.1 = (bf16[256,128]{1,0:T(8,128)(2,1)S(1)}, bf16[256,128]{1,0:T(8,128)(2,1)S(1)}, u32[]{:S(2)}, u32[]{:S(2)}) collective-permute-start(bf16[256,128]{1,0:T(8,128)(2,1)S(1)} %get-tuple-element.17.refs_0_), channel_id=1, source_target_pairs={{0,2},{1,3},{2,0},{3,1},{4,6},{5,7},{6,4},{7,5},{8,10},{9,11},{10,... | collective-permute-start | bytes 196616 | tf_op jit(solution)/shard_map/ppermute | solution.py:15
  6.1 0.1 collective-permute-start
  6.9 0.0 copy-done
  6.9 3.3 %shard_map.78._.total = f32[48,256,128]{2,1,0:T(8,128)S(1)} custom-call(s32[1]{0:T(128)S(6)} %copy.10.live_ref, s32[192]{0:T(256)S(4)} %get-tuple-element.14.target_ref, s32[192]{0:T(256)S(4)} %get-tuple-element.15.source_ref, bf16[192,2,128,128]{3,2,1,0:T(8,128)(2,1)S(1)} %copy-done, ...), custom_call_target="tpu_custom_call", output_to_operand_aliasing={{}: (4, {})} | custom-call | flops 8589934592 | bytes 1048576 | tf_op jit(solution)/shard_map/pallas_call | solution.py:305
  10.2 0.0 collective-permute-done.2.refs_3_
  10.2 0.0 collective-permute-done.1.refs_2_
  10.2 0.2 collective-permute-done.refs_1_
  10.4 0.1 collective-permute-start.3
  10.5 0.8 %shard_map.80 = (bf16[2,16,256,128]{3,2,1,0:T(8,128)(2,1)S(1)}, bf16[128,1024]{1,0:T(8,128)(2,1)S(1)}, s16[1040,128]{1,0:T(8,128)(2,1)S(1)}) custom-call(bf16[512,128]{1,0:T(8,128)(2,1)S(1)} %shard_map.79._, f32[48,256,128]{2,1,0:T(8,128)S(1)} %shard_map.78._.total, bf16[256,128]{1,0:T(8,128)(2,1)S(1)} %get-tuple-element.17.refs_0_, ...), custom_call_target="tpu_custom_call" | custom-call | flops 8589934592 | bytes 1048576 | tf_op jit(solution)/shard_map/pallas_call | solution.py:305
  11.3 0.7 %collective-permute-start.5 = (s16[1040,128]{1,0:T(8,128)(2,1)S(1)}, s16[1040,128]{1,0:T(8,128)(2,1)S(1)}, u32[]{:S(2)}, u32[]{:S(2)}) collective-permute-start(s16[1040,128]{1,0:T(8,128)(2,1)S(1)} %get-tuple-element.23), channel_id=1, source_target_pairs={{0,0},{4,8},{8,4},{12,16},{16,12},{20,24},{24,20},{28,28},{1,1},{5... | collective-permute-start | bytes 798728 | tf_op jit(solution)/shard_map/ppermute | solution.py:21
  12.0 0.0 collective-permute-done.3._.first_ref
  12.0 1.3 %shard_map.81 = (bf16[2,32,256,128]{3,2,1,0:T(8,128)(2,1)S(1)}, f32[4,128,128]{2,1,0:T(8,128)S(1)}, s16[528,128]{1,0:T(8,128)(2,1)S(1)}) custom-call(bf16[512,128]{1,0:T(8,128)(2,1)S(1)} %collective-permute-done.3._.first_ref, f32[48,256,128]{2,1,0:T(8,128)S(1)} %shard_map.78._.total, bf16[128,1024]{1,0:T(8,128)(2,1)S(1)} %get-tuple-element.19.across_ref), custom_call_target="tpu_custom_call" | custom-call | flops 8589934592 | bytes 1048576 | tf_op jit(solution)/shard_map/pallas_call | solution.py:305
  13.4 3.0 %collective-permute-start.4 = (s16[528,128]{1,0:T(8,128)(2,1)S(1)}, s16[528,128]{1,0:T(8,128)(2,1)S(1)}, u32[]{:S(2)}, u32[]{:S(2)}) collective-permute-start(s16[528,128]{1,0:T(8,128)(2,1)S(1)} %get-tuple-element.22), channel_id=1, source_target_pairs={{0,4},{4,0},{8,12},{12,8},{16,20},{20,16},{24,28},{28,24},{1,5},{5... | collective-permute-start | bytes 405512 | tf_op jit(solution)/shard_map/ppermute | solution.py:21
  16.3 1.3 %shard_map.82.potential_ref = f32[4,128,128]{2,1,0:T(8,128)S(1)} custom-call(bf16[2,32,256,128]{3,2,1,0:T(8,128)(2,1)S(1)} %get-tuple-element.20.pairs_ref, bf16[512,128]{1,0:T(8,128)(2,1)S(1)} %collective-permute-done.3._.first_ref, bf16[256,128]{1,0:T(8,128)(2,1)S(1)} %get-tuple-element.17.refs_0_, bf16[256,128]{1,0:T(8,128)(2,1)S(1)} %collective-permute-done.refs_1_, ...), custom_call_target="tpu_custom_call" | custom-call | bytes 1048576 | tf_op jit(solution)/shard_map/pallas_call | solution.py:305
  17.7 0.0 collective-permute-done.4.first_ref
  17.7 0.0 collective-permute-done.5.second_ref
  17.7 0.8 %shard_map.83 = (f32[256,128]{1,0:T(8,128)S(1)}, s16[4,272,128]{2,1,0:T(8,128)(2,1)S(1)}) custom-call(bf16[2,16,256,128]{3,2,1,0:T(8,128)(2,1)S(1)} %get-tuple-element.18.pairs_ref, f32[4,128,128]{2,1,0:T(8,128)S(1)} %shard_map.82.potential_ref, f32[4,128,128]{2,1,0:T(8,128)S(1)} %get-tuple-element.21.middle_ref, ...), custom_call_target="tpu_custom_call" | custom-call | bytes 1048576 | tf_op jit(solution)/shard_map/pallas_call | solution.py:305
  18.5 11.3 %all_to_all.5.parts_ref = s16[4,272,128]{2,1,0:T(8,128)(2,1)S(1)} all-to-all(s16[4,272,128]{2,1,0:T(8,128)(2,1)S(1)} %get-tuple-element.25), channel_id=1, replica_groups=mesh['grp'=8,'clu'=4] {'clu'}, dimensions={0} | all-to-all | bytes 557056 | tf_op jit(solution)/shard_map/all_to_all | solution.py:406
  29.8 0.7 %shard_map.84 = (f32[128,128]{1,0:T(8,128)}, f32[128,128]{1,0:T(8,128)}) custom-call(f32[256,128]{1,0:T(8,128)S(1)} %get-tuple-element.24.own_ref, s16[4,272,128]{2,1,0:T(8,128)(2,1)S(1)} %all_to_all.5.parts_ref), custom_call_target="tpu_custom_call" | custom-call | bytes 1048576 | tf_op jit(solution)/shard_map/pallas_call | solution.py:305
  (1 shorter events, 0.0 us)
Async XLA Ops:
  0.6 6.3 %copy-start = (bf16[192,2,128,128]{3,2,1,0:T(8,128)(2,1)S(1)}, bf16[192,2,128,128]{3,2,1,0:T(8,128)(2,1)}, u32[]{:S(2)}) copy-start(bf16[192,2,128,128]{3,2,1,0:T(8,128)(2,1)} %kernels_ref.1) | copy-start | bytes 37748740
  1.6 8.5 %collective-permute-start.2 = (bf16[256,128]{1,0:T(8,128)(2,1)S(1)}, bf16[256,128]{1,0:T(8,128)(2,1)S(1)}, u32[]{:S(2)}, u32[]{:S(2)}) collective-permute-start(bf16[256,128]{1,0:T(8,128)(2,1)S(1)} %get-tuple-element.17.refs_0_), channel_id=1, source_target_pairs={{0,3},{1,2},{2,1},{3,0},{4,7},{5,6},{6,5},{7,4},{8,11},{9,10},{10,... | collective-permute-start | bytes 196616 | tf_op jit(solution)/shard_map/ppermute | solution.py:15
  5.6 4.6 %collective-permute-start.1 = (bf16[256,128]{1,0:T(8,128)(2,1)S(1)}, bf16[256,128]{1,0:T(8,128)(2,1)S(1)}, u32[]{:S(2)}, u32[]{:S(2)}) collective-permute-start(bf16[256,128]{1,0:T(8,128)(2,1)S(1)} %get-tuple-element.17.refs_0_), channel_id=1, source_target_pairs={{0,2},{1,3},{2,0},{3,1},{4,6},{5,7},{6,4},{7,5},{8,10},{9,11},{10,... | collective-permute-start | bytes 196616 | tf_op jit(solution)/shard_map/ppermute | solution.py:15
  6.1 4.3 %collective-permute-start = (bf16[256,128]{1,0:T(8,128)(2,1)S(1)}, bf16[256,128]{1,0:T(8,128)(2,1)S(1)}, u32[]{:S(2)}, u32[]{:S(2)}) collective-permute-start(bf16[256,128]{1,0:T(8,128)(2,1)S(1)} %get-tuple-element.17.refs_0_), channel_id=1, source_target_pairs={{0,1},{1,0},{2,3},{3,2},{4,5},{5,4},{6,7},{7,6},{8,9},{9,8},{10,11... | collective-permute-start | bytes 196616 | tf_op jit(solution)/shard_map/ppermute | solution.py:15
  10.4 1.6 %collective-permute-start.3 = (bf16[512,128]{1,0:T(8,128)(2,1)S(1)}, bf16[512,128]{1,0:T(8,128)(2,1)S(1)}, u32[]{:S(2)}, u32[]{:S(2)}) collective-permute-start(bf16[512,128]{1,0:T(8,128)(2,1)S(1)} %shard_map.79._), channel_id=1, source_target_pairs={{0,4},{4,0},{8,12},{12,8},{16,20},{20,16},{24,28},{28,24},{1,5},{5... | collective-permute-start | bytes 393224 | tf_op jit(solution)/shard_map/ppermute | solution.py:21
  11.3 6.4 %collective-permute-start.5 = (s16[1040,128]{1,0:T(8,128)(2,1)S(1)}, s16[1040,128]{1,0:T(8,128)(2,1)S(1)}, u32[]{:S(2)}, u32[]{:S(2)}) collective-permute-start(s16[1040,128]{1,0:T(8,128)(2,1)S(1)} %get-tuple-element.23), channel_id=1, source_target_pairs={{0,0},{4,8},{8,4},{12,16},{16,12},{20,24},{24,20},{28,28},{1,1},{5... | collective-permute-start | bytes 798728 | tf_op jit(solution)/shard_map/ppermute | solution.py:21
  13.4 4.3 %collective-permute-start.4 = (s16[528,128]{1,0:T(8,128)(2,1)S(1)}, s16[528,128]{1,0:T(8,128)(2,1)S(1)}, u32[]{:S(2)}, u32[]{:S(2)}) collective-permute-start(s16[528,128]{1,0:T(8,128)(2,1)S(1)} %get-tuple-element.22), channel_id=1, source_target_pairs={{0,4},{4,0},{8,12},{12,8},{16,20},{20,16},{24,28},{28,24},{1,5},{5... | collective-permute-start | bytes 405512 | tf_op jit(solution)/shard_map/ppermute | solution.py:21

commit v15 on v13

--- a/solution.py
+++ b/solution.py
@@ -8,7 +8,7 @@
 from jax.sharding import PartitionSpec as P
 
 EXPONENT_ROWS = 16
-TINY = 2.0**-100
+TINY = 2.0**-110
 
 
 def exchange(value, axis, step):
@@ -179,11 +179,9 @@
     encode(strengths + list(adjoint_of(pairs_ref, across_ref, 0, count)), out_ref)
 
 
-def first_kernel(count, _, total, across_ref, pairs_ref, middle_ref, out_ref):
+def first_kernel(count, _, total, across_ref, pairs_ref, out_ref):
     split(total, 0, pairs_ref)
     encode(list(adjoint_of(pairs_ref, across_ref, 0, count)), out_ref)
-    for i, value in enumerate(adjoint_of(pairs_ref, across_ref, count, count)):
-        middle_ref[i] = value
 
 
 def forward_of(pairs_ref, strengths, targets):
@@ -200,13 +198,18 @@
         yield product[:panels] + product[panels:]
 
 
-def forward_kernel(blocks, pairs_ref, first_ref, *refs):
-    *gathered, potential_ref = refs
+def inner_kernel(blocks, total, across_ref, first_pairs_ref, first_ref, *refs):
+    *gathered, potential_ref, middle_ref, pairs_ref = refs
     targets, panels = potential_ref.shape[:2]
+    split(total, pairs_ref.shape[1], pairs_ref)
+    for i, value in enumerate(adjoint_of(pairs_ref, across_ref, 0, targets)):
+        middle_ref[i] = value
     strengths = [first_ref[rows_of(i, panels)] for i in range(targets)]
-    strengths += part_of(gathered, blocks, panels, 0)
-    for t, value in enumerate(forward_of(pairs_ref, strengths, targets)):
+    own = list(part_of(gathered, blocks, panels, 0))
+    for t, value in enumerate(forward_of(first_pairs_ref, strengths, targets)):
         potential_ref[t] = value
+    for t, value in enumerate(forward_of(pairs_ref, own, targets)):
+        potential_ref[t] += value
 
 
 def parts_of(blocks, potential, adjoint, own_ref, *outs):
@@ -354,11 +357,11 @@
         own = group_strengths(total)
         first = exchange_beside(own, 0)
         total = pltpu.with_memory_space_constraint(total, pltpu.VMEM)
-        second_pairs = pairs // 3
+        kept_shape = pltpu.VMEM((2, pairs // 3, 2 * panels, panels), bf16)
         kept_second, across, upper = call(
             functools.partial(second_kernel, blocks, panels, group_blocks),
             (
-                pltpu.VMEM((2, second_pairs, 2 * panels, panels), bf16),
+                kept_shape,
                 shape(width, 2 * group_blocks * panels, kind=bf16),
                 coded(2 * group_blocks),
             ),
@@ -366,15 +369,20 @@
             [in_hbm] + [in_vmem] * (1 + clusters),
             flops=1 << 33,
         )
-        kept, middle, lower = call(
+        kept_first, lower = call(
             functools.partial(first_kernel, group_blocks),
-            (pltpu.VMEM((2, pairs - second_pairs, 2 * panels, panels), bf16), block_sums, coded(group_blocks)),
+            (kept_shape, coded(group_blocks)),
             (first, total, across),
             [in_hbm] + [in_vmem] * 2,
             flops=1 << 33,
         )
-        kept, kept_second = (pltpu.with_memory_space_constraint(x, pltpu.VMEM) for x in (kept, kept_second))
-        potential = call(functools.partial(forward_kernel, blocks), block_sums, (kept, first, *gathered))
+        kept_first, kept_second = (pltpu.with_memory_space_constraint(x, pltpu.VMEM) for x in (kept_first, kept_second))
+        potential, middle = call(
+            functools.partial(inner_kernel, blocks),
+            (block_sums, block_sums),
+            (total, across, kept_first, first, *gathered),
+            scratch=[kept_shape],
+        )
         upper, lower = exchange_beside(upper, 1), exchange_beside(lower, 0)
         parts_body, parts_args = parts_kernel, (kept_second, potential, middle, lower, upper)
     else:

time: 27.3 us -> 27.4 us (level); the launches traced: 27.3 us -> 27 us
  Pallas kernels: 9.07 us -> 8.41 us
    pallas_call x8, Pallas kernels: 9.07 us -> 8.41 us  [call(): pl.pallas_call(body, out_shape=shapes, input_output_aliases=dict(aliases)...]
  transfers between devices with their start and end apart: 9 -> 9, of which waited for: 4 -> 4; matrix products, arithmetic and copies ran while one was open for 0% -> 0% of each run, Pallas kernels for 24% -> 21%
where the time goes in v15:
time: 27.4 us; the launch traced here: 27 us
  starting transfers between devices  12.1 us (44%)
  Pallas kernels  8.41 us (31%)
  waiting for transfers between devices  5.01 us (18%)
  between operations  1.4 us (5%)
    pallas_call x8, Pallas kernels, call(): pl.pallas_call(body, out_shape=shapes, input_output_aliases=dict(aliases)...  8.41 us
    ppermute x6, starting transfers between devices, exchange(): lax.ppermute(value, axis, [(i, i ^ step) for i in range(lax.axis_size(axi...  8.16 us
    ppermute x6, waiting for transfers between devices, exchange(): lax.ppermute(value, axis, [(i, i ^ step) for i in range(lax.axis_size(axi...  5 us
    ppermute x3, starting transfers between devices, exchange_beside(): lax.ppermute(value, 'grp', [(i, j if 0 <= j < groups else i) for i, j in...  3.99 us
  transfers between devices with their start and end apart: 9, of which 4 were waited for; matrix products, arithmetic and copies ran while one was open for 0% of the time, Pallas kernels for 21%

profile of v15, /device:TPU:0, one launch (start us, length us, event | category | flops | bytes accessed | tf_op | source)
XLA Modules:
  0.0 27.0 jit_solution(17916935501245469759)
XLA Ops:
  0.6 1.0 %shard_map.77 = (bf16[256,128]{1,0:T(8,128)(2,1)S(1)}, s32[192]{0:T(256)S(4)}, s32[192]{0:T(256)S(4)}, f32[48,256,128]{2,1,0:T(8,128)S(1)}) custom-call(bf16[128,128]{1,0:T(8,128)(2,1)} %strengths_ref.1, bf16[128,128]{1,0:T(8,128)(2,1)} %weights_ref.1, s32[192]{0:T(256)} %target_ref.1, s32[192]{0:T(256)} %source_ref.1), custom_call_target="tpu_custom_call" | custom-call | flops 17179869184 | bytes 1048576 | tf_op jit(solution)/shard_map/pallas_call | solution.py:306
  1.6 4.0 %collective-permute-start.2 = (bf16[256,128]{1,0:T(8,128)(2,1)S(1)}, bf16[256,128]{1,0:T(8,128)(2,1)S(1)}, u32[]{:S(2)}, u32[]{:S(2)}) collective-permute-start(bf16[256,128]{1,0:T(8,128)(2,1)S(1)} %get-tuple-element.20.refs_0_), channel_id=1, source_target_pairs={{0,3},{1,2},{2,1},{3,0},{4,7},{5,6},{6,5},{7,4},{8,11},{9,10},{10,... | collective-permute-start | bytes 196616 | tf_op jit(solution)/shard_map/ppermute | solution.py:15
  5.6 0.5 %collective-permute-start.1 = (bf16[256,128]{1,0:T(8,128)(2,1)S(1)}, bf16[256,128]{1,0:T(8,128)(2,1)S(1)}, u32[]{:S(2)}, u32[]{:S(2)}) collective-permute-start(bf16[256,128]{1,0:T(8,128)(2,1)S(1)} %get-tuple-element.20.refs_0_), channel_id=1, source_target_pairs={{0,2},{1,3},{2,0},{3,1},{4,6},{5,7},{6,4},{7,5},{8,10},{9,11},{10,... | collective-permute-start | bytes 196616 | tf_op jit(solution)/shard_map/ppermute | solution.py:15
  6.1 0.1 collective-permute-start
  6.9 2.3 %shard_map.78._.total = f32[48,256,128]{2,1,0:T(8,128)S(1)} custom-call(s32[1]{0:T(128)S(6)} %copy.10.live_ref, s32[192]{0:T(256)S(4)} %get-tuple-element.17.target_ref, s32[192]{0:T(256)S(4)} %get-tuple-element.18.source_ref, bf16[192,2,128,128]{3,2,1,0:T(8,128)(2,1)S(1)} %copy-done, ...), custom_call_target="tpu_custom_call", output_to_operand_aliasing={{}: (4, {})} | custom-call | flops 8589934592 | bytes 1048576 | tf_op jit(solution)/shard_map/pallas_call | solution.py:306
  9.2 0.0 collective-permute-done.2.refs_3_
  9.3 0.6 %collective-permute-done.1.refs_2_ = bf16[256,128]{1,0:T(8,128)(2,1)S(1)} collective-permute-done((bf16[256,128]{1,0:T(8,128)(2,1)S(1)}, bf16[256,128]{1,0:T(8,128)(2,1)S(1)}, u32[]{:S(2)}, u32[]{:S(2)}) %collective-permute-start.1) | collective-permute-done | bytes 65568 | tf_op jit(solution)/shard_map/ppermute | solution.py:15
  9.9 0.5 %collective-permute-done.refs_1_ = bf16[256,128]{1,0:T(8,128)(2,1)S(1)} collective-permute-done((bf16[256,128]{1,0:T(8,128)(2,1)S(1)}, bf16[256,128]{1,0:T(8,128)(2,1)S(1)}, u32[]{:S(2)}, u32[]{:S(2)}) %collective-permute-start) | collective-permute-done | bytes 65568 | tf_op jit(solution)/shard_map/ppermute | solution.py:15
  10.4 0.1 collective-permute-start.3
  10.5 0.8 %shard_map.80 = (bf16[2,16,256,128]{3,2,1,0:T(8,128)(2,1)S(1)}, bf16[128,1024]{1,0:T(8,128)(2,1)S(1)}, s16[1040,128]{1,0:T(8,128)(2,1)S(1)}) custom-call(bf16[512,128]{1,0:T(8,128)(2,1)S(1)} %shard_map.79._, f32[48,256,128]{2,1,0:T(8,128)S(1)} %shard_map.78._.total, bf16[256,128]{1,0:T(8,128)(2,1)S(1)} %get-tuple-element.20.refs_0_, ...), custom_call_target="tpu_custom_call" | custom-call | flops 8589934592 | bytes 1048576 | tf_op jit(solution)/shard_map/pallas_call | solution.py:306
  11.3 0.7 %collective-permute-start.5 = (s16[1040,128]{1,0:T(8,128)(2,1)S(1)}, s16[1040,128]{1,0:T(8,128)(2,1)S(1)}, u32[]{:S(2)}, u32[]{:S(2)}) collective-permute-start(s16[1040,128]{1,0:T(8,128)(2,1)S(1)} %get-tuple-element.27), channel_id=1, source_target_pairs={{0,0},{4,8},{8,4},{12,16},{16,12},{20,24},{24,20},{28,28},{1,1},{5... | collective-permute-start | bytes 798728 | tf_op jit(solution)/shard_map/ppermute | solution.py:21
  12.0 0.0 collective-permute-done.3._.first_ref
  12.0 0.8 %shard_map.81 = (bf16[2,16,256,128]{3,2,1,0:T(8,128)(2,1)S(1)}, s16[528,128]{1,0:T(8,128)(2,1)S(1)}) custom-call(bf16[512,128]{1,0:T(8,128)(2,1)S(1)} %collective-permute-done.3._.first_ref, f32[48,256,128]{2,1,0:T(8,128)S(1)} %shard_map.78._.total, bf16[128,1024]{1,0:T(8,128)(2,1)S(1)} %get-tuple-element.22.across_ref), custom_call_target="tpu_custom_call" | custom-call | flops 8589934592 | bytes 1048576 | tf_op jit(solution)/shard_map/pallas_call | solution.py:306
  12.8 3.2 %collective-permute-start.4 = (s16[528,128]{1,0:T(8,128)(2,1)S(1)}, s16[528,128]{1,0:T(8,128)(2,1)S(1)}, u32[]{:S(2)}, u32[]{:S(2)}) collective-permute-start(s16[528,128]{1,0:T(8,128)(2,1)S(1)} %get-tuple-element.26), channel_id=1, source_target_pairs={{0,4},{4,0},{8,12},{12,8},{16,20},{20,16},{24,28},{28,24},{1,5},{5... | collective-permute-start | bytes 405512 | tf_op jit(solution)/shard_map/ppermute | solution.py:21
  16.0 1.8 %shard_map.82 = (f32[4,128,128]{2,1,0:T(8,128)S(1)}, f32[4,128,128]{2,1,0:T(8,128)S(1)}) custom-call(f32[48,256,128]{2,1,0:T(8,128)S(1)} %shard_map.78._.total, bf16[128,1024]{1,0:T(8,128)(2,1)S(1)} %get-tuple-element.22.across_ref, bf16[2,16,256,128]{3,2,1,0:T(8,128)(2,1)S(1)} %get-tuple-element.23.first_pairs_ref, ...), custom_call_target="tpu_custom_call" | custom-call | bytes 1048576 | tf_op jit(solution)/shard_map/pallas_call | solution.py:306
  17.9 0.0 collective-permute-done.4.first_ref
  17.9 0.9 %shard_map.83 = (f32[256,128]{1,0:T(8,128)S(1)}, s16[272,128]{1,0:T(8,128)(2,1)S(1)}, s16[272,128]{1,0:T(8,128)(2,1)S(1)}, s16[272,128]{1,0:T(8,128)(2,1)S(1)}) custom-call(bf16[2,16,256,128]{3,2,1,0:T(8,128)(2,1)S(1)} %get-tuple-element.21.pairs_ref, f32[4,128,128]{2,1,0:T(8,128)S(1)} %get-tuple-element.24.potential_ref, ...), custom_call_target="tpu_custom_call" | custom-call | bytes 1048576 | tf_op jit(solution)/shard_map/pallas_call | solution.py:306
  18.8 1.3 %collective-permute-start.6 = (s16[272,128]{1,0:T(8,128)(2,1)S(1)}, s16[272,128]{1,0:T(8,128)(2,1)S(1)}, u32[]{:S(2)}, u32[]{:S(2)}) collective-permute-start(s16[272,128]{1,0:T(8,128)(2,1)S(1)} %get-tuple-element.29), channel_id=1, source_target_pairs={{0,3},{1,2},{2,1},{3,0},{4,7},{5,6},{6,5},{7,4},{8,11},{9,10},{10,... | collective-permute-start | bytes 208904 | tf_op jit(solution)/shard_map/ppermute | solution.py:15
  20.1 0.6 %collective-permute-start.7 = (s16[272,128]{1,0:T(8,128)(2,1)S(1)}, s16[272,128]{1,0:T(8,128)(2,1)S(1)}, u32[]{:S(2)}, u32[]{:S(2)}) collective-permute-start(s16[272,128]{1,0:T(8,128)(2,1)S(1)} %get-tuple-element.30), channel_id=1, source_target_pairs={{0,2},{1,3},{2,0},{3,1},{4,6},{5,7},{6,4},{7,5},{8,10},{9,11},{10,... | collective-permute-start | bytes 208904 | tf_op jit(solution)/shard_map/ppermute | solution.py:15
  20.6 1.7 %collective-permute-start.8 = (s16[272,128]{1,0:T(8,128)(2,1)S(1)}, s16[272,128]{1,0:T(8,128)(2,1)S(1)}, u32[]{:S(2)}, u32[]{:S(2)}) collective-permute-start(s16[272,128]{1,0:T(8,128)(2,1)S(1)} %get-tuple-element.31), channel_id=1, source_target_pairs={{0,1},{1,0},{2,3},{3,2},{4,5},{5,4},{6,7},{7,6},{8,9},{9,8},{10,11... | collective-permute-start | bytes 208904 | tf_op jit(solution)/shard_map/ppermute | solution.py:15
  22.3 1.9 %collective-permute-done.6.refs_0_ = s16[272,128]{1,0:T(8,128)(2,1)S(1)} collective-permute-done((s16[272,128]{1,0:T(8,128)(2,1)S(1)}, s16[272,128]{1,0:T(8,128)(2,1)S(1)}, u32[]{:S(2)}, u32[]{:S(2)}) %collective-permute-start.6) | collective-permute-done | bytes 69664 | tf_op jit(solution)/shard_map/ppermute | solution.py:15
  24.2 2.0 %collective-permute-done.7.refs_1_ = s16[272,128]{1,0:T(8,128)(2,1)S(1)} collective-permute-done((s16[272,128]{1,0:T(8,128)(2,1)S(1)}, s16[272,128]{1,0:T(8,128)(2,1)S(1)}, u32[]{:S(2)}, u32[]{:S(2)}) %collective-permute-start.7) | collective-permute-done | bytes 69664 | tf_op jit(solution)/shard_map/ppermute | solution.py:15
  26.2 0.0 collective-permute-done.8.refs_2_
  26.2 0.7 %shard_map.84 = (f32[128,128]{1,0:T(8,128)}, f32[128,128]{1,0:T(8,128)}) custom-call(f32[256,128]{1,0:T(8,128)S(1)} %get-tuple-element.28.own_ref, s16[272,128]{1,0:T(8,128)(2,1)S(1)} %collective-permute-done.6.refs_0_, s16[272,128]{1,0:T(8,128)(2,1)S(1)} %collective-permute-done.7.refs_1_, s16[272,128]{1,0:T(8,128)(2,1)S(1)} %collective-permute-done.8.refs_2_), custom_call_target="tpu_custom_call" | custom-call | bytes 1048576 | tf_op jit(solution)/shard_map/pallas_call | solution.py:306
  (4 shorter events, 0.0 us)
Async XLA Ops:
  0.6 6.3 %copy-start = (bf16[192,2,128,128]{3,2,1,0:T(8,128)(2,1)S(1)}, bf16[192,2,128,128]{3,2,1,0:T(8,128)(2,1)}, u32[]{:S(2)}) copy-start(bf16[192,2,128,128]{3,2,1,0:T(8,128)(2,1)} %kernels_ref.1) | copy-start | bytes 37748740
  1.6 7.6 %collective-permute-start.2 = (bf16[256,128]{1,0:T(8,128)(2,1)S(1)}, bf16[256,128]{1,0:T(8,128)(2,1)S(1)}, u32[]{:S(2)}, u32[]{:S(2)}) collective-permute-start(bf16[256,128]{1,0:T(8,128)(2,1)S(1)} %get-tuple-element.20.refs_0_), channel_id=1, source_target_pairs={{0,3},{1,2},{2,1},{3,0},{4,7},{5,6},{6,5},{7,4},{8,11},{9,10},{10,... | collective-permute-start | bytes 196616 | tf_op jit(solution)/shard_map/ppermute | solution.py:15
  5.6 4.3 %collective-permute-start.1 = (bf16[256,128]{1,0:T(8,128)(2,1)S(1)}, bf16[256,128]{1,0:T(8,128)(2,1)S(1)}, u32[]{:S(2)}, u32[]{:S(2)}) collective-permute-start(bf16[256,128]{1,0:T(8,128)(2,1)S(1)} %get-tuple-element.20.refs_0_), channel_id=1, source_target_pairs={{0,2},{1,3},{2,0},{3,1},{4,6},{5,7},{6,4},{7,5},{8,10},{9,11},{10,... | collective-permute-start | bytes 196616 | tf_op jit(solution)/shard_map/ppermute | solution.py:15
  6.1 4.3 %collective-permute-start = (bf16[256,128]{1,0:T(8,128)(2,1)S(1)}, bf16[256,128]{1,0:T(8,128)(2,1)S(1)}, u32[]{:S(2)}, u32[]{:S(2)}) collective-permute-start(bf16[256,128]{1,0:T(8,128)(2,1)S(1)} %get-tuple-element.20.refs_0_), channel_id=1, source_target_pairs={{0,1},{1,0},{2,3},{3,2},{4,5},{5,4},{6,7},{7,6},{8,9},{9,8},{10,11... | collective-permute-start | bytes 196616 | tf_op jit(solution)/shard_map/ppermute | solution.py:15
  10.4 1.6 %collective-permute-start.3 = (bf16[512,128]{1,0:T(8,128)(2,1)S(1)}, bf16[512,128]{1,0:T(8,128)(2,1)S(1)}, u32[]{:S(2)}, u32[]{:S(2)}) collective-permute-start(bf16[512,128]{1,0:T(8,128)(2,1)S(1)} %shard_map.79._), channel_id=1, source_target_pairs={{0,4},{4,0},{8,12},{12,8},{16,20},{20,16},{24,28},{28,24},{1,5},{5... | collective-permute-start | bytes 393224 | tf_op jit(solution)/shard_map/ppermute | solution.py:21
  11.3 6.6 %collective-permute-start.5 = (s16[1040,128]{1,0:T(8,128)(2,1)S(1)}, s16[1040,128]{1,0:T(8,128)(2,1)S(1)}, u32[]{:S(2)}, u32[]{:S(2)}) collective-permute-start(s16[1040,128]{1,0:T(8,128)(2,1)S(1)} %get-tuple-element.27), channel_id=1, source_target_pairs={{0,0},{4,8},{8,4},{12,16},{16,12},{20,24},{24,20},{28,28},{1,1},{5... | collective-permute-start | bytes 798728 | tf_op jit(solution)/shard_map/ppermute | solution.py:21
  12.8 5.1 %collective-permute-start.4 = (s16[528,128]{1,0:T(8,128)(2,1)S(1)}, s16[528,128]{1,0:T(8,128)(2,1)S(1)}, u32[]{:S(2)}, u32[]{:S(2)}) collective-permute-start(s16[528,128]{1,0:T(8,128)(2,1)S(1)} %get-tuple-element.26), channel_id=1, source_target_pairs={{0,4},{4,0},{8,12},{12,8},{16,20},{20,16},{24,28},{28,24},{1,5},{5... | collective-permute-start | bytes 405512 | tf_op jit(solution)/shard_map/ppermute | solution.py:21
  18.8 5.4 %collective-permute-start.6 = (s16[272,128]{1,0:T(8,128)(2,1)S(1)}, s16[272,128]{1,0:T(8,128)(2,1)S(1)}, u32[]{:S(2)}, u32[]{:S(2)}) collective-permute-start(s16[272,128]{1,0:T(8,128)(2,1)S(1)} %get-tuple-element.29), channel_id=1, source_target_pairs={{0,3},{1,2},{2,1},{3,0},{4,7},{5,6},{6,5},{7,4},{8,11},{9,10},{10,... | collective-permute-start | bytes 208904 | tf_op jit(solution)/shard_map/ppermute | solution.py:15
  20.1 6.1 %collective-permute-start.7 = (s16[272,128]{1,0:T(8,128)(2,1)S(1)}, s16[272,128]{1,0:T(8,128)(2,1)S(1)}, u32[]{:S(2)}, u32[]{:S(2)}) collective-permute-start(s16[272,128]{1,0:T(8,128)(2,1)S(1)} %get-tuple-element.30), channel_id=1, source_target_pairs={{0,2},{1,3},{2,0},{3,1},{4,6},{5,7},{6,4},{7,5},{8,10},{9,11},{10,... | collective-permute-start | bytes 208904 | tf_op jit(solution)/shard_map/ppermute | solution.py:15
  20.6 5.6 %collective-permute-start.8 = (s16[272,128]{1,0:T(8,128)(2,1)S(1)}, s16[272,128]{1,0:T(8,128)(2,1)S(1)}, u32[]{:S(2)}, u32[]{:S(2)}) collective-permute-start(s16[272,128]{1,0:T(8,128)(2,1)S(1)} %get-tuple-element.31), channel_id=1, source_target_pairs={{0,1},{1,0},{2,3},{3,2},{4,5},{5,4},{6,7},{7,6},{8,9},{9,8},{10,11... | collective-permute-start | bytes 208904 | tf_op jit(solution)/shard_map/ppermute | solution.py:15

commit v16 on v15

--- a/solution.py
+++ b/solution.py
@@ -279,14 +279,22 @@
         encode([adjoint_ref[first + i] for i in range(count)], out_ref)
 
 
-def finish_kernel(blocks, panels, own_ref, *refs):
-    *parts, potential_ref, adjoint_ref = refs
+def add_kernel(blocks, panels, own_ref, *refs):
+    *parts, out_ref = refs
     total = [own_ref[rows_of(i, panels)] for i in range(2 * blocks)]
     for ref in parts:
         total = [a + b for a, b in zip(total, decode(ref, 2 * blocks, panels))]
-    for b in range(blocks):
-        potential_ref[rows_of(b, panels)] = total[b]
-        adjoint_ref[rows_of(b, panels)] = total[blocks + b].T
+    for i, value in enumerate(total):
+        out_ref[rows_of(i, panels)] = value
+
+
+def finish_kernel(blocks, panels, sum_ref, last_ref, potential_ref, adjoint_ref):
+    for i, value in enumerate(decode(last_ref, 2 * blocks, panels)):
+        total = sum_ref[rows_of(i, panels)] + value
+        if i < blocks:
+            potential_ref[rows_of(i, panels)] = total
+        else:
+            adjoint_ref[rows_of(i - blocks, panels)] = total.T
 
 
 def local(strengths, adjoint_weights, kernels, target_ids, source_ids, live_slots):
@@ -409,9 +417,11 @@
         (shape(2 * blocks * panels, width),) + (coded(2 * blocks),) * (clusters - 1),
         parts_args,
     )
-    parts = [exchange(parts[k - 1], "clu", k) for k in range(clusters - 1, 0, -1)]
+    order = sorted(range(1, clusters), key=lambda k: (k == 1, k & 1))
+    *early, last = [exchange(parts[k - 1], "clu", k) for k in order]
+    early = call(functools.partial(add_kernel, blocks, panels), shape(2 * blocks * panels, width), (mine, *early))
     out = shape(blocks * panels, width)
-    return tuple(call(functools.partial(finish_kernel, blocks, panels), (out, out), (mine, *parts)))
+    return tuple(call(functools.partial(finish_kernel, blocks, panels), (out, out), (early, last)))
 
 
 def solution(mesh):

time: 27.4 us -> 27.3 us (level)
    pallas_call x8 -> x9, Pallas kernels: 8.41 us -> 8.6 us  [call(): pl.pallas_call(body, out_shape=shapes, input_output_aliases=dict(aliases)...]
  transfers between devices with their start and end apart: 9 -> 9, of which waited for: 4 -> 5; matrix products, arithmetic and copies ran while one was open for 0% -> 0% of each run, Pallas kernels for 21% -> 22%
where the time goes in v16:
time: 27.3 us; the launch traced here: 26.9 us
  starting transfers between devices  11.9 us (44%)
  Pallas kernels  8.6 us (32%)
  waiting for transfers between devices  5.03 us (18%)
  between operations  1.4 us (5%)
    pallas_call x9, Pallas kernels, call(): pl.pallas_call(body, out_shape=shapes, input_output_aliases=dict(aliases)...  8.6 us
    ppermute x6, starting transfers between devices, exchange(): lax.ppermute(value, axis, [(i, i ^ step) for i in range(lax.axis_size(axi...  8.16 us
    ppermute x6, waiting for transfers between devices, exchange(): lax.ppermute(value, axis, [(i, i ^ step) for i in range(lax.axis_size(axi...  5.03 us
    ppermute x3, starting transfers between devices, exchange_beside(): lax.ppermute(value, 'grp', [(i, j if 0 <= j < groups else i) for i, j in...  3.74 us
  transfers between devices with their start and end apart: 9, of which 5 were waited for; matrix products, arithmetic and copies ran while one was open for 0% of the time, Pallas kernels for 22%

profile of v16, /device:TPU:0, one launch (start us, length us, event | category | flops | bytes accessed | tf_op | source)
XLA Modules:
  0.0 26.9 jit_solution(6887296995110319314)
XLA Ops:
  0.6 1.0 %shard_map.77 = (bf16[256,128]{1,0:T(8,128)(2,1)S(1)}, s32[192]{0:T(256)S(4)}, s32[192]{0:T(256)S(4)}, f32[48,256,128]{2,1,0:T(8,128)S(1)}) custom-call(bf16[128,128]{1,0:T(8,128)(2,1)} %strengths_ref.1, bf16[128,128]{1,0:T(8,128)(2,1)} %weights_ref.1, s32[192]{0:T(256)} %target_ref.1, s32[192]{0:T(256)} %source_ref.1), custom_call_target="tpu_custom_call" | custom-call | flops 17179869184 | bytes 1048576 | tf_op jit(solution)/shard_map/pallas_call | solution.py:314
  1.6 4.0 %collective-permute-start.2 = (bf16[256,128]{1,0:T(8,128)(2,1)S(1)}, bf16[256,128]{1,0:T(8,128)(2,1)S(1)}, u32[]{:S(2)}, u32[]{:S(2)}) collective-permute-start(bf16[256,128]{1,0:T(8,128)(2,1)S(1)} %get-tuple-element.20.refs_0_), channel_id=1, source_target_pairs={{0,3},{1,2},{2,1},{3,0},{4,7},{5,6},{6,5},{7,4},{8,11},{9,10},{10,... | collective-permute-start | bytes 196616 | tf_op jit(solution)/shard_map/ppermute | solution.py:15
  5.6 0.5 %collective-permute-start.1 = (bf16[256,128]{1,0:T(8,128)(2,1)S(1)}, bf16[256,128]{1,0:T(8,128)(2,1)S(1)}, u32[]{:S(2)}, u32[]{:S(2)}) collective-permute-start(bf16[256,128]{1,0:T(8,128)(2,1)S(1)} %get-tuple-element.20.refs_0_), channel_id=1, source_target_pairs={{0,2},{1,3},{2,0},{3,1},{4,6},{5,7},{6,4},{7,5},{8,10},{9,11},{10,... | collective-permute-start | bytes 196616 | tf_op jit(solution)/shard_map/ppermute | solution.py:15
  6.1 0.1 collective-permute-start
  6.9 2.5 %shard_map.78._.total = f32[48,256,128]{2,1,0:T(8,128)S(1)} custom-call(s32[1]{0:T(128)S(6)} %copy.10.live_ref, s32[192]{0:T(256)S(4)} %get-tuple-element.17.target_ref, s32[192]{0:T(256)S(4)} %get-tuple-element.18.source_ref, bf16[192,2,128,128]{3,2,1,0:T(8,128)(2,1)S(1)} %copy-done, ...), custom_call_target="tpu_custom_call", output_to_operand_aliasing={{}: (4, {})} | custom-call | flops 8589934592 | bytes 1048576 | tf_op jit(solution)/shard_map/pallas_call | solution.py:314
  9.4 0.0 collective-permute-done.2.refs_3_
  9.4 0.4 %collective-permute-done.1.refs_2_ = bf16[256,128]{1,0:T(8,128)(2,1)S(1)} collective-permute-done((bf16[256,128]{1,0:T(8,128)(2,1)S(1)}, bf16[256,128]{1,0:T(8,128)(2,1)S(1)}, u32[]{:S(2)}, u32[]{:S(2)}) %collective-permute-start.1) | collective-permute-done | bytes 65568 | tf_op jit(solution)/shard_map/ppermute | solution.py:15
  9.9 0.5 %collective-permute-done.refs_1_ = bf16[256,128]{1,0:T(8,128)(2,1)S(1)} collective-permute-done((bf16[256,128]{1,0:T(8,128)(2,1)S(1)}, bf16[256,128]{1,0:T(8,128)(2,1)S(1)}, u32[]{:S(2)}, u32[]{:S(2)}) %collective-permute-start) | collective-permute-done | bytes 65568 | tf_op jit(solution)/shard_map/ppermute | solution.py:15
  10.4 0.1 collective-permute-start.3
  10.5 0.8 %shard_map.80 = (bf16[2,16,256,128]{3,2,1,0:T(8,128)(2,1)S(1)}, bf16[128,1024]{1,0:T(8,128)(2,1)S(1)}, s16[1040,128]{1,0:T(8,128)(2,1)S(1)}) custom-call(bf16[512,128]{1,0:T(8,128)(2,1)S(1)} %shard_map.79._, f32[48,256,128]{2,1,0:T(8,128)S(1)} %shard_map.78._.total, bf16[256,128]{1,0:T(8,128)(2,1)S(1)} %get-tuple-element.20.refs_0_, ...), custom_call_target="tpu_custom_call" | custom-call | flops 8589934592 | bytes 1048576 | tf_op jit(solution)/shard_map/pallas_call | solution.py:314
  11.3 0.7 %collective-permute-start.5 = (s16[1040,128]{1,0:T(8,128)(2,1)S(1)}, s16[1040,128]{1,0:T(8,128)(2,1)S(1)}, u32[]{:S(2)}, u32[]{:S(2)}) collective-permute-start(s16[1040,128]{1,0:T(8,128)(2,1)S(1)} %get-tuple-element.27), channel_id=1, source_target_pairs={{0,0},{4,8},{8,4},{12,16},{16,12},{20,24},{24,20},{28,28},{1,1},{5... | collective-permute-start | bytes 798728 | tf_op jit(solution)/shard_map/ppermute | solution.py:21
  12.0 0.0 collective-permute-done.3._.first_ref
  12.0 0.8 %shard_map.81 = (bf16[2,16,256,128]{3,2,1,0:T(8,128)(2,1)S(1)}, s16[528,128]{1,0:T(8,128)(2,1)S(1)}) custom-call(bf16[512,128]{1,0:T(8,128)(2,1)S(1)} %collective-permute-done.3._.first_ref, f32[48,256,128]{2,1,0:T(8,128)S(1)} %shard_map.78._.total, bf16[128,1024]{1,0:T(8,128)(2,1)S(1)} %get-tuple-element.22.across_ref), custom_call_target="tpu_custom_call" | custom-call | flops 8589934592 | bytes 1048576 | tf_op jit(solution)/shard_map/pallas_call | solution.py:314
  12.8 3.0 %collective-permute-start.4 = (s16[528,128]{1,0:T(8,128)(2,1)S(1)}, s16[528,128]{1,0:T(8,128)(2,1)S(1)}, u32[]{:S(2)}, u32[]{:S(2)}) collective-permute-start(s16[528,128]{1,0:T(8,128)(2,1)S(1)} %get-tuple-element.26), channel_id=1, source_target_pairs={{0,4},{4,0},{8,12},{12,8},{16,20},{20,16},{24,28},{28,24},{1,5},{5... | collective-permute-start | bytes 405512 | tf_op jit(solution)/shard_map/ppermute | solution.py:21
  15.8 1.8 %shard_map.82 = (f32[4,128,128]{2,1,0:T(8,128)S(1)}, f32[4,128,128]{2,1,0:T(8,128)S(1)}) custom-call(f32[48,256,128]{2,1,0:T(8,128)S(1)} %shard_map.78._.total, bf16[128,1024]{1,0:T(8,128)(2,1)S(1)} %get-tuple-element.22.across_ref, bf16[2,16,256,128]{3,2,1,0:T(8,128)(2,1)S(1)} %get-tuple-element.23.first_pairs_ref, ...), custom_call_target="tpu_custom_call" | custom-call | bytes 1048576 | tf_op jit(solution)/shard_map/pallas_call | solution.py:314
  17.6 0.0 collective-permute-done.5.second_ref
  17.6 0.9 %shard_map.83 = (f32[256,128]{1,0:T(8,128)S(1)}, s16[272,128]{1,0:T(8,128)(2,1)S(1)}, s16[272,128]{1,0:T(8,128)(2,1)S(1)}, s16[272,128]{1,0:T(8,128)(2,1)S(1)}) custom-call(bf16[2,16,256,128]{3,2,1,0:T(8,128)(2,1)S(1)} %get-tuple-element.21.pairs_ref, f32[4,128,128]{2,1,0:T(8,128)S(1)} %get-tuple-element.24.potential_ref, ...), custom_call_target="tpu_custom_call" | custom-call | bytes 1048576 | tf_op jit(solution)/shard_map/pallas_call | solution.py:314
  18.5 1.6 %collective-permute-start.6 = (s16[272,128]{1,0:T(8,128)(2,1)S(1)}, s16[272,128]{1,0:T(8,128)(2,1)S(1)}, u32[]{:S(2)}, u32[]{:S(2)}) collective-permute-start(s16[272,128]{1,0:T(8,128)(2,1)S(1)} %get-tuple-element.29), channel_id=1, source_target_pairs={{0,2},{1,3},{2,0},{3,1},{4,6},{5,7},{6,4},{7,5},{8,10},{9,11},{10,... | collective-permute-start | bytes 208904 | tf_op jit(solution)/shard_map/ppermute | solution.py:15
  20.1 1.1 %collective-permute-start.7 = (s16[272,128]{1,0:T(8,128)(2,1)S(1)}, s16[272,128]{1,0:T(8,128)(2,1)S(1)}, u32[]{:S(2)}, u32[]{:S(2)}) collective-permute-start(s16[272,128]{1,0:T(8,128)(2,1)S(1)} %get-tuple-element.30), channel_id=1, source_target_pairs={{0,3},{1,2},{2,1},{3,0},{4,7},{5,6},{6,5},{7,4},{8,11},{9,10},{10,... | collective-permute-start | bytes 208904 | tf_op jit(solution)/shard_map/ppermute | solution.py:15
  21.2 0.9 %collective-permute-start.8 = (s16[272,128]{1,0:T(8,128)(2,1)S(1)}, s16[272,128]{1,0:T(8,128)(2,1)S(1)}, u32[]{:S(2)}, u32[]{:S(2)}) collective-permute-start(s16[272,128]{1,0:T(8,128)(2,1)S(1)} %get-tuple-element.31), channel_id=1, source_target_pairs={{0,1},{1,0},{2,3},{3,2},{4,5},{5,4},{6,7},{7,6},{8,9},{9,8},{10,11... | collective-permute-start | bytes 208904 | tf_op jit(solution)/shard_map/ppermute | solution.py:15
  22.1 0.8 %collective-permute-done.6.refs_0_ = s16[272,128]{1,0:T(8,128)(2,1)S(1)} collective-permute-done((s16[272,128]{1,0:T(8,128)(2,1)S(1)}, s16[272,128]{1,0:T(8,128)(2,1)S(1)}, u32[]{:S(2)}, u32[]{:S(2)}) %collective-permute-start.6) | collective-permute-done | bytes 69664 | tf_op jit(solution)/shard_map/ppermute | solution.py:15
  22.9 2.6 %collective-permute-done.7.refs_1_ = s16[272,128]{1,0:T(8,128)(2,1)S(1)} collective-permute-done((s16[272,128]{1,0:T(8,128)(2,1)S(1)}, s16[272,128]{1,0:T(8,128)(2,1)S(1)}, u32[]{:S(2)}, u32[]{:S(2)}) %collective-permute-start.7) | collective-permute-done | bytes 69664 | tf_op jit(solution)/shard_map/ppermute | solution.py:15
  25.5 0.7 %collective-permute-done.8.last_ref = s16[272,128]{1,0:T(8,128)(2,1)S(1)} collective-permute-done((s16[272,128]{1,0:T(8,128)(2,1)S(1)}, s16[272,128]{1,0:T(8,128)(2,1)S(1)}, u32[]{:S(2)}, u32[]{:S(2)}) %collective-permute-start.8) | collective-permute-done | bytes 69664 | tf_op jit(solution)/shard_map/ppermute | solution.py:15
  26.2 0.7 %shard_map.85 = (f32[128,128]{1,0:T(8,128)}, f32[128,128]{1,0:T(8,128)}) custom-call(f32[256,128]{1,0:T(8,128)S(1)} %shard_map.84.sum_ref, s16[272,128]{1,0:T(8,128)(2,1)S(1)} %collective-permute-done.8.last_ref), custom_call_target="tpu_custom_call" | custom-call | bytes 1048576 | tf_op jit(solution)/shard_map/pallas_call | solution.py:314
  (5 shorter events, 0.1 us)
Async XLA Ops:
  0.6 6.3 %copy-start = (bf16[192,2,128,128]{3,2,1,0:T(8,128)(2,1)S(1)}, bf16[192,2,128,128]{3,2,1,0:T(8,128)(2,1)}, u32[]{:S(2)}) copy-start(bf16[192,2,128,128]{3,2,1,0:T(8,128)(2,1)} %kernels_ref.1) | copy-start | bytes 37748740
  1.6 7.8 %collective-permute-start.2 = (bf16[256,128]{1,0:T(8,128)(2,1)S(1)}, bf16[256,128]{1,0:T(8,128)(2,1)S(1)}, u32[]{:S(2)}, u32[]{:S(2)}) collective-permute-start(bf16[256,128]{1,0:T(8,128)(2,1)S(1)} %get-tuple-element.20.refs_0_), channel_id=1, source_target_pairs={{0,3},{1,2},{2,1},{3,0},{4,7},{5,6},{6,5},{7,4},{8,11},{9,10},{10,... | collective-permute-start | bytes 196616 | tf_op jit(solution)/shard_map/ppermute | solution.py:15
  5.6 4.3 %collective-permute-start.1 = (bf16[256,128]{1,0:T(8,128)(2,1)S(1)}, bf16[256,128]{1,0:T(8,128)(2,1)S(1)}, u32[]{:S(2)}, u32[]{:S(2)}) collective-permute-start(bf16[256,128]{1,0:T(8,128)(2,1)S(1)} %get-tuple-element.20.refs_0_), channel_id=1, source_target_pairs={{0,2},{1,3},{2,0},{3,1},{4,6},{5,7},{6,4},{7,5},{8,10},{9,11},{10,... | collective-permute-start | bytes 196616 | tf_op jit(solution)/shard_map/ppermute | solution.py:15
  6.1 4.3 %collective-permute-start = (bf16[256,128]{1,0:T(8,128)(2,1)S(1)}, bf16[256,128]{1,0:T(8,128)(2,1)S(1)}, u32[]{:S(2)}, u32[]{:S(2)}) collective-permute-start(bf16[256,128]{1,0:T(8,128)(2,1)S(1)} %get-tuple-element.20.refs_0_), channel_id=1, source_target_pairs={{0,1},{1,0},{2,3},{3,2},{4,5},{5,4},{6,7},{7,6},{8,9},{9,8},{10,11... | collective-permute-start | bytes 196616 | tf_op jit(solution)/shard_map/ppermute | solution.py:15
  10.4 1.6 %collective-permute-start.3 = (bf16[512,128]{1,0:T(8,128)(2,1)S(1)}, bf16[512,128]{1,0:T(8,128)(2,1)S(1)}, u32[]{:S(2)}, u32[]{:S(2)}) collective-permute-start(bf16[512,128]{1,0:T(8,128)(2,1)S(1)} %shard_map.79._), channel_id=1, source_target_pairs={{0,4},{4,0},{8,12},{12,8},{16,20},{20,16},{24,28},{28,24},{1,5},{5... | collective-permute-start | bytes 393224 | tf_op jit(solution)/shard_map/ppermute | solution.py:21
  11.3 6.3 %collective-permute-start.5 = (s16[1040,128]{1,0:T(8,128)(2,1)S(1)}, s16[1040,128]{1,0:T(8,128)(2,1)S(1)}, u32[]{:S(2)}, u32[]{:S(2)}) collective-permute-start(s16[1040,128]{1,0:T(8,128)(2,1)S(1)} %get-tuple-element.27), channel_id=1, source_target_pairs={{0,0},{4,8},{8,4},{12,16},{16,12},{20,24},{24,20},{28,28},{1,1},{5... | collective-permute-start | bytes 798728 | tf_op jit(solution)/shard_map/ppermute | solution.py:21
  12.8 4.8 %collective-permute-start.4 = (s16[528,128]{1,0:T(8,128)(2,1)S(1)}, s16[528,128]{1,0:T(8,128)(2,1)S(1)}, u32[]{:S(2)}, u32[]{:S(2)}) collective-permute-start(s16[528,128]{1,0:T(8,128)(2,1)S(1)} %get-tuple-element.26), channel_id=1, source_target_pairs={{0,4},{4,0},{8,12},{12,8},{16,20},{20,16},{24,28},{28,24},{1,5},{5... | collective-permute-start | bytes 405512 | tf_op jit(solution)/shard_map/ppermute | solution.py:21
  18.5 4.4 %collective-permute-start.6 = (s16[272,128]{1,0:T(8,128)(2,1)S(1)}, s16[272,128]{1,0:T(8,128)(2,1)S(1)}, u32[]{:S(2)}, u32[]{:S(2)}) collective-permute-start(s16[272,128]{1,0:T(8,128)(2,1)S(1)} %get-tuple-element.29), channel_id=1, source_target_pairs={{0,2},{1,3},{2,0},{3,1},{4,6},{5,7},{6,4},{7,5},{8,10},{9,11},{10,... | collective-permute-start | bytes 208904 | tf_op jit(solution)/shard_map/ppermute | solution.py:15
  20.1 5.4 %collective-permute-start.7 = (s16[272,128]{1,0:T(8,128)(2,1)S(1)}, s16[272,128]{1,0:T(8,128)(2,1)S(1)}, u32[]{:S(2)}, u32[]{:S(2)}) collective-permute-start(s16[272,128]{1,0:T(8,128)(2,1)S(1)} %get-tuple-element.30), channel_id=1, source_target_pairs={{0,3},{1,2},{2,1},{3,0},{4,7},{5,6},{6,5},{7,4},{8,11},{9,10},{10,... | collective-permute-start | bytes 208904 | tf_op jit(solution)/shard_map/ppermute | solution.py:15
  21.2 5.0 %collective-permute-start.8 = (s16[272,128]{1,0:T(8,128)(2,1)S(1)}, s16[272,128]{1,0:T(8,128)(2,1)S(1)}, u32[]{:S(2)}, u32[]{:S(2)}) collective-permute-start(s16[272,128]{1,0:T(8,128)(2,1)S(1)} %get-tuple-element.31), channel_id=1, source_target_pairs={{0,1},{1,0},{2,3},{3,2},{4,5},{5,4},{6,7},{7,6},{8,9},{9,8},{10,11... | collective-permute-start | bytes 208904 | tf_op jit(solution)/shard_map/ppermute | solution.py:15

commit v17 on v15

--- a/solution.py
+++ b/solution.py
@@ -170,7 +170,7 @@
             yield product[:, j * width : (j + 1) * width]
 
 
-def second_kernel(blocks, panels, count, _, total, *refs):
+def second_kernel(blocks, panels, count, total, *refs):
     *gathered, pairs_ref, across_ref, out_ref = refs
     split(total, total.shape[0] - pairs_ref.shape[1], pairs_ref)
     for i, block in enumerate(part_of(gathered, blocks, panels, 1)):
@@ -179,7 +179,7 @@
     encode(strengths + list(adjoint_of(pairs_ref, across_ref, 0, count)), out_ref)
 
 
-def first_kernel(count, _, total, across_ref, pairs_ref, out_ref):
+def first_kernel(count, total, across_ref, pairs_ref, out_ref):
     split(total, 0, pairs_ref)
     encode(list(adjoint_of(pairs_ref, across_ref, 0, count)), out_ref)
 
@@ -198,18 +198,22 @@
         yield product[:panels] + product[panels:]
 
 
-def inner_kernel(blocks, total, across_ref, first_pairs_ref, first_ref, *refs):
+def own_kernel(blocks, total, across_ref, *refs):
     *gathered, potential_ref, middle_ref, pairs_ref = refs
     targets, panels = potential_ref.shape[:2]
     split(total, pairs_ref.shape[1], pairs_ref)
     for i, value in enumerate(adjoint_of(pairs_ref, across_ref, 0, targets)):
         middle_ref[i] = value
+    strengths = list(part_of(gathered, blocks, panels, 0))
+    for t, value in enumerate(forward_of(pairs_ref, strengths, targets)):
+        potential_ref[t] = value
+
+
+def forward_kernel(pairs_ref, first_ref, own_ref, potential_ref):
+    targets, panels = potential_ref.shape[:2]
     strengths = [first_ref[rows_of(i, panels)] for i in range(targets)]
-    own = list(part_of(gathered, blocks, panels, 0))
-    for t, value in enumerate(forward_of(first_pairs_ref, strengths, targets)):
-        potential_ref[t] = value
-    for t, value in enumerate(forward_of(pairs_ref, own, targets)):
-        potential_ref[t] += value
+    for t, value in enumerate(forward_of(pairs_ref, strengths, targets)):
+        potential_ref[t] = own_ref[t] + value
 
 
 def parts_of(blocks, potential, adjoint, own_ref, *outs):
@@ -354,8 +358,6 @@
             flops=1 << 33,
             aliases=[(4, 0)],
         )
-        own = group_strengths(total)
-        first = exchange_beside(own, 0)
         total = pltpu.with_memory_space_constraint(total, pltpu.VMEM)
         kept_shape = pltpu.VMEM((2, pairs // 3, 2 * panels, panels), bf16)
         kept_second, across, upper = call(
@@ -365,24 +367,24 @@
                 shape(width, 2 * group_blocks * panels, kind=bf16),
                 coded(2 * group_blocks),
             ),
-            (own, total, *gathered),
-            [in_hbm] + [in_vmem] * (1 + clusters),
+            (total, *gathered),
             flops=1 << 33,
         )
         kept_first, lower = call(
             functools.partial(first_kernel, group_blocks),
             (kept_shape, coded(group_blocks)),
-            (first, total, across),
-            [in_hbm] + [in_vmem] * 2,
+            (total, across),
             flops=1 << 33,
         )
+        first = exchange_beside(group_strengths(lower), 0)
         kept_first, kept_second = (pltpu.with_memory_space_constraint(x, pltpu.VMEM) for x in (kept_first, kept_second))
-        potential, middle = call(
-            functools.partial(inner_kernel, blocks),
+        own, middle = call(
+            functools.partial(own_kernel, blocks),
             (block_sums, block_sums),
-            (total, across, kept_first, first, *gathered),
+            (total, across, *gathered),
             scratch=[kept_shape],
         )
+        potential = call(forward_kernel, block_sums, (kept_first, first, own))
         upper, lower = exchange_beside(upper, 1), exchange_beside(lower, 0)
         parts_body, parts_args = parts_kernel, (kept_second, potential, middle, lower, upper)
     else:

time: 27.4 us -> 27.3 us (level)
  waiting for transfers between devices: 5.01 us -> 6.61 us
  Pallas kernels: 8.41 us -> 7.2 us
    ppermute x6, waiting for transfers between devices: 5 us -> 6.57 us  [exchange(): lax.ppermute(value, axis, [(i, i ^ step) for i in range(lax.axis_size(axi...]
    pallas_call x8 -> x9, Pallas kernels: 8.41 us -> 7.2 us  [call(): pl.pallas_call(body, out_shape=shapes, input_output_aliases=dict(aliases)...]
  transfers between devices with their start and end apart: 9 -> 9, of which waited for: 4 -> 4; matrix products, arithmetic and copies ran while one was open for 0% -> 0% of each run, Pallas kernels for 21% -> 14%
where the time goes in v17:
time: 27.3 us; the launch traced here: 27.1 us
  starting transfers between devices  11.9 us (44%)
  Pallas kernels  7.2 us (26%)
  waiting for transfers between devices  6.61 us (24%)
  between operations  1.38 us (5%)
    ppermute x6, starting transfers between devices, exchange(): lax.ppermute(value, axis, [(i, i ^ step) for i in range(lax.axis_size(axi...  8.16 us
    pallas_call x9, Pallas kernels, call(): pl.pallas_call(body, out_shape=shapes, input_output_aliases=dict(aliases)...  7.2 us
    ppermute x6, waiting for transfers between devices, exchange(): lax.ppermute(value, axis, [(i, i ^ step) for i in range(lax.axis_size(axi...  6.57 us
    ppermute x3, starting transfers between devices, exchange_beside(): lax.ppermute(value, 'grp', [(i, j if 0 <= j < groups else i) for i, j in...  3.75 us
  transfers between devices with their start and end apart: 9, of which 4 were waited for; matrix products, arithmetic and copies ran while one was open for 0% of the time, Pallas kernels for 14%

profile of v17, /device:TPU:0, one launch (start us, length us, event | category | flops | bytes accessed | tf_op | source)
XLA Modules:
  0.0 27.1 jit_solution(10653483300851308427)
XLA Ops:
  0.6 1.0 %shard_map.77 = (bf16[256,128]{1,0:T(8,128)(2,1)S(1)}, s32[192]{0:T(256)S(4)}, s32[192]{0:T(256)S(4)}, f32[48,256,128]{2,1,0:T(8,128)S(1)}) custom-call(bf16[128,128]{1,0:T(8,128)(2,1)} %strengths_ref.1, bf16[128,128]{1,0:T(8,128)(2,1)} %weights_ref.1, s32[192]{0:T(256)} %target_ref.1, s32[192]{0:T(256)} %source_ref.1), custom_call_target="tpu_custom_call" | custom-call | flops 17179869184 | bytes 1048576 | tf_op jit(solution)/shard_map/pallas_call | solution.py:310
  1.6 4.0 %collective-permute-start.2 = (bf16[256,128]{1,0:T(8,128)(2,1)S(1)}, bf16[256,128]{1,0:T(8,128)(2,1)S(1)}, u32[]{:S(2)}, u32[]{:S(2)}) collective-permute-start(bf16[256,128]{1,0:T(8,128)(2,1)S(1)} %get-tuple-element.20.refs_0_), channel_id=1, source_target_pairs={{0,3},{1,2},{2,1},{3,0},{4,7},{5,6},{6,5},{7,4},{8,11},{9,10},{10,... | collective-permute-start | bytes 196616 | tf_op jit(solution)/shard_map/ppermute | solution.py:15
  5.6 0.5 %collective-permute-start.1 = (bf16[256,128]{1,0:T(8,128)(2,1)S(1)}, bf16[256,128]{1,0:T(8,128)(2,1)S(1)}, u32[]{:S(2)}, u32[]{:S(2)}) collective-permute-start(bf16[256,128]{1,0:T(8,128)(2,1)S(1)} %get-tuple-element.20.refs_0_), channel_id=1, source_target_pairs={{0,2},{1,3},{2,0},{3,1},{4,6},{5,7},{6,4},{7,5},{8,10},{9,11},{10,... | collective-permute-start | bytes 196616 | tf_op jit(solution)/shard_map/ppermute | solution.py:15
  6.1 0.1 collective-permute-start
  6.9 0.9 %shard_map.78.total = f32[48,256,128]{2,1,0:T(8,128)S(1)} custom-call(s32[1]{0:T(128)S(6)} %copy.10.live_ref, s32[192]{0:T(256)S(4)} %get-tuple-element.17.target_ref, s32[192]{0:T(256)S(4)} %get-tuple-element.18.source_ref, bf16[192,2,128,128]{3,2,1,0:T(8,128)(2,1)S(1)} %copy-done, ...), custom_call_target="tpu_custom_call", output_to_operand_aliasing={{}: (4, {})} | custom-call | flops 8589934592 | bytes 1048576 | tf_op jit(solution)/shard_map/pallas_call | solution.py:310
  7.8 0.0 collective-permute-done.2.refs_3_
  7.8 2.0 %collective-permute-done.1.refs_2_ = bf16[256,128]{1,0:T(8,128)(2,1)S(1)} collective-permute-done((bf16[256,128]{1,0:T(8,128)(2,1)S(1)}, bf16[256,128]{1,0:T(8,128)(2,1)S(1)}, u32[]{:S(2)}, u32[]{:S(2)}) %collective-permute-start.1) | collective-permute-done | bytes 65568 | tf_op jit(solution)/shard_map/ppermute | solution.py:15
  9.9 0.5 %collective-permute-done.refs_1_ = bf16[256,128]{1,0:T(8,128)(2,1)S(1)} collective-permute-done((bf16[256,128]{1,0:T(8,128)(2,1)S(1)}, bf16[256,128]{1,0:T(8,128)(2,1)S(1)}, u32[]{:S(2)}, u32[]{:S(2)}) %collective-permute-start) | collective-permute-done | bytes 65568 | tf_op jit(solution)/shard_map/ppermute | solution.py:15
  10.4 0.8 %shard_map.79 = (bf16[2,16,256,128]{3,2,1,0:T(8,128)(2,1)S(1)}, bf16[128,1024]{1,0:T(8,128)(2,1)S(1)}, s16[1040,128]{1,0:T(8,128)(2,1)S(1)}) custom-call(f32[48,256,128]{2,1,0:T(8,128)S(1)} %shard_map.78.total, bf16[256,128]{1,0:T(8,128)(2,1)S(1)} %get-tuple-element.20.refs_0_, bf16[256,128]{1,0:T(8,128)(2,1)S(1)} %collective-permute-done.refs_1_, ...), custom_call_target="tpu_custom_call" | custom-call | flops 8589934592 | bytes 1048576 | tf_op jit(solution)/shard_map/pallas_call | solution.py:310
  11.2 0.7 %collective-permute-start.5 = (s16[1040,128]{1,0:T(8,128)(2,1)S(1)}, s16[1040,128]{1,0:T(8,128)(2,1)S(1)}, u32[]{:S(2)}, u32[]{:S(2)}) collective-permute-start(s16[1040,128]{1,0:T(8,128)(2,1)S(1)} %get-tuple-element.27), channel_id=1, source_target_pairs={{0,0},{4,8},{8,4},{12,16},{16,12},{20,24},{24,20},{28,28},{1,1},{5... | collective-permute-start | bytes 798728 | tf_op jit(solution)/shard_map/ppermute | solution.py:21
  11.9 0.8 %shard_map.80 = (bf16[2,16,256,128]{3,2,1,0:T(8,128)(2,1)S(1)}, s16[528,128]{1,0:T(8,128)(2,1)S(1)}) custom-call(f32[48,256,128]{2,1,0:T(8,128)S(1)} %shard_map.78.total, bf16[128,1024]{1,0:T(8,128)(2,1)S(1)} %get-tuple-element.22.across_ref), custom_call_target="tpu_custom_call" | custom-call | flops 8589934592 | bytes 1048576 | tf_op jit(solution)/shard_map/pallas_call | solution.py:310
  12.7 3.0 %collective-permute-start.4 = (s16[528,128]{1,0:T(8,128)(2,1)S(1)}, s16[528,128]{1,0:T(8,128)(2,1)S(1)}, u32[]{:S(2)}, u32[]{:S(2)}) collective-permute-start(s16[528,128]{1,0:T(8,128)(2,1)S(1)} %get-tuple-element.24._), channel_id=1, source_target_pairs={{0,4},{4,0},{8,12},{12,8},{16,20},{20,16},{24,28},{28,24},{1,5},{5... | collective-permute-start | bytes 405512 | tf_op jit(solution)/shard_map/ppermute | solution.py:21
  15.7 0.1 collective-permute-start.3
  15.8 1.3 %shard_map.82 = (f32[4,128,128]{2,1,0:T(8,128)S(1)}, f32[4,128,128]{2,1,0:T(8,128)S(1)}) custom-call(f32[48,256,128]{2,1,0:T(8,128)S(1)} %shard_map.78.total, bf16[128,1024]{1,0:T(8,128)(2,1)S(1)} %get-tuple-element.22.across_ref, bf16[256,128]{1,0:T(8,128)(2,1)S(1)} %get-tuple-element.20.refs_0_, bf16[256,128]{1,0:T(8,128)(2,1)S(1)} %collective-permute-done.refs_1_, ...), custom_call_target="tpu_custom_call" | custom-call | bytes 1048576 | tf_op jit(solution)/shard_map/pallas_call | solution.py:310
  17.1 0.0 collective-permute-done.3.first_ref
  17.1 0.8 %shard_map.83.potential_ref = f32[4,128,128]{2,1,0:T(8,128)S(1)} custom-call(bf16[2,16,256,128]{3,2,1,0:T(8,128)(2,1)S(1)} %get-tuple-element.23.pairs_ref, bf16[512,128]{1,0:T(8,128)(2,1)S(1)} %collective-permute-done.3.first_ref, f32[4,128,128]{2,1,0:T(8,128)S(1)} %get-tuple-element.25.own_ref), custom_call_target="tpu_custom_call" | custom-call | bytes 1048576 | tf_op jit(solution)/shard_map/pallas_call | solution.py:310
  17.9 0.0 collective-permute-done.4.first_ref
  17.9 0.9 %shard_map.84 = (f32[256,128]{1,0:T(8,128)S(1)}, s16[272,128]{1,0:T(8,128)(2,1)S(1)}, s16[272,128]{1,0:T(8,128)(2,1)S(1)}, s16[272,128]{1,0:T(8,128)(2,1)S(1)}) custom-call(bf16[2,16,256,128]{3,2,1,0:T(8,128)(2,1)S(1)} %get-tuple-element.21.pairs_ref, f32[4,128,128]{2,1,0:T(8,128)S(1)} %shard_map.83.potential_ref, ...), custom_call_target="tpu_custom_call" | custom-call | bytes 1048576 | tf_op jit(solution)/shard_map/pallas_call | solution.py:310
  18.8 2.8 %collective-permute-start.6 = (s16[272,128]{1,0:T(8,128)(2,1)S(1)}, s16[272,128]{1,0:T(8,128)(2,1)S(1)}, u32[]{:S(2)}, u32[]{:S(2)}) collective-permute-start(s16[272,128]{1,0:T(8,128)(2,1)S(1)} %get-tuple-element.29), channel_id=1, source_target_pairs={{0,3},{1,2},{2,1},{3,0},{4,7},{5,6},{6,5},{7,4},{8,11},{9,10},{10,... | collective-permute-start | bytes 208904 | tf_op jit(solution)/shard_map/ppermute | solution.py:15
  21.5 0.8 %collective-permute-start.8 = (s16[272,128]{1,0:T(8,128)(2,1)S(1)}, s16[272,128]{1,0:T(8,128)(2,1)S(1)}, u32[]{:S(2)}, u32[]{:S(2)}) collective-permute-start(s16[272,128]{1,0:T(8,128)(2,1)S(1)} %get-tuple-element.31), channel_id=1, source_target_pairs={{0,1},{1,0},{2,3},{3,2},{4,5},{5,4},{6,7},{7,6},{8,9},{9,8},{10,11... | collective-permute-start | bytes 208904 | tf_op jit(solution)/shard_map/ppermute | solution.py:15
  22.3 2.4 %collective-permute-done.6.refs_0_ = s16[272,128]{1,0:T(8,128)(2,1)S(1)} collective-permute-done((s16[272,128]{1,0:T(8,128)(2,1)S(1)}, s16[272,128]{1,0:T(8,128)(2,1)S(1)}, u32[]{:S(2)}, u32[]{:S(2)}) %collective-permute-start.6) | collective-permute-done | bytes 69664 | tf_op jit(solution)/shard_map/ppermute | solution.py:15
  24.7 1.6 %collective-permute-done.7.refs_1_ = s16[272,128]{1,0:T(8,128)(2,1)S(1)} collective-permute-done((s16[272,128]{1,0:T(8,128)(2,1)S(1)}, s16[272,128]{1,0:T(8,128)(2,1)S(1)}, u32[]{:S(2)}, u32[]{:S(2)}) %collective-permute-start.7) | collective-permute-done | bytes 69664 | tf_op jit(solution)/shard_map/ppermute | solution.py:15
  26.3 0.0 collective-permute-done.8.refs_2_
  26.4 0.7 %shard_map.85 = (f32[128,128]{1,0:T(8,128)}, f32[128,128]{1,0:T(8,128)}) custom-call(f32[256,128]{1,0:T(8,128)S(1)} %get-tuple-element.28.own_ref, s16[272,128]{1,0:T(8,128)(2,1)S(1)} %collective-permute-done.6.refs_0_, s16[272,128]{1,0:T(8,128)(2,1)S(1)} %collective-permute-done.7.refs_1_, s16[272,128]{1,0:T(8,128)(2,1)S(1)} %collective-permute-done.8.refs_2_), custom_call_target="tpu_custom_call" | custom-call | bytes 1048576 | tf_op jit(solution)/shard_map/pallas_call | solution.py:310
  (5 shorter events, 0.0 us)
Async XLA Ops:
  0.6 6.3 %copy-start = (bf16[192,2,128,128]{3,2,1,0:T(8,128)(2,1)S(1)}, bf16[192,2,128,128]{3,2,1,0:T(8,128)(2,1)}, u32[]{:S(2)}) copy-start(bf16[192,2,128,128]{3,2,1,0:T(8,128)(2,1)} %kernels_ref.1) | copy-start | bytes 37748740
  1.6 6.2 %collective-permute-start.2 = (bf16[256,128]{1,0:T(8,128)(2,1)S(1)}, bf16[256,128]{1,0:T(8,128)(2,1)S(1)}, u32[]{:S(2)}, u32[]{:S(2)}) collective-permute-start(bf16[256,128]{1,0:T(8,128)(2,1)S(1)} %get-tuple-element.20.refs_0_), channel_id=1, source_target_pairs={{0,3},{1,2},{2,1},{3,0},{4,7},{5,6},{6,5},{7,4},{8,11},{9,10},{10,... | collective-permute-start | bytes 196616 | tf_op jit(solution)/shard_map/ppermute | solution.py:15
  5.6 4.3 %collective-permute-start.1 = (bf16[256,128]{1,0:T(8,128)(2,1)S(1)}, bf16[256,128]{1,0:T(8,128)(2,1)S(1)}, u32[]{:S(2)}, u32[]{:S(2)}) collective-permute-start(bf16[256,128]{1,0:T(8,128)(2,1)S(1)} %get-tuple-element.20.refs_0_), channel_id=1, source_target_pairs={{0,2},{1,3},{2,0},{3,1},{4,6},{5,7},{6,4},{7,5},{8,10},{9,11},{10,... | collective-permute-start | bytes 196616 | tf_op jit(solution)/shard_map/ppermute | solution.py:15
  6.1 4.3 %collective-permute-start = (bf16[256,128]{1,0:T(8,128)(2,1)S(1)}, bf16[256,128]{1,0:T(8,128)(2,1)S(1)}, u32[]{:S(2)}, u32[]{:S(2)}) collective-permute-start(bf16[256,128]{1,0:T(8,128)(2,1)S(1)} %get-tuple-element.20.refs_0_), channel_id=1, source_target_pairs={{0,1},{1,0},{2,3},{3,2},{4,5},{5,4},{6,7},{7,6},{8,9},{9,8},{10,11... | collective-permute-start | bytes 196616 | tf_op jit(solution)/shard_map/ppermute | solution.py:15
  11.2 6.7 %collective-permute-start.5 = (s16[1040,128]{1,0:T(8,128)(2,1)S(1)}, s16[1040,128]{1,0:T(8,128)(2,1)S(1)}, u32[]{:S(2)}, u32[]{:S(2)}) collective-permute-start(s16[1040,128]{1,0:T(8,128)(2,1)S(1)} %get-tuple-element.27), channel_id=1, source_target_pairs={{0,0},{4,8},{8,4},{12,16},{16,12},{20,24},{24,20},{28,28},{1,1},{5... | collective-permute-start | bytes 798728 | tf_op jit(solution)/shard_map/ppermute | solution.py:21
  12.7 5.2 %collective-permute-start.4 = (s16[528,128]{1,0:T(8,128)(2,1)S(1)}, s16[528,128]{1,0:T(8,128)(2,1)S(1)}, u32[]{:S(2)}, u32[]{:S(2)}) collective-permute-start(s16[528,128]{1,0:T(8,128)(2,1)S(1)} %get-tuple-element.24._), channel_id=1, source_target_pairs={{0,4},{4,0},{8,12},{12,8},{16,20},{20,16},{24,28},{28,24},{1,5},{5... | collective-permute-start | bytes 405512 | tf_op jit(solution)/shard_map/ppermute | solution.py:21
  15.7 1.4 %collective-permute-start.3 = (bf16[512,128]{1,0:T(8,128)(2,1)S(1)}, bf16[512,128]{1,0:T(8,128)(2,1)S(1)}, u32[]{:S(2)}, u32[]{:S(2)}) collective-permute-start(bf16[512,128]{1,0:T(8,128)(2,1)S(1)} %shard_map.81), channel_id=1, source_target_pairs={{0,4},{4,0},{8,12},{12,8},{16,20},{20,16},{24,28},{28,24},{1,5},{5... | collective-permute-start | bytes 393224 | tf_op jit(solution)/shard_map/ppermute | solution.py:21
  18.8 5.9 %collective-permute-start.6 = (s16[272,128]{1,0:T(8,128)(2,1)S(1)}, s16[272,128]{1,0:T(8,128)(2,1)S(1)}, u32[]{:S(2)}, u32[]{:S(2)}) collective-permute-start(s16[272,128]{1,0:T(8,128)(2,1)S(1)} %get-tuple-element.29), channel_id=1, source_target_pairs={{0,3},{1,2},{2,1},{3,0},{4,7},{5,6},{6,5},{7,4},{8,11},{9,10},{10,... | collective-permute-start | bytes 208904 | tf_op jit(solution)/shard_map/ppermute | solution.py:15
  21.5 4.8 %collective-permute-start.7 = (s16[272,128]{1,0:T(8,128)(2,1)S(1)}, s16[272,128]{1,0:T(8,128)(2,1)S(1)}, u32[]{:S(2)}, u32[]{:S(2)}) collective-permute-start(s16[272,128]{1,0:T(8,128)(2,1)S(1)} %get-tuple-element.30), channel_id=1, source_target_pairs={{0,2},{1,3},{2,0},{3,1},{4,6},{5,7},{6,4},{7,5},{8,10},{9,11},{10,... | collective-permute-start | bytes 208904 | tf_op jit(solution)/shard_map/ppermute | solution.py:15
  21.5 4.8 %collective-permute-start.8 = (s16[272,128]{1,0:T(8,128)(2,1)S(1)}, s16[272,128]{1,0:T(8,128)(2,1)S(1)}, u32[]{:S(2)}, u32[]{:S(2)}) collective-permute-start(s16[272,128]{1,0:T(8,128)(2,1)S(1)} %get-tuple-element.31), channel_id=1, source_target_pairs={{0,1},{1,0},{2,3},{3,2},{4,5},{5,4},{6,7},{7,6},{8,9},{9,8},{10,11... | collective-permute-start | bytes 208904 | tf_op jit(solution)/shard_map/ppermute | solution.py:15

commit v18 on v15

--- a/solution.py
+++ b/solution.py
@@ -409,7 +409,8 @@
         (shape(2 * blocks * panels, width),) + (coded(2 * blocks),) * (clusters - 1),
         parts_args,
     )
-    parts = [exchange(parts[k - 1], "clu", k) for k in range(clusters - 1, 0, -1)]
+    order = sorted(range(1, clusters), key=lambda k: -k.bit_count())
+    parts = [exchange(parts[k - 1], "clu", k) for k in order]
     out = shape(blocks * panels, width)
     return tuple(call(functools.partial(finish_kernel, blocks, panels), (out, out), (mine, *parts)))
 

time: 27.4 us -> 27.5 us (level)
  waiting for transfers between devices: 5.01 us -> 5.97 us
  Pallas kernels: 8.41 us -> 8.05 us
    ppermute x6, waiting for transfers between devices: 5 us -> 5.96 us  [exchange(): lax.ppermute(value, axis, [(i, i ^ step) for i in range(lax.axis_size(axi...]
    pallas_call x8, Pallas kernels: 8.41 us -> 8.05 us  [call(): pl.pallas_call(body, out_shape=shapes, input_output_aliases=dict(aliases)...]
  transfers between devices with their start and end apart: 9 -> 9, of which waited for: 4 -> 5; matrix products, arithmetic and copies ran while one was open for 0% -> 0% of each run, Pallas kernels for 21% -> 20%
where the time goes in v18:
time: 27.5 us; the launch traced here: 27.3 us
  starting transfers between devices  11.9 us (43%)
  Pallas kernels  8.05 us (29%)
  waiting for transfers between devices  5.97 us (22%)
  between operations  1.4 us (5%)
    ppermute x6, starting transfers between devices, exchange(): lax.ppermute(value, axis, [(i, i ^ step) for i in range(lax.axis_size(axi...  8.16 us
    pallas_call x8, Pallas kernels, call(): pl.pallas_call(body, out_shape=shapes, input_output_aliases=dict(aliases)...  8.05 us
    ppermute x6, waiting for transfers between devices, exchange(): lax.ppermute(value, axis, [(i, i ^ step) for i in range(lax.axis_size(axi...  5.96 us
    ppermute x3, starting transfers between devices, exchange_beside(): lax.ppermute(value, 'grp', [(i, j if 0 <= j < groups else i) for i, j in...  3.74 us
  transfers between devices with their start and end apart: 9, of which 5 were waited for; matrix products, arithmetic and copies ran while one was open for 0% of the time, Pallas kernels for 20%

profile of v18, /device:TPU:0, one launch (start us, length us, event | category | flops | bytes accessed | tf_op | source)
XLA Modules:
  0.0 27.3 jit_solution(16873657791134115146)
XLA Ops:
  0.6 1.0 %shard_map.77 = (bf16[256,128]{1,0:T(8,128)(2,1)S(1)}, s32[192]{0:T(256)S(4)}, s32[192]{0:T(256)S(4)}, f32[48,256,128]{2,1,0:T(8,128)S(1)}) custom-call(bf16[128,128]{1,0:T(8,128)(2,1)} %strengths_ref.1, bf16[128,128]{1,0:T(8,128)(2,1)} %weights_ref.1, s32[192]{0:T(256)} %target_ref.1, s32[192]{0:T(256)} %source_ref.1), custom_call_target="tpu_custom_call" | custom-call | flops 17179869184 | bytes 1048576 | tf_op jit(solution)/shard_map/pallas_call | solution.py:306
  1.6 4.0 %collective-permute-start.2 = (bf16[256,128]{1,0:T(8,128)(2,1)S(1)}, bf16[256,128]{1,0:T(8,128)(2,1)S(1)}, u32[]{:S(2)}, u32[]{:S(2)}) collective-permute-start(bf16[256,128]{1,0:T(8,128)(2,1)S(1)} %get-tuple-element.20.refs_0_), channel_id=1, source_target_pairs={{0,3},{1,2},{2,1},{3,0},{4,7},{5,6},{6,5},{7,4},{8,11},{9,10},{10,... | collective-permute-start | bytes 196616 | tf_op jit(solution)/shard_map/ppermute | solution.py:15
  5.6 0.5 %collective-permute-start.1 = (bf16[256,128]{1,0:T(8,128)(2,1)S(1)}, bf16[256,128]{1,0:T(8,128)(2,1)S(1)}, u32[]{:S(2)}, u32[]{:S(2)}) collective-permute-start(bf16[256,128]{1,0:T(8,128)(2,1)S(1)} %get-tuple-element.20.refs_0_), channel_id=1, source_target_pairs={{0,2},{1,3},{2,0},{3,1},{4,6},{5,7},{6,4},{7,5},{8,10},{9,11},{10,... | collective-permute-start | bytes 196616 | tf_op jit(solution)/shard_map/ppermute | solution.py:15
  6.1 0.1 collective-permute-start
  6.9 2.0 %shard_map.78._.total = f32[48,256,128]{2,1,0:T(8,128)S(1)} custom-call(s32[1]{0:T(128)S(6)} %copy.10.live_ref, s32[192]{0:T(256)S(4)} %get-tuple-element.17.target_ref, s32[192]{0:T(256)S(4)} %get-tuple-element.18.source_ref, bf16[192,2,128,128]{3,2,1,0:T(8,128)(2,1)S(1)} %copy-done, ...), custom_call_target="tpu_custom_call", output_to_operand_aliasing={{}: (4, {})} | custom-call | flops 8589934592 | bytes 1048576 | tf_op jit(solution)/shard_map/pallas_call | solution.py:306
  8.9 0.0 collective-permute-done.2.refs_3_
  8.9 1.0 %collective-permute-done.1.refs_2_ = bf16[256,128]{1,0:T(8,128)(2,1)S(1)} collective-permute-done((bf16[256,128]{1,0:T(8,128)(2,1)S(1)}, bf16[256,128]{1,0:T(8,128)(2,1)S(1)}, u32[]{:S(2)}, u32[]{:S(2)}) %collective-permute-start.1) | collective-permute-done | bytes 65568 | tf_op jit(solution)/shard_map/ppermute | solution.py:15
  9.9 0.5 %collective-permute-done.refs_1_ = bf16[256,128]{1,0:T(8,128)(2,1)S(1)} collective-permute-done((bf16[256,128]{1,0:T(8,128)(2,1)S(1)}, bf16[256,128]{1,0:T(8,128)(2,1)S(1)}, u32[]{:S(2)}, u32[]{:S(2)}) %collective-permute-start) | collective-permute-done | bytes 65568 | tf_op jit(solution)/shard_map/ppermute | solution.py:15
  10.4 0.1 collective-permute-start.3
  10.5 0.8 %shard_map.80 = (bf16[2,16,256,128]{3,2,1,0:T(8,128)(2,1)S(1)}, bf16[128,1024]{1,0:T(8,128)(2,1)S(1)}, s16[1040,128]{1,0:T(8,128)(2,1)S(1)}) custom-call(bf16[512,128]{1,0:T(8,128)(2,1)S(1)} %shard_map.79._, f32[48,256,128]{2,1,0:T(8,128)S(1)} %shard_map.78._.total, bf16[256,128]{1,0:T(8,128)(2,1)S(1)} %get-tuple-element.20.refs_0_, ...), custom_call_target="tpu_custom_call" | custom-call | flops 8589934592 | bytes 1048576 | tf_op jit(solution)/shard_map/pallas_call | solution.py:306
  11.3 0.7 %collective-permute-start.5 = (s16[1040,128]{1,0:T(8,128)(2,1)S(1)}, s16[1040,128]{1,0:T(8,128)(2,1)S(1)}, u32[]{:S(2)}, u32[]{:S(2)}) collective-permute-start(s16[1040,128]{1,0:T(8,128)(2,1)S(1)} %get-tuple-element.27), channel_id=1, source_target_pairs={{0,0},{4,8},{8,4},{12,16},{16,12},{20,24},{24,20},{28,28},{1,1},{5... | collective-permute-start | bytes 798728 | tf_op jit(solution)/shard_map/ppermute | solution.py:21
  12.0 0.0 collective-permute-done.3._.first_ref
  12.0 0.8 %shard_map.81 = (bf16[2,16,256,128]{3,2,1,0:T(8,128)(2,1)S(1)}, s16[528,128]{1,0:T(8,128)(2,1)S(1)}) custom-call(bf16[512,128]{1,0:T(8,128)(2,1)S(1)} %collective-permute-done.3._.first_ref, f32[48,256,128]{2,1,0:T(8,128)S(1)} %shard_map.78._.total, bf16[128,1024]{1,0:T(8,128)(2,1)S(1)} %get-tuple-element.22.across_ref), custom_call_target="tpu_custom_call" | custom-call | flops 8589934592 | bytes 1048576 | tf_op jit(solution)/shard_map/pallas_call | solution.py:306
  12.8 3.0 %collective-permute-start.4 = (s16[528,128]{1,0:T(8,128)(2,1)S(1)}, s16[528,128]{1,0:T(8,128)(2,1)S(1)}, u32[]{:S(2)}, u32[]{:S(2)}) collective-permute-start(s16[528,128]{1,0:T(8,128)(2,1)S(1)} %get-tuple-element.26), channel_id=1, source_target_pairs={{0,4},{4,0},{8,12},{12,8},{16,20},{20,16},{24,28},{28,24},{1,5},{5... | collective-permute-start | bytes 405512 | tf_op jit(solution)/shard_map/ppermute | solution.py:21
  15.8 1.8 %shard_map.82 = (f32[4,128,128]{2,1,0:T(8,128)S(1)}, f32[4,128,128]{2,1,0:T(8,128)S(1)}) custom-call(f32[48,256,128]{2,1,0:T(8,128)S(1)} %shard_map.78._.total, bf16[128,1024]{1,0:T(8,128)(2,1)S(1)} %get-tuple-element.22.across_ref, bf16[2,16,256,128]{3,2,1,0:T(8,128)(2,1)S(1)} %get-tuple-element.23.first_pairs_ref, ...), custom_call_target="tpu_custom_call" | custom-call | bytes 1048576 | tf_op jit(solution)/shard_map/pallas_call | solution.py:306
  17.6 0.0 collective-permute-done.5.second_ref
  17.6 0.9 %shard_map.83 = (f32[256,128]{1,0:T(8,128)S(1)}, s16[272,128]{1,0:T(8,128)(2,1)S(1)}, s16[272,128]{1,0:T(8,128)(2,1)S(1)}, s16[272,128]{1,0:T(8,128)(2,1)S(1)}) custom-call(bf16[2,16,256,128]{3,2,1,0:T(8,128)(2,1)S(1)} %get-tuple-element.21.pairs_ref, f32[4,128,128]{2,1,0:T(8,128)S(1)} %get-tuple-element.24.potential_ref, ...), custom_call_target="tpu_custom_call" | custom-call | bytes 1048576 | tf_op jit(solution)/shard_map/pallas_call | solution.py:306
  18.5 2.5 %collective-permute-start.6 = (s16[272,128]{1,0:T(8,128)(2,1)S(1)}, s16[272,128]{1,0:T(8,128)(2,1)S(1)}, u32[]{:S(2)}, u32[]{:S(2)}) collective-permute-start(s16[272,128]{1,0:T(8,128)(2,1)S(1)} %get-tuple-element.29), channel_id=1, source_target_pairs={{0,3},{1,2},{2,1},{3,0},{4,7},{5,6},{6,5},{7,4},{8,11},{9,10},{10,... | collective-permute-start | bytes 208904 | tf_op jit(solution)/shard_map/ppermute | solution.py:15
  21.1 0.5 %collective-permute-start.7 = (s16[272,128]{1,0:T(8,128)(2,1)S(1)}, s16[272,128]{1,0:T(8,128)(2,1)S(1)}, u32[]{:S(2)}, u32[]{:S(2)}) collective-permute-start(s16[272,128]{1,0:T(8,128)(2,1)S(1)} %get-tuple-element.30), channel_id=1, source_target_pairs={{0,1},{1,0},{2,3},{3,2},{4,5},{5,4},{6,7},{7,6},{8,9},{9,8},{10,11... | collective-permute-start | bytes 208904 | tf_op jit(solution)/shard_map/ppermute | solution.py:15
  21.6 0.5 %collective-permute-start.8 = (s16[272,128]{1,0:T(8,128)(2,1)S(1)}, s16[272,128]{1,0:T(8,128)(2,1)S(1)}, u32[]{:S(2)}, u32[]{:S(2)}) collective-permute-start(s16[272,128]{1,0:T(8,128)(2,1)S(1)} %get-tuple-element.31), channel_id=1, source_target_pairs={{0,2},{1,3},{2,0},{3,1},{4,6},{5,7},{6,4},{7,5},{8,10},{9,11},{10,... | collective-permute-start | bytes 208904 | tf_op jit(solution)/shard_map/ppermute | solution.py:15
  22.1 1.7 %collective-permute-done.6.refs_0_ = s16[272,128]{1,0:T(8,128)(2,1)S(1)} collective-permute-done((s16[272,128]{1,0:T(8,128)(2,1)S(1)}, s16[272,128]{1,0:T(8,128)(2,1)S(1)}, u32[]{:S(2)}, u32[]{:S(2)}) %collective-permute-start.6) | collective-permute-done | bytes 69664 | tf_op jit(solution)/shard_map/ppermute | solution.py:15
  23.8 1.8 %collective-permute-done.7.refs_1_ = s16[272,128]{1,0:T(8,128)(2,1)S(1)} collective-permute-done((s16[272,128]{1,0:T(8,128)(2,1)S(1)}, s16[272,128]{1,0:T(8,128)(2,1)S(1)}, u32[]{:S(2)}, u32[]{:S(2)}) %collective-permute-start.7) | collective-permute-done | bytes 69664 | tf_op jit(solution)/shard_map/ppermute | solution.py:15
  25.6 1.0 %collective-permute-done.8.refs_2_ = s16[272,128]{1,0:T(8,128)(2,1)S(1)} collective-permute-done((s16[272,128]{1,0:T(8,128)(2,1)S(1)}, s16[272,128]{1,0:T(8,128)(2,1)S(1)}, u32[]{:S(2)}, u32[]{:S(2)}) %collective-permute-start.8) | collective-permute-done | bytes 69664 | tf_op jit(solution)/shard_map/ppermute | solution.py:15
  26.6 0.7 %shard_map.84 = (f32[128,128]{1,0:T(8,128)}, f32[128,128]{1,0:T(8,128)}) custom-call(f32[256,128]{1,0:T(8,128)S(1)} %get-tuple-element.28.own_ref, s16[272,128]{1,0:T(8,128)(2,1)S(1)} %collective-permute-done.6.refs_0_, s16[272,128]{1,0:T(8,128)(2,1)S(1)} %collective-permute-done.7.refs_1_, s16[272,128]{1,0:T(8,128)(2,1)S(1)} %collective-permute-done.8.refs_2_), custom_call_target="tpu_custom_call" | custom-call | bytes 1048576 | tf_op jit(solution)/shard_map/pallas_call | solution.py:306
  (4 shorter events, 0.0 us)
Async XLA Ops:
  0.6 6.3 %copy-start = (bf16[192,2,128,128]{3,2,1,0:T(8,128)(2,1)S(1)}, bf16[192,2,128,128]{3,2,1,0:T(8,128)(2,1)}, u32[]{:S(2)}) copy-start(bf16[192,2,128,128]{3,2,1,0:T(8,128)(2,1)} %kernels_ref.1) | copy-start | bytes 37748740
  1.6 7.3 %collective-permute-start.2 = (bf16[256,128]{1,0:T(8,128)(2,1)S(1)}, bf16[256,128]{1,0:T(8,128)(2,1)S(1)}, u32[]{:S(2)}, u32[]{:S(2)}) collective-permute-start(bf16[256,128]{1,0:T(8,128)(2,1)S(1)} %get-tuple-element.20.refs_0_), channel_id=1, source_target_pairs={{0,3},{1,2},{2,1},{3,0},{4,7},{5,6},{6,5},{7,4},{8,11},{9,10},{10,... | collective-permute-start | bytes 196616 | tf_op jit(solution)/shard_map/ppermute | solution.py:15
  5.6 4.3 %collective-permute-start.1 = (bf16[256,128]{1,0:T(8,128)(2,1)S(1)}, bf16[256,128]{1,0:T(8,128)(2,1)S(1)}, u32[]{:S(2)}, u32[]{:S(2)}) collective-permute-start(bf16[256,128]{1,0:T(8,128)(2,1)S(1)} %get-tuple-element.20.refs_0_), channel_id=1, source_target_pairs={{0,2},{1,3},{2,0},{3,1},{4,6},{5,7},{6,4},{7,5},{8,10},{9,11},{10,... | collective-permute-start | bytes 196616 | tf_op jit(solution)/shard_map/ppermute | solution.py:15
  6.1 4.3 %collective-permute-start = (bf16[256,128]{1,0:T(8,128)(2,1)S(1)}, bf16[256,128]{1,0:T(8,128)(2,1)S(1)}, u32[]{:S(2)}, u32[]{:S(2)}) collective-permute-start(bf16[256,128]{1,0:T(8,128)(2,1)S(1)} %get-tuple-element.20.refs_0_), channel_id=1, source_target_pairs={{0,1},{1,0},{2,3},{3,2},{4,5},{5,4},{6,7},{7,6},{8,9},{9,8},{10,11... | collective-permute-start | bytes 196616 | tf_op jit(solution)/shard_map/ppermute | solution.py:15
  10.4 1.6 %collective-permute-start.3 = (bf16[512,128]{1,0:T(8,128)(2,1)S(1)}, bf16[512,128]{1,0:T(8,128)(2,1)S(1)}, u32[]{:S(2)}, u32[]{:S(2)}) collective-permute-start(bf16[512,128]{1,0:T(8,128)(2,1)S(1)} %shard_map.79._), channel_id=1, source_target_pairs={{0,4},{4,0},{8,12},{12,8},{16,20},{20,16},{24,28},{28,24},{1,5},{5... | collective-permute-start | bytes 393224 | tf_op jit(solution)/shard_map/ppermute | solution.py:21
  11.3 6.3 %collective-permute-start.5 = (s16[1040,128]{1,0:T(8,128)(2,1)S(1)}, s16[1040,128]{1,0:T(8,128)(2,1)S(1)}, u32[]{:S(2)}, u32[]{:S(2)}) collective-permute-start(s16[1040,128]{1,0:T(8,128)(2,1)S(1)} %get-tuple-element.27), channel_id=1, source_target_pairs={{0,0},{4,8},{8,4},{12,16},{16,12},{20,24},{24,20},{28,28},{1,1},{5... | collective-permute-start | bytes 798728 | tf_op jit(solution)/shard_map/ppermute | solution.py:21
  12.8 4.8 %collective-permute-start.4 = (s16[528,128]{1,0:T(8,128)(2,1)S(1)}, s16[528,128]{1,0:T(8,128)(2,1)S(1)}, u32[]{:S(2)}, u32[]{:S(2)}) collective-permute-start(s16[528,128]{1,0:T(8,128)(2,1)S(1)} %get-tuple-element.26), channel_id=1, source_target_pairs={{0,4},{4,0},{8,12},{12,8},{16,20},{20,16},{24,28},{28,24},{1,5},{5... | collective-permute-start | bytes 405512 | tf_op jit(solution)/shard_map/ppermute | solution.py:21
  18.5 5.3 %collective-permute-start.6 = (s16[272,128]{1,0:T(8,128)(2,1)S(1)}, s16[272,128]{1,0:T(8,128)(2,1)S(1)}, u32[]{:S(2)}, u32[]{:S(2)}) collective-permute-start(s16[272,128]{1,0:T(8,128)(2,1)S(1)} %get-tuple-element.29), channel_id=1, source_target_pairs={{0,3},{1,2},{2,1},{3,0},{4,7},{5,6},{6,5},{7,4},{8,11},{9,10},{10,... | collective-permute-start | bytes 208904 | tf_op jit(solution)/shard_map/ppermute | solution.py:15
  21.1 4.5 %collective-permute-start.7 = (s16[272,128]{1,0:T(8,128)(2,1)S(1)}, s16[272,128]{1,0:T(8,128)(2,1)S(1)}, u32[]{:S(2)}, u32[]{:S(2)}) collective-permute-start(s16[272,128]{1,0:T(8,128)(2,1)S(1)} %get-tuple-element.30), channel_id=1, source_target_pairs={{0,1},{1,0},{2,3},{3,2},{4,5},{5,4},{6,7},{7,6},{8,9},{9,8},{10,11... | collective-permute-start | bytes 208904 | tf_op jit(solution)/shard_map/ppermute | solution.py:15
  21.6 5.0 %collective-permute-start.8 = (s16[272,128]{1,0:T(8,128)(2,1)S(1)}, s16[272,128]{1,0:T(8,128)(2,1)S(1)}, u32[]{:S(2)}, u32[]{:S(2)}) collective-permute-start(s16[272,128]{1,0:T(8,128)(2,1)S(1)} %get-tuple-element.31), channel_id=1, source_target_pairs={{0,2},{1,3},{2,0},{3,1},{4,6},{5,7},{6,4},{7,5},{8,10},{9,11},{10,... | collective-permute-start | bytes 208904 | tf_op jit(solution)/shard_map/ppermute | solution.py:15

commit v19 on v15

--- a/solution.py
+++ b/solution.py
@@ -297,7 +297,7 @@
     group_blocks = clusters * blocks
     sources = 3 * group_blocks
     pairs = group_blocks * sources
-    chunk = 8 if slots % 8 == 0 else 1
+    chunk = 16 if slots % 16 == 0 else 1
     in_vmem, in_smem, in_hbm = (pl.BlockSpec(memory_space=m) for m in (pltpu.VMEM, pltpu.SMEM, pltpu.HBM))
     f32, bf16 = jnp.float32, jnp.bfloat16
 

time: 27.4 us -> 27.4 us (level); the launches traced: 27 us -> 27.3 us
  waiting for transfers between devices: 5.01 us -> 5.32 us
  Pallas kernels: 8.41 us -> 8.69 us
    ppermute x6, waiting for transfers between devices: 5 us -> 5.32 us  [exchange(): lax.ppermute(value, axis, [(i, i ^ step) for i in range(lax.axis_size(axi...]
    pallas_call x8, Pallas kernels: 8.41 us -> 8.69 us  [call(): pl.pallas_call(body, out_shape=shapes, input_output_aliases=dict(aliases)...]
  transfers between devices with their start and end apart: 9 -> 9, of which waited for: 4 -> 5; matrix products, arithmetic and copies ran while one was open for 0% -> 0% of each run, Pallas kernels for 21% -> 22%
where the time goes in v19:
time: 27.4 us; the launch traced here: 27.3 us
  starting transfers between devices  11.9 us (43%)
  Pallas kernels  8.69 us (32%)
  waiting for transfers between devices  5.32 us (19%)
  between operations  1.4 us (5%)
    pallas_call x8, Pallas kernels, call(): pl.pallas_call(body, out_shape=shapes, input_output_aliases=dict(aliases)...  8.69 us
    ppermute x6, starting transfers between devices, exchange(): lax.ppermute(value, axis, [(i, i ^ step) for i in range(lax.axis_size(axi...  8.16 us
    ppermute x6, waiting for transfers between devices, exchange(): lax.ppermute(value, axis, [(i, i ^ step) for i in range(lax.axis_size(axi...  5.32 us
    ppermute x3, starting transfers between devices, exchange_beside(): lax.ppermute(value, 'grp', [(i, j if 0 <= j < groups else i) for i, j in...  3.74 us
  transfers between devices with their start and end apart: 9, of which 5 were waited for; matrix products, arithmetic and copies ran while one was open for 0% of the time, Pallas kernels for 22%

profile of v19, /device:TPU:0, one launch (start us, length us, event | category | flops | bytes accessed | tf_op | source)
XLA Modules:
  0.0 27.3 jit_solution(8245566760790054600)
XLA Ops:
  0.6 1.0 %shard_map.77 = (bf16[256,128]{1,0:T(8,128)(2,1)S(1)}, s32[192]{0:T(256)S(4)}, s32[192]{0:T(256)S(4)}, f32[48,256,128]{2,1,0:T(8,128)S(1)}) custom-call(bf16[128,128]{1,0:T(8,128)(2,1)} %strengths_ref.1, bf16[128,128]{1,0:T(8,128)(2,1)} %weights_ref.1, s32[192]{0:T(256)} %target_ref.1, s32[192]{0:T(256)} %source_ref.1), custom_call_target="tpu_custom_call" | custom-call | flops 17179869184 | bytes 1048576 | tf_op jit(solution)/shard_map/pallas_call | solution.py:306
  1.6 4.0 %collective-permute-start.2 = (bf16[256,128]{1,0:T(8,128)(2,1)S(1)}, bf16[256,128]{1,0:T(8,128)(2,1)S(1)}, u32[]{:S(2)}, u32[]{:S(2)}) collective-permute-start(bf16[256,128]{1,0:T(8,128)(2,1)S(1)} %get-tuple-element.20.refs_0_), channel_id=1, source_target_pairs={{0,3},{1,2},{2,1},{3,0},{4,7},{5,6},{6,5},{7,4},{8,11},{9,10},{10,... | collective-permute-start | bytes 196616 | tf_op jit(solution)/shard_map/ppermute | solution.py:15
  5.6 0.5 %collective-permute-start.1 = (bf16[256,128]{1,0:T(8,128)(2,1)S(1)}, bf16[256,128]{1,0:T(8,128)(2,1)S(1)}, u32[]{:S(2)}, u32[]{:S(2)}) collective-permute-start(bf16[256,128]{1,0:T(8,128)(2,1)S(1)} %get-tuple-element.20.refs_0_), channel_id=1, source_target_pairs={{0,2},{1,3},{2,0},{3,1},{4,6},{5,7},{6,4},{7,5},{8,10},{9,11},{10,... | collective-permute-start | bytes 196616 | tf_op jit(solution)/shard_map/ppermute | solution.py:15
  6.1 0.1 collective-permute-start
  6.9 2.6 %shard_map.78._.total = f32[48,256,128]{2,1,0:T(8,128)S(1)} custom-call(s32[1]{0:T(128)S(6)} %copy.10.live_ref, s32[192]{0:T(256)S(4)} %get-tuple-element.17.target_ref, s32[192]{0:T(256)S(4)} %get-tuple-element.18.source_ref, bf16[192,2,128,128]{3,2,1,0:T(8,128)(2,1)S(1)} %copy-done, ...), custom_call_target="tpu_custom_call", output_to_operand_aliasing={{}: (4, {})} | custom-call | flops 8589934592 | bytes 1048576 | tf_op jit(solution)/shard_map/pallas_call | solution.py:306
  9.5 0.0 collective-permute-done.2.refs_3_
  9.5 0.3 %collective-permute-done.1.refs_2_ = bf16[256,128]{1,0:T(8,128)(2,1)S(1)} collective-permute-done((bf16[256,128]{1,0:T(8,128)(2,1)S(1)}, bf16[256,128]{1,0:T(8,128)(2,1)S(1)}, u32[]{:S(2)}, u32[]{:S(2)}) %collective-permute-start.1) | collective-permute-done | bytes 65568 | tf_op jit(solution)/shard_map/ppermute | solution.py:15
  9.9 0.5 %collective-permute-done.refs_1_ = bf16[256,128]{1,0:T(8,128)(2,1)S(1)} collective-permute-done((bf16[256,128]{1,0:T(8,128)(2,1)S(1)}, bf16[256,128]{1,0:T(8,128)(2,1)S(1)}, u32[]{:S(2)}, u32[]{:S(2)}) %collective-permute-start) | collective-permute-done | bytes 65568 | tf_op jit(solution)/shard_map/ppermute | solution.py:15
  10.4 0.1 collective-permute-start.3
  10.5 0.8 %shard_map.80 = (bf16[2,16,256,128]{3,2,1,0:T(8,128)(2,1)S(1)}, bf16[128,1024]{1,0:T(8,128)(2,1)S(1)}, s16[1040,128]{1,0:T(8,128)(2,1)S(1)}) custom-call(bf16[512,128]{1,0:T(8,128)(2,1)S(1)} %shard_map.79._, f32[48,256,128]{2,1,0:T(8,128)S(1)} %shard_map.78._.total, bf16[256,128]{1,0:T(8,128)(2,1)S(1)} %get-tuple-element.20.refs_0_, ...), custom_call_target="tpu_custom_call" | custom-call | flops 8589934592 | bytes 1048576 | tf_op jit(solution)/shard_map/pallas_call | solution.py:306
  11.3 0.7 %collective-permute-start.5 = (s16[1040,128]{1,0:T(8,128)(2,1)S(1)}, s16[1040,128]{1,0:T(8,128)(2,1)S(1)}, u32[]{:S(2)}, u32[]{:S(2)}) collective-permute-start(s16[1040,128]{1,0:T(8,128)(2,1)S(1)} %get-tuple-element.27), channel_id=1, source_target_pairs={{0,0},{4,8},{8,4},{12,16},{16,12},{20,24},{24,20},{28,28},{1,1},{5... | collective-permute-start | bytes 798728 | tf_op jit(solution)/shard_map/ppermute | solution.py:21
  12.0 0.0 collective-permute-done.3._.first_ref
  12.0 0.8 %shard_map.81 = (bf16[2,16,256,128]{3,2,1,0:T(8,128)(2,1)S(1)}, s16[528,128]{1,0:T(8,128)(2,1)S(1)}) custom-call(bf16[512,128]{1,0:T(8,128)(2,1)S(1)} %collective-permute-done.3._.first_ref, f32[48,256,128]{2,1,0:T(8,128)S(1)} %shard_map.78._.total, bf16[128,1024]{1,0:T(8,128)(2,1)S(1)} %get-tuple-element.22.across_ref), custom_call_target="tpu_custom_call" | custom-call | flops 8589934592 | bytes 1048576 | tf_op jit(solution)/shard_map/pallas_call | solution.py:306
  12.8 3.0 %collective-permute-start.4 = (s16[528,128]{1,0:T(8,128)(2,1)S(1)}, s16[528,128]{1,0:T(8,128)(2,1)S(1)}, u32[]{:S(2)}, u32[]{:S(2)}) collective-permute-start(s16[528,128]{1,0:T(8,128)(2,1)S(1)} %get-tuple-element.26), channel_id=1, source_target_pairs={{0,4},{4,0},{8,12},{12,8},{16,20},{20,16},{24,28},{28,24},{1,5},{5... | collective-permute-start | bytes 405512 | tf_op jit(solution)/shard_map/ppermute | solution.py:21
  15.8 1.8 %shard_map.82 = (f32[4,128,128]{2,1,0:T(8,128)S(1)}, f32[4,128,128]{2,1,0:T(8,128)S(1)}) custom-call(f32[48,256,128]{2,1,0:T(8,128)S(1)} %shard_map.78._.total, bf16[128,1024]{1,0:T(8,128)(2,1)S(1)} %get-tuple-element.22.across_ref, bf16[2,16,256,128]{3,2,1,0:T(8,128)(2,1)S(1)} %get-tuple-element.23.first_pairs_ref, ...), custom_call_target="tpu_custom_call" | custom-call | bytes 1048576 | tf_op jit(solution)/shard_map/pallas_call | solution.py:306
  17.6 0.0 collective-permute-done.5.second_ref
  17.6 0.9 %shard_map.83 = (f32[256,128]{1,0:T(8,128)S(1)}, s16[272,128]{1,0:T(8,128)(2,1)S(1)}, s16[272,128]{1,0:T(8,128)(2,1)S(1)}, s16[272,128]{1,0:T(8,128)(2,1)S(1)}) custom-call(bf16[2,16,256,128]{3,2,1,0:T(8,128)(2,1)S(1)} %get-tuple-element.21.pairs_ref, f32[4,128,128]{2,1,0:T(8,128)S(1)} %get-tuple-element.24.potential_ref, ...), custom_call_target="tpu_custom_call" | custom-call | bytes 1048576 | tf_op jit(solution)/shard_map/pallas_call | solution.py:306
  18.5 2.4 %collective-permute-start.6 = (s16[272,128]{1,0:T(8,128)(2,1)S(1)}, s16[272,128]{1,0:T(8,128)(2,1)S(1)}, u32[]{:S(2)}, u32[]{:S(2)}) collective-permute-start(s16[272,128]{1,0:T(8,128)(2,1)S(1)} %get-tuple-element.29), channel_id=1, source_target_pairs={{0,3},{1,2},{2,1},{3,0},{4,7},{5,6},{6,5},{7,4},{8,11},{9,10},{10,... | collective-permute-start | bytes 208904 | tf_op jit(solution)/shard_map/ppermute | solution.py:15
  20.9 0.8 %collective-permute-start.7 = (s16[272,128]{1,0:T(8,128)(2,1)S(1)}, s16[272,128]{1,0:T(8,128)(2,1)S(1)}, u32[]{:S(2)}, u32[]{:S(2)}) collective-permute-start(s16[272,128]{1,0:T(8,128)(2,1)S(1)} %get-tuple-element.30), channel_id=1, source_target_pairs={{0,2},{1,3},{2,0},{3,1},{4,6},{5,7},{6,4},{7,5},{8,10},{9,11},{10,... | collective-permute-start | bytes 208904 | tf_op jit(solution)/shard_map/ppermute | solution.py:15
  21.7 0.4 %collective-permute-start.8 = (s16[272,128]{1,0:T(8,128)(2,1)S(1)}, s16[272,128]{1,0:T(8,128)(2,1)S(1)}, u32[]{:S(2)}, u32[]{:S(2)}) collective-permute-start(s16[272,128]{1,0:T(8,128)(2,1)S(1)} %get-tuple-element.31), channel_id=1, source_target_pairs={{0,1},{1,0},{2,3},{3,2},{4,5},{5,4},{6,7},{7,6},{8,9},{9,8},{10,11... | collective-permute-start | bytes 208904 | tf_op jit(solution)/shard_map/ppermute | solution.py:15
  22.1 1.7 %collective-permute-done.6.refs_0_ = s16[272,128]{1,0:T(8,128)(2,1)S(1)} collective-permute-done((s16[272,128]{1,0:T(8,128)(2,1)S(1)}, s16[272,128]{1,0:T(8,128)(2,1)S(1)}, u32[]{:S(2)}, u32[]{:S(2)}) %collective-permute-start.6) | collective-permute-done | bytes 69664 | tf_op jit(solution)/shard_map/ppermute | solution.py:15
  23.8 2.4 %collective-permute-done.7.refs_1_ = s16[272,128]{1,0:T(8,128)(2,1)S(1)} collective-permute-done((s16[272,128]{1,0:T(8,128)(2,1)S(1)}, s16[272,128]{1,0:T(8,128)(2,1)S(1)}, u32[]{:S(2)}, u32[]{:S(2)}) %collective-permute-start.7) | collective-permute-done | bytes 69664 | tf_op jit(solution)/shard_map/ppermute | solution.py:15
  26.2 0.4 %collective-permute-done.8.refs_2_ = s16[272,128]{1,0:T(8,128)(2,1)S(1)} collective-permute-done((s16[272,128]{1,0:T(8,128)(2,1)S(1)}, s16[272,128]{1,0:T(8,128)(2,1)S(1)}, u32[]{:S(2)}, u32[]{:S(2)}) %collective-permute-start.8) | collective-permute-done | bytes 69664 | tf_op jit(solution)/shard_map/ppermute | solution.py:15
  26.6 0.7 %shard_map.84 = (f32[128,128]{1,0:T(8,128)}, f32[128,128]{1,0:T(8,128)}) custom-call(f32[256,128]{1,0:T(8,128)S(1)} %get-tuple-element.28.own_ref, s16[272,128]{1,0:T(8,128)(2,1)S(1)} %collective-permute-done.6.refs_0_, s16[272,128]{1,0:T(8,128)(2,1)S(1)} %collective-permute-done.7.refs_1_, s16[272,128]{1,0:T(8,128)(2,1)S(1)} %collective-permute-done.8.refs_2_), custom_call_target="tpu_custom_call" | custom-call | bytes 1048576 | tf_op jit(solution)/shard_map/pallas_call | solution.py:306
  (4 shorter events, 0.0 us)
Async XLA Ops:
  0.6 6.3 %copy-start = (bf16[192,2,128,128]{3,2,1,0:T(8,128)(2,1)S(1)}, bf16[192,2,128,128]{3,2,1,0:T(8,128)(2,1)}, u32[]{:S(2)}) copy-start(bf16[192,2,128,128]{3,2,1,0:T(8,128)(2,1)} %kernels_ref.1) | copy-start | bytes 37748740
  1.6 7.9 %collective-permute-start.2 = (bf16[256,128]{1,0:T(8,128)(2,1)S(1)}, bf16[256,128]{1,0:T(8,128)(2,1)S(1)}, u32[]{:S(2)}, u32[]{:S(2)}) collective-permute-start(bf16[256,128]{1,0:T(8,128)(2,1)S(1)} %get-tuple-element.20.refs_0_), channel_id=1, source_target_pairs={{0,3},{1,2},{2,1},{3,0},{4,7},{5,6},{6,5},{7,4},{8,11},{9,10},{10,... | collective-permute-start | bytes 196616 | tf_op jit(solution)/shard_map/ppermute | solution.py:15
  5.6 4.3 %collective-permute-start.1 = (bf16[256,128]{1,0:T(8,128)(2,1)S(1)}, bf16[256,128]{1,0:T(8,128)(2,1)S(1)}, u32[]{:S(2)}, u32[]{:S(2)}) collective-permute-start(bf16[256,128]{1,0:T(8,128)(2,1)S(1)} %get-tuple-element.20.refs_0_), channel_id=1, source_target_pairs={{0,2},{1,3},{2,0},{3,1},{4,6},{5,7},{6,4},{7,5},{8,10},{9,11},{10,... | collective-permute-start | bytes 196616 | tf_op jit(solution)/shard_map/ppermute | solution.py:15
  6.1 4.3 %collective-permute-start = (bf16[256,128]{1,0:T(8,128)(2,1)S(1)}, bf16[256,128]{1,0:T(8,128)(2,1)S(1)}, u32[]{:S(2)}, u32[]{:S(2)}) collective-permute-start(bf16[256,128]{1,0:T(8,128)(2,1)S(1)} %get-tuple-element.20.refs_0_), channel_id=1, source_target_pairs={{0,1},{1,0},{2,3},{3,2},{4,5},{5,4},{6,7},{7,6},{8,9},{9,8},{10,11... | collective-permute-start | bytes 196616 | tf_op jit(solution)/shard_map/ppermute | solution.py:15
  10.4 1.6 %collective-permute-start.3 = (bf16[512,128]{1,0:T(8,128)(2,1)S(1)}, bf16[512,128]{1,0:T(8,128)(2,1)S(1)}, u32[]{:S(2)}, u32[]{:S(2)}) collective-permute-start(bf16[512,128]{1,0:T(8,128)(2,1)S(1)} %shard_map.79._), channel_id=1, source_target_pairs={{0,4},{4,0},{8,12},{12,8},{16,20},{20,16},{24,28},{28,24},{1,5},{5... | collective-permute-start | bytes 393224 | tf_op jit(solution)/shard_map/ppermute | solution.py:21
  11.3 6.3 %collective-permute-start.5 = (s16[1040,128]{1,0:T(8,128)(2,1)S(1)}, s16[1040,128]{1,0:T(8,128)(2,1)S(1)}, u32[]{:S(2)}, u32[]{:S(2)}) collective-permute-start(s16[1040,128]{1,0:T(8,128)(2,1)S(1)} %get-tuple-element.27), channel_id=1, source_target_pairs={{0,0},{4,8},{8,4},{12,16},{16,12},{20,24},{24,20},{28,28},{1,1},{5... | collective-permute-start | bytes 798728 | tf_op jit(solution)/shard_map/ppermute | solution.py:21
  12.8 4.8 %collective-permute-start.4 = (s16[528,128]{1,0:T(8,128)(2,1)S(1)}, s16[528,128]{1,0:T(8,128)(2,1)S(1)}, u32[]{:S(2)}, u32[]{:S(2)}) collective-permute-start(s16[528,128]{1,0:T(8,128)(2,1)S(1)} %get-tuple-element.26), channel_id=1, source_target_pairs={{0,4},{4,0},{8,12},{12,8},{16,20},{20,16},{24,28},{28,24},{1,5},{5... | collective-permute-start | bytes 405512 | tf_op jit(solution)/shard_map/ppermute | solution.py:21
  18.5 5.3 %collective-permute-start.6 = (s16[272,128]{1,0:T(8,128)(2,1)S(1)}, s16[272,128]{1,0:T(8,128)(2,1)S(1)}, u32[]{:S(2)}, u32[]{:S(2)}) collective-permute-start(s16[272,128]{1,0:T(8,128)(2,1)S(1)} %get-tuple-element.29), channel_id=1, source_target_pairs={{0,3},{1,2},{2,1},{3,0},{4,7},{5,6},{6,5},{7,4},{8,11},{9,10},{10,... | collective-permute-start | bytes 208904 | tf_op jit(solution)/shard_map/ppermute | solution.py:15
  20.9 5.3 %collective-permute-start.7 = (s16[272,128]{1,0:T(8,128)(2,1)S(1)}, s16[272,128]{1,0:T(8,128)(2,1)S(1)}, u32[]{:S(2)}, u32[]{:S(2)}) collective-permute-start(s16[272,128]{1,0:T(8,128)(2,1)S(1)} %get-tuple-element.30), channel_id=1, source_target_pairs={{0,2},{1,3},{2,0},{3,1},{4,6},{5,7},{6,4},{7,5},{8,10},{9,11},{10,... | collective-permute-start | bytes 208904 | tf_op jit(solution)/shard_map/ppermute | solution.py:15
  21.7 4.9 %collective-permute-start.8 = (s16[272,128]{1,0:T(8,128)(2,1)S(1)}, s16[272,128]{1,0:T(8,128)(2,1)S(1)}, u32[]{:S(2)}, u32[]{:S(2)}) collective-permute-start(s16[272,128]{1,0:T(8,128)(2,1)S(1)} %get-tuple-element.31), channel_id=1, source_target_pairs={{0,1},{1,0},{2,3},{3,2},{4,5},{5,4},{6,7},{7,6},{8,9},{9,8},{10,11... | collective-permute-start | bytes 208904 | tf_op jit(solution)/shard_map/ppermute | solution.py:15

commit v20 on v15

--- a/solution.py
+++ b/solution.py
@@ -98,7 +98,7 @@
 
 
 def split(total, first, out_ref):
-    @pl.loop(0, out_ref.shape[1])
+    @pl.loop(0, out_ref.shape[1], unroll=4 if out_ref.shape[1] % 4 == 0 else 1)
     def _(pair):
         value = total[first + pair]
         high = value.astype(jnp.bfloat16)

time: 27.4 us -> 27 us (0.985); the launches traced: 27 us -> 27 us
  waiting for transfers between devices: 5.01 us -> 6.48 us
  Pallas kernels: 8.41 us -> 7.18 us
    ppermute x6, waiting for transfers between devices: 5 us -> 6.47 us  [exchange(): lax.ppermute(value, axis, [(i, i ^ step) for i in range(lax.axis_size(axi...]
    pallas_call x8, Pallas kernels: 8.41 us -> 7.18 us  [call(): pl.pallas_call(body, out_shape=shapes, input_output_aliases=dict(aliases)...]
  transfers between devices with their start and end apart: 9 -> 9, of which waited for: 4 -> 5; matrix products, arithmetic and copies ran while one was open for 0% -> 0% of each run, Pallas kernels for 21% -> 17%
where the time goes in v20:
time: 27 us
  starting transfers between devices  11.9 us (44%)
  Pallas kernels  7.18 us (27%)
  waiting for transfers between devices  6.48 us (24%)
  between operations  1.4 us (5%)
    ppermute x6, starting transfers between devices, exchange(): lax.ppermute(value, axis, [(i, i ^ step) for i in range(lax.axis_size(axi...  8.16 us
    pallas_call x8, Pallas kernels, call(): pl.pallas_call(body, out_shape=shapes, input_output_aliases=dict(aliases)...  7.18 us
    ppermute x6, waiting for transfers between devices, exchange(): lax.ppermute(value, axis, [(i, i ^ step) for i in range(lax.axis_size(axi...  6.47 us
    ppermute x3, starting transfers between devices, exchange_beside(): lax.ppermute(value, 'grp', [(i, j if 0 <= j < groups else i) for i, j in...  3.73 us
  transfers between devices with their start and end apart: 9, of which 5 were waited for; matrix products, arithmetic and copies ran while one was open for 0% of the time, Pallas kernels for 17%

profile of v20, /device:TPU:0, one launch (start us, length us, event | category | flops | bytes accessed | tf_op | source)
XLA Modules:
  0.0 27.0 jit_solution(11514951236424183895)
XLA Ops:
  0.6 1.0 %shard_map.77 = (bf16[256,128]{1,0:T(8,128)(2,1)S(1)}, s32[192]{0:T(256)S(4)}, s32[192]{0:T(256)S(4)}, f32[48,256,128]{2,1,0:T(8,128)S(1)}) custom-call(bf16[128,128]{1,0:T(8,128)(2,1)} %strengths_ref.1, bf16[128,128]{1,0:T(8,128)(2,1)} %weights_ref.1, s32[192]{0:T(256)} %target_ref.1, s32[192]{0:T(256)} %source_ref.1), custom_call_target="tpu_custom_call" | custom-call | flops 17179869184 | bytes 1048576 | tf_op jit(solution)/shard_map/pallas_call | solution.py:306
  1.6 4.0 %collective-permute-start.2 = (bf16[256,128]{1,0:T(8,128)(2,1)S(1)}, bf16[256,128]{1,0:T(8,128)(2,1)S(1)}, u32[]{:S(2)}, u32[]{:S(2)}) collective-permute-start(bf16[256,128]{1,0:T(8,128)(2,1)S(1)} %get-tuple-element.20.refs_0_), channel_id=1, source_target_pairs={{0,3},{1,2},{2,1},{3,0},{4,7},{5,6},{6,5},{7,4},{8,11},{9,10},{10,... | collective-permute-start | bytes 196616 | tf_op jit(solution)/shard_map/ppermute | solution.py:15
  5.6 0.5 %collective-permute-start.1 = (bf16[256,128]{1,0:T(8,128)(2,1)S(1)}, bf16[256,128]{1,0:T(8,128)(2,1)S(1)}, u32[]{:S(2)}, u32[]{:S(2)}) collective-permute-start(bf16[256,128]{1,0:T(8,128)(2,1)S(1)} %get-tuple-element.20.refs_0_), channel_id=1, source_target_pairs={{0,2},{1,3},{2,0},{3,1},{4,6},{5,7},{6,4},{7,5},{8,10},{9,11},{10,... | collective-permute-start | bytes 196616 | tf_op jit(solution)/shard_map/ppermute | solution.py:15
  6.1 0.1 collective-permute-start
  6.9 1.3 %shard_map.78._.total = f32[48,256,128]{2,1,0:T(8,128)S(1)} custom-call(s32[1]{0:T(128)S(6)} %copy.10.live_ref, s32[192]{0:T(256)S(4)} %get-tuple-element.17.target_ref, s32[192]{0:T(256)S(4)} %get-tuple-element.18.source_ref, bf16[192,2,128,128]{3,2,1,0:T(8,128)(2,1)S(1)} %copy-done, ...), custom_call_target="tpu_custom_call", output_to_operand_aliasing={{}: (4, {})} | custom-call | flops 8589934592 | bytes 1048576 | tf_op jit(solution)/shard_map/pallas_call | solution.py:306
  8.2 0.0 collective-permute-done.2.refs_3_
  8.2 1.7 %collective-permute-done.1.refs_2_ = bf16[256,128]{1,0:T(8,128)(2,1)S(1)} collective-permute-done((bf16[256,128]{1,0:T(8,128)(2,1)S(1)}, bf16[256,128]{1,0:T(8,128)(2,1)S(1)}, u32[]{:S(2)}, u32[]{:S(2)}) %collective-permute-start.1) | collective-permute-done | bytes 65568 | tf_op jit(solution)/shard_map/ppermute | solution.py:15
  9.9 0.5 %collective-permute-done.refs_1_ = bf16[256,128]{1,0:T(8,128)(2,1)S(1)} collective-permute-done((bf16[256,128]{1,0:T(8,128)(2,1)S(1)}, bf16[256,128]{1,0:T(8,128)(2,1)S(1)}, u32[]{:S(2)}, u32[]{:S(2)}) %collective-permute-start) | collective-permute-done | bytes 65568 | tf_op jit(solution)/shard_map/ppermute | solution.py:15
  10.4 0.1 collective-permute-start.3
  10.5 0.8 %shard_map.80 = (bf16[2,16,256,128]{3,2,1,0:T(8,128)(2,1)S(1)}, bf16[128,1024]{1,0:T(8,128)(2,1)S(1)}, s16[1040,128]{1,0:T(8,128)(2,1)S(1)}) custom-call(bf16[512,128]{1,0:T(8,128)(2,1)S(1)} %shard_map.79._, f32[48,256,128]{2,1,0:T(8,128)S(1)} %shard_map.78._.total, bf16[256,128]{1,0:T(8,128)(2,1)S(1)} %get-tuple-element.20.refs_0_, ...), custom_call_target="tpu_custom_call" | custom-call | flops 8589934592 | bytes 1048576 | tf_op jit(solution)/shard_map/pallas_call | solution.py:306
  11.2 0.7 %collective-permute-start.5 = (s16[1040,128]{1,0:T(8,128)(2,1)S(1)}, s16[1040,128]{1,0:T(8,128)(2,1)S(1)}, u32[]{:S(2)}, u32[]{:S(2)}) collective-permute-start(s16[1040,128]{1,0:T(8,128)(2,1)S(1)} %get-tuple-element.27), channel_id=1, source_target_pairs={{0,0},{4,8},{8,4},{12,16},{16,12},{20,24},{24,20},{28,28},{1,1},{5... | collective-permute-start | bytes 798728 | tf_op jit(solution)/shard_map/ppermute | solution.py:21
  11.9 0.0 collective-permute-done.3._.first_ref
  11.9 0.7 %shard_map.81 = (bf16[2,16,256,128]{3,2,1,0:T(8,128)(2,1)S(1)}, s16[528,128]{1,0:T(8,128)(2,1)S(1)}) custom-call(bf16[512,128]{1,0:T(8,128)(2,1)S(1)} %collective-permute-done.3._.first_ref, f32[48,256,128]{2,1,0:T(8,128)S(1)} %shard_map.78._.total, bf16[128,1024]{1,0:T(8,128)(2,1)S(1)} %get-tuple-element.22.across_ref), custom_call_target="tpu_custom_call" | custom-call | flops 8589934592 | bytes 1048576 | tf_op jit(solution)/shard_map/pallas_call | solution.py:306
  12.7 3.0 %collective-permute-start.4 = (s16[528,128]{1,0:T(8,128)(2,1)S(1)}, s16[528,128]{1,0:T(8,128)(2,1)S(1)}, u32[]{:S(2)}, u32[]{:S(2)}) collective-permute-start(s16[528,128]{1,0:T(8,128)(2,1)S(1)} %get-tuple-element.26), channel_id=1, source_target_pairs={{0,4},{4,0},{8,12},{12,8},{16,20},{20,16},{24,28},{28,24},{1,5},{5... | collective-permute-start | bytes 405512 | tf_op jit(solution)/shard_map/ppermute | solution.py:21
  15.7 1.8 %shard_map.82 = (f32[4,128,128]{2,1,0:T(8,128)S(1)}, f32[4,128,128]{2,1,0:T(8,128)S(1)}) custom-call(f32[48,256,128]{2,1,0:T(8,128)S(1)} %shard_map.78._.total, bf16[128,1024]{1,0:T(8,128)(2,1)S(1)} %get-tuple-element.22.across_ref, bf16[2,16,256,128]{3,2,1,0:T(8,128)(2,1)S(1)} %get-tuple-element.23.first_pairs_ref, ...), custom_call_target="tpu_custom_call" | custom-call | bytes 1048576 | tf_op jit(solution)/shard_map/pallas_call | solution.py:306
  17.4 0.0 collective-permute-done.5.second_ref
  17.5 0.9 %shard_map.83 = (f32[256,128]{1,0:T(8,128)S(1)}, s16[272,128]{1,0:T(8,128)(2,1)S(1)}, s16[272,128]{1,0:T(8,128)(2,1)S(1)}, s16[272,128]{1,0:T(8,128)(2,1)S(1)}) custom-call(bf16[2,16,256,128]{3,2,1,0:T(8,128)(2,1)S(1)} %get-tuple-element.21.pairs_ref, f32[4,128,128]{2,1,0:T(8,128)S(1)} %get-tuple-element.24.potential_ref, ...), custom_call_target="tpu_custom_call" | custom-call | bytes 1048576 | tf_op jit(solution)/shard_map/pallas_call | solution.py:306
  18.3 1.6 %collective-permute-start.6 = (s16[272,128]{1,0:T(8,128)(2,1)S(1)}, s16[272,128]{1,0:T(8,128)(2,1)S(1)}, u32[]{:S(2)}, u32[]{:S(2)}) collective-permute-start(s16[272,128]{1,0:T(8,128)(2,1)S(1)} %get-tuple-element.29), channel_id=1, source_target_pairs={{0,3},{1,2},{2,1},{3,0},{4,7},{5,6},{6,5},{7,4},{8,11},{9,10},{10,... | collective-permute-start | bytes 208904 | tf_op jit(solution)/shard_map/ppermute | solution.py:15
  19.9 1.3 %collective-permute-start.7 = (s16[272,128]{1,0:T(8,128)(2,1)S(1)}, s16[272,128]{1,0:T(8,128)(2,1)S(1)}, u32[]{:S(2)}, u32[]{:S(2)}) collective-permute-start(s16[272,128]{1,0:T(8,128)(2,1)S(1)} %get-tuple-element.30), channel_id=1, source_target_pairs={{0,2},{1,3},{2,0},{3,1},{4,6},{5,7},{6,4},{7,5},{8,10},{9,11},{10,... | collective-permute-start | bytes 208904 | tf_op jit(solution)/shard_map/ppermute | solution.py:15
  21.2 0.7 %collective-permute-start.8 = (s16[272,128]{1,0:T(8,128)(2,1)S(1)}, s16[272,128]{1,0:T(8,128)(2,1)S(1)}, u32[]{:S(2)}, u32[]{:S(2)}) collective-permute-start(s16[272,128]{1,0:T(8,128)(2,1)S(1)} %get-tuple-element.31), channel_id=1, source_target_pairs={{0,1},{1,0},{2,3},{3,2},{4,5},{5,4},{6,7},{7,6},{8,9},{9,8},{10,11... | collective-permute-start | bytes 208904 | tf_op jit(solution)/shard_map/ppermute | solution.py:15
  21.9 1.7 %collective-permute-done.6.refs_0_ = s16[272,128]{1,0:T(8,128)(2,1)S(1)} collective-permute-done((s16[272,128]{1,0:T(8,128)(2,1)S(1)}, s16[272,128]{1,0:T(8,128)(2,1)S(1)}, u32[]{:S(2)}, u32[]{:S(2)}) %collective-permute-start.6) | collective-permute-done | bytes 69664 | tf_op jit(solution)/shard_map/ppermute | solution.py:15
  23.6 1.9 %collective-permute-done.7.refs_1_ = s16[272,128]{1,0:T(8,128)(2,1)S(1)} collective-permute-done((s16[272,128]{1,0:T(8,128)(2,1)S(1)}, s16[272,128]{1,0:T(8,128)(2,1)S(1)}, u32[]{:S(2)}, u32[]{:S(2)}) %collective-permute-start.7) | collective-permute-done | bytes 69664 | tf_op jit(solution)/shard_map/ppermute | solution.py:15
  25.5 0.7 %collective-permute-done.8.refs_2_ = s16[272,128]{1,0:T(8,128)(2,1)S(1)} collective-permute-done((s16[272,128]{1,0:T(8,128)(2,1)S(1)}, s16[272,128]{1,0:T(8,128)(2,1)S(1)}, u32[]{:S(2)}, u32[]{:S(2)}) %collective-permute-start.8) | collective-permute-done | bytes 69664 | tf_op jit(solution)/shard_map/ppermute | solution.py:15
  26.2 0.7 %shard_map.84 = (f32[128,128]{1,0:T(8,128)}, f32[128,128]{1,0:T(8,128)}) custom-call(f32[256,128]{1,0:T(8,128)S(1)} %get-tuple-element.28.own_ref, s16[272,128]{1,0:T(8,128)(2,1)S(1)} %collective-permute-done.6.refs_0_, s16[272,128]{1,0:T(8,128)(2,1)S(1)} %collective-permute-done.7.refs_1_, s16[272,128]{1,0:T(8,128)(2,1)S(1)} %collective-permute-done.8.refs_2_), custom_call_target="tpu_custom_call" | custom-call | bytes 1048576 | tf_op jit(solution)/shard_map/pallas_call | solution.py:306
  (4 shorter events, 0.0 us)
Async XLA Ops:
  0.6 6.3 %copy-start = (bf16[192,2,128,128]{3,2,1,0:T(8,128)(2,1)S(1)}, bf16[192,2,128,128]{3,2,1,0:T(8,128)(2,1)}, u32[]{:S(2)}) copy-start(bf16[192,2,128,128]{3,2,1,0:T(8,128)(2,1)} %kernels_ref.1) | copy-start | bytes 37748740
  1.6 6.6 %collective-permute-start.2 = (bf16[256,128]{1,0:T(8,128)(2,1)S(1)}, bf16[256,128]{1,0:T(8,128)(2,1)S(1)}, u32[]{:S(2)}, u32[]{:S(2)}) collective-permute-start(bf16[256,128]{1,0:T(8,128)(2,1)S(1)} %get-tuple-element.20.refs_0_), channel_id=1, source_target_pairs={{0,3},{1,2},{2,1},{3,0},{4,7},{5,6},{6,5},{7,4},{8,11},{9,10},{10,... | collective-permute-start | bytes 196616 | tf_op jit(solution)/shard_map/ppermute | solution.py:15
  5.6 4.3 %collective-permute-start.1 = (bf16[256,128]{1,0:T(8,128)(2,1)S(1)}, bf16[256,128]{1,0:T(8,128)(2,1)S(1)}, u32[]{:S(2)}, u32[]{:S(2)}) collective-permute-start(bf16[256,128]{1,0:T(8,128)(2,1)S(1)} %get-tuple-element.20.refs_0_), channel_id=1, source_target_pairs={{0,2},{1,3},{2,0},{3,1},{4,6},{5,7},{6,4},{7,5},{8,10},{9,11},{10,... | collective-permute-start | bytes 196616 | tf_op jit(solution)/shard_map/ppermute | solution.py:15
  6.1 4.3 %collective-permute-start = (bf16[256,128]{1,0:T(8,128)(2,1)S(1)}, bf16[256,128]{1,0:T(8,128)(2,1)S(1)}, u32[]{:S(2)}, u32[]{:S(2)}) collective-permute-start(bf16[256,128]{1,0:T(8,128)(2,1)S(1)} %get-tuple-element.20.refs_0_), channel_id=1, source_target_pairs={{0,1},{1,0},{2,3},{3,2},{4,5},{5,4},{6,7},{7,6},{8,9},{9,8},{10,11... | collective-permute-start | bytes 196616 | tf_op jit(solution)/shard_map/ppermute | solution.py:15
  10.4 1.6 %collective-permute-start.3 = (bf16[512,128]{1,0:T(8,128)(2,1)S(1)}, bf16[512,128]{1,0:T(8,128)(2,1)S(1)}, u32[]{:S(2)}, u32[]{:S(2)}) collective-permute-start(bf16[512,128]{1,0:T(8,128)(2,1)S(1)} %shard_map.79._), channel_id=1, source_target_pairs={{0,4},{4,0},{8,12},{12,8},{16,20},{20,16},{24,28},{28,24},{1,5},{5... | collective-permute-start | bytes 393224 | tf_op jit(solution)/shard_map/ppermute | solution.py:21
  11.2 6.2 %collective-permute-start.5 = (s16[1040,128]{1,0:T(8,128)(2,1)S(1)}, s16[1040,128]{1,0:T(8,128)(2,1)S(1)}, u32[]{:S(2)}, u32[]{:S(2)}) collective-permute-start(s16[1040,128]{1,0:T(8,128)(2,1)S(1)} %get-tuple-element.27), channel_id=1, source_target_pairs={{0,0},{4,8},{8,4},{12,16},{16,12},{20,24},{24,20},{28,28},{1,1},{5... | collective-permute-start | bytes 798728 | tf_op jit(solution)/shard_map/ppermute | solution.py:21
  12.7 4.8 %collective-permute-start.4 = (s16[528,128]{1,0:T(8,128)(2,1)S(1)}, s16[528,128]{1,0:T(8,128)(2,1)S(1)}, u32[]{:S(2)}, u32[]{:S(2)}) collective-permute-start(s16[528,128]{1,0:T(8,128)(2,1)S(1)} %get-tuple-element.26), channel_id=1, source_target_pairs={{0,4},{4,0},{8,12},{12,8},{16,20},{20,16},{24,28},{28,24},{1,5},{5... | collective-permute-start | bytes 405512 | tf_op jit(solution)/shard_map/ppermute | solution.py:21
  18.3 5.3 %collective-permute-start.6 = (s16[272,128]{1,0:T(8,128)(2,1)S(1)}, s16[272,128]{1,0:T(8,128)(2,1)S(1)}, u32[]{:S(2)}, u32[]{:S(2)}) collective-permute-start(s16[272,128]{1,0:T(8,128)(2,1)S(1)} %get-tuple-element.29), channel_id=1, source_target_pairs={{0,3},{1,2},{2,1},{3,0},{4,7},{5,6},{6,5},{7,4},{8,11},{9,10},{10,... | collective-permute-start | bytes 208904 | tf_op jit(solution)/shard_map/ppermute | solution.py:15
  19.9 5.6 %collective-permute-start.7 = (s16[272,128]{1,0:T(8,128)(2,1)S(1)}, s16[272,128]{1,0:T(8,128)(2,1)S(1)}, u32[]{:S(2)}, u32[]{:S(2)}) collective-permute-start(s16[272,128]{1,0:T(8,128)(2,1)S(1)} %get-tuple-element.30), channel_id=1, source_target_pairs={{0,2},{1,3},{2,0},{3,1},{4,6},{5,7},{6,4},{7,5},{8,10},{9,11},{10,... | collective-permute-start | bytes 208904 | tf_op jit(solution)/shard_map/ppermute | solution.py:15
  21.2 5.0 %collective-permute-start.8 = (s16[272,128]{1,0:T(8,128)(2,1)S(1)}, s16[272,128]{1,0:T(8,128)(2,1)S(1)}, u32[]{:S(2)}, u32[]{:S(2)}) collective-permute-start(s16[272,128]{1,0:T(8,128)(2,1)S(1)} %get-tuple-element.31), channel_id=1, source_target_pairs={{0,1},{1,0},{2,3},{3,2},{4,5},{5,4},{6,7},{7,6},{8,9},{9,8},{10,11... | collective-permute-start | bytes 208904 | tf_op jit(solution)/shard_map/ppermute | solution.py:15
